TPU v7x, 32 devices: a whole 2x2x4 slice. The times are simulated.
32 devices in a mesh: scen: 4 (over y, core), vox: 8 (over z, x).
Axes of the slice: x: 2, y: 2, z: 4, core: 2. Of those that a mesh axis runs over, the one named last changes fastest.
Arguments:
- dose_blocks: float32 [8, 640, 128, 128], P('scen', 'vox'), may hold values from 0 to 0.046875
- block_map: int32 [640, 2], P('vox'), may hold values from 0 to 127, as said below
- block_counts: int32 [8], P('vox'), may hold values from 10 to 80, as said below
- target: float32 [131072], P('vox'), may hold values from 0.5 to 15
- fluence_init: float32 [16384], P('vox'), may hold values from 0.5 to 1.5
Outputs:
- fluence: float32 [16384], P('vox')
- weights: float32 [8, 131072], P('scen', 'vox')
Inputs may be any that keep to these rules, and one draw needn't show every extreme that they name: `block_map`: column 0 is a row block of the slot's voxel group, 0 to 127; column 1 a beamlet block, 0 to 127; pairs may repeat. `block_counts`: the slots in use are the first ones of their group; some group uses all 80.
All inputs are finite; a program needn't handle non-finite values.
Results may differ from a plain program's by a relative error of at most 0.0003.
Values sent between devices are 32-bit elements; how exact they have to be, the bound alone decides.
No kernel may reach another device: no remote copies, remote signals or barrier semaphores. Data moves between devices by JAX's collectives and lax.ppermute only.
A program may use at most 64 MiB of HBM per device.

v0:
```python
import jax
import jax.numpy as jnp
from jax import lax
from jax.sharding import PartitionSpec as P

ROUNDS = 2
ITERS = 2


HIGHEST = lax.Precision.HIGHEST
SHARPNESS = 2.0
STEP_SIZE = 0.5


def tables(block_map, block_counts, row_blocks, beam_blocks):
    slots = jnp.arange(block_map.shape[0])
    usable = (slots < block_counts[0]).astype(jnp.float32)
    row_hot = (block_map[:, 0][:, None] == jnp.arange(row_blocks)[None, :]).astype(
        jnp.float32
    ) * usable[:, None]
    col_hot = (block_map[:, 1][:, None] == jnp.arange(beam_blocks)[None, :]).astype(jnp.float32)
    return (row_hot, col_hot)


def forward(blocks, row_hot, col_hot, copies):
    scen_here = copies.shape[0]
    side = blocks.shape[2]
    pieces = copies.reshape(scen_here, col_hot.shape[1], side)
    picked = jnp.einsum("nb,sbj->snj", col_hot, pieces, precision=HIGHEST)
    products = jnp.einsum("snij,snj->sni", blocks, picked, precision=HIGHEST)
    summed = jnp.einsum("nr,sni->sri", row_hot, products, precision=HIGHEST)
    return summed.reshape(scen_here, row_hot.shape[1] * side)


def backward(blocks, row_hot, col_hot, weighted):
    scen_here = weighted.shape[0]
    side = blocks.shape[2]
    pieces = weighted.reshape(scen_here, row_hot.shape[1], side)
    picked = jnp.einsum("nr,sri->sni", row_hot, pieces, precision=HIGHEST)
    products = jnp.einsum("snij,sni->snj", blocks, picked, precision=HIGHEST)
    summed = jnp.einsum("nb,snj->sbj", col_hot, products, precision=HIGHEST)
    return summed.reshape(scen_here, col_hot.shape[1] * side)


def scenario_weights(score):
    peak = lax.pmax(jnp.max(score, axis=0), "scen")
    total = lax.psum(jnp.sum(jnp.exp(score - peak[None, :]), axis=0), "scen")
    return jnp.exp(score - peak[None, :]) / total[None, :]


def body(dose_blocks, block_map, block_counts, target, fluence_init):
    side = dose_blocks.shape[2]
    scen_here = dose_blocks.shape[0]
    share = fluence_init.shape[0]
    beamlets = share * lax.axis_size("vox")
    row_hot, col_hot = tables(block_map, block_counts, target.shape[0] // side, beamlets // side)
    scen_total = scen_here * lax.axis_size("scen")
    weights = jnp.zeros((scen_here, target.shape[0]), jnp.float32)
    fluence = lax.all_gather(fluence_init, "vox", axis=0, tiled=True)
    for outer_round in range(ROUNDS):
        copies = jnp.broadcast_to(fluence[None, :], (scen_here, beamlets))
        for inner_step in range(ITERS):
            dose = forward(dose_blocks, row_hot, col_hot, copies)
            excess = dose - target[None, :]
            if inner_step == 0:
                weights = scenario_weights(SHARPNESS * excess * excess)
            terms = backward(dose_blocks, row_hot, col_hot, 2.0 * weights * excess)
            gradient = lax.psum(terms, "vox")
            copies = jnp.maximum(copies - STEP_SIZE * gradient, 0.0)
        fluence = lax.psum(jnp.sum(copies, axis=0), "scen") / scen_total
    result = lax.dynamic_slice_in_dim(fluence, lax.axis_index("vox") * share, share, 0)
    return (result, weights)


def solution(mesh):
    placed = (P("scen", "vox", None, None), P("vox", None), P("vox"), P("vox"), P("vox"))
    return jax.shard_map(
        body, mesh=mesh, in_specs=placed, out_specs=(P("vox"), P("scen", "vox")), check_vma=False
    )
```

profile of v0, /device:TPU:0, one launch (start us, length us, event | category | flops | bytes accessed | tf_op | source)
XLA Modules:
  0.0 662.1 jit_solution(8453983628246439179)
XLA Ops:
  7.2 0.8 slice_bitcast_fusion
  8.0 32.5 %all_gather.3 = f32[16384]{0:T(1024)S(1)} all-gather(f32[2048]{0:T(1024)} %param.9), channel_id=1, replica_groups=mesh['scen'=4,'vox'=8] {'vox'}, dimensions={0}, use_global_device_ids=true | all-gather | bytes 73728 | tf_op jit(solution)/shard_map/all_gather | solution.py:59
  41.1 0.9 copy.27
  42.3 18.9 %fusion.106 = f32[2,80,1,128]{3,2,1,0:T(1,128)S(1)} fusion(f32[2,80,128,1]{2,3,1,0:T(1,128)S(1)} %bitcast.203, f32[2,80,128,128]{3,2,1,0:T(8,128)} %param.5), kind=kOutput, calls=%fused_computation.129 | convolution fusion | flops 31457280 | bytes 10649600 | tf_op jit(solution)/shard_map/snij,snj->sni/dot_general | solution.py:30
  61.2 1.1 fusion.21
  62.4 32.1 %all-reduce.11.cloned.1.call-done = f32[128,128]{0,1:T(8,128)} async-done(((f32[128,128]{0,1:T(8,128)}), f32[128,128]{0,1:T(8,128)}) %all-reduce.11.cloned.1.call-update) | async-done | bytes 65552 | tf_op jit(solution)/shard_map/pmax | solution.py:46
  94.5 1.5 fusion.19
  96.0 0.5 all-reduce.15.cloned.1.call-start
  96.5 32.1 %all-reduce.13.cloned.1.call-done = f32[128,128]{0,1:T(8,128)} async-done(((f32[128,128]{0,1:T(8,128)}), f32[128,128]{0,1:T(8,128)}) %all-reduce.13.cloned.1.call-update) | async-done | bytes 65552 | tf_op jit(solution)/shard_map/psum | solution.py:47
  128.6 1.2 fusion.16
  129.8 11.5 %fusion.107 = f32[2,80,1,128]{3,2,1,0:T(1,128)S(1)} fusion(f32[2,80,128,1]{2,3,1,0:T(1,128)S(1)} %bitcast.213, f32[2,80,128,128]{3,2,1,0:T(8,128)} %param.5), kind=kOutput, calls=%fused_computation.130 | convolution fusion | flops 31457280 | bytes 10649600 | tf_op jit(solution)/shard_map/snij,sni->snj/dot_general | solution.py:40
  141.3 0.3 convolution_bitcast_fusion.3
  141.7 0.8 copy.84
  142.7 69.6 %all-reduce.15.cloned.1.call-done = f32[2,16384]{1,0:T(2,128)} async-done(((f32[2,16384]{1,0:T(2,128)}), f32[2,16384]{1,0:T(2,128)}) %all-reduce.15.cloned.1.call-update) | async-done | bytes 131088 | tf_op jit(solution)/shard_map/psum | solution.py:68
  212.3 1.0 fusion.93
  213.6 19.0 %fusion.108 = f32[2,80,1,128]{3,2,1,0:T(1,128)S(1)} fusion(f32[2,80,128,1]{2,3,1,0:T(1,128)S(1)} %bitcast.197, f32[2,80,128,128]{3,2,1,0:T(8,128)} %param.5), kind=kOutput, calls=%fused_computation.131 | convolution fusion | flops 31457280 | bytes 10649600 | tf_op jit(solution)/shard_map/snij,snj->sni/dot_general | solution.py:30
  232.5 0.4 fusion.2
  233.3 11.4 %fusion.109 = f32[2,80,1,128]{3,2,1,0:T(1,128)S(1)} fusion(f32[2,80,128,1]{2,3,1,0:T(1,128)S(1)} %bitcast.198, f32[2,80,128,128]{3,2,1,0:T(8,128)} %param.5), kind=kOutput, calls=%fused_computation.132 | convolution fusion | flops 31457280 | bytes 10649600 | tf_op jit(solution)/shard_map/snij,sni->snj/dot_general | solution.py:40
  244.7 0.3 convolution_bitcast_fusion.2
  245.2 0.8 copy.83
  245.9 0.4 all-reduce.19.cloned.1.call-start
  246.4 68.6 %all-reduce.17.cloned.1.call-done = f32[2,16384]{1,0:T(2,128)} async-done(((f32[2,16384]{1,0:T(2,128)}), f32[2,16384]{1,0:T(2,128)}) %all-reduce.17.cloned.1.call-update) | async-done | bytes 131088 | tf_op jit(solution)/shard_map/psum | solution.py:68
  315.0 1.8 maximum_reduce_fusion.1
  316.9 31.2 %all-reduce.19.cloned.1.call-done = f32[16384]{0:T(1024)} async-done(((f32[16384]{0:T(1024)}), f32[16384]{0:T(1024)}) %all-reduce.19.cloned.1.call-update) | async-done | bytes 65552 | tf_op jit(solution)/shard_map/psum | solution.py:70
  348.1 0.8 broadcast_multiply_fusion
  349.2 18.9 %fusion.110 = f32[2,80,1,128]{3,2,1,0:T(1,128)S(1)} fusion(f32[2,80,128,1]{2,3,1,0:T(1,128)S(1)} %bitcast.200, f32[2,80,128,128]{3,2,1,0:T(8,128)} %param.5), kind=kOutput, calls=%fused_computation.133 | convolution fusion | flops 31457280 | bytes 10649600 | tf_op jit(solution)/shard_map/snij,snj->sni/dot_general | solution.py:30
  368.2 0.4 fusion.22
  368.6 0.7 copy.32
  369.4 31.2 %all-reduce.21.cloned.1.call-done = f32[16384]{0:T(1024)} async-done(((f32[16384]{0:T(1024)}), f32[16384]{0:T(1024)}) %all-reduce.21.cloned.1.call-update) | async-done | bytes 65552 | tf_op jit(solution)/shard_map/pmax | solution.py:46
  400.6 0.9 copy.33
  401.6 0.7 copy.34
  402.4 32.2 %all-reduce.23.cloned.1.call-done = f32[16384]{0:T(1024)} async-done(((f32[16384]{0:T(1024)}), f32[16384]{0:T(1024)}) %all-reduce.23.cloned.1.call-update) | async-done | bytes 65552 | tf_op jit(solution)/shard_map/psum | solution.py:47
  434.6 0.9 copy.35
  435.5 0.3 fusion.14
  435.8 11.4 %fusion.111 = f32[2,80,1,128]{3,2,1,0:T(1,128)S(1)} fusion(f32[2,80,128,1]{2,3,1,0:T(1,128)S(1)} %bitcast.214, f32[2,80,128,128]{3,2,1,0:T(8,128)} %param.5), kind=kOutput, calls=%fused_computation.134 | convolution fusion | flops 31457280 | bytes 10649600 | tf_op jit(solution)/shard_map/snij,sni->snj/dot_general | solution.py:40
  447.3 0.3 convolution_bitcast_fusion.1
  447.7 0.8 copy.82
  448.7 69.6 %all-reduce.25.cloned.1.call-done = f32[2,16384]{1,0:T(2,128)} async-done(((f32[2,16384]{1,0:T(2,128)}), f32[2,16384]{1,0:T(2,128)}) %all-reduce.25.cloned.1.call-update) | async-done | bytes 131088 | tf_op jit(solution)/shard_map/psum | solution.py:68
  518.3 1.0 fusion.94
  519.6 19.0 %fusion.112 = f32[2,80,1,128]{3,2,1,0:T(1,128)S(1)} fusion(f32[2,80,128,1]{2,3,1,0:T(1,128)S(1)} %bitcast.202, f32[2,80,128,128]{3,2,1,0:T(8,128)} %param.5), kind=kOutput, calls=%fused_computation.135 | convolution fusion | flops 31457280 | bytes 10649600 | tf_op jit(solution)/shard_map/snij,snj->sni/dot_general | solution.py:30
  538.6 0.4 fusion.4
  539.4 11.4 %fusion.113 = f32[2,80,1,128]{3,2,1,0:T(1,128)S(1)} fusion(f32[2,80,128,1]{2,3,1,0:T(1,128)S(1)} %bitcast.194, f32[2,80,128,128]{3,2,1,0:T(8,128)} %param.5), kind=kOutput, calls=%fused_computation.136 | convolution fusion | flops 31457280 | bytes 10649600 | tf_op jit(solution)/shard_map/snij,sni->snj/dot_general | solution.py:40
  551.2 0.8 copy.81
  552.2 69.0 %all-reduce.27.cloned.1.call-done = f32[2,16384]{1,0:T(2,128)} async-done(((f32[2,16384]{1,0:T(2,128)}), f32[2,16384]{1,0:T(2,128)}) %all-reduce.27.cloned.1.call-update) | async-done | bytes 131088 | tf_op jit(solution)/shard_map/psum | solution.py:68
  621.2 1.8 maximum_reduce_fusion
  623.0 0.9 fusion.7
  623.9 29.9 %all-reduce.29.cloned.1.call-done = f32[16384]{0:T(1024)} async-done(((f32[16384]{0:T(1024)}), f32[16384]{0:T(1024)}) %all-reduce.29.cloned.1.call-update) | async-done | bytes 65552 | tf_op jit(solution)/shard_map/psum | solution.py:70
  653.8 1.3 dynamic-slice_multiply_fusion
  (46 shorter events, 3.2 us)
Async XLA Ops:
  7.2 87.3 %all-reduce.11.cloned.1.call-start = ((), (), s32[]{:S(2)}) async-start(), calls=%async_computation | async-start | bytes 131072 | tf_op jit(solution)/shard_map/pmax | solution.py:46
  62.3 66.3 %all-reduce.13.cloned.1.call-start = ((), (), s32[]{:S(2)}) async-start(), calls=%async_computation.1 | async-start | bytes 131072 | tf_op jit(solution)/shard_map/psum | solution.py:47
  96.0 116.3 %all-reduce.15.cloned.1.call-start = ((), (), s32[]{:S(2)}) async-start(), calls=%async_computation.2 | async-start | bytes 262144 | tf_op jit(solution)/shard_map/psum | solution.py:68
  129.8 102.8 %copy-start.5 = (f32[128,128]{0,1:T(8,128)S(1)}, f32[128,128]{0,1:T(8,128)}, u32[]{:S(2)}) copy-start(f32[128,128]{0,1:T(8,128)} %all-reduce.11.cloned.1.call-done) | copy-start | bytes 196612
  129.8 102.8 %copy-start.6 = (f32[128,128]{0,1:T(8,128)S(1)}, f32[128,128]{0,1:T(8,128)}, u32[]{:S(2)}) copy-start(f32[128,128]{0,1:T(8,128)} %all-reduce.13.cloned.1.call-done) | copy-start | bytes 196612
  142.5 172.6 %all-reduce.17.cloned.1.call-start = ((), (), s32[]{:S(2)}) async-start(), calls=%async_computation.3 | async-start | bytes 262144 | tf_op jit(solution)/shard_map/psum | solution.py:68
  213.6 101.5 %copy-start.1 = (f32[2,16384]{1,0:T(2,128)S(1)}, f32[2,16384]{1,0:T(2,128)}, u32[]{:S(2)}) copy-start(f32[2,16384]{1,0:T(2,128)} %all-reduce.15.cloned.1.call-done) | copy-start | bytes 393220
  245.9 102.2 %all-reduce.19.cloned.1.call-start = ((), (), s32[]{:S(2)}) async-start(), calls=%async_computation.4 | async-start | bytes 131072 | tf_op jit(solution)/shard_map/psum | solution.py:70
  316.9 83.7 %all-reduce.21.cloned.1.call-start = ((), (), s32[]{:S(2)}) async-start(), calls=%async_computation.5 | async-start | bytes 131072 | tf_op jit(solution)/shard_map/pmax | solution.py:46
  369.4 65.2 %all-reduce.23.cloned.1.call-start = ((), (), s32[]{:S(2)}) async-start(), calls=%async_computation.6 | async-start | bytes 131072 | tf_op jit(solution)/shard_map/psum | solution.py:47
  402.3 116.0 %all-reduce.25.cloned.1.call-start = ((), (), s32[]{:S(2)}) async-start(), calls=%async_computation.7 | async-start | bytes 262144 | tf_op jit(solution)/shard_map/psum | solution.py:68
  448.5 172.7 %all-reduce.27.cloned.1.call-start = ((), (), s32[]{:S(2)}) async-start(), calls=%async_computation.8 | async-start | bytes 262144 | tf_op jit(solution)/shard_map/psum | solution.py:68
  519.6 101.6 %copy-start = (f32[2,16384]{1,0:T(2,128)S(1)}, f32[2,16384]{1,0:T(2,128)}, u32[]{:S(2)}) copy-start(f32[2,16384]{1,0:T(2,128)} %all-reduce.25.cloned.1.call-done) | copy-start | bytes 393220
  519.6 103.4 %copy-start.2 = (f32[16384]{0:T(1024)S(1)}, f32[16384]{0:T(1024)}, u32[]{:S(2)}) copy-start(f32[16384]{0:T(1024)} %param.8) | copy-start | bytes 196612
  519.6 103.4 %copy-start.3 = (f32[16384]{0:T(1024)S(1)}, f32[16384]{0:T(1024)}, u32[]{:S(2)}) copy-start(f32[16384]{0:T(1024)} %all-reduce.21.cloned.1.call-done) | copy-start | bytes 196612
  519.6 103.4 %copy-start.4 = (f32[16384]{0:T(1024)S(1)}, f32[16384]{0:T(1024)}, u32[]{:S(2)}) copy-start(f32[16384]{0:T(1024)} %all-reduce.23.cloned.1.call-done) | copy-start | bytes 196612
  552.0 101.8 %all-reduce.29.cloned.1.call-start = ((), (), s32[]{:S(2)}) async-start(), calls=%async_computation.9 | async-start | bytes 131072 | tf_op jit(solution)/shard_map/psum | solution.py:70
Sparse Core Ops, SparseCore 0:
  62.4 31.9 all-reduce.10
  97.5 31.0 all-reduce.12
  142.6 69.6 all-reduce.14
  246.1 68.9 all-reduce.16
  317.8 30.3 all-reduce.18
  369.5 31.0 all-reduce.20
  403.5 31.0 all-reduce.22
  448.6 69.6 all-reduce.24
  552.2 68.9 all-reduce.26
  623.4 30.3 all-reduce.28
where the time goes:
time: 668 us; the launch traced here: 662 us
  waiting for transfers between devices  466 us (70%)
  matrix products  128 us (19%)
  blocking collectives  32.5 us (5%)
  between operations  15.3 us (2%)
  other arithmetic  10.2 us (2%)
  local copies, waits for them, and re-layouts  8.54 us (1%)
    psum x4, waiting for transfers between devices, body(): gradient = lax.psum(terms, 'vox')  277 us
    dot_general x4, matrix products, forward(): products = jnp.einsum('snij,snj->sni', blocks, picked, precision=HIGHEST)  75.8 us
    psum x2, waiting for transfers between devices, scenario_weights(): total = lax.psum(jnp.sum(jnp.exp(score - peak[None, :]), axis=0), 'scen')  64.3 us
    pmax x2, waiting for transfers between devices, scenario_weights(): peak = lax.pmax(jnp.max(score, axis=0), 'scen')  63.3 us
    psum x2, waiting for transfers between devices, body(): fluence = lax.psum(jnp.sum(copies, axis=0), 'scen') / scen_total  61.1 us
    dot_general x4, matrix products, backward(): products = jnp.einsum('snij,sni->snj', blocks, picked, precision=HIGHEST)  45.8 us
    all_gather x1, blocking collectives, body(): fluence = lax.all_gather(fluence_init, 'vox', axis=0, tiled=True)  32.5 us
  transfers between devices with their start and end apart: 10, of which 10 were waited for; matrix products, arithmetic and copies ran while one was open for 0% of the time, Pallas kernels for 0%

commit v1 on v0

v1 whole, which is shorter than its diff:
```python
import functools

import jax
import jax.numpy as jnp
from jax import lax
from jax.experimental import pallas as pl
from jax.experimental.pallas import tpu as pltpu
from jax.sharding import PartitionSpec as P

ROUNDS = 2
SHARPNESS = 2.0
STEP_SIZE = 0.5
F32 = jnp.float32
BF16 = jnp.bfloat16
VMEM = pl.BlockSpec(memory_space=pltpu.VMEM)


def split3(x):
    high = x.astype(BF16)
    rest = x - high.astype(F32)
    mid = rest.astype(BF16)
    low = (rest - mid.astype(F32)).astype(BF16)
    return jnp.concatenate([high, mid, low], axis=-1)


def exact(hot, x):
    n = x.shape[1]
    y = jnp.dot(hot, split3(x), preferred_element_type=F32)
    return y[:, :n] + y[:, n : 2 * n] + y[:, 2 * n :]


def columns(x):
    pad = -x.shape[0] % 128
    if pad:
        x = jnp.concatenate([x, jnp.zeros((pad, x.shape[1]), x.dtype)], axis=0)
    return x.T


def products(blocks, vectors, rows):
    scen, slots, side, _ = blocks.shape
    for k in range(slots):
        for s in range(scen):
            if s == 0 or vectors[s] is not vectors[0]:
                wide = jnp.broadcast_to(vectors[s][:, k : k + 1], (side, side))
            rows[s, k : k + 1, :] = jnp.sum(blocks[s, k] * wide, axis=0, keepdims=True)


def merge(a, b):
    top = jnp.maximum(a, b)
    return top + jnp.log(jnp.exp(a - top) + jnp.exp(b - top))


def prepare_kernel(blocks, block_map, counts, flipped, row_hot, row_hot_t, col_hot, col_hot_t):
    scen, slots, side, _ = blocks.shape
    row_blocks, beam_blocks = row_hot.shape[1], col_hot.shape[1]
    slot = lax.broadcasted_iota(jnp.int32, (slots, row_blocks), 0)
    usable = slot < counts[0]
    rows = lax.broadcasted_iota(jnp.int32, (slots, row_blocks), 1) == block_map[:, 0:1]
    cols = lax.broadcasted_iota(jnp.int32, (slots, beam_blocks), 1) == block_map[:, 1:2]
    row = jnp.where(rows & usable, 1.0, 0.0).astype(F32)
    col = jnp.where(cols, 1.0, 0.0).astype(F32)
    row_hot[...] = row.astype(BF16)
    col_hot[...] = col.astype(BF16)
    row_hot_t[...] = columns(row)[:, :slots].astype(BF16)
    col_hot_t[...] = columns(col)[:, :slots].astype(BF16)

    def flip(k, _):
        for s in range(scen):
            flipped[s, k] = blocks[s, k].T
        return 0

    lax.fori_loop(0, slots, flip, 0)


def first_kernel(flipped, fluence, target, col_hot, row_hot_t, excess, score_sum, rows):
    scen = flipped.shape[0]
    vector = columns(exact(col_hot[...], fluence[...]))
    products(flipped, [vector] * scen, rows)
    scores = []
    for s in range(scen):
        e = exact(row_hot_t[...], rows[s]) - target[...]
        excess[s] = e
        scores.append(SHARPNESS * e * e)
    top = functools.reduce(jnp.maximum, scores)
    total = functools.reduce(jnp.add, [jnp.exp(score - top) for score in scores])
    score_sum[...] = top + jnp.log(total)


def second_kernel(blocks, excess, sum_a, sum_b, row_hot, col_hot_t, weights, gradient, rows):
    scen = blocks.shape[0]
    total = merge(sum_a[...], sum_b[...])
    vectors = []
    for s in range(scen):
        e = excess[s]
        w = jnp.exp(SHARPNESS * e * e - total)
        weights[s] = w
        vectors.append(columns(exact(row_hot[...], 2.0 * w * e)))
    products(blocks, vectors, rows)
    for s in range(scen):
        gradient[s] = exact(col_hot_t[...], rows[s])


def third_kernel(
    blocks, flipped, fluence, grad_a, grad_b, weights, target,
    col_hot, col_hot_t, row_hot, row_hot_t, copies, gradient, rows
):
    scen = blocks.shape[0]
    vectors = []
    for s in range(scen):
        c = jnp.maximum(fluence[...] - STEP_SIZE * (grad_a[s] + grad_b[s]), 0.0)
        copies[s] = c
        vectors.append(columns(exact(col_hot[...], c)))
    products(flipped, vectors, rows)
    vectors = []
    for s in range(scen):
        e = exact(row_hot_t[...], rows[s]) - target[...]
        vectors.append(columns(exact(row_hot[...], 2.0 * weights[s] * e)))
    products(blocks, vectors, rows)
    for s in range(scen):
        gradient[s] = exact(col_hot_t[...], rows[s])


def near(x):
    return pltpu.with_memory_space_constraint(x, pltpu.VMEM)


def swap(x, axis, bit):
    return lax.ppermute(x, axis, [(i, i ^ bit) for i in range(lax.axis_size(axis))])


def bits(axis):
    size = lax.axis_size(axis)
    if size & (size - 1) or size < 2:
        raise ValueError("axis size")
    return [1 << b for b in range(size.bit_length() - 1)]


def reduce_but_last(x, axis, combine):
    steps = bits(axis)
    for bit in steps[:-1]:
        x = combine(x, swap(x, axis, bit))
    return x, swap(x, axis, steps[-1])


def gather(x, axis):
    me = lax.axis_index(axis)
    for bit in bits(axis):
        other = swap(x, axis, bit)
        x = jnp.where(
            me & bit == 0, jnp.concatenate([x, other], axis=0), jnp.concatenate([other, x], axis=0)
        )
    return x


def body(dose_blocks, block_map, block_counts, target, fluence_init):
    scen, slots, side, _ = dose_blocks.shape
    share = fluence_init.shape[0]
    parts = lax.axis_size("vox")
    beam_blocks = share * parts // side
    row_blocks = target.shape[0] // side
    scen_total = scen * lax.axis_size("scen")
    params = pltpu.CompilerParams(vmem_limit_bytes=16 * 2**20)
    passes = scen * slots * side * side
    dense = lambda *shape: jax.ShapeDtypeStruct(shape, F32)
    scratch = [pltpu.VMEM((scen, slots, side), F32)]

    blocks = near(dose_blocks)
    target = target.reshape(row_blocks, side)
    flipped, row_hot, row_hot_t, col_hot, col_hot_t = pl.pallas_call(
        prepare_kernel,
        name="prepare",
        out_shape=(
            pltpu.VMEM((scen, slots, side, side), F32),
            jax.ShapeDtypeStruct((slots, row_blocks), BF16),
            jax.ShapeDtypeStruct((row_blocks, slots), BF16),
            jax.ShapeDtypeStruct((slots, beam_blocks), BF16),
            jax.ShapeDtypeStruct((beam_blocks, slots), BF16),
        ),
        in_specs=[VMEM, VMEM, pl.BlockSpec(memory_space=pltpu.SMEM)],
        out_specs=(VMEM,) * 5,
        compiler_params=params,
        cost_estimate=pl.CostEstimate(flops=passes, bytes_accessed=8 * passes, transcendentals=0),
    )(blocks, block_map, block_counts)
    flipped = near(flipped)

    fluence = gather(fluence_init.reshape(share // side, side), "vox")
    for outer_round in range(ROUNDS):
        excess, score_sum = pl.pallas_call(
            first_kernel,
            name="first",
            out_shape=(dense(scen, row_blocks, side), dense(row_blocks, side)),
            in_specs=[VMEM] * 5,
            out_specs=(VMEM,) * 2,
            scratch_shapes=scratch,
            compiler_params=params,
        )(flipped, fluence, target, col_hot, row_hot_t)
        sum_a, sum_b = reduce_but_last(score_sum, "scen", merge)
        weights, gradient = pl.pallas_call(
            second_kernel,
            name="second",
            out_shape=(dense(scen, row_blocks, side), dense(scen, beam_blocks, side)),
            in_specs=[VMEM] * 6,
            out_specs=(VMEM,) * 2,
            scratch_shapes=scratch,
            compiler_params=params,
        )(blocks, excess, sum_a, sum_b, row_hot, col_hot_t)
        grad_a, grad_b = reduce_but_last(gradient, "vox", jnp.add)
        copies, gradient = pl.pallas_call(
            third_kernel,
            name="third",
            out_shape=(dense(scen, beam_blocks, side), dense(scen, beam_blocks, side)),
            in_specs=[VMEM] * 11,
            out_specs=(VMEM,) * 2,
            scratch_shapes=scratch,
            compiler_params=params,
        )(
            blocks, flipped, fluence, grad_a, grad_b, weights, target,
            col_hot, col_hot_t, row_hot, row_hot_t,
        )
        if outer_round < ROUNDS - 1:
            grad_a, grad_b = reduce_but_last(gradient, "vox", jnp.add)
        else:
            pieces = gradient.reshape(scen, parts, share // side, side)
            pieces = lax.all_to_all(pieces, "vox", split_axis=1, concat_axis=1, tiled=True)
            grad_a, grad_b = jnp.sum(pieces, axis=1), 0.0
            start = lax.axis_index("vox") * (share // side)
            copies = lax.dynamic_slice_in_dim(copies, start, share // side, 1)
        copies = jnp.maximum(copies - STEP_SIZE * (grad_a + grad_b), 0.0)
        mean_a, mean_b = reduce_but_last(jnp.sum(copies, axis=0), "scen", jnp.add)
        fluence = (mean_a + mean_b) / scen_total
    return fluence.reshape(share), weights.reshape(scen, row_blocks * side)


def solution(mesh):
    placed = (P("scen", "vox", None, None), P("vox", None), P("vox"), P("vox"), P("vox"))
    return jax.shard_map(
        body, mesh=mesh, in_specs=placed, out_specs=(P("vox"), P("scen", "vox")), check_vma=False
    )
```

time: 668 us -> 140 us (0.21)
  waiting for transfers between devices: 466 us -> 68.2 us
  matrix products: 128 us -> 0 us
  Pallas kernels: 0 us -> 34.3 us
  blocking collectives: 32.5 us -> 0 us
  starting transfers between devices: 1.63 us -> 27.9 us
  between operations: 15.3 us -> 1.51 us
  other arithmetic: 10.2 us -> 1.66 us
    psum x8 -> x0, waiting for transfers between devices: 402 us -> none  [the longest x4 277 us: body(): gradient = lax.psum(terms, 'vox')]
    dot_general x24 -> x0, matrix products: 128 us -> none  [the longest x4 75.8 us: forward(): products = jnp.einsum('snij,snj->sni', blocks, picked, precision=HIGHEST)]
    pmax x2 -> x0, waiting for transfers between devices: 63.3 us -> none  [scenario_weights(): peak = lax.pmax(jnp.max(score, axis=0), 'scen')]
    ppermute x0 -> x20, waiting for transfers between devices: none -> 60.8 us  [swap(): lax.ppermute(x, axis, [(i, i ^ bit) for i in range(lax.axis_size(axis))])]
    pallas_call x0 -> x7, Pallas kernels: none -> 34.3 us  [the longest x2 14.5 us: body(): pl.pallas_call(third_kernel, name='third', out_shape=(dense(scen, beam_bl...]
    all_gather x1 -> x0, blocking collectives: 32.5 us -> none  [body(): fluence = lax.all_gather(fluence_init, 'vox', axis=0, tiled=True)]
    ppermute x0 -> x20, starting transfers between devices: none -> 24.4 us  [swap(): lax.ppermute(x, axis, [(i, i ^ bit) for i in range(lax.axis_size(axis))])]
    all_to_all x0 -> x1, waiting for transfers between devices: none -> 7.34 us  [body(): lax.all_to_all(pieces, 'vox', split_axis=1, concat_axis=1, tiled=True)]
  transfers between devices with their start and end apart: 10 -> 21, of which waited for: 10 -> 20; matrix products, arithmetic and copies ran while one was open for 0% -> 1% of each run, Pallas kernels for 0% -> 6%
where the time goes in v1:
time: 140 us
  waiting for transfers between devices  68.2 us (49%)
  Pallas kernels  34.3 us (24%)
  starting transfers between devices  27.9 us (20%)
  local copies, waits for them, and re-layouts  6.19 us (4%)
  other arithmetic  1.66 us (1%)
  between operations  1.51 us (1%)
    ppermute x20, waiting for transfers between devices, swap(): lax.ppermute(x, axis, [(i, i ^ bit) for i in range(lax.axis_size(axis))])  60.8 us
    ppermute x20, starting transfers between devices, swap(): lax.ppermute(x, axis, [(i, i ^ bit) for i in range(lax.axis_size(axis))])  24.4 us
    pallas_call x2, Pallas kernels, body(): pl.pallas_call(third_kernel, name='third', out_shape=(dense(scen, beam_bl...  14.5 us
    pallas_call x1, Pallas kernels, body(): pl.pallas_call(prepare_kernel, name='prepare', out_shape=(pltpu.VMEM((sce...  8.21 us
    all_to_all x1, waiting for transfers between devices, body(): lax.all_to_all(pieces, 'vox', split_axis=1, concat_axis=1, tiled=True)  7.34 us
    pallas_call x2, Pallas kernels, body(): pl.pallas_call(second_kernel, name='second', out_shape=(dense(scen, row_b...  7.07 us
    unnamed x12, local copies, waits for them, and re-layouts  5.52 us
    pallas_call x2, Pallas kernels, body(): pl.pallas_call(first_kernel, name='first', out_shape=(dense(scen, row_blo...  4.52 us
  transfers between devices with their start and end apart: 21, of which 20 were waited for; matrix products, arithmetic and copies ran while one was open for 1% of the time, Pallas kernels for 6%

profile of v1, /device:TPU:0, one launch (start us, length us, event | category | flops | bytes accessed | tf_op | source)
XLA Modules:
  0.0 139.7 jit_solution(17949001568762192832)
XLA Ops:
  0.6 3.0 %collective-permute-start = (f32[16,128]{1,0:T(8,128)}, f32[16,128]{1,0:T(8,128)S(1)}, u32[]{:S(2)}, u32[]{:S(2)}) collective-permute-start(f32[16,128]{1,0:T(8,128)} %bitcast.18), channel_id=1, source_target_pairs={{0,1},{1,0},{2,3},{3,2},{4,5},{5,4},{6,7},{7,6},{8,9},{9,8},{10,11... | collective-permute-start | bytes 24584 | tf_op jit(solution)/shard_map/ppermute | solution.py:128
  3.6 1.8 %collective-permute-done = f32[16,128]{1,0:T(8,128)S(1)} collective-permute-done((f32[16,128]{1,0:T(8,128)}, f32[16,128]{1,0:T(8,128)S(1)}, u32[]{:S(2)}, u32[]{:S(2)}) %collective-permute-start) | collective-permute-done | bytes 8224 | tf_op jit(solution)/shard_map/ppermute | solution.py:128
  5.5 0.8 maximum_select_fusion.2
  6.3 2.1 %collective-permute-start.1 = (f32[32,128]{1,0:T(8,128)S(1)}, f32[32,128]{1,0:T(8,128)S(1)}, u32[]{:S(2)}, u32[]{:S(2)}) collective-permute-start(f32[32,128]{1,0:T(8,128)S(1)} %maximum_select_fusion.2), channel_id=1, source_target_pairs={{0,2},{1,3},{2,0},{3,1},{4,6},{5,7},{6,4},{7,5},{8,10},{9,11},{10,... | collective-permute-start | bytes 49160 | tf_op jit(solution)/shard_map/ppermute | solution.py:128
  8.4 1.7 %collective-permute-done.1 = f32[32,128]{1,0:T(8,128)S(1)} collective-permute-done((f32[32,128]{1,0:T(8,128)S(1)}, f32[32,128]{1,0:T(8,128)S(1)}, u32[]{:S(2)}, u32[]{:S(2)}) %collective-permute-start.1) | collective-permute-done | bytes 16416 | tf_op jit(solution)/shard_map/ppermute | solution.py:128
  10.1 3.0 %collective-permute-start.2 = (f32[64,128]{1,0:T(8,128)S(1)}, f32[64,128]{1,0:T(8,128)S(1)}, u32[]{:S(2)}, u32[]{:S(2)}) collective-permute-start(f32[64,128]{1,0:T(8,128)S(1)} %maximum_select_fusion.1), channel_id=1, source_target_pairs={{0,4},{1,5},{2,6},{3,7},{4,0},{5,1},{6,2},{7,3},{8,12},{9,13},{10,... | collective-permute-start | bytes 98312 | tf_op jit(solution)/shard_map/ppermute | solution.py:128
  13.1 0.8 copy.8.block_map
  14.6 4.0 %copy-done = f32[2,80,128,128]{3,2,1,0:T(8,128)S(1)} copy-done((f32[2,80,128,128]{3,2,1,0:T(8,128)S(1)}, f32[2,80,128,128]{3,2,1,0:T(8,128)}, u32[]{:S(2)}) %copy-start) | copy-done | bytes 10485784
  18.5 8.2 %prepare.1 = (f32[2,80,128,128]{3,2,1,0:T(8,128)S(1)}, bf16[80,128]{1,0:T(8,128)(2,1)S(1)}, bf16[128,80]{1,0:T(8,128)(2,1)S(1)}, bf16[80,128]{1,0:T(8,128)(2,1)S(1)}, bf16[128,80]{1,0:T(8,128)(2,1)S(1)}) custom-call(f32[2,80,128,128]{3,2,1,0:T(8,128)S(1)} %copy-done, s32[80,2]{1,0:T(8,128)S(1)} %copy.8.block_map, s32[1]{0:T(128)S(6)} %copy.13.counts), custom_call_target="tpu_custom_call" | custom-call | flops 2621440 | bytes 20971520 | tf_op jit(solution)/shard_map/prepare/pallas_call | solution.py:169
  26.8 2.3 %first.2 = (f32[2,128,128]{2,1,0:T(8,128)S(1)}, f32[128,128]{1,0:T(8,128)S(1)}) custom-call(f32[2,80,128,128]{3,2,1,0:T(8,128)S(1)} %get-tuple-element.19.flipped, f32[128,128]{1,0:T(8,128)S(1)} %maximum_select_fusion.fluence, f32[128,128]{1,0:T(8,128)S(1)} %bitcast.11, bf16[80,128]{1,0:T(8,128)(2,1)S(1)} %get-tuple-element.20.col_hot, ...), custom_call_target="tpu_custom_call" | custom-call | tf_op jit(solution)/shard_map/first/pallas_call | solution.py:188
  29.2 1.2 collective-permute-done.3
  30.4 1.6 %collective-permute-start.4 = (f32[128,128]{1,0:T(8,128)S(1)}, f32[128,128]{1,0:T(8,128)S(1)}, u32[]{:S(2)}, u32[]{:S(2)}) collective-permute-start(f32[128,128]{1,0:T(8,128)S(1)} %log_add_fusion.1.sum_a), channel_id=1, source_target_pairs={{0,16},{8,24},{16,0},{24,8},{1,17},{9,25},{17,1},{25,9},{2,18},{10... | collective-permute-start | bytes 196616 | tf_op jit(solution)/shard_map/ppermute | solution.py:128
  32.0 2.7 %collective-permute-done.4.sum_b = f32[128,128]{1,0:T(8,128)S(1)} collective-permute-done((f32[128,128]{1,0:T(8,128)S(1)}, f32[128,128]{1,0:T(8,128)S(1)}, u32[]{:S(2)}, u32[]{:S(2)}) %collective-permute-start.4) | collective-permute-done | bytes 65568 | tf_op jit(solution)/shard_map/ppermute | solution.py:128
  34.8 3.5 %second.2 = (f32[2,128,128]{2,1,0:T(8,128)S(1)}, f32[2,128,128]{2,1,0:T(8,128)S(1)}) custom-call(f32[2,80,128,128]{3,2,1,0:T(8,128)S(1)} %bitcast.10, f32[2,128,128]{2,1,0:T(8,128)S(1)} %get-tuple-element.22.excess, f32[128,128]{1,0:T(8,128)S(1)} %log_add_fusion.1.sum_a, f32[128,128]{1,0:T(8,128)S(1)} %collective-permute-done.4.sum_b, ...), custom_call_target="tpu_custom_call" | custom-call | tf_op jit(solution)/shard_map/second/pallas_call | solution.py:198
  38.3 1.6 %collective-permute-start.5 = (f32[2,128,128]{2,1,0:T(8,128)S(1)}, f32[2,128,128]{2,1,0:T(8,128)S(1)}, u32[]{:S(2)}, u32[]{:S(2)}) collective-permute-start(f32[2,128,128]{2,1,0:T(8,128)S(1)} %get-tuple-element.26), channel_id=1, source_target_pairs={{0,1},{1,0},{2,3},{3,2},{4,5},{5,4},{6,7},{7,6},{8,9},{9,8},{10,11... | collective-permute-start | bytes 393224 | tf_op jit(solution)/shard_map/ppermute | solution.py:128
  39.9 3.5 %collective-permute-done.5 = f32[2,128,128]{2,1,0:T(8,128)S(1)} collective-permute-done((f32[2,128,128]{2,1,0:T(8,128)S(1)}, f32[2,128,128]{2,1,0:T(8,128)S(1)}, u32[]{:S(2)}, u32[]{:S(2)}) %collective-permute-start.5) | collective-permute-done | bytes 131104 | tf_op jit(solution)/shard_map/ppermute | solution.py:128
  43.4 1.6 %collective-permute-start.6 = (f32[2,128,128]{2,1,0:T(8,128)S(1)}, f32[2,128,128]{2,1,0:T(8,128)S(1)}, u32[]{:S(2)}, u32[]{:S(2)}) collective-permute-start(f32[2,128,128]{2,1,0:T(8,128)S(1)} %add.50), channel_id=1, source_target_pairs={{0,2},{1,3},{2,0},{3,1},{4,6},{5,7},{6,4},{7,5},{8,10},{9,11},{10,... | collective-permute-start | bytes 393224 | tf_op jit(solution)/shard_map/ppermute | solution.py:128
  45.0 3.4 %collective-permute-done.6 = f32[2,128,128]{2,1,0:T(8,128)S(1)} collective-permute-done((f32[2,128,128]{2,1,0:T(8,128)S(1)}, f32[2,128,128]{2,1,0:T(8,128)S(1)}, u32[]{:S(2)}, u32[]{:S(2)}) %collective-permute-start.6) | collective-permute-done | bytes 131104 | tf_op jit(solution)/shard_map/ppermute | solution.py:128
  48.4 0.1 collective-permute-start.7
  48.5 5.8 %collective-permute-done.7.grad_b = f32[2,128,128]{2,1,0:T(8,128)S(1)} collective-permute-done((f32[2,128,128]{2,1,0:T(8,128)S(1)}, f32[2,128,128]{2,1,0:T(8,128)S(1)}, u32[]{:S(2)}, u32[]{:S(2)}) %collective-permute-start.7) | collective-permute-done | bytes 131104 | tf_op jit(solution)/shard_map/ppermute | solution.py:128
  54.4 7.3 %third.2 = (f32[2,128,128]{2,1,0:T(8,128)S(1)}, f32[2,128,128]{2,1,0:T(8,128)S(1)}) custom-call(f32[2,80,128,128]{3,2,1,0:T(8,128)S(1)} %bitcast.10, f32[2,80,128,128]{3,2,1,0:T(8,128)S(1)} %get-tuple-element.19.flipped, f32[128,128]{1,0:T(8,128)S(1)} %maximum_select_fusion.fluence, f32[2,128,128]{2,1,0:T(8,128)S(1)} %add.51.grad_a, ...), custom_call_target="tpu_custom_call" | custom-call | tf_op jit(solution)/shard_map/third/pallas_call | solution.py:208
  61.6 1.6 %collective-permute-start.8 = (f32[2,128,128]{2,1,0:T(8,128)S(1)}, f32[2,128,128]{2,1,0:T(8,128)S(1)}, u32[]{:S(2)}, u32[]{:S(2)}) collective-permute-start(f32[2,128,128]{2,1,0:T(8,128)S(1)} %get-tuple-element.29), channel_id=1, source_target_pairs={{0,1},{1,0},{2,3},{3,2},{4,5},{5,4},{6,7},{7,6},{8,9},{9,8},{10,11... | collective-permute-start | bytes 393224 | tf_op jit(solution)/shard_map/ppermute | solution.py:128
  63.3 3.4 %collective-permute-done.8 = f32[2,128,128]{2,1,0:T(8,128)S(1)} collective-permute-done((f32[2,128,128]{2,1,0:T(8,128)S(1)}, f32[2,128,128]{2,1,0:T(8,128)S(1)}, u32[]{:S(2)}, u32[]{:S(2)}) %collective-permute-start.8) | collective-permute-done | bytes 131104 | tf_op jit(solution)/shard_map/ppermute | solution.py:128
  66.7 2.5 %collective-permute-start.9 = (f32[2,128,128]{2,1,0:T(8,128)S(1)}, f32[2,128,128]{2,1,0:T(8,128)S(1)}, u32[]{:S(2)}, u32[]{:S(2)}) collective-permute-start(f32[2,128,128]{2,1,0:T(8,128)S(1)} %add.52), channel_id=1, source_target_pairs={{0,2},{1,3},{2,0},{3,1},{4,6},{5,7},{6,4},{7,5},{8,10},{9,11},{10,... | collective-permute-start | bytes 393224 | tf_op jit(solution)/shard_map/ppermute | solution.py:128
  69.2 4.3 %collective-permute-done.9 = f32[2,128,128]{2,1,0:T(8,128)S(1)} collective-permute-done((f32[2,128,128]{2,1,0:T(8,128)S(1)}, f32[2,128,128]{2,1,0:T(8,128)S(1)}, u32[]{:S(2)}, u32[]{:S(2)}) %collective-permute-start.9) | collective-permute-done | bytes 131104 | tf_op jit(solution)/shard_map/ppermute | solution.py:128
  73.5 0.3 collective-permute-start.10
  73.8 7.3 %collective-permute-done.10 = f32[2,128,128]{2,1,0:T(8,128)S(1)} collective-permute-done((f32[2,128,128]{2,1,0:T(8,128)S(1)}, f32[2,128,128]{2,1,0:T(8,128)S(1)}, u32[]{:S(2)}, u32[]{:S(2)}) %collective-permute-start.10) | collective-permute-done | bytes 131104 | tf_op jit(solution)/shard_map/ppermute | solution.py:128
  81.1 1.2 collective-permute-done.11
  82.4 1.7 %collective-permute-start.12 = (f32[128,128]{1,0:T(8,128)S(1)}, f32[128,128]{1,0:T(8,128)S(1)}, u32[]{:S(2)}, u32[]{:S(2)}) collective-permute-start(f32[128,128]{1,0:T(8,128)S(1)} %add.55), channel_id=1, source_target_pairs={{0,16},{8,24},{16,0},{24,8},{1,17},{9,25},{17,1},{25,9},{2,18},{10... | collective-permute-start | bytes 196616 | tf_op jit(solution)/shard_map/ppermute | solution.py:128
  84.1 2.6 %collective-permute-done.12 = f32[128,128]{1,0:T(8,128)S(1)} collective-permute-done((f32[128,128]{1,0:T(8,128)S(1)}, f32[128,128]{1,0:T(8,128)S(1)}, u32[]{:S(2)}, u32[]{:S(2)}) %collective-permute-start.12) | collective-permute-done | bytes 65568 | tf_op jit(solution)/shard_map/ppermute | solution.py:128
  86.7 2.3 %first.3 = (f32[2,128,128]{2,1,0:T(8,128)S(1)}, f32[128,128]{1,0:T(8,128)S(1)}) custom-call(f32[2,80,128,128]{3,2,1,0:T(8,128)S(1)} %get-tuple-element.19.flipped, f32[128,128]{1,0:T(8,128)S(1)} %add_multiply_fusion.fluence, f32[128,128]{1,0:T(8,128)S(1)} %bitcast.13, bf16[80,128]{1,0:T(8,128)(2,1)S(1)} %get-tuple-element.20.col_hot, ...), custom_call_target="tpu_custom_call" | custom-call | tf_op jit(solution)/shard_map/first/pallas_call | solution.py:188
  89.1 1.2 collective-permute-done.13
  90.4 1.7 %collective-permute-start.14 = (f32[128,128]{1,0:T(8,128)S(1)}, f32[128,128]{1,0:T(8,128)S(1)}, u32[]{:S(2)}, u32[]{:S(2)}) collective-permute-start(f32[128,128]{1,0:T(8,128)S(1)} %log_add_fusion.sum_a), channel_id=1, source_target_pairs={{0,16},{8,24},{16,0},{24,8},{1,17},{9,25},{17,1},{25,9},{2,18},{10... | collective-permute-start | bytes 196616 | tf_op jit(solution)/shard_map/ppermute | solution.py:128
  92.1 2.6 %collective-permute-done.14.sum_b = f32[128,128]{1,0:T(8,128)S(1)} collective-permute-done((f32[128,128]{1,0:T(8,128)S(1)}, f32[128,128]{1,0:T(8,128)S(1)}, u32[]{:S(2)}, u32[]{:S(2)}) %collective-permute-start.14) | collective-permute-done | bytes 65568 | tf_op jit(solution)/shard_map/ppermute | solution.py:128
  94.7 3.5 %second.3 = (f32[2,128,128]{2,1,0:T(8,128)S(1)}, f32[2,128,128]{2,1,0:T(8,128)S(1)}) custom-call(f32[2,80,128,128]{3,2,1,0:T(8,128)S(1)} %bitcast.10, f32[2,128,128]{2,1,0:T(8,128)S(1)} %get-tuple-element.30.excess, f32[128,128]{1,0:T(8,128)S(1)} %log_add_fusion.sum_a, f32[128,128]{1,0:T(8,128)S(1)} %collective-permute-done.14.sum_b, ...), custom_call_target="tpu_custom_call" | custom-call | tf_op jit(solution)/shard_map/second/pallas_call | solution.py:198
  98.2 1.7 %collective-permute-start.15 = (f32[2,128,128]{2,1,0:T(8,128)S(1)}, f32[2,128,128]{2,1,0:T(8,128)S(1)}, u32[]{:S(2)}, u32[]{:S(2)}) collective-permute-start(f32[2,128,128]{2,1,0:T(8,128)S(1)} %get-tuple-element.32), channel_id=1, source_target_pairs={{0,1},{1,0},{2,3},{3,2},{4,5},{5,4},{6,7},{7,6},{8,9},{9,8},{10,11... | collective-permute-start | bytes 393224 | tf_op jit(solution)/shard_map/ppermute | solution.py:128
  99.9 3.4 %collective-permute-done.15 = f32[2,128,128]{2,1,0:T(8,128)S(1)} collective-permute-done((f32[2,128,128]{2,1,0:T(8,128)S(1)}, f32[2,128,128]{2,1,0:T(8,128)S(1)}, u32[]{:S(2)}, u32[]{:S(2)}) %collective-permute-start.15) | collective-permute-done | bytes 131104 | tf_op jit(solution)/shard_map/ppermute | solution.py:128
  103.4 5.0 %collective-permute-done.16 = f32[2,128,128]{2,1,0:T(8,128)S(1)} collective-permute-done((f32[2,128,128]{2,1,0:T(8,128)S(1)}, f32[2,128,128]{2,1,0:T(8,128)S(1)}, u32[]{:S(2)}, u32[]{:S(2)}) %collective-permute-start.16) | collective-permute-done | bytes 131104 | tf_op jit(solution)/shard_map/ppermute | solution.py:128
  108.4 7.0 %collective-permute-done.17.grad_b = f32[2,128,128]{2,1,0:T(8,128)S(1)} collective-permute-done((f32[2,128,128]{2,1,0:T(8,128)S(1)}, f32[2,128,128]{2,1,0:T(8,128)S(1)}, u32[]{:S(2)}, u32[]{:S(2)}) %collective-permute-start.17) | collective-permute-done | bytes 131104 | tf_op jit(solution)/shard_map/ppermute | solution.py:128
  115.5 7.3 %third.3 = (f32[2,128,128]{2,1,0:T(8,128)S(1)}, f32[2,128,128]{2,1,0:T(8,128)S(1)}) custom-call(f32[2,80,128,128]{3,2,1,0:T(8,128)S(1)} %bitcast.10, f32[2,80,128,128]{3,2,1,0:T(8,128)S(1)} %get-tuple-element.19.flipped, f32[128,128]{1,0:T(8,128)S(1)} %add_multiply_fusion.fluence, f32[2,128,128]{2,1,0:T(8,128)S(1)} %add.60.grad_a, ...), custom_call_target="tpu_custom_call" | custom-call | tf_op jit(solution)/shard_map/third/pallas_call | solution.py:208
  122.7 0.7 copy.9
  123.4 3.5 %all-to-all-start = ((f32[2,8,16,128]{3,2,0,1:T(8,128)}), f32[2,8,16,128]{3,2,0,1:T(8,128)S(1)}, u32[]{:S(2)}, u32[]{:S(2)}) async-start(f32[2,8,16,128]{3,2,0,1:T(8,128)} %copy.9), calls=%async_computation | async-start | bytes 262144 | tf_op jit(solution)/shard_map/all_to_all | solution.py:224
  126.8 7.3 %all-to-all-done = f32[2,8,16,128]{3,2,0,1:T(8,128)S(1)} async-done(((f32[2,8,16,128]{3,2,0,1:T(8,128)}), f32[2,8,16,128]{3,2,0,1:T(8,128)S(1)}, u32[]{:S(2)}, u32[]{:S(2)}) %all-to-all-start) | async-done | bytes 131104 | tf_op jit(solution)/shard_map/all_to_all | solution.py:224
  134.3 1.2 collective-permute-done.18
  135.5 1.5 %collective-permute-start.19 = (f32[16,128]{1,0:T(8,128)S(1)}, f32[16,128]{1,0:T(8,128)S(1)}, u32[]{:S(2)}, u32[]{:S(2)}) collective-permute-start(f32[16,128]{1,0:T(8,128)S(1)} %add.62), channel_id=1, source_target_pairs={{0,16},{8,24},{16,0},{24,8},{1,17},{9,25},{17,1},{25,9},{2,18},{10... | collective-permute-start | bytes 24584 | tf_op jit(solution)/shard_map/ppermute | solution.py:128
  137.0 0.8 copy.12
  137.7 1.4 collective-permute-done.19
  139.1 0.6 multiply_bitcast_fusion
  (33 shorter events, 0.7 us)
Async XLA Ops:
  0.6 26.2 %copy-start.1 = (f32[16384]{0:T(1024)S(1)}, f32[16384]{0:T(1024)}, u32[]{:S(2)}) copy-start(f32[16384]{0:T(1024)} %param.8) | copy-start | bytes 196612
  0.6 4.8 %collective-permute-start = (f32[16,128]{1,0:T(8,128)}, f32[16,128]{1,0:T(8,128)S(1)}, u32[]{:S(2)}, u32[]{:S(2)}) collective-permute-start(f32[16,128]{1,0:T(8,128)} %bitcast.18), channel_id=1, source_target_pairs={{0,1},{1,0},{2,3},{3,2},{4,5},{5,4},{6,7},{7,6},{8,9},{9,8},{10,11... | collective-permute-start | bytes 24584 | tf_op jit(solution)/shard_map/ppermute | solution.py:128
  6.3 3.8 %collective-permute-start.1 = (f32[32,128]{1,0:T(8,128)S(1)}, f32[32,128]{1,0:T(8,128)S(1)}, u32[]{:S(2)}, u32[]{:S(2)}) collective-permute-start(f32[32,128]{1,0:T(8,128)S(1)} %maximum_select_fusion.2), channel_id=1, source_target_pairs={{0,2},{1,3},{2,0},{3,1},{4,6},{5,7},{6,4},{7,5},{8,10},{9,11},{10,... | collective-permute-start | bytes 49160 | tf_op jit(solution)/shard_map/ppermute | solution.py:128
  10.1 16.7 %collective-permute-start.2 = (f32[64,128]{1,0:T(8,128)S(1)}, f32[64,128]{1,0:T(8,128)S(1)}, u32[]{:S(2)}, u32[]{:S(2)}) collective-permute-start(f32[64,128]{1,0:T(8,128)S(1)} %maximum_select_fusion.1), channel_id=1, source_target_pairs={{0,4},{1,5},{2,6},{3,7},{4,0},{5,1},{6,2},{7,3},{8,12},{9,13},{10,... | collective-permute-start | bytes 98312 | tf_op jit(solution)/shard_map/ppermute | solution.py:128
  14.5 4.0 %copy-start = (f32[2,80,128,128]{3,2,1,0:T(8,128)S(1)}, f32[2,80,128,128]{3,2,1,0:T(8,128)}, u32[]{:S(2)}) copy-start(f32[2,80,128,128]{3,2,1,0:T(8,128)} %blocks.9) | copy-start | bytes 31457284
  18.5 16.2 %slice-start = ((s8[10485760]{0:T(1024)(128)(4,1)}), s8[4194304]{0:T(1024)(128)(4,1)S(1)}, s32[]{:S(2)}) async-start(s8[10485760]{0:T(1024)(128)(4,1)} %bitcast.9), calls=%async_computation.1 | async-start | bytes 8388608
  18.5 16.2 %slice-start.1 = ((s8[10485760]{0:T(1024)(128)(4,1)}), s8[4194304]{0:T(1024)(128)(4,1)S(1)}, s32[]{:S(2)}) async-start(s8[10485760]{0:T(1024)(128)(4,1)} %bitcast.9), calls=%async_computation.2 | async-start | bytes 8388608
  26.8 8.0 %slice-start.2 = ((s8[10485760]{0:T(1024)(128)(4,1)}), s8[2097152]{0:T(1024)(128)(4,1)S(1)}, s32[]{:S(2)}) async-start(s8[10485760]{0:T(1024)(128)(4,1)} %bitcast.9), calls=%async_computation.3 | async-start | bytes 4194304
  29.1 1.3 collective-permute-start.3
  30.4 4.3 %collective-permute-start.4 = (f32[128,128]{1,0:T(8,128)S(1)}, f32[128,128]{1,0:T(8,128)S(1)}, u32[]{:S(2)}, u32[]{:S(2)}) collective-permute-start(f32[128,128]{1,0:T(8,128)S(1)} %log_add_fusion.1.sum_a), channel_id=1, source_target_pairs={{0,16},{8,24},{16,0},{24,8},{1,17},{9,25},{17,1},{25,9},{2,18},{10... | collective-permute-start | bytes 196616 | tf_op jit(solution)/shard_map/ppermute | solution.py:128
  38.3 5.0 %collective-permute-start.5 = (f32[2,128,128]{2,1,0:T(8,128)S(1)}, f32[2,128,128]{2,1,0:T(8,128)S(1)}, u32[]{:S(2)}, u32[]{:S(2)}) collective-permute-start(f32[2,128,128]{2,1,0:T(8,128)S(1)} %get-tuple-element.26), channel_id=1, source_target_pairs={{0,1},{1,0},{2,3},{3,2},{4,5},{5,4},{6,7},{7,6},{8,9},{9,8},{10,11... | collective-permute-start | bytes 393224 | tf_op jit(solution)/shard_map/ppermute | solution.py:128
  43.4 5.0 %collective-permute-start.6 = (f32[2,128,128]{2,1,0:T(8,128)S(1)}, f32[2,128,128]{2,1,0:T(8,128)S(1)}, u32[]{:S(2)}, u32[]{:S(2)}) collective-permute-start(f32[2,128,128]{2,1,0:T(8,128)S(1)} %add.50), channel_id=1, source_target_pairs={{0,2},{1,3},{2,0},{3,1},{4,6},{5,7},{6,4},{7,5},{8,10},{9,11},{10,... | collective-permute-start | bytes 393224 | tf_op jit(solution)/shard_map/ppermute | solution.py:128
  48.4 5.9 %collective-permute-start.7 = (f32[2,128,128]{2,1,0:T(8,128)S(1)}, f32[2,128,128]{2,1,0:T(8,128)S(1)}, u32[]{:S(2)}, u32[]{:S(2)}) collective-permute-start(f32[2,128,128]{2,1,0:T(8,128)S(1)} %add.51.grad_a), channel_id=1, source_target_pairs={{0,4},{1,5},{2,6},{3,7},{4,0},{5,1},{6,2},{7,3},{8,12},{9,13},{10,... | collective-permute-start | bytes 393224 | tf_op jit(solution)/shard_map/ppermute | solution.py:128
  61.6 5.0 %collective-permute-start.8 = (f32[2,128,128]{2,1,0:T(8,128)S(1)}, f32[2,128,128]{2,1,0:T(8,128)S(1)}, u32[]{:S(2)}, u32[]{:S(2)}) collective-permute-start(f32[2,128,128]{2,1,0:T(8,128)S(1)} %get-tuple-element.29), channel_id=1, source_target_pairs={{0,1},{1,0},{2,3},{3,2},{4,5},{5,4},{6,7},{7,6},{8,9},{9,8},{10,11... | collective-permute-start | bytes 393224 | tf_op jit(solution)/shard_map/ppermute | solution.py:128
  66.7 6.8 %collective-permute-start.9 = (f32[2,128,128]{2,1,0:T(8,128)S(1)}, f32[2,128,128]{2,1,0:T(8,128)S(1)}, u32[]{:S(2)}, u32[]{:S(2)}) collective-permute-start(f32[2,128,128]{2,1,0:T(8,128)S(1)} %add.52), channel_id=1, source_target_pairs={{0,2},{1,3},{2,0},{3,1},{4,6},{5,7},{6,4},{7,5},{8,10},{9,11},{10,... | collective-permute-start | bytes 393224 | tf_op jit(solution)/shard_map/ppermute | solution.py:128
  73.5 7.5 %collective-permute-start.10 = (f32[2,128,128]{2,1,0:T(8,128)S(1)}, f32[2,128,128]{2,1,0:T(8,128)S(1)}, u32[]{:S(2)}, u32[]{:S(2)}) collective-permute-start(f32[2,128,128]{2,1,0:T(8,128)S(1)} %add.53), channel_id=1, source_target_pairs={{0,4},{1,5},{2,6},{3,7},{4,0},{5,1},{6,2},{7,3},{8,12},{9,13},{10,... | collective-permute-start | bytes 393224 | tf_op jit(solution)/shard_map/ppermute | solution.py:128
  81.1 1.3 collective-permute-start.11
  82.4 4.3 %collective-permute-start.12 = (f32[128,128]{1,0:T(8,128)S(1)}, f32[128,128]{1,0:T(8,128)S(1)}, u32[]{:S(2)}, u32[]{:S(2)}) collective-permute-start(f32[128,128]{1,0:T(8,128)S(1)} %add.55), channel_id=1, source_target_pairs={{0,16},{8,24},{16,0},{24,8},{1,17},{9,25},{17,1},{25,9},{2,18},{10... | collective-permute-start | bytes 196616 | tf_op jit(solution)/shard_map/ppermute | solution.py:128
  89.0 1.3 collective-permute-start.13
  90.4 4.3 %collective-permute-start.14 = (f32[128,128]{1,0:T(8,128)S(1)}, f32[128,128]{1,0:T(8,128)S(1)}, u32[]{:S(2)}, u32[]{:S(2)}) collective-permute-start(f32[128,128]{1,0:T(8,128)S(1)} %log_add_fusion.sum_a), channel_id=1, source_target_pairs={{0,16},{8,24},{16,0},{24,8},{1,17},{9,25},{17,1},{25,9},{2,18},{10... | collective-permute-start | bytes 196616 | tf_op jit(solution)/shard_map/ppermute | solution.py:128
  98.2 5.0 %collective-permute-start.15 = (f32[2,128,128]{2,1,0:T(8,128)S(1)}, f32[2,128,128]{2,1,0:T(8,128)S(1)}, u32[]{:S(2)}, u32[]{:S(2)}) collective-permute-start(f32[2,128,128]{2,1,0:T(8,128)S(1)} %get-tuple-element.32), channel_id=1, source_target_pairs={{0,1},{1,0},{2,3},{3,2},{4,5},{5,4},{6,7},{7,6},{8,9},{9,8},{10,11... | collective-permute-start | bytes 393224 | tf_op jit(solution)/shard_map/ppermute | solution.py:128
  103.3 5.0 %collective-permute-start.16 = (f32[2,128,128]{2,1,0:T(8,128)S(1)}, f32[2,128,128]{2,1,0:T(8,128)S(1)}, u32[]{:S(2)}, u32[]{:S(2)}) collective-permute-start(f32[2,128,128]{2,1,0:T(8,128)S(1)} %add.59), channel_id=1, source_target_pairs={{0,2},{1,3},{2,0},{3,1},{4,6},{5,7},{6,4},{7,5},{8,10},{9,11},{10,... | collective-permute-start | bytes 393224 | tf_op jit(solution)/shard_map/ppermute | solution.py:128
  108.4 7.1 %collective-permute-start.17 = (f32[2,128,128]{2,1,0:T(8,128)S(1)}, f32[2,128,128]{2,1,0:T(8,128)S(1)}, u32[]{:S(2)}, u32[]{:S(2)}) collective-permute-start(f32[2,128,128]{2,1,0:T(8,128)S(1)} %add.60.grad_a), channel_id=1, source_target_pairs={{0,4},{1,5},{2,6},{3,7},{4,0},{5,1},{6,2},{7,3},{8,12},{9,13},{10,... | collective-permute-start | bytes 393224 | tf_op jit(solution)/shard_map/ppermute | solution.py:128
  123.4 10.8 %all-to-all-start = ((f32[2,8,16,128]{3,2,0,1:T(8,128)}), f32[2,8,16,128]{3,2,0,1:T(8,128)S(1)}, u32[]{:S(2)}, u32[]{:S(2)}) async-start(f32[2,8,16,128]{3,2,0,1:T(8,128)} %copy.9), calls=%async_computation | async-start | bytes 262144 | tf_op jit(solution)/shard_map/all_to_all | solution.py:224
  134.2 1.2 collective-permute-start.18
  135.5 3.7 %collective-permute-start.19 = (f32[16,128]{1,0:T(8,128)S(1)}, f32[16,128]{1,0:T(8,128)S(1)}, u32[]{:S(2)}, u32[]{:S(2)}) collective-permute-start(f32[16,128]{1,0:T(8,128)S(1)} %add.62), channel_id=1, source_target_pairs={{0,16},{8,24},{16,0},{24,8},{1,17},{9,25},{17,1},{25,9},{2,18},{10... | collective-permute-start | bytes 24584 | tf_op jit(solution)/shard_map/ppermute | solution.py:128

commit v2 on v1

--- a/solution.py
+++ b/solution.py
@@ -34,6 +34,14 @@
     if pad:
         x = jnp.concatenate([x, jnp.zeros((pad, x.shape[1]), x.dtype)], axis=0)
     return x.T
+
+
+def flat(x):
+    pad = -x.shape[1] % 128
+    slots = x.shape[1]
+    if pad:
+        x = jnp.concatenate([x, jnp.zeros((x.shape[0], pad), x.dtype)], axis=1)
+    return x.T[:slots]
 
 
 def products(blocks, vectors, rows):
@@ -50,34 +58,36 @@
     return top + jnp.log(jnp.exp(a - top) + jnp.exp(b - top))
 
 
-def prepare_kernel(blocks, block_map, counts, flipped, row_hot, row_hot_t, col_hot, col_hot_t):
-    scen, slots, side, _ = blocks.shape
-    row_blocks, beam_blocks = row_hot.shape[1], col_hot.shape[1]
-    slot = lax.broadcasted_iota(jnp.int32, (slots, row_blocks), 0)
-    usable = slot < counts[0]
-    rows = lax.broadcasted_iota(jnp.int32, (slots, row_blocks), 1) == block_map[:, 0:1]
-    cols = lax.broadcasted_iota(jnp.int32, (slots, beam_blocks), 1) == block_map[:, 1:2]
+def flip_kernel(blocks, flipped):
+    scen, slots, _, _ = blocks.shape
+    group = next(n for n in (8, 4, 2, 1) if slots % n == 0)
+
+    def flip(t, _):
+        for u in range(group):
+            for s in range(scen):
+                flipped[s, t * group + u] = blocks[s, t * group + u].T
+        return 0
+
+    lax.fori_loop(0, slots // group, flip, 0)
+
+
+def hot_kernel(block_map, counts, row_hot, row_hot_t, col_hot, col_hot_t):
+    row_blocks, slots = row_hot_t.shape
+    usable = lax.broadcasted_iota(jnp.int32, (row_blocks, slots), 1) < counts[0]
+    rows = lax.broadcasted_iota(jnp.int32, (row_blocks, slots), 0) == block_map[0:1, :]
     row = jnp.where(rows & usable, 1.0, 0.0).astype(F32)
+    beam_blocks = col_hot_t.shape[0]
+    cols = lax.broadcasted_iota(jnp.int32, (beam_blocks, slots), 0) == block_map[1:2, :]
     col = jnp.where(cols, 1.0, 0.0).astype(F32)
-    row_hot[...] = row.astype(BF16)
-    col_hot[...] = col.astype(BF16)
-    row_hot_t[...] = columns(row)[:, :slots].astype(BF16)
-    col_hot_t[...] = columns(col)[:, :slots].astype(BF16)
-
-    def flip(k, _):
-        for s in range(scen):
-            flipped[s, k] = blocks[s, k].T
-        return 0
-
-    lax.fori_loop(0, slots, flip, 0)
-
-
-def first_kernel(flipped, fluence, target, col_hot, row_hot_t, excess, score_sum, rows):
-    scen = flipped.shape[0]
-    vector = columns(exact(col_hot[...], fluence[...]))
-    products(flipped, [vector] * scen, rows)
+    row_hot_t[...] = row.astype(BF16)
+    col_hot_t[...] = col.astype(BF16)
+    row_hot[...] = flat(row).astype(BF16)
+    col_hot[...] = flat(col).astype(BF16)
+
+
+def finish_first(rows, target, row_hot_t, excess, score_sum):
     scores = []
-    for s in range(scen):
+    for s in range(len(rows)):
         e = exact(row_hot_t[...], rows[s]) - target[...]
         excess[s] = e
         scores.append(SHARPNESS * e * e)
@@ -86,8 +96,38 @@
     score_sum[...] = top + jnp.log(total)
 
 
+def first_kernel(flipped, fluence, target, col_hot, row_hot_t, excess, score_sum, rows):
+    scen = flipped.shape[0]
+    vector = columns(exact(col_hot[...], fluence[...]))
+    products(flipped, [vector] * scen, rows)
+    finish_first([rows[s] for s in range(scen)], target, row_hot_t, excess, score_sum)
+
+
+def open_kernel(sizes, source, fluence, target, col_hot, row_hot_t, blocks, excess, score_sum, sems):
+    scen, slots, side, _ = source.shape
+    copies, first = [], 0
+    for n, size in enumerate(sizes):
+        part = pl.ds(first, size)
+        copies.append(pltpu.make_async_copy(source.at[:, part], blocks.at[:, part], sems.at[n]))
+        first += size
+    for copy in copies:
+        copy.start()
+    picked = exact(col_hot[...], fluence[...])
+    lane = lax.broadcasted_iota(jnp.int32, (side, -(-slots // 128) * 128), 1)
+    sums = [jnp.zeros(lane.shape, F32) for _ in range(scen)]
+    first = 0
+    for copy, size in zip(copies, sizes):
+        copy.wait()
+        for k in range(first, first + size):
+            for s in range(scen):
+                total = jnp.sum(blocks[s, k] * picked[k : k + 1, :], axis=1, keepdims=True)
+                sums[s] = jnp.where(lane == k, total, sums[s])
+        first += size
+    finish_first([x.T[:slots] for x in sums], target, row_hot_t, excess, score_sum)
+
+
 def second_kernel(blocks, excess, sum_a, sum_b, row_hot, col_hot_t, weights, gradient, rows):
-    scen = blocks.shape[0]
+    scen = excess.shape[0]
     total = merge(sum_a[...], sum_b[...])
     vectors = []
     for s in range(scen):
@@ -104,7 +144,7 @@
     blocks, flipped, fluence, grad_a, grad_b, weights, target,
     col_hot, col_hot_t, row_hot, row_hot_t, copies, gradient, rows
 ):
-    scen = blocks.shape[0]
+    scen = weights.shape[0]
     vectors = []
     for s in range(scen):
         c = jnp.maximum(fluence[...] - STEP_SIZE * (grad_a[s] + grad_b[s]), 0.0)
@@ -135,21 +175,30 @@
     return [1 << b for b in range(size.bit_length() - 1)]
 
 
-def reduce_but_last(x, axis, combine):
-    steps = bits(axis)
+def reduce_vox(x):
+    steps = bits("vox")
     for bit in steps[:-1]:
-        x = combine(x, swap(x, axis, bit))
-    return x, swap(x, axis, steps[-1])
-
-
-def gather(x, axis):
-    me = lax.axis_index(axis)
-    for bit in bits(axis):
-        other = swap(x, axis, bit)
-        x = jnp.where(
-            me & bit == 0, jnp.concatenate([x, other], axis=0), jnp.concatenate([other, x], axis=0)
-        )
+        x = x + swap(x, "vox", bit)
+    return x, swap(x, "vox", steps[-1])
+
+
+def reduce_scen(x, combine):
+    steps = bits("scen")
+    x = [x, swap(x, "scen", steps[0])]
+    for bit in steps[1:]:
+        both = combine(*x)
+        x = [both, swap(both, "scen", bit ^ 1)]
     return x
+
+
+def swap_both(x, bit):
+    scen, vox = lax.axis_size("scen"), lax.axis_size("vox")
+    pairs = [(s * vox + v, (s ^ 1) * vox + (v ^ bit)) for s in range(scen) for v in range(vox)]
+    return lax.ppermute(x, ("scen", "vox"), pairs)
+
+
+def split(total, parts):
+    return [total * (n + 1) // parts - total * n // parts for n in range(parts)]
 
 
 def body(dose_blocks, block_map, block_counts, target, fluence_init):
@@ -164,37 +213,71 @@
     dense = lambda *shape: jax.ShapeDtypeStruct(shape, F32)
     scratch = [pltpu.VMEM((scen, slots, side), F32)]
 
-    blocks = near(dose_blocks)
     target = target.reshape(row_blocks, side)
-    flipped, row_hot, row_hot_t, col_hot, col_hot_t = pl.pallas_call(
-        prepare_kernel,
-        name="prepare",
+    row_hot, row_hot_t, col_hot, col_hot_t = pl.pallas_call(
+        hot_kernel,
+        name="hot",
         out_shape=(
-            pltpu.VMEM((scen, slots, side, side), F32),
             jax.ShapeDtypeStruct((slots, row_blocks), BF16),
             jax.ShapeDtypeStruct((row_blocks, slots), BF16),
             jax.ShapeDtypeStruct((slots, beam_blocks), BF16),
             jax.ShapeDtypeStruct((beam_blocks, slots), BF16),
         ),
-        in_specs=[VMEM, VMEM, pl.BlockSpec(memory_space=pltpu.SMEM)],
-        out_specs=(VMEM,) * 5,
+        in_specs=[VMEM, pl.BlockSpec(memory_space=pltpu.SMEM)],
+        out_specs=(VMEM,) * 4,
         compiler_params=params,
-        cost_estimate=pl.CostEstimate(flops=passes, bytes_accessed=8 * passes, transcendentals=0),
-    )(blocks, block_map, block_counts)
-    flipped = near(flipped)
-
-    fluence = gather(fluence_init.reshape(share // side, side), "vox")
+    )(block_map.T, block_counts)
+
+    fluence = fluence_init.reshape(share // side, side)
+    me = lax.axis_index("vox")
+    for bit in bits("vox"):
+        other = swap_both(fluence, bit)
+        fluence = jnp.where(
+            me & bit == 0,
+            jnp.concatenate([fluence, other], axis=0),
+            jnp.concatenate([other, fluence], axis=0),
+        )
+
+    whole = pltpu.VMEM((scen, slots, side, side), F32)
     for outer_round in range(ROUNDS):
-        excess, score_sum = pl.pallas_call(
-            first_kernel,
-            name="first",
-            out_shape=(dense(scen, row_blocks, side), dense(row_blocks, side)),
-            in_specs=[VMEM] * 5,
-            out_specs=(VMEM,) * 2,
-            scratch_shapes=scratch,
-            compiler_params=params,
-        )(flipped, fluence, target, col_hot, row_hot_t)
-        sum_a, sum_b = reduce_but_last(score_sum, "scen", merge)
+        if outer_round == 0:
+            sizes = split(slots, 10)
+            blocks, excess, score_sum = pl.pallas_call(
+                functools.partial(open_kernel, sizes),
+                name="open",
+                out_shape=(whole, dense(scen, row_blocks, side), dense(row_blocks, side)),
+                in_specs=[pl.BlockSpec(memory_space=pltpu.HBM)] + [VMEM] * 4,
+                out_specs=(VMEM,) * 3,
+                scratch_shapes=[pltpu.SemaphoreType.DMA((len(sizes),))],
+                compiler_params=params,
+            )(
+                pltpu.with_memory_space_constraint(dose_blocks, pltpu.HBM),
+                fluence, target, col_hot, row_hot_t,
+            )
+            blocks = near(blocks)
+            flipped = pl.pallas_call(
+                flip_kernel,
+                name="flip",
+                out_shape=whole,
+                in_specs=[VMEM],
+                out_specs=VMEM,
+                compiler_params=params,
+                cost_estimate=pl.CostEstimate(
+                    flops=0, bytes_accessed=8 * passes, transcendentals=0
+                ),
+            )(blocks)
+            flipped = near(flipped)
+        else:
+            excess, score_sum = pl.pallas_call(
+                first_kernel,
+                name="first",
+                out_shape=(dense(scen, row_blocks, side), dense(row_blocks, side)),
+                in_specs=[VMEM] * 5,
+                out_specs=(VMEM,) * 2,
+                scratch_shapes=scratch,
+                compiler_params=params,
+            )(flipped, fluence, target, col_hot, row_hot_t)
+        sum_a, sum_b = reduce_scen(score_sum, merge)
         weights, gradient = pl.pallas_call(
             second_kernel,
             name="second",
@@ -204,7 +287,7 @@
             scratch_shapes=scratch,
             compiler_params=params,
         )(blocks, excess, sum_a, sum_b, row_hot, col_hot_t)
-        grad_a, grad_b = reduce_but_last(gradient, "vox", jnp.add)
+        grad_a, grad_b = reduce_vox(gradient)
         copies, gradient = pl.pallas_call(
             third_kernel,
             name="third",
@@ -218,7 +301,7 @@
             col_hot, col_hot_t, row_hot, row_hot_t,
         )
         if outer_round < ROUNDS - 1:
-            grad_a, grad_b = reduce_but_last(gradient, "vox", jnp.add)
+            grad_a, grad_b = reduce_vox(gradient)
         else:
             pieces = gradient.reshape(scen, parts, share // side, side)
             pieces = lax.all_to_all(pieces, "vox", split_axis=1, concat_axis=1, tiled=True)
@@ -226,7 +309,7 @@
             start = lax.axis_index("vox") * (share // side)
             copies = lax.dynamic_slice_in_dim(copies, start, share // side, 1)
         copies = jnp.maximum(copies - STEP_SIZE * (grad_a + grad_b), 0.0)
-        mean_a, mean_b = reduce_but_last(jnp.sum(copies, axis=0), "scen", jnp.add)
+        mean_a, mean_b = reduce_scen(jnp.sum(copies, axis=0), jnp.add)
         fluence = (mean_a + mean_b) / scen_total
     return fluence.reshape(share), weights.reshape(scen, row_blocks * side)
 

time: 140 us -> 133 us (0.950)
  waiting for transfers between devices: 68.2 us -> 60.9 us
  starting transfers between devices: 27.9 us -> 33.4 us
  local copies, waits for them, and re-layouts: 6.19 us -> 2.94 us
  Pallas kernels: 34.3 us -> 32.5 us
    ppermute x20 -> x17, waiting for transfers between devices: 60.8 us -> 50.4 us  [swap(): lax.ppermute(x, axis, [(i, i ^ bit) for i in range(lax.axis_size(axis))])]
    ppermute x0 -> x3, starting transfers between devices: none -> 7.29 us  [swap_both(): return lax.ppermute(x, ('scen', 'vox'), pairs)]
    unnamed x12 -> x7, local copies, waits for them, and re-layouts: 5.52 us -> 2.27 us
    ppermute x20 -> x17, starting transfers between devices: 24.4 us -> 21.2 us  [swap(): lax.ppermute(x, axis, [(i, i ^ bit) for i in range(lax.axis_size(axis))])]
    ppermute x0 -> x3, waiting for transfers between devices: none -> 3.19 us  [swap_both(): return lax.ppermute(x, ('scen', 'vox'), pairs)]
    pallas_call x2 -> x1, Pallas kernels: 4.52 us -> 2.26 us  [body(): pl.pallas_call(first_kernel, name='first', out_shape=(dense(scen, row_blo...]
    all_to_all x1, starting transfers between devices: 3.46 us -> 4.89 us  [body(): lax.all_to_all(pieces, 'vox', split_axis=1, concat_axis=1, tiled=True)]
    pallas_call x1 -> x3, Pallas kernels: 8.21 us -> 8.68 us  [the longest x1 5.06 us: body(): pl.pallas_call(functools.partial(open_kernel, sizes), name='open', out_sh...]
  transfers between devices with their start and end apart: 21 -> 21, of which waited for: 20 -> 21; matrix products, arithmetic and copies ran while one was open for 1% -> 1% of each run, Pallas kernels for 6% -> 3%
where the time goes in v2:
time: 133 us
  waiting for transfers between devices  60.9 us (46%)
  starting transfers between devices  33.4 us (25%)
  Pallas kernels  32.5 us (24%)
  local copies, waits for them, and re-layouts  2.94 us (2%)
  other arithmetic  1.65 us (1%)
  between operations  1.44 us (1%)
    ppermute x17, waiting for transfers between devices, swap(): lax.ppermute(x, axis, [(i, i ^ bit) for i in range(lax.axis_size(axis))])  50.4 us
    ppermute x17, starting transfers between devices, swap(): lax.ppermute(x, axis, [(i, i ^ bit) for i in range(lax.axis_size(axis))])  21.2 us
    pallas_call x2, Pallas kernels, body(): pl.pallas_call(third_kernel, name='third', out_shape=(dense(scen, beam_bl...  14.5 us
    all_to_all x1, waiting for transfers between devices, body(): lax.all_to_all(pieces, 'vox', split_axis=1, concat_axis=1, tiled=True)  7.34 us
    ppermute x3, starting transfers between devices, swap_both(): return lax.ppermute(x, ('scen', 'vox'), pairs)  7.29 us
    pallas_call x2, Pallas kernels, body(): pl.pallas_call(second_kernel, name='second', out_shape=(dense(scen, row_b...  7.07 us
    pallas_call x1, Pallas kernels, body(): pl.pallas_call(functools.partial(open_kernel, sizes), name='open', out_sh...  5.06 us
    all_to_all x1, starting transfers between devices, body(): lax.all_to_all(pieces, 'vox', split_axis=1, concat_axis=1, tiled=True)  4.89 us
  transfers between devices with their start and end apart: 21, of which 21 were waited for; matrix products, arithmetic and copies ran while one was open for 1% of the time, Pallas kernels for 3%

profile of v2, /device:TPU:0, one launch (start us, length us, event | category | flops | bytes accessed | tf_op | source)
XLA Modules:
  0.0 132.9 jit_solution(14115219705795006802)
XLA Ops:
  0.6 2.4 %collective-permute-start = (f32[16,128]{1,0:T(8,128)}, f32[16,128]{1,0:T(8,128)S(1)}, u32[]{:S(2)}, u32[]{:S(2)}) collective-permute-start(f32[16,128]{1,0:T(8,128)} %bitcast.18), channel_id=1, source_target_pairs={{0,9},{1,8},{2,11},{3,10},{4,13},{5,12},{6,15},{7,14},{8,1},{9,0},... | collective-permute-start | bytes 24584 | tf_op jit(solution)/shard_map/ppermute | solution.py:197
  3.1 1.6 %collective-permute-done = f32[16,128]{1,0:T(8,128)S(1)} collective-permute-done((f32[16,128]{1,0:T(8,128)}, f32[16,128]{1,0:T(8,128)S(1)}, u32[]{:S(2)}, u32[]{:S(2)}) %collective-permute-start) | collective-permute-done | bytes 8224 | tf_op jit(solution)/shard_map/ppermute | solution.py:197
  4.7 0.8 maximum_select_fusion.2
  5.4 2.1 %collective-permute-start.1 = (f32[32,128]{1,0:T(8,128)S(1)}, f32[32,128]{1,0:T(8,128)S(1)}, u32[]{:S(2)}, u32[]{:S(2)}) collective-permute-start(f32[32,128]{1,0:T(8,128)S(1)} %maximum_select_fusion.2), channel_id=1, source_target_pairs={{0,10},{1,11},{2,8},{3,9},{4,14},{5,15},{6,12},{7,13},{8,2},{9,3},... | collective-permute-start | bytes 49160 | tf_op jit(solution)/shard_map/ppermute | solution.py:197
  7.5 1.4 %collective-permute-done.1 = f32[32,128]{1,0:T(8,128)S(1)} collective-permute-done((f32[32,128]{1,0:T(8,128)S(1)}, f32[32,128]{1,0:T(8,128)S(1)}, u32[]{:S(2)}, u32[]{:S(2)}) %collective-permute-start.1) | collective-permute-done | bytes 16416 | tf_op jit(solution)/shard_map/ppermute | solution.py:197
  9.0 2.7 %collective-permute-start.2 = (f32[64,128]{1,0:T(8,128)S(1)}, f32[64,128]{1,0:T(8,128)S(1)}, u32[]{:S(2)}, u32[]{:S(2)}) collective-permute-start(f32[64,128]{1,0:T(8,128)S(1)} %maximum_select_fusion.1), channel_id=1, source_target_pairs={{0,12},{1,13},{2,14},{3,15},{4,8},{5,9},{6,10},{7,11},{8,4},{9,5},... | collective-permute-start | bytes 98312 | tf_op jit(solution)/shard_map/ppermute | solution.py:197
  12.4 0.7 copy-done.2
  13.3 0.8 copy-done
  14.2 5.1 %open.1 = (f32[2,80,128,128]{3,2,1,0:T(8,128)S(1)}, f32[2,128,128]{2,1,0:T(8,128)S(1)}, f32[128,128]{1,0:T(8,128)S(1)}) custom-call(f32[2,80,128,128]{3,2,1,0:T(8,128)} %source.1, f32[128,128]{1,0:T(8,128)S(1)} %maximum_select_fusion.fluence, f32[128,128]{1,0:T(8,128)S(1)} %bitcast.10, bf16[80,128]{1,0:T(8,128)(2,1)S(1)} %get-tuple-element.19.col_hot, ...), custom_call_target="tpu_custom_call" | custom-call | tf_op jit(solution)/shard_map/open/pallas_call | solution.py:245
  19.7 0.9 collective-permute-done.3
  20.6 1.7 %collective-permute-start.4 = (f32[128,128]{1,0:T(8,128)S(1)}, f32[128,128]{1,0:T(8,128)S(1)}, u32[]{:S(2)}, u32[]{:S(2)}) collective-permute-start(f32[128,128]{1,0:T(8,128)S(1)} %log_add_fusion.1.sum_a), channel_id=1, source_target_pairs={{0,24},{8,16},{16,8},{24,0},{1,25},{9,17},{17,9},{25,1},{2,26},{10... | collective-permute-start | bytes 196616 | tf_op jit(solution)/shard_map/ppermute | solution.py:168
  22.3 2.3 %collective-permute-done.4.sum_b = f32[128,128]{1,0:T(8,128)S(1)} collective-permute-done((f32[128,128]{1,0:T(8,128)S(1)}, f32[128,128]{1,0:T(8,128)S(1)}, u32[]{:S(2)}, u32[]{:S(2)}) %collective-permute-start.4) | collective-permute-done | bytes 65568 | tf_op jit(solution)/shard_map/ppermute | solution.py:168
  24.6 3.5 %second.2 = (f32[2,128,128]{2,1,0:T(8,128)S(1)}, f32[2,128,128]{2,1,0:T(8,128)S(1)}) custom-call(f32[2,80,128,128]{3,2,1,0:T(8,128)S(1)} %get-tuple-element.21.blocks, f32[2,128,128]{2,1,0:T(8,128)S(1)} %get-tuple-element.22.excess, f32[128,128]{1,0:T(8,128)S(1)} %log_add_fusion.1.sum_a, f32[128,128]{1,0:T(8,128)S(1)} %collective-permute-done.4.sum_b, ...), custom_call_target="tpu_custom_call" | custom-call | tf_op jit(solution)/shard_map/second/pallas_call | solution.py:281
  28.2 2.1 %collective-permute-start.5 = (f32[2,128,128]{2,1,0:T(8,128)S(1)}, f32[2,128,128]{2,1,0:T(8,128)S(1)}, u32[]{:S(2)}, u32[]{:S(2)}) collective-permute-start(f32[2,128,128]{2,1,0:T(8,128)S(1)} %get-tuple-element.26), channel_id=1, source_target_pairs={{0,1},{1,0},{2,3},{3,2},{4,5},{5,4},{6,7},{7,6},{8,9},{9,8},{10,11... | collective-permute-start | bytes 393224 | tf_op jit(solution)/shard_map/ppermute | solution.py:168
  30.2 3.8 %collective-permute-done.5 = f32[2,128,128]{2,1,0:T(8,128)S(1)} collective-permute-done((f32[2,128,128]{2,1,0:T(8,128)S(1)}, f32[2,128,128]{2,1,0:T(8,128)S(1)}, u32[]{:S(2)}, u32[]{:S(2)}) %collective-permute-start.5) | collective-permute-done | bytes 131104 | tf_op jit(solution)/shard_map/ppermute | solution.py:168
  34.1 2.0 %collective-permute-start.6 = (f32[2,128,128]{2,1,0:T(8,128)S(1)}, f32[2,128,128]{2,1,0:T(8,128)S(1)}, u32[]{:S(2)}, u32[]{:S(2)}) collective-permute-start(f32[2,128,128]{2,1,0:T(8,128)S(1)} %add.50), channel_id=1, source_target_pairs={{0,2},{1,3},{2,0},{3,1},{4,6},{5,7},{6,4},{7,5},{8,10},{9,11},{10,... | collective-permute-start | bytes 393224 | tf_op jit(solution)/shard_map/ppermute | solution.py:168
  36.0 3.1 %collective-permute-done.6 = f32[2,128,128]{2,1,0:T(8,128)S(1)} collective-permute-done((f32[2,128,128]{2,1,0:T(8,128)S(1)}, f32[2,128,128]{2,1,0:T(8,128)S(1)}, u32[]{:S(2)}, u32[]{:S(2)}) %collective-permute-start.6) | collective-permute-done | bytes 131104 | tf_op jit(solution)/shard_map/ppermute | solution.py:168
  39.2 3.3 %collective-permute-start.7 = (f32[2,128,128]{2,1,0:T(8,128)S(1)}, f32[2,128,128]{2,1,0:T(8,128)S(1)}, u32[]{:S(2)}, u32[]{:S(2)}) collective-permute-start(f32[2,128,128]{2,1,0:T(8,128)S(1)} %add.51.grad_a), channel_id=1, source_target_pairs={{0,4},{1,5},{2,6},{3,7},{4,0},{5,1},{6,2},{7,3},{8,12},{9,13},{10,... | collective-permute-start | bytes 393224 | tf_op jit(solution)/shard_map/ppermute | solution.py:168
  42.5 3.5 %flip.1.flipped = f32[2,80,128,128]{3,2,1,0:T(8,128)S(1)} custom-call(f32[2,80,128,128]{3,2,1,0:T(8,128)S(1)} %get-tuple-element.21.blocks), custom_call_target="tpu_custom_call" | custom-call | bytes 20971520 | tf_op jit(solution)/shard_map/flip/pallas_call | solution.py:258
  46.0 1.3 %collective-permute-done.7.grad_b = f32[2,128,128]{2,1,0:T(8,128)S(1)} collective-permute-done((f32[2,128,128]{2,1,0:T(8,128)S(1)}, f32[2,128,128]{2,1,0:T(8,128)S(1)}, u32[]{:S(2)}, u32[]{:S(2)}) %collective-permute-start.7) | collective-permute-done | bytes 131104 | tf_op jit(solution)/shard_map/ppermute | solution.py:168
  47.4 7.3 %third.2 = (f32[2,128,128]{2,1,0:T(8,128)S(1)}, f32[2,128,128]{2,1,0:T(8,128)S(1)}) custom-call(f32[2,80,128,128]{3,2,1,0:T(8,128)S(1)} %get-tuple-element.21.blocks, f32[2,80,128,128]{3,2,1,0:T(8,128)S(1)} %flip.1.flipped, f32[128,128]{1,0:T(8,128)S(1)} %maximum_select_fusion.fluence, f32[2,128,128]{2,1,0:T(8,128)S(1)} %add.51.grad_a, ...), custom_call_target="tpu_custom_call" | custom-call | tf_op jit(solution)/shard_map/third/pallas_call | solution.py:291
  54.6 1.6 %collective-permute-start.8 = (f32[2,128,128]{2,1,0:T(8,128)S(1)}, f32[2,128,128]{2,1,0:T(8,128)S(1)}, u32[]{:S(2)}, u32[]{:S(2)}) collective-permute-start(f32[2,128,128]{2,1,0:T(8,128)S(1)} %get-tuple-element.29), channel_id=1, source_target_pairs={{0,1},{1,0},{2,3},{3,2},{4,5},{5,4},{6,7},{7,6},{8,9},{9,8},{10,11... | collective-permute-start | bytes 393224 | tf_op jit(solution)/shard_map/ppermute | solution.py:168
  56.2 3.4 %collective-permute-done.8 = f32[2,128,128]{2,1,0:T(8,128)S(1)} collective-permute-done((f32[2,128,128]{2,1,0:T(8,128)S(1)}, f32[2,128,128]{2,1,0:T(8,128)S(1)}, u32[]{:S(2)}, u32[]{:S(2)}) %collective-permute-start.8) | collective-permute-done | bytes 131104 | tf_op jit(solution)/shard_map/ppermute | solution.py:168
  59.7 0.8 collective-permute-start.9
  60.5 5.5 %collective-permute-done.9 = f32[2,128,128]{2,1,0:T(8,128)S(1)} collective-permute-done((f32[2,128,128]{2,1,0:T(8,128)S(1)}, f32[2,128,128]{2,1,0:T(8,128)S(1)}, u32[]{:S(2)}, u32[]{:S(2)}) %collective-permute-start.9) | collective-permute-done | bytes 131104 | tf_op jit(solution)/shard_map/ppermute | solution.py:168
  66.0 1.5 %collective-permute-start.10 = (f32[2,128,128]{2,1,0:T(8,128)S(1)}, f32[2,128,128]{2,1,0:T(8,128)S(1)}, u32[]{:S(2)}, u32[]{:S(2)}) collective-permute-start(f32[2,128,128]{2,1,0:T(8,128)S(1)} %add.53), channel_id=1, source_target_pairs={{0,4},{1,5},{2,6},{3,7},{4,0},{5,1},{6,2},{7,3},{8,12},{9,13},{10,... | collective-permute-start | bytes 393224 | tf_op jit(solution)/shard_map/ppermute | solution.py:168
  67.5 5.2 %collective-permute-done.10 = f32[2,128,128]{2,1,0:T(8,128)S(1)} collective-permute-done((f32[2,128,128]{2,1,0:T(8,128)S(1)}, f32[2,128,128]{2,1,0:T(8,128)S(1)}, u32[]{:S(2)}, u32[]{:S(2)}) %collective-permute-start.10) | collective-permute-done | bytes 131104 | tf_op jit(solution)/shard_map/ppermute | solution.py:168
  72.8 1.2 collective-permute-done.11
  74.1 1.3 %collective-permute-start.12 = (f32[128,128]{1,0:T(8,128)S(1)}, f32[128,128]{1,0:T(8,128)S(1)}, u32[]{:S(2)}, u32[]{:S(2)}) collective-permute-start(f32[128,128]{1,0:T(8,128)S(1)} %add.55), channel_id=1, source_target_pairs={{0,24},{8,16},{16,8},{24,0},{1,25},{9,17},{17,9},{25,1},{2,26},{10... | collective-permute-start | bytes 196616 | tf_op jit(solution)/shard_map/ppermute | solution.py:168
  75.4 2.8 %collective-permute-done.12 = f32[128,128]{1,0:T(8,128)S(1)} collective-permute-done((f32[128,128]{1,0:T(8,128)S(1)}, f32[128,128]{1,0:T(8,128)S(1)}, u32[]{:S(2)}, u32[]{:S(2)}) %collective-permute-start.12) | collective-permute-done | bytes 65568 | tf_op jit(solution)/shard_map/ppermute | solution.py:168
  78.2 2.3 %first.1 = (f32[2,128,128]{2,1,0:T(8,128)S(1)}, f32[128,128]{1,0:T(8,128)S(1)}) custom-call(f32[2,80,128,128]{3,2,1,0:T(8,128)S(1)} %flip.1.flipped, f32[128,128]{1,0:T(8,128)S(1)} %add_multiply_fusion.fluence, f32[128,128]{1,0:T(8,128)S(1)} %bitcast.12, bf16[80,128]{1,0:T(8,128)(2,1)S(1)} %get-tuple-element.19.col_hot, ...), custom_call_target="tpu_custom_call" | custom-call | tf_op jit(solution)/shard_map/first/pallas_call | solution.py:271
  80.7 1.1 collective-permute-done.13
  81.8 1.4 %collective-permute-start.14 = (f32[128,128]{1,0:T(8,128)S(1)}, f32[128,128]{1,0:T(8,128)S(1)}, u32[]{:S(2)}, u32[]{:S(2)}) collective-permute-start(f32[128,128]{1,0:T(8,128)S(1)} %log_add_fusion.sum_a), channel_id=1, source_target_pairs={{0,24},{8,16},{16,8},{24,0},{1,25},{9,17},{17,9},{25,1},{2,26},{10... | collective-permute-start | bytes 196616 | tf_op jit(solution)/shard_map/ppermute | solution.py:168
  83.2 2.8 %collective-permute-done.14.sum_b = f32[128,128]{1,0:T(8,128)S(1)} collective-permute-done((f32[128,128]{1,0:T(8,128)S(1)}, f32[128,128]{1,0:T(8,128)S(1)}, u32[]{:S(2)}, u32[]{:S(2)}) %collective-permute-start.14) | collective-permute-done | bytes 65568 | tf_op jit(solution)/shard_map/ppermute | solution.py:168
  85.9 3.5 %second.3 = (f32[2,128,128]{2,1,0:T(8,128)S(1)}, f32[2,128,128]{2,1,0:T(8,128)S(1)}) custom-call(f32[2,80,128,128]{3,2,1,0:T(8,128)S(1)} %get-tuple-element.21.blocks, f32[2,128,128]{2,1,0:T(8,128)S(1)} %get-tuple-element.30.excess, f32[128,128]{1,0:T(8,128)S(1)} %log_add_fusion.sum_a, f32[128,128]{1,0:T(8,128)S(1)} %collective-permute-done.14.sum_b, ...), custom_call_target="tpu_custom_call" | custom-call | tf_op jit(solution)/shard_map/second/pallas_call | solution.py:281
  89.5 1.8 %collective-permute-start.15 = (f32[2,128,128]{2,1,0:T(8,128)S(1)}, f32[2,128,128]{2,1,0:T(8,128)S(1)}, u32[]{:S(2)}, u32[]{:S(2)}) collective-permute-start(f32[2,128,128]{2,1,0:T(8,128)S(1)} %get-tuple-element.32), channel_id=1, source_target_pairs={{0,1},{1,0},{2,3},{3,2},{4,5},{5,4},{6,7},{7,6},{8,9},{9,8},{10,11... | collective-permute-start | bytes 393224 | tf_op jit(solution)/shard_map/ppermute | solution.py:168
  91.3 4.0 %collective-permute-done.15 = f32[2,128,128]{2,1,0:T(8,128)S(1)} collective-permute-done((f32[2,128,128]{2,1,0:T(8,128)S(1)}, f32[2,128,128]{2,1,0:T(8,128)S(1)}, u32[]{:S(2)}, u32[]{:S(2)}) %collective-permute-start.15) | collective-permute-done | bytes 131104 | tf_op jit(solution)/shard_map/ppermute | solution.py:168
  95.5 4.9 %collective-permute-done.16 = f32[2,128,128]{2,1,0:T(8,128)S(1)} collective-permute-done((f32[2,128,128]{2,1,0:T(8,128)S(1)}, f32[2,128,128]{2,1,0:T(8,128)S(1)}, u32[]{:S(2)}, u32[]{:S(2)}) %collective-permute-start.16) | collective-permute-done | bytes 131104 | tf_op jit(solution)/shard_map/ppermute | solution.py:168
  100.4 1.6 %collective-permute-start.17 = (f32[2,128,128]{2,1,0:T(8,128)S(1)}, f32[2,128,128]{2,1,0:T(8,128)S(1)}, u32[]{:S(2)}, u32[]{:S(2)}) collective-permute-start(f32[2,128,128]{2,1,0:T(8,128)S(1)} %add.60.grad_a), channel_id=1, source_target_pairs={{0,4},{1,5},{2,6},{3,7},{4,0},{5,1},{6,2},{7,3},{8,12},{9,13},{10,... | collective-permute-start | bytes 393224 | tf_op jit(solution)/shard_map/ppermute | solution.py:168
  102.0 5.8 %collective-permute-done.17.grad_b = f32[2,128,128]{2,1,0:T(8,128)S(1)} collective-permute-done((f32[2,128,128]{2,1,0:T(8,128)S(1)}, f32[2,128,128]{2,1,0:T(8,128)S(1)}, u32[]{:S(2)}, u32[]{:S(2)}) %collective-permute-start.17) | collective-permute-done | bytes 131104 | tf_op jit(solution)/shard_map/ppermute | solution.py:168
  107.8 7.3 %third.3 = (f32[2,128,128]{2,1,0:T(8,128)S(1)}, f32[2,128,128]{2,1,0:T(8,128)S(1)}) custom-call(f32[2,80,128,128]{3,2,1,0:T(8,128)S(1)} %get-tuple-element.21.blocks, f32[2,80,128,128]{3,2,1,0:T(8,128)S(1)} %flip.1.flipped, f32[128,128]{1,0:T(8,128)S(1)} %add_multiply_fusion.fluence, f32[2,128,128]{2,1,0:T(8,128)S(1)} %add.60.grad_a, ...), custom_call_target="tpu_custom_call" | custom-call | tf_op jit(solution)/shard_map/third/pallas_call | solution.py:291
  115.0 0.7 copy.7
  115.7 4.9 %all-to-all-start = ((f32[2,8,16,128]{3,2,0,1:T(8,128)}), f32[2,8,16,128]{3,2,0,1:T(8,128)S(1)}, u32[]{:S(2)}, u32[]{:S(2)}) async-start(f32[2,8,16,128]{3,2,0,1:T(8,128)} %copy.7), calls=%async_computation | async-start | bytes 262144 | tf_op jit(solution)/shard_map/all_to_all | solution.py:307
  120.6 7.3 %all-to-all-done = f32[2,8,16,128]{3,2,0,1:T(8,128)S(1)} async-done(((f32[2,8,16,128]{3,2,0,1:T(8,128)}), f32[2,8,16,128]{3,2,0,1:T(8,128)S(1)}, u32[]{:S(2)}, u32[]{:S(2)}) %all-to-all-start) | async-done | bytes 131104 | tf_op jit(solution)/shard_map/all_to_all | solution.py:307
  128.1 1.2 collective-permute-done.18
  129.2 1.3 collective-permute-start.19
  130.5 0.8 copy.10
  131.3 1.0 collective-permute-done.19
  (28 shorter events, 2.1 us)
Async XLA Ops:
  0.6 4.0 %collective-permute-start = (f32[16,128]{1,0:T(8,128)}, f32[16,128]{1,0:T(8,128)S(1)}, u32[]{:S(2)}, u32[]{:S(2)}) collective-permute-start(f32[16,128]{1,0:T(8,128)} %bitcast.18), channel_id=1, source_target_pairs={{0,9},{1,8},{2,11},{3,10},{4,13},{5,12},{6,15},{7,14},{8,1},{9,0},... | collective-permute-start | bytes 24584 | tf_op jit(solution)/shard_map/ppermute | solution.py:197
  5.4 3.6 %collective-permute-start.1 = (f32[32,128]{1,0:T(8,128)S(1)}, f32[32,128]{1,0:T(8,128)S(1)}, u32[]{:S(2)}, u32[]{:S(2)}) collective-permute-start(f32[32,128]{1,0:T(8,128)S(1)} %maximum_select_fusion.2), channel_id=1, source_target_pairs={{0,10},{1,11},{2,8},{3,9},{4,14},{5,15},{6,12},{7,13},{8,2},{9,3},... | collective-permute-start | bytes 49160 | tf_op jit(solution)/shard_map/ppermute | solution.py:197
  9.0 4.3 %collective-permute-start.2 = (f32[64,128]{1,0:T(8,128)S(1)}, f32[64,128]{1,0:T(8,128)S(1)}, u32[]{:S(2)}, u32[]{:S(2)}) collective-permute-start(f32[64,128]{1,0:T(8,128)S(1)} %maximum_select_fusion.1), channel_id=1, source_target_pairs={{0,12},{1,13},{2,14},{3,15},{4,8},{5,9},{6,10},{7,11},{8,4},{9,5},... | collective-permute-start | bytes 98312 | tf_op jit(solution)/shard_map/ppermute | solution.py:197
  12.4 0.7 copy-start.2
  13.3 0.8 copy-start
  19.2 1.4 %collective-permute-start.3 = (f32[128,128]{1,0:T(8,128)S(1)}, f32[128,128]{1,0:T(8,128)S(1)}, u32[]{:S(2)}, u32[]{:S(2)}) collective-permute-start(f32[128,128]{1,0:T(8,128)S(1)} %get-tuple-element.23), channel_id=1, source_target_pairs={{0,8},{8,0},{16,24},{24,16},{1,9},{9,1},{17,25},{25,17},{2,10},{10... | collective-permute-start | bytes 196616 | tf_op jit(solution)/shard_map/ppermute | solution.py:168
  20.6 4.0 %collective-permute-start.4 = (f32[128,128]{1,0:T(8,128)S(1)}, f32[128,128]{1,0:T(8,128)S(1)}, u32[]{:S(2)}, u32[]{:S(2)}) collective-permute-start(f32[128,128]{1,0:T(8,128)S(1)} %log_add_fusion.1.sum_a), channel_id=1, source_target_pairs={{0,24},{8,16},{16,8},{24,0},{1,25},{9,17},{17,9},{25,1},{2,26},{10... | collective-permute-start | bytes 196616 | tf_op jit(solution)/shard_map/ppermute | solution.py:168
  28.2 5.9 %collective-permute-start.5 = (f32[2,128,128]{2,1,0:T(8,128)S(1)}, f32[2,128,128]{2,1,0:T(8,128)S(1)}, u32[]{:S(2)}, u32[]{:S(2)}) collective-permute-start(f32[2,128,128]{2,1,0:T(8,128)S(1)} %get-tuple-element.26), channel_id=1, source_target_pairs={{0,1},{1,0},{2,3},{3,2},{4,5},{5,4},{6,7},{7,6},{8,9},{9,8},{10,11... | collective-permute-start | bytes 393224 | tf_op jit(solution)/shard_map/ppermute | solution.py:168
  34.1 5.1 %collective-permute-start.6 = (f32[2,128,128]{2,1,0:T(8,128)S(1)}, f32[2,128,128]{2,1,0:T(8,128)S(1)}, u32[]{:S(2)}, u32[]{:S(2)}) collective-permute-start(f32[2,128,128]{2,1,0:T(8,128)S(1)} %add.50), channel_id=1, source_target_pairs={{0,2},{1,3},{2,0},{3,1},{4,6},{5,7},{6,4},{7,5},{8,10},{9,11},{10,... | collective-permute-start | bytes 393224 | tf_op jit(solution)/shard_map/ppermute | solution.py:168
  39.2 8.2 %copy-start.1 = (f32[16384]{0:T(1024)S(1)}, f32[16384]{0:T(1024)}, u32[]{:S(2)}) copy-start(f32[16384]{0:T(1024)} %param.8) | copy-start | bytes 196612
  39.2 8.2 %collective-permute-start.7 = (f32[2,128,128]{2,1,0:T(8,128)S(1)}, f32[2,128,128]{2,1,0:T(8,128)S(1)}, u32[]{:S(2)}, u32[]{:S(2)}) collective-permute-start(f32[2,128,128]{2,1,0:T(8,128)S(1)} %add.51.grad_a), channel_id=1, source_target_pairs={{0,4},{1,5},{2,6},{3,7},{4,0},{5,1},{6,2},{7,3},{8,12},{9,13},{10,... | collective-permute-start | bytes 393224 | tf_op jit(solution)/shard_map/ppermute | solution.py:168
  54.6 5.0 %collective-permute-start.8 = (f32[2,128,128]{2,1,0:T(8,128)S(1)}, f32[2,128,128]{2,1,0:T(8,128)S(1)}, u32[]{:S(2)}, u32[]{:S(2)}) collective-permute-start(f32[2,128,128]{2,1,0:T(8,128)S(1)} %get-tuple-element.29), channel_id=1, source_target_pairs={{0,1},{1,0},{2,3},{3,2},{4,5},{5,4},{6,7},{7,6},{8,9},{9,8},{10,11... | collective-permute-start | bytes 393224 | tf_op jit(solution)/shard_map/ppermute | solution.py:168
  59.7 6.3 %collective-permute-start.9 = (f32[2,128,128]{2,1,0:T(8,128)S(1)}, f32[2,128,128]{2,1,0:T(8,128)S(1)}, u32[]{:S(2)}, u32[]{:S(2)}) collective-permute-start(f32[2,128,128]{2,1,0:T(8,128)S(1)} %add.52), channel_id=1, source_target_pairs={{0,2},{1,3},{2,0},{3,1},{4,6},{5,7},{6,4},{7,5},{8,10},{9,11},{10,... | collective-permute-start | bytes 393224 | tf_op jit(solution)/shard_map/ppermute | solution.py:168
  66.0 6.7 %collective-permute-start.10 = (f32[2,128,128]{2,1,0:T(8,128)S(1)}, f32[2,128,128]{2,1,0:T(8,128)S(1)}, u32[]{:S(2)}, u32[]{:S(2)}) collective-permute-start(f32[2,128,128]{2,1,0:T(8,128)S(1)} %add.53), channel_id=1, source_target_pairs={{0,4},{1,5},{2,6},{3,7},{4,0},{5,1},{6,2},{7,3},{8,12},{9,13},{10,... | collective-permute-start | bytes 393224 | tf_op jit(solution)/shard_map/ppermute | solution.py:168
  72.7 1.3 collective-permute-start.11
  74.1 4.1 %collective-permute-start.12 = (f32[128,128]{1,0:T(8,128)S(1)}, f32[128,128]{1,0:T(8,128)S(1)}, u32[]{:S(2)}, u32[]{:S(2)}) collective-permute-start(f32[128,128]{1,0:T(8,128)S(1)} %add.55), channel_id=1, source_target_pairs={{0,24},{8,16},{16,8},{24,0},{1,25},{9,17},{17,9},{25,1},{2,26},{10... | collective-permute-start | bytes 196616 | tf_op jit(solution)/shard_map/ppermute | solution.py:168
  80.5 1.3 collective-permute-start.13
  81.8 4.1 %collective-permute-start.14 = (f32[128,128]{1,0:T(8,128)S(1)}, f32[128,128]{1,0:T(8,128)S(1)}, u32[]{:S(2)}, u32[]{:S(2)}) collective-permute-start(f32[128,128]{1,0:T(8,128)S(1)} %log_add_fusion.sum_a), channel_id=1, source_target_pairs={{0,24},{8,16},{16,8},{24,0},{1,25},{9,17},{17,9},{25,1},{2,26},{10... | collective-permute-start | bytes 196616 | tf_op jit(solution)/shard_map/ppermute | solution.py:168
  89.5 5.9 %collective-permute-start.15 = (f32[2,128,128]{2,1,0:T(8,128)S(1)}, f32[2,128,128]{2,1,0:T(8,128)S(1)}, u32[]{:S(2)}, u32[]{:S(2)}) collective-permute-start(f32[2,128,128]{2,1,0:T(8,128)S(1)} %get-tuple-element.32), channel_id=1, source_target_pairs={{0,1},{1,0},{2,3},{3,2},{4,5},{5,4},{6,7},{7,6},{8,9},{9,8},{10,11... | collective-permute-start | bytes 393224 | tf_op jit(solution)/shard_map/ppermute | solution.py:168
  95.4 5.0 %collective-permute-start.16 = (f32[2,128,128]{2,1,0:T(8,128)S(1)}, f32[2,128,128]{2,1,0:T(8,128)S(1)}, u32[]{:S(2)}, u32[]{:S(2)}) collective-permute-start(f32[2,128,128]{2,1,0:T(8,128)S(1)} %add.59), channel_id=1, source_target_pairs={{0,2},{1,3},{2,0},{3,1},{4,6},{5,7},{6,4},{7,5},{8,10},{9,11},{10,... | collective-permute-start | bytes 393224 | tf_op jit(solution)/shard_map/ppermute | solution.py:168
  100.4 7.4 %collective-permute-start.17 = (f32[2,128,128]{2,1,0:T(8,128)S(1)}, f32[2,128,128]{2,1,0:T(8,128)S(1)}, u32[]{:S(2)}, u32[]{:S(2)}) collective-permute-start(f32[2,128,128]{2,1,0:T(8,128)S(1)} %add.60.grad_a), channel_id=1, source_target_pairs={{0,4},{1,5},{2,6},{3,7},{4,0},{5,1},{6,2},{7,3},{8,12},{9,13},{10,... | collective-permute-start | bytes 393224 | tf_op jit(solution)/shard_map/ppermute | solution.py:168
  115.7 12.2 %all-to-all-start = ((f32[2,8,16,128]{3,2,0,1:T(8,128)}), f32[2,8,16,128]{3,2,0,1:T(8,128)S(1)}, u32[]{:S(2)}, u32[]{:S(2)}) async-start(f32[2,8,16,128]{3,2,0,1:T(8,128)} %copy.7), calls=%async_computation | async-start | bytes 262144 | tf_op jit(solution)/shard_map/all_to_all | solution.py:307
  128.0 1.2 collective-permute-start.18
  129.2 3.1 %collective-permute-start.19 = (f32[16,128]{1,0:T(8,128)S(1)}, f32[16,128]{1,0:T(8,128)S(1)}, u32[]{:S(2)}, u32[]{:S(2)}) collective-permute-start(f32[16,128]{1,0:T(8,128)S(1)} %add.62), channel_id=1, source_target_pairs={{0,24},{8,16},{16,8},{24,0},{1,25},{9,17},{17,9},{25,1},{2,26},{10... | collective-permute-start | bytes 24584 | tf_op jit(solution)/shard_map/ppermute | solution.py:168

commit v3 on v2

--- a/solution.py
+++ b/solution.py
@@ -16,11 +16,7 @@
 
 
 def split3(x):
-    high = x.astype(BF16)
-    rest = x - high.astype(F32)
-    mid = rest.astype(BF16)
-    low = (rest - mid.astype(F32)).astype(BF16)
-    return jnp.concatenate([high, mid, low], axis=-1)
+    return jnp.concatenate(pieces(x), axis=-1)
 
 
 def exact(hot, x):
@@ -44,13 +40,35 @@
     return x.T[:slots]
 
 
-def products(blocks, vectors, rows):
+def pieces(x):
+    high = x.astype(BF16)
+    rest = x - high.astype(F32)
+    mid = rest.astype(BF16)
+    return high, mid, (rest - mid.astype(F32)).astype(BF16)
+
+
+def products(blocks, picked, rows):
     scen, slots, side, _ = blocks.shape
+    index = [lax.broadcasted_iota(jnp.int32, (side, side), n) for n in range(2)]
+    eye = jnp.where(index[0] == index[1], 1.0, 0.0).astype(BF16)
+    ones = jnp.ones((3 * side, side), BF16)
+    turned = {id(x): columns(x) for x in picked}
+    parts = {id(x): pieces(x) for x in picked}
+    count = 0
     for k in range(slots):
+        wide = {}
         for s in range(scen):
-            if s == 0 or vectors[s] is not vectors[0]:
-                wide = jnp.broadcast_to(vectors[s][:, k : k + 1], (side, side))
-            rows[s, k : k + 1, :] = jnp.sum(blocks[s, k] * wide, axis=0, keepdims=True)
+            key = id(picked[s])
+            if key not in wide:
+                if count % 2:
+                    wide[key] = jnp.broadcast_to(turned[key][:, k : k + 1], (side, side))
+                else:
+                    diagonals = [eye * x[k : k + 1, :] for x in parts[key]]
+                    wide[key] = jnp.dot(
+                        jnp.concatenate(diagonals, axis=1), ones, preferred_element_type=F32
+                    )
+                count += 1
+            rows[s, k : k + 1, :] = jnp.sum(blocks[s, k] * wide[key], axis=0, keepdims=True)
 
 
 def merge(a, b):
@@ -58,17 +76,22 @@
     return top + jnp.log(jnp.exp(a - top) + jnp.exp(b - top))
 
 
-def flip_kernel(blocks, flipped):
-    scen, slots, _, _ = blocks.shape
-    group = next(n for n in (8, 4, 2, 1) if slots % n == 0)
-
-    def flip(t, _):
-        for u in range(group):
+def load_kernel(sizes, source, blocks, flipped, sems):
+    scen = source.shape[0]
+    copies, first = [], 0
+    for n, size in enumerate(sizes):
+        part = pl.ds(first, size)
+        copies.append(pltpu.make_async_copy(source.at[:, part], blocks.at[:, part], sems.at[n]))
+        first += size
+    for copy in copies:
+        copy.start()
+    first = 0
+    for copy, size in zip(copies, sizes):
+        copy.wait()
+        for k in range(first, first + size):
             for s in range(scen):
-                flipped[s, t * group + u] = blocks[s, t * group + u].T
-        return 0
-
-    lax.fori_loop(0, slots // group, flip, 0)
+                flipped[s, k] = blocks[s, k].T
+        first += size
 
 
 def hot_kernel(block_map, counts, row_hot, row_hot_t, col_hot, col_hot_t):
@@ -85,9 +108,12 @@
     col_hot[...] = flat(col).astype(BF16)
 
 
-def finish_first(rows, target, row_hot_t, excess, score_sum):
+def first_kernel(flipped, fluence, target, col_hot, row_hot_t, excess, score_sum, rows):
+    scen = flipped.shape[0]
+    picked = exact(col_hot[...], fluence[...])
+    products(flipped, [picked] * scen, rows)
     scores = []
-    for s in range(len(rows)):
+    for s in range(scen):
         e = exact(row_hot_t[...], rows[s]) - target[...]
         excess[s] = e
         scores.append(SHARPNESS * e * e)
@@ -96,46 +122,16 @@
     score_sum[...] = top + jnp.log(total)
 
 
-def first_kernel(flipped, fluence, target, col_hot, row_hot_t, excess, score_sum, rows):
-    scen = flipped.shape[0]
-    vector = columns(exact(col_hot[...], fluence[...]))
-    products(flipped, [vector] * scen, rows)
-    finish_first([rows[s] for s in range(scen)], target, row_hot_t, excess, score_sum)
-
-
-def open_kernel(sizes, source, fluence, target, col_hot, row_hot_t, blocks, excess, score_sum, sems):
-    scen, slots, side, _ = source.shape
-    copies, first = [], 0
-    for n, size in enumerate(sizes):
-        part = pl.ds(first, size)
-        copies.append(pltpu.make_async_copy(source.at[:, part], blocks.at[:, part], sems.at[n]))
-        first += size
-    for copy in copies:
-        copy.start()
-    picked = exact(col_hot[...], fluence[...])
-    lane = lax.broadcasted_iota(jnp.int32, (side, -(-slots // 128) * 128), 1)
-    sums = [jnp.zeros(lane.shape, F32) for _ in range(scen)]
-    first = 0
-    for copy, size in zip(copies, sizes):
-        copy.wait()
-        for k in range(first, first + size):
-            for s in range(scen):
-                total = jnp.sum(blocks[s, k] * picked[k : k + 1, :], axis=1, keepdims=True)
-                sums[s] = jnp.where(lane == k, total, sums[s])
-        first += size
-    finish_first([x.T[:slots] for x in sums], target, row_hot_t, excess, score_sum)
-
-
 def second_kernel(blocks, excess, sum_a, sum_b, row_hot, col_hot_t, weights, gradient, rows):
     scen = excess.shape[0]
     total = merge(sum_a[...], sum_b[...])
-    vectors = []
+    picked = []
     for s in range(scen):
         e = excess[s]
         w = jnp.exp(SHARPNESS * e * e - total)
         weights[s] = w
-        vectors.append(columns(exact(row_hot[...], 2.0 * w * e)))
-    products(blocks, vectors, rows)
+        picked.append(exact(row_hot[...], 2.0 * w * e))
+    products(blocks, picked, rows)
     for s in range(scen):
         gradient[s] = exact(col_hot_t[...], rows[s])
 
@@ -145,17 +141,17 @@
     col_hot, col_hot_t, row_hot, row_hot_t, copies, gradient, rows
 ):
     scen = weights.shape[0]
-    vectors = []
+    picked = []
     for s in range(scen):
         c = jnp.maximum(fluence[...] - STEP_SIZE * (grad_a[s] + grad_b[s]), 0.0)
         copies[s] = c
-        vectors.append(columns(exact(col_hot[...], c)))
-    products(flipped, vectors, rows)
-    vectors = []
+        picked.append(exact(col_hot[...], c))
+    products(flipped, picked, rows)
+    picked = []
     for s in range(scen):
         e = exact(row_hot_t[...], rows[s]) - target[...]
-        vectors.append(columns(exact(row_hot[...], 2.0 * weights[s] * e)))
-    products(blocks, vectors, rows)
+        picked.append(exact(row_hot[...], 2.0 * weights[s] * e))
+    products(blocks, picked, rows)
     for s in range(scen):
         gradient[s] = exact(col_hot_t[...], rows[s])
 
@@ -238,45 +234,30 @@
             jnp.concatenate([other, fluence], axis=0),
         )
 
+    sizes = split(slots, 10)
     whole = pltpu.VMEM((scen, slots, side, side), F32)
+    blocks, flipped = pl.pallas_call(
+        functools.partial(load_kernel, sizes),
+        name="load",
+        out_shape=(whole, whole),
+        in_specs=[pl.BlockSpec(memory_space=pltpu.HBM)],
+        out_specs=(VMEM,) * 2,
+        scratch_shapes=[pltpu.SemaphoreType.DMA((len(sizes),))],
+        compiler_params=params,
+        cost_estimate=pl.CostEstimate(flops=0, bytes_accessed=8 * passes, transcendentals=0),
+    )(pltpu.with_memory_space_constraint(dose_blocks, pltpu.HBM))
+    blocks, flipped = near(blocks), near(flipped)
+
     for outer_round in range(ROUNDS):
-        if outer_round == 0:
-            sizes = split(slots, 10)
-            blocks, excess, score_sum = pl.pallas_call(
-                functools.partial(open_kernel, sizes),
-                name="open",
-                out_shape=(whole, dense(scen, row_blocks, side), dense(row_blocks, side)),
-                in_specs=[pl.BlockSpec(memory_space=pltpu.HBM)] + [VMEM] * 4,
-                out_specs=(VMEM,) * 3,
-                scratch_shapes=[pltpu.SemaphoreType.DMA((len(sizes),))],
-                compiler_params=params,
-            )(
-                pltpu.with_memory_space_constraint(dose_blocks, pltpu.HBM),
-                fluence, target, col_hot, row_hot_t,
-            )
-            blocks = near(blocks)
-            flipped = pl.pallas_call(
-                flip_kernel,
-                name="flip",
-                out_shape=whole,
-                in_specs=[VMEM],
-                out_specs=VMEM,
-                compiler_params=params,
-                cost_estimate=pl.CostEstimate(
-                    flops=0, bytes_accessed=8 * passes, transcendentals=0
-                ),
-            )(blocks)
-            flipped = near(flipped)
-        else:
-            excess, score_sum = pl.pallas_call(
-                first_kernel,
-                name="first",
-                out_shape=(dense(scen, row_blocks, side), dense(row_blocks, side)),
-                in_specs=[VMEM] * 5,
-                out_specs=(VMEM,) * 2,
-                scratch_shapes=scratch,
-                compiler_params=params,
-            )(flipped, fluence, target, col_hot, row_hot_t)
+        excess, score_sum = pl.pallas_call(
+            first_kernel,
+            name="first",
+            out_shape=(dense(scen, row_blocks, side), dense(row_blocks, side)),
+            in_specs=[VMEM] * 5,
+            out_specs=(VMEM,) * 2,
+            scratch_shapes=scratch,
+            compiler_params=params,
+        )(flipped, fluence, target, col_hot, row_hot_t)
         sum_a, sum_b = reduce_scen(score_sum, merge)
         weights, gradient = pl.pallas_call(
             second_kernel,

time: 133 us -> 126 us (0.947)
  waiting for transfers between devices: 60.9 us -> 70.1 us
  starting transfers between devices: 33.4 us -> 24.6 us
  Pallas kernels: 32.5 us -> 26.2 us
  local copies, waits for them, and re-layouts: 2.94 us -> 1.43 us
    ppermute x17, waiting for transfers between devices: 50.4 us -> 59.8 us  [swap(): lax.ppermute(x, axis, [(i, i ^ bit) for i in range(lax.axis_size(axis))])]
    ppermute x17, starting transfers between devices: 21.2 us -> 13.9 us  [swap(): lax.ppermute(x, axis, [(i, i ^ bit) for i in range(lax.axis_size(axis))])]
    pallas_call x2 -> x1, Pallas kernels: 8.6 us -> 4.69 us  [body(): pl.pallas_call(functools.partial(load_kernel, sizes), name='load', out_sh...]
    pallas_call x2, Pallas kernels: 14.5 us -> 11.7 us  [body(): pl.pallas_call(third_kernel, name='third', out_shape=(dense(scen, beam_bl...]
    pallas_call x1 -> x2, Pallas kernels: 2.26 us -> 4.24 us  [body(): pl.pallas_call(first_kernel, name='first', out_shape=(dense(scen, row_blo...]
    pallas_call x2, Pallas kernels: 7.07 us -> 5.52 us  [body(): pl.pallas_call(second_kernel, name='second', out_shape=(dense(scen, row_b...]
    all_to_all x1, starting transfers between devices: 4.89 us -> 3.37 us  [body(): lax.all_to_all(pieces, 'vox', split_axis=1, concat_axis=1, tiled=True)]
    unnamed x7 -> x5, local copies, waits for them, and re-layouts: 2.27 us -> 0.77 us
  transfers between devices with their start and end apart: 21 -> 21, of which waited for: 21 -> 20; matrix products, arithmetic and copies ran while one was open for 1% -> 1% of each run, Pallas kernels for 3% -> 4%
where the time goes in v3:
time: 126 us
  waiting for transfers between devices  70.1 us (56%)
  Pallas kernels  26.2 us (21%)
  starting transfers between devices  24.6 us (20%)
  other arithmetic  1.66 us (1%)
  between operations  1.49 us (1%)
  local copies, waits for them, and re-layouts  1.43 us (1%)
    ppermute x17, waiting for transfers between devices, swap(): lax.ppermute(x, axis, [(i, i ^ bit) for i in range(lax.axis_size(axis))])  59.8 us
    ppermute x17, starting transfers between devices, swap(): lax.ppermute(x, axis, [(i, i ^ bit) for i in range(lax.axis_size(axis))])  13.9 us
    pallas_call x2, Pallas kernels, body(): pl.pallas_call(third_kernel, name='third', out_shape=(dense(scen, beam_bl...  11.7 us
    ppermute x3, starting transfers between devices, swap_both(): return lax.ppermute(x, ('scen', 'vox'), pairs)  7.29 us
    all_to_all x1, waiting for transfers between devices, body(): lax.all_to_all(pieces, 'vox', split_axis=1, concat_axis=1, tiled=True)  7.28 us
    pallas_call x2, Pallas kernels, body(): pl.pallas_call(second_kernel, name='second', out_shape=(dense(scen, row_b...  5.52 us
    pallas_call x1, Pallas kernels, body(): pl.pallas_call(functools.partial(load_kernel, sizes), name='load', out_sh...  4.69 us
    pallas_call x2, Pallas kernels, body(): pl.pallas_call(first_kernel, name='first', out_shape=(dense(scen, row_blo...  4.24 us
  transfers between devices with their start and end apart: 21, of which 20 were waited for; matrix products, arithmetic and copies ran while one was open for 1% of the time, Pallas kernels for 4%

profile of v3, /device:TPU:0, one launch (start us, length us, event | category | flops | bytes accessed | tf_op | source)
XLA Modules:
  0.0 125.5 jit_solution(16726932979674666259)
XLA Ops:
  0.7 2.4 %collective-permute-start = (f32[16,128]{1,0:T(8,128)}, f32[16,128]{1,0:T(8,128)S(1)}, u32[]{:S(2)}, u32[]{:S(2)}) collective-permute-start(f32[16,128]{1,0:T(8,128)} %bitcast.18), channel_id=1, source_target_pairs={{0,9},{1,8},{2,11},{3,10},{4,13},{5,12},{6,15},{7,14},{8,1},{9,0},... | collective-permute-start | bytes 24584 | tf_op jit(solution)/shard_map/ppermute | solution.py:193
  3.1 1.6 %collective-permute-done = f32[16,128]{1,0:T(8,128)S(1)} collective-permute-done((f32[16,128]{1,0:T(8,128)}, f32[16,128]{1,0:T(8,128)S(1)}, u32[]{:S(2)}, u32[]{:S(2)}) %collective-permute-start) | collective-permute-done | bytes 8224 | tf_op jit(solution)/shard_map/ppermute | solution.py:193
  4.7 0.8 maximum_select_fusion.2
  5.4 2.1 %collective-permute-start.1 = (f32[32,128]{1,0:T(8,128)S(1)}, f32[32,128]{1,0:T(8,128)S(1)}, u32[]{:S(2)}, u32[]{:S(2)}) collective-permute-start(f32[32,128]{1,0:T(8,128)S(1)} %maximum_select_fusion.2), channel_id=1, source_target_pairs={{0,10},{1,11},{2,8},{3,9},{4,14},{5,15},{6,12},{7,13},{8,2},{9,3},... | collective-permute-start | bytes 49160 | tf_op jit(solution)/shard_map/ppermute | solution.py:193
  7.6 1.4 %collective-permute-done.1 = f32[32,128]{1,0:T(8,128)S(1)} collective-permute-done((f32[32,128]{1,0:T(8,128)S(1)}, f32[32,128]{1,0:T(8,128)S(1)}, u32[]{:S(2)}, u32[]{:S(2)}) %collective-permute-start.1) | collective-permute-done | bytes 16416 | tf_op jit(solution)/shard_map/ppermute | solution.py:193
  9.0 2.7 %collective-permute-start.2 = (f32[64,128]{1,0:T(8,128)S(1)}, f32[64,128]{1,0:T(8,128)S(1)}, u32[]{:S(2)}, u32[]{:S(2)}) collective-permute-start(f32[64,128]{1,0:T(8,128)S(1)} %maximum_select_fusion.1), channel_id=1, source_target_pairs={{0,12},{1,13},{2,14},{3,15},{4,8},{5,9},{6,10},{7,11},{8,4},{9,5},... | collective-permute-start | bytes 98312 | tf_op jit(solution)/shard_map/ppermute | solution.py:193
  12.4 4.7 %load.1 = (f32[2,80,128,128]{3,2,1,0:T(8,128)S(1)}, f32[2,80,128,128]{3,2,1,0:T(8,128)S(1)}) custom-call(f32[2,80,128,128]{3,2,1,0:T(8,128)} %source.1), custom_call_target="tpu_custom_call" | custom-call | bytes 20971520 | tf_op jit(solution)/shard_map/load/pallas_call | solution.py:239
  17.1 0.1 hot.1
  17.2 2.1 %first.2 = (f32[2,128,128]{2,1,0:T(8,128)S(1)}, f32[128,128]{1,0:T(8,128)S(1)}) custom-call(f32[2,80,128,128]{3,2,1,0:T(8,128)S(1)} %get-tuple-element.21.flipped, f32[128,128]{1,0:T(8,128)S(1)} %maximum_select_fusion.fluence, f32[128,128]{1,0:T(8,128)S(1)} %bitcast.10, bf16[80,128]{1,0:T(8,128)(2,1)S(1)} %get-tuple-element.22.col_hot, ...), custom_call_target="tpu_custom_call" | custom-call | tf_op jit(solution)/shard_map/first/pallas_call | solution.py:252
  19.4 0.5 collective-permute-start.3
  19.8 0.9 collective-permute-done.3
  20.8 1.5 %collective-permute-start.4 = (f32[128,128]{1,0:T(8,128)S(1)}, f32[128,128]{1,0:T(8,128)S(1)}, u32[]{:S(2)}, u32[]{:S(2)}) collective-permute-start(f32[128,128]{1,0:T(8,128)S(1)} %log_add_fusion.1.sum_a), channel_id=1, source_target_pairs={{0,24},{8,16},{16,8},{24,0},{1,25},{9,17},{17,9},{25,1},{2,26},{10... | collective-permute-start | bytes 196616 | tf_op jit(solution)/shard_map/ppermute | solution.py:164
  22.3 2.4 %collective-permute-done.4.sum_b = f32[128,128]{1,0:T(8,128)S(1)} collective-permute-done((f32[128,128]{1,0:T(8,128)S(1)}, f32[128,128]{1,0:T(8,128)S(1)}, u32[]{:S(2)}, u32[]{:S(2)}) %collective-permute-start.4) | collective-permute-done | bytes 65568 | tf_op jit(solution)/shard_map/ppermute | solution.py:164
  24.8 2.8 %second.2 = (f32[2,128,128]{2,1,0:T(8,128)S(1)}, f32[2,128,128]{2,1,0:T(8,128)S(1)}) custom-call(f32[2,80,128,128]{3,2,1,0:T(8,128)S(1)} %get-tuple-element.20.blocks, f32[2,128,128]{2,1,0:T(8,128)S(1)} %get-tuple-element.24.excess, f32[128,128]{1,0:T(8,128)S(1)} %log_add_fusion.1.sum_a, f32[128,128]{1,0:T(8,128)S(1)} %collective-permute-done.4.sum_b, ...), custom_call_target="tpu_custom_call" | custom-call | tf_op jit(solution)/shard_map/second/pallas_call | solution.py:262
  27.5 1.6 %collective-permute-start.5 = (f32[2,128,128]{2,1,0:T(8,128)S(1)}, f32[2,128,128]{2,1,0:T(8,128)S(1)}, u32[]{:S(2)}, u32[]{:S(2)}) collective-permute-start(f32[2,128,128]{2,1,0:T(8,128)S(1)} %get-tuple-element.28), channel_id=1, source_target_pairs={{0,1},{1,0},{2,3},{3,2},{4,5},{5,4},{6,7},{7,6},{8,9},{9,8},{10,11... | collective-permute-start | bytes 393224 | tf_op jit(solution)/shard_map/ppermute | solution.py:164
  29.1 4.2 %collective-permute-done.5 = f32[2,128,128]{2,1,0:T(8,128)S(1)} collective-permute-done((f32[2,128,128]{2,1,0:T(8,128)S(1)}, f32[2,128,128]{2,1,0:T(8,128)S(1)}, u32[]{:S(2)}, u32[]{:S(2)}) %collective-permute-start.5) | collective-permute-done | bytes 131104 | tf_op jit(solution)/shard_map/ppermute | solution.py:164
  33.3 1.6 %collective-permute-start.6 = (f32[2,128,128]{2,1,0:T(8,128)S(1)}, f32[2,128,128]{2,1,0:T(8,128)S(1)}, u32[]{:S(2)}, u32[]{:S(2)}) collective-permute-start(f32[2,128,128]{2,1,0:T(8,128)S(1)} %add.50), channel_id=1, source_target_pairs={{0,2},{1,3},{2,0},{3,1},{4,6},{5,7},{6,4},{7,5},{8,10},{9,11},{10,... | collective-permute-start | bytes 393224 | tf_op jit(solution)/shard_map/ppermute | solution.py:164
  34.9 3.4 %collective-permute-done.6 = f32[2,128,128]{2,1,0:T(8,128)S(1)} collective-permute-done((f32[2,128,128]{2,1,0:T(8,128)S(1)}, f32[2,128,128]{2,1,0:T(8,128)S(1)}, u32[]{:S(2)}, u32[]{:S(2)}) %collective-permute-start.6) | collective-permute-done | bytes 131104 | tf_op jit(solution)/shard_map/ppermute | solution.py:164
  38.4 0.3 collective-permute-start.7
  38.7 7.2 %collective-permute-done.7.grad_b = f32[2,128,128]{2,1,0:T(8,128)S(1)} collective-permute-done((f32[2,128,128]{2,1,0:T(8,128)S(1)}, f32[2,128,128]{2,1,0:T(8,128)S(1)}, u32[]{:S(2)}, u32[]{:S(2)}) %collective-permute-start.7) | collective-permute-done | bytes 131104 | tf_op jit(solution)/shard_map/ppermute | solution.py:164
  45.9 5.9 %third.2 = (f32[2,128,128]{2,1,0:T(8,128)S(1)}, f32[2,128,128]{2,1,0:T(8,128)S(1)}) custom-call(f32[2,80,128,128]{3,2,1,0:T(8,128)S(1)} %get-tuple-element.20.blocks, f32[2,80,128,128]{3,2,1,0:T(8,128)S(1)} %get-tuple-element.21.flipped, f32[128,128]{1,0:T(8,128)S(1)} %maximum_select_fusion.fluence, f32[2,128,128]{2,1,0:T(8,128)S(1)} %add.51.grad_a, ...), custom_call_target="tpu_custom_call" | custom-call | tf_op jit(solution)/shard_map/third/pallas_call | solution.py:272
  51.8 1.6 %collective-permute-start.8 = (f32[2,128,128]{2,1,0:T(8,128)S(1)}, f32[2,128,128]{2,1,0:T(8,128)S(1)}, u32[]{:S(2)}, u32[]{:S(2)}) collective-permute-start(f32[2,128,128]{2,1,0:T(8,128)S(1)} %get-tuple-element.31), channel_id=1, source_target_pairs={{0,1},{1,0},{2,3},{3,2},{4,5},{5,4},{6,7},{7,6},{8,9},{9,8},{10,11... | collective-permute-start | bytes 393224 | tf_op jit(solution)/shard_map/ppermute | solution.py:164
  53.4 3.4 %collective-permute-done.8 = f32[2,128,128]{2,1,0:T(8,128)S(1)} collective-permute-done((f32[2,128,128]{2,1,0:T(8,128)S(1)}, f32[2,128,128]{2,1,0:T(8,128)S(1)}, u32[]{:S(2)}, u32[]{:S(2)}) %collective-permute-start.8) | collective-permute-done | bytes 131104 | tf_op jit(solution)/shard_map/ppermute | solution.py:164
  56.9 0.4 collective-permute-start.9
  57.3 5.2 %collective-permute-done.9 = f32[2,128,128]{2,1,0:T(8,128)S(1)} collective-permute-done((f32[2,128,128]{2,1,0:T(8,128)S(1)}, f32[2,128,128]{2,1,0:T(8,128)S(1)}, u32[]{:S(2)}, u32[]{:S(2)}) %collective-permute-start.9) | collective-permute-done | bytes 131104 | tf_op jit(solution)/shard_map/ppermute | solution.py:164
  62.6 7.3 %collective-permute-done.10 = f32[2,128,128]{2,1,0:T(8,128)S(1)} collective-permute-done((f32[2,128,128]{2,1,0:T(8,128)S(1)}, f32[2,128,128]{2,1,0:T(8,128)S(1)}, u32[]{:S(2)}, u32[]{:S(2)}) %collective-permute-start.10) | collective-permute-done | bytes 131104 | tf_op jit(solution)/shard_map/ppermute | solution.py:164
  69.9 1.2 collective-permute-done.11
  71.2 1.4 %collective-permute-start.12 = (f32[128,128]{1,0:T(8,128)S(1)}, f32[128,128]{1,0:T(8,128)S(1)}, u32[]{:S(2)}, u32[]{:S(2)}) collective-permute-start(f32[128,128]{1,0:T(8,128)S(1)} %add.55), channel_id=1, source_target_pairs={{0,24},{8,16},{16,8},{24,0},{1,25},{9,17},{17,9},{25,1},{2,26},{10... | collective-permute-start | bytes 196616 | tf_op jit(solution)/shard_map/ppermute | solution.py:164
  72.6 2.7 %collective-permute-done.12 = f32[128,128]{1,0:T(8,128)S(1)} collective-permute-done((f32[128,128]{1,0:T(8,128)S(1)}, f32[128,128]{1,0:T(8,128)S(1)}, u32[]{:S(2)}, u32[]{:S(2)}) %collective-permute-start.12) | collective-permute-done | bytes 65568 | tf_op jit(solution)/shard_map/ppermute | solution.py:164
  75.3 2.1 %first.3 = (f32[2,128,128]{2,1,0:T(8,128)S(1)}, f32[128,128]{1,0:T(8,128)S(1)}) custom-call(f32[2,80,128,128]{3,2,1,0:T(8,128)S(1)} %get-tuple-element.21.flipped, f32[128,128]{1,0:T(8,128)S(1)} %add_multiply_fusion.fluence, f32[128,128]{1,0:T(8,128)S(1)} %bitcast.12, bf16[80,128]{1,0:T(8,128)(2,1)S(1)} %get-tuple-element.22.col_hot, ...), custom_call_target="tpu_custom_call" | custom-call | tf_op jit(solution)/shard_map/first/pallas_call | solution.py:252
  77.4 0.2 collective-permute-start.13
  77.7 1.1 collective-permute-done.13
  78.8 1.4 %collective-permute-start.14 = (f32[128,128]{1,0:T(8,128)S(1)}, f32[128,128]{1,0:T(8,128)S(1)}, u32[]{:S(2)}, u32[]{:S(2)}) collective-permute-start(f32[128,128]{1,0:T(8,128)S(1)} %log_add_fusion.sum_a), channel_id=1, source_target_pairs={{0,24},{8,16},{16,8},{24,0},{1,25},{9,17},{17,9},{25,1},{2,26},{10... | collective-permute-start | bytes 196616 | tf_op jit(solution)/shard_map/ppermute | solution.py:164
  80.2 2.7 %collective-permute-done.14.sum_b = f32[128,128]{1,0:T(8,128)S(1)} collective-permute-done((f32[128,128]{1,0:T(8,128)S(1)}, f32[128,128]{1,0:T(8,128)S(1)}, u32[]{:S(2)}, u32[]{:S(2)}) %collective-permute-start.14) | collective-permute-done | bytes 65568 | tf_op jit(solution)/shard_map/ppermute | solution.py:164
  82.9 2.8 %second.3 = (f32[2,128,128]{2,1,0:T(8,128)S(1)}, f32[2,128,128]{2,1,0:T(8,128)S(1)}) custom-call(f32[2,80,128,128]{3,2,1,0:T(8,128)S(1)} %get-tuple-element.20.blocks, f32[2,128,128]{2,1,0:T(8,128)S(1)} %get-tuple-element.32.excess, f32[128,128]{1,0:T(8,128)S(1)} %log_add_fusion.sum_a, f32[128,128]{1,0:T(8,128)S(1)} %collective-permute-done.14.sum_b, ...), custom_call_target="tpu_custom_call" | custom-call | tf_op jit(solution)/shard_map/second/pallas_call | solution.py:262
  85.7 1.7 %collective-permute-start.15 = (f32[2,128,128]{2,1,0:T(8,128)S(1)}, f32[2,128,128]{2,1,0:T(8,128)S(1)}, u32[]{:S(2)}, u32[]{:S(2)}) collective-permute-start(f32[2,128,128]{2,1,0:T(8,128)S(1)} %get-tuple-element.34), channel_id=1, source_target_pairs={{0,1},{1,0},{2,3},{3,2},{4,5},{5,4},{6,7},{7,6},{8,9},{9,8},{10,11... | collective-permute-start | bytes 393224 | tf_op jit(solution)/shard_map/ppermute | solution.py:164
  87.4 3.9 %collective-permute-done.15 = f32[2,128,128]{2,1,0:T(8,128)S(1)} collective-permute-done((f32[2,128,128]{2,1,0:T(8,128)S(1)}, f32[2,128,128]{2,1,0:T(8,128)S(1)}, u32[]{:S(2)}, u32[]{:S(2)}) %collective-permute-start.15) | collective-permute-done | bytes 131104 | tf_op jit(solution)/shard_map/ppermute | solution.py:164
  91.4 5.0 %collective-permute-done.16 = f32[2,128,128]{2,1,0:T(8,128)S(1)} collective-permute-done((f32[2,128,128]{2,1,0:T(8,128)S(1)}, f32[2,128,128]{2,1,0:T(8,128)S(1)}, u32[]{:S(2)}, u32[]{:S(2)}) %collective-permute-start.16) | collective-permute-done | bytes 131104 | tf_op jit(solution)/shard_map/ppermute | solution.py:164
  96.5 7.0 %collective-permute-done.17.grad_b = f32[2,128,128]{2,1,0:T(8,128)S(1)} collective-permute-done((f32[2,128,128]{2,1,0:T(8,128)S(1)}, f32[2,128,128]{2,1,0:T(8,128)S(1)}, u32[]{:S(2)}, u32[]{:S(2)}) %collective-permute-start.17) | collective-permute-done | bytes 131104 | tf_op jit(solution)/shard_map/ppermute | solution.py:164
  103.5 5.8 %third.3 = (f32[2,128,128]{2,1,0:T(8,128)S(1)}, f32[2,128,128]{2,1,0:T(8,128)S(1)}) custom-call(f32[2,80,128,128]{3,2,1,0:T(8,128)S(1)} %get-tuple-element.20.blocks, f32[2,80,128,128]{3,2,1,0:T(8,128)S(1)} %get-tuple-element.21.flipped, f32[128,128]{1,0:T(8,128)S(1)} %add_multiply_fusion.fluence, f32[2,128,128]{2,1,0:T(8,128)S(1)} %add.60.grad_a, ...), custom_call_target="tpu_custom_call" | custom-call | tf_op jit(solution)/shard_map/third/pallas_call | solution.py:272
  109.2 0.7 copy.7
  109.9 3.4 %all-to-all-start = ((f32[2,8,16,128]{3,2,0,1:T(8,128)}), f32[2,8,16,128]{3,2,0,1:T(8,128)S(1)}, u32[]{:S(2)}, u32[]{:S(2)}) async-start(f32[2,8,16,128]{3,2,0,1:T(8,128)} %copy.7), calls=%async_computation | async-start | bytes 262144 | tf_op jit(solution)/shard_map/all_to_all | solution.py:288
  113.3 7.3 %all-to-all-done = f32[2,8,16,128]{3,2,0,1:T(8,128)S(1)} async-done(((f32[2,8,16,128]{3,2,0,1:T(8,128)}), f32[2,8,16,128]{3,2,0,1:T(8,128)S(1)}, u32[]{:S(2)}, u32[]{:S(2)}) %all-to-all-start) | async-done | bytes 131104 | tf_op jit(solution)/shard_map/all_to_all | solution.py:288
  120.7 1.2 collective-permute-done.18
  121.8 1.3 %collective-permute-start.19 = (f32[16,128]{1,0:T(8,128)S(1)}, f32[16,128]{1,0:T(8,128)S(1)}, u32[]{:S(2)}, u32[]{:S(2)}) collective-permute-start(f32[16,128]{1,0:T(8,128)S(1)} %add.62), channel_id=1, source_target_pairs={{0,24},{8,16},{16,8},{24,0},{1,25},{9,17},{17,9},{25,1},{2,26},{10... | collective-permute-start | bytes 24584 | tf_op jit(solution)/shard_map/ppermute | solution.py:164
  123.2 0.8 copy.10
  123.9 1.0 collective-permute-done.19
  124.9 0.6 multiply_bitcast_fusion
  (26 shorter events, 0.6 us)
Async XLA Ops:
  0.6 16.5 %copy-start.1 = (s32[80,2]{0,1:T(2,128)S(1)}, s32[80,2]{0,1:T(2,128)}, u32[]{:S(2)}) copy-start(s32[80,2]{0,1:T(2,128)} %param.6) | copy-start | bytes 1924
  0.6 16.6 %copy-start = (f32[16384]{0:T(1024)S(1)}, f32[16384]{0:T(1024)}, u32[]{:S(2)}) copy-start(f32[16384]{0:T(1024)} %param.8) | copy-start | bytes 196612
  0.7 4.0 %collective-permute-start = (f32[16,128]{1,0:T(8,128)}, f32[16,128]{1,0:T(8,128)S(1)}, u32[]{:S(2)}, u32[]{:S(2)}) collective-permute-start(f32[16,128]{1,0:T(8,128)} %bitcast.18), channel_id=1, source_target_pairs={{0,9},{1,8},{2,11},{3,10},{4,13},{5,12},{6,15},{7,14},{8,1},{9,0},... | collective-permute-start | bytes 24584 | tf_op jit(solution)/shard_map/ppermute | solution.py:193
  5.4 3.6 %collective-permute-start.1 = (f32[32,128]{1,0:T(8,128)S(1)}, f32[32,128]{1,0:T(8,128)S(1)}, u32[]{:S(2)}, u32[]{:S(2)}) collective-permute-start(f32[32,128]{1,0:T(8,128)S(1)} %maximum_select_fusion.2), channel_id=1, source_target_pairs={{0,10},{1,11},{2,8},{3,9},{4,14},{5,15},{6,12},{7,13},{8,2},{9,3},... | collective-permute-start | bytes 49160 | tf_op jit(solution)/shard_map/ppermute | solution.py:193
  9.0 8.2 %collective-permute-start.2 = (f32[64,128]{1,0:T(8,128)S(1)}, f32[64,128]{1,0:T(8,128)S(1)}, u32[]{:S(2)}, u32[]{:S(2)}) collective-permute-start(f32[64,128]{1,0:T(8,128)S(1)} %maximum_select_fusion.1), channel_id=1, source_target_pairs={{0,12},{1,13},{2,14},{3,15},{4,8},{5,9},{6,10},{7,11},{8,4},{9,5},... | collective-permute-start | bytes 98312 | tf_op jit(solution)/shard_map/ppermute | solution.py:193
  19.4 1.4 %collective-permute-start.3 = (f32[128,128]{1,0:T(8,128)S(1)}, f32[128,128]{1,0:T(8,128)S(1)}, u32[]{:S(2)}, u32[]{:S(2)}) collective-permute-start(f32[128,128]{1,0:T(8,128)S(1)} %get-tuple-element.25), channel_id=1, source_target_pairs={{0,8},{8,0},{16,24},{24,16},{1,9},{9,1},{17,25},{25,17},{2,10},{10... | collective-permute-start | bytes 196616 | tf_op jit(solution)/shard_map/ppermute | solution.py:164
  20.8 4.0 %collective-permute-start.4 = (f32[128,128]{1,0:T(8,128)S(1)}, f32[128,128]{1,0:T(8,128)S(1)}, u32[]{:S(2)}, u32[]{:S(2)}) collective-permute-start(f32[128,128]{1,0:T(8,128)S(1)} %log_add_fusion.1.sum_a), channel_id=1, source_target_pairs={{0,24},{8,16},{16,8},{24,0},{1,25},{9,17},{17,9},{25,1},{2,26},{10... | collective-permute-start | bytes 196616 | tf_op jit(solution)/shard_map/ppermute | solution.py:164
  27.5 5.8 %collective-permute-start.5 = (f32[2,128,128]{2,1,0:T(8,128)S(1)}, f32[2,128,128]{2,1,0:T(8,128)S(1)}, u32[]{:S(2)}, u32[]{:S(2)}) collective-permute-start(f32[2,128,128]{2,1,0:T(8,128)S(1)} %get-tuple-element.28), channel_id=1, source_target_pairs={{0,1},{1,0},{2,3},{3,2},{4,5},{5,4},{6,7},{7,6},{8,9},{9,8},{10,11... | collective-permute-start | bytes 393224 | tf_op jit(solution)/shard_map/ppermute | solution.py:164
  33.3 5.0 %collective-permute-start.6 = (f32[2,128,128]{2,1,0:T(8,128)S(1)}, f32[2,128,128]{2,1,0:T(8,128)S(1)}, u32[]{:S(2)}, u32[]{:S(2)}) collective-permute-start(f32[2,128,128]{2,1,0:T(8,128)S(1)} %add.50), channel_id=1, source_target_pairs={{0,2},{1,3},{2,0},{3,1},{4,6},{5,7},{6,4},{7,5},{8,10},{9,11},{10,... | collective-permute-start | bytes 393224 | tf_op jit(solution)/shard_map/ppermute | solution.py:164
  38.4 7.5 %collective-permute-start.7 = (f32[2,128,128]{2,1,0:T(8,128)S(1)}, f32[2,128,128]{2,1,0:T(8,128)S(1)}, u32[]{:S(2)}, u32[]{:S(2)}) collective-permute-start(f32[2,128,128]{2,1,0:T(8,128)S(1)} %add.51.grad_a), channel_id=1, source_target_pairs={{0,4},{1,5},{2,6},{3,7},{4,0},{5,1},{6,2},{7,3},{8,12},{9,13},{10,... | collective-permute-start | bytes 393224 | tf_op jit(solution)/shard_map/ppermute | solution.py:164
  51.8 5.0 %collective-permute-start.8 = (f32[2,128,128]{2,1,0:T(8,128)S(1)}, f32[2,128,128]{2,1,0:T(8,128)S(1)}, u32[]{:S(2)}, u32[]{:S(2)}) collective-permute-start(f32[2,128,128]{2,1,0:T(8,128)S(1)} %get-tuple-element.31), channel_id=1, source_target_pairs={{0,1},{1,0},{2,3},{3,2},{4,5},{5,4},{6,7},{7,6},{8,9},{9,8},{10,11... | collective-permute-start | bytes 393224 | tf_op jit(solution)/shard_map/ppermute | solution.py:164
  56.9 5.6 %collective-permute-start.9 = (f32[2,128,128]{2,1,0:T(8,128)S(1)}, f32[2,128,128]{2,1,0:T(8,128)S(1)}, u32[]{:S(2)}, u32[]{:S(2)}) collective-permute-start(f32[2,128,128]{2,1,0:T(8,128)S(1)} %add.52), channel_id=1, source_target_pairs={{0,2},{1,3},{2,0},{3,1},{4,6},{5,7},{6,4},{7,5},{8,10},{9,11},{10,... | collective-permute-start | bytes 393224 | tf_op jit(solution)/shard_map/ppermute | solution.py:164
  62.5 7.3 %collective-permute-start.10 = (f32[2,128,128]{2,1,0:T(8,128)S(1)}, f32[2,128,128]{2,1,0:T(8,128)S(1)}, u32[]{:S(2)}, u32[]{:S(2)}) collective-permute-start(f32[2,128,128]{2,1,0:T(8,128)S(1)} %add.53), channel_id=1, source_target_pairs={{0,4},{1,5},{2,6},{3,7},{4,0},{5,1},{6,2},{7,3},{8,12},{9,13},{10,... | collective-permute-start | bytes 393224 | tf_op jit(solution)/shard_map/ppermute | solution.py:164
  69.9 1.3 %collective-permute-start.11 = (f32[128,128]{1,0:T(8,128)S(1)}, f32[128,128]{1,0:T(8,128)S(1)}, u32[]{:S(2)}, u32[]{:S(2)}) collective-permute-start(f32[128,128]{1,0:T(8,128)S(1)} %maximum_reduce_fusion), channel_id=1, source_target_pairs={{0,8},{8,0},{16,24},{24,16},{1,9},{9,1},{17,25},{25,17},{2,10},{10... | collective-permute-start | bytes 196616 | tf_op jit(solution)/shard_map/ppermute | solution.py:164
  71.2 4.1 %collective-permute-start.12 = (f32[128,128]{1,0:T(8,128)S(1)}, f32[128,128]{1,0:T(8,128)S(1)}, u32[]{:S(2)}, u32[]{:S(2)}) collective-permute-start(f32[128,128]{1,0:T(8,128)S(1)} %add.55), channel_id=1, source_target_pairs={{0,24},{8,16},{16,8},{24,0},{1,25},{9,17},{17,9},{25,1},{2,26},{10... | collective-permute-start | bytes 196616 | tf_op jit(solution)/shard_map/ppermute | solution.py:164
  77.4 1.3 %collective-permute-start.13 = (f32[128,128]{1,0:T(8,128)S(1)}, f32[128,128]{1,0:T(8,128)S(1)}, u32[]{:S(2)}, u32[]{:S(2)}) collective-permute-start(f32[128,128]{1,0:T(8,128)S(1)} %get-tuple-element.33), channel_id=1, source_target_pairs={{0,8},{8,0},{16,24},{24,16},{1,9},{9,1},{17,25},{25,17},{2,10},{10... | collective-permute-start | bytes 196616 | tf_op jit(solution)/shard_map/ppermute | solution.py:164
  78.8 4.1 %collective-permute-start.14 = (f32[128,128]{1,0:T(8,128)S(1)}, f32[128,128]{1,0:T(8,128)S(1)}, u32[]{:S(2)}, u32[]{:S(2)}) collective-permute-start(f32[128,128]{1,0:T(8,128)S(1)} %log_add_fusion.sum_a), channel_id=1, source_target_pairs={{0,24},{8,16},{16,8},{24,0},{1,25},{9,17},{17,9},{25,1},{2,26},{10... | collective-permute-start | bytes 196616 | tf_op jit(solution)/shard_map/ppermute | solution.py:164
  85.7 5.6 %collective-permute-start.15 = (f32[2,128,128]{2,1,0:T(8,128)S(1)}, f32[2,128,128]{2,1,0:T(8,128)S(1)}, u32[]{:S(2)}, u32[]{:S(2)}) collective-permute-start(f32[2,128,128]{2,1,0:T(8,128)S(1)} %get-tuple-element.34), channel_id=1, source_target_pairs={{0,1},{1,0},{2,3},{3,2},{4,5},{5,4},{6,7},{7,6},{8,9},{9,8},{10,11... | collective-permute-start | bytes 393224 | tf_op jit(solution)/shard_map/ppermute | solution.py:164
  91.3 5.0 %collective-permute-start.16 = (f32[2,128,128]{2,1,0:T(8,128)S(1)}, f32[2,128,128]{2,1,0:T(8,128)S(1)}, u32[]{:S(2)}, u32[]{:S(2)}) collective-permute-start(f32[2,128,128]{2,1,0:T(8,128)S(1)} %add.59), channel_id=1, source_target_pairs={{0,2},{1,3},{2,0},{3,1},{4,6},{5,7},{6,4},{7,5},{8,10},{9,11},{10,... | collective-permute-start | bytes 393224 | tf_op jit(solution)/shard_map/ppermute | solution.py:164
  96.4 7.1 %collective-permute-start.17 = (f32[2,128,128]{2,1,0:T(8,128)S(1)}, f32[2,128,128]{2,1,0:T(8,128)S(1)}, u32[]{:S(2)}, u32[]{:S(2)}) collective-permute-start(f32[2,128,128]{2,1,0:T(8,128)S(1)} %add.60.grad_a), channel_id=1, source_target_pairs={{0,4},{1,5},{2,6},{3,7},{4,0},{5,1},{6,2},{7,3},{8,12},{9,13},{10,... | collective-permute-start | bytes 393224 | tf_op jit(solution)/shard_map/ppermute | solution.py:164
  109.9 10.7 %all-to-all-start = ((f32[2,8,16,128]{3,2,0,1:T(8,128)}), f32[2,8,16,128]{3,2,0,1:T(8,128)S(1)}, u32[]{:S(2)}, u32[]{:S(2)}) async-start(f32[2,8,16,128]{3,2,0,1:T(8,128)} %copy.7), calls=%async_computation | async-start | bytes 262144 | tf_op jit(solution)/shard_map/all_to_all | solution.py:288
  120.6 1.2 collective-permute-start.18
  121.8 3.1 %collective-permute-start.19 = (f32[16,128]{1,0:T(8,128)S(1)}, f32[16,128]{1,0:T(8,128)S(1)}, u32[]{:S(2)}, u32[]{:S(2)}) collective-permute-start(f32[16,128]{1,0:T(8,128)S(1)} %add.62), channel_id=1, source_target_pairs={{0,24},{8,16},{16,8},{24,0},{1,25},{9,17},{17,9},{25,1},{2,26},{10... | collective-permute-start | bytes 24584 | tf_op jit(solution)/shard_map/ppermute | solution.py:164

commit v4 on v3

v4 whole, which is shorter than its diff:
```python
import functools

import jax
import jax.numpy as jnp
from jax import lax
from jax.experimental import pallas as pl
from jax.experimental.pallas import tpu as pltpu
from jax.sharding import PartitionSpec as P

ROUNDS = 2
SHARPNESS = 2.0
STEP_SIZE = 0.5
F32 = jnp.float32
BF16 = jnp.bfloat16
VMEM = pl.BlockSpec(memory_space=pltpu.VMEM)
FAR = pl.BlockSpec(memory_space=pltpu.HBM)


def split3(x):
    return jnp.concatenate(pieces(x), axis=-1)


def exact(hot, x):
    n = x.shape[1]
    y = jnp.dot(hot, split3(x), preferred_element_type=F32)
    return y[:, :n] + y[:, n : 2 * n] + y[:, 2 * n :]


def columns(x):
    pad = -x.shape[0] % 128
    if pad:
        x = jnp.concatenate([x, jnp.zeros((pad, x.shape[1]), x.dtype)], axis=0)
    return x.T


def flat(x):
    pad = -x.shape[1] % 128
    slots = x.shape[1]
    if pad:
        x = jnp.concatenate([x, jnp.zeros((x.shape[0], pad), x.dtype)], axis=1)
    return x.T[:slots]


def pieces(x):
    high = x.astype(BF16)
    rest = x - high.astype(F32)
    mid = rest.astype(BF16)
    return high, mid, (rest - mid.astype(F32)).astype(BF16)


def products(whole, upper, lower, picked, rows):
    scen, kept, side, _ = whole.shape
    split_slots = upper.shape[1]
    turned, parts = {}, {}
    for x in picked:
        if id(x) not in turned:
            turned[id(x)] = columns(x[:kept])
            parts[id(x)] = [y.astype(F32) for y in pieces(x)]
    depth = max(16, 8 * scen)
    sub = lax.broadcasted_iota(jnp.int32, (depth, side), 0)
    order = [(k + 0.5) / kept for k in range(kept)]
    order += [(m + 0.5) / split_slots for m in range(split_slots)]
    for k in sorted(range(kept + split_slots), key=lambda k: (order[k], k)):
        if k < kept:
            wide = {}
            for s in range(scen):
                key = id(picked[s])
                if key not in wide:
                    wide[key] = jnp.broadcast_to(turned[key][:, k : k + 1], (side, side))
                rows[s, k : k + 1, :] = jnp.sum(whole[s, k] * wide[key], axis=0, keepdims=True)
            continue
        m = k - kept
        firsts, stacks = [], {}
        for s in range(scen):
            key = id(picked[s])
            high, mid, low = [x[k : k + 1, :] for x in parts[key]]
            firsts.append(jnp.where(sub == 8 * s, high, 0.0).astype(BF16))
            if key not in stacks:
                stack = jnp.where(sub == 0, high, jnp.where(sub == 1, mid, jnp.where(sub == 2, low, 0.0)))
                stacks[key] = jnp.concatenate([stack.astype(BF16)] * 2, axis=1)
        rest = jnp.dot(jnp.concatenate(firsts, axis=1), lower[m], preferred_element_type=F32)
        for s in range(scen):
            main = jnp.dot(stacks[id(picked[s])], upper[s, m], preferred_element_type=F32)
            total = main[:8] + rest[8 * s : 8 * s + 8]
            rows[s, k : k + 1, :] = jnp.sum(total, axis=0, keepdims=True)


def merge(a, b):
    top = jnp.maximum(a, b)
    return top + jnp.log(jnp.exp(a - top) + jnp.exp(b - top))


def load_kernel(chunks, source, whole, whole_t, upper, upper_t, lower, lower_t, held, sems):
    scen, _, side, _ = source.shape
    kept = whole.shape[1]
    copies = []
    for n, (first, size) in enumerate(chunks):
        part = pl.ds(first, size)
        to = whole.at[:, part] if first < kept else held.at[:, pl.ds(first - kept, size)]
        copies.append(pltpu.make_async_copy(source.at[:, part], to, sems.at[n]))
    for copy in copies:
        copy.start()
    for copy, (first, size) in zip(copies, chunks):
        copy.wait()
        for k in range(first, first + size):
            for s in range(scen):
                if k < kept:
                    whole_t[s, k] = whole[s, k].T
                    continue
                m = k - kept
                block = held[s, m]
                for x, up, low in ((block, upper, lower), (block.T, upper_t, lower_t)):
                    high, mid, rest = pieces(x)
                    up[s, m, :side] = high
                    up[s, m, side:] = mid
                    low[m, s * side : (s + 1) * side] = rest


def hot_kernel(
    map_far, fluence, counts, row_hot, row_hot_t, col_hot, col_hot_t, mine, block_map, sems
):
    copies = [
        pltpu.make_async_copy(map_far, block_map, sems.at[0]),
        pltpu.make_async_copy(fluence, mine, sems.at[1]),
    ]
    for copy in copies:
        copy.start()
    for copy in copies:
        copy.wait()
    row_blocks, slots = row_hot_t.shape
    usable = lax.broadcasted_iota(jnp.int32, (row_blocks, slots), 1) < counts[...]
    rows = lax.broadcasted_iota(jnp.int32, (row_blocks, slots), 0) == block_map[0:1, :]
    row = jnp.where(rows & usable, 1.0, 0.0).astype(F32)
    beam_blocks = col_hot_t.shape[0]
    cols = lax.broadcasted_iota(jnp.int32, (beam_blocks, slots), 0) == block_map[1:2, :]
    col = jnp.where(cols, 1.0, 0.0).astype(F32)
    row_hot_t[...] = row.astype(BF16)
    col_hot_t[...] = col.astype(BF16)
    row_hot[...] = flat(row).astype(BF16)
    col_hot[...] = flat(col).astype(BF16)


def join_kernel(bit, mine, other, joined):
    size = mine.shape[0]
    low = lax.axis_index("vox") & bit == 0
    joined[:size] = jnp.where(low, mine[...], other[...])
    joined[size:] = jnp.where(low, other[...], mine[...])


def first_kernel(
    whole, upper, lower, fluence, target, col_hot, row_hot_t, excess, score_sum, rows
):
    scen = whole.shape[0]
    picked = exact(col_hot[...], fluence[...])
    products(whole, upper, lower, [picked] * scen, rows)
    scores = []
    for s in range(scen):
        e = exact(row_hot_t[...], rows[s]) - target[...]
        excess[s] = e
        scores.append(SHARPNESS * e * e)
    top = functools.reduce(jnp.maximum, scores)
    total = functools.reduce(jnp.add, [jnp.exp(score - top) for score in scores])
    score_sum[...] = top + jnp.log(total)


def second_kernel(
    whole, upper, lower, excess, sum_a, sum_b, row_hot, col_hot_t, weights, gradient, rows
):
    scen = excess.shape[0]
    total = merge(sum_a[...], sum_b[...])
    picked = []
    for s in range(scen):
        e = excess[s]
        w = jnp.exp(SHARPNESS * e * e - total)
        weights[s] = w
        picked.append(exact(row_hot[...], 2.0 * w * e))
    products(whole, upper, lower, picked, rows)
    for s in range(scen):
        gradient[s] = exact(col_hot_t[...], rows[s])


def third_kernel(
    whole, upper, lower, whole_t, upper_t, lower_t, fluence, grad_a, grad_b, weights, target,
    col_hot, col_hot_t, row_hot, row_hot_t, copies, gradient, rows
):
    scen = weights.shape[0]
    picked = []
    for s in range(scen):
        c = jnp.maximum(fluence[...] - STEP_SIZE * (grad_a[s] + grad_b[s]), 0.0)
        copies[s] = c
        picked.append(exact(col_hot[...], c))
    products(whole_t, upper_t, lower_t, picked, rows)
    picked = []
    for s in range(scen):
        e = exact(row_hot_t[...], rows[s]) - target[...]
        picked.append(exact(row_hot[...], 2.0 * weights[s] * e))
    products(whole, upper, lower, picked, rows)
    for s in range(scen):
        g = exact(col_hot_t[...], rows[s])
        if len(gradient.shape) == 3:
            gradient[s] = g
        else:
            gradient[:, s] = g.reshape(gradient.shape[0], *gradient.shape[2:])


def near(x):
    return pltpu.with_memory_space_constraint(x, pltpu.VMEM)


def far(x):
    return pltpu.with_memory_space_constraint(x, pltpu.HBM)


def swap(x, axis, bit):
    return lax.ppermute(x, axis, [(i, i ^ bit) for i in range(lax.axis_size(axis))])


def bits(axis):
    size = lax.axis_size(axis)
    if size & (size - 1) or size < 2:
        raise ValueError("axis size")
    return [1 << b for b in range(size.bit_length() - 1)]


def reduce_vox(x):
    steps = bits("vox")
    orders = [steps, steps]
    if len(steps) > 2:
        first, far, *between = steps[0], steps[-1], *steps[1:-1]
        orders = [[far, first, *between], [first, far, *between]]
    other = None
    for pair in zip(*orders):
        if other is not None:
            x = x + other
        other = lax.ppermute(
            x,
            "vox",
            [(v, v ^ pair[(v & steps[-2]) // steps[-2]]) for v in range(lax.axis_size("vox"))],
        )
    return x, other


def reduce_scen(x, combine):
    steps = bits("scen")
    x = [x, swap(x, "scen", steps[0])]
    for bit in steps[1:]:
        both = combine(*x)
        x = [both, swap(both, "scen", bit ^ 1)]
    return x


def swap_both(x, bit):
    scen, vox = lax.axis_size("scen"), lax.axis_size("vox")
    pairs = [(s * vox + v, (s ^ 1) * vox + (v ^ bit)) for s in range(scen) for v in range(vox)]
    return lax.ppermute(x, ("scen", "vox"), pairs)


def split(total, parts):
    return [total * (n + 1) // parts - total * n // parts for n in range(parts)]


def body(dose_blocks, block_map, block_counts, target, fluence_init):
    scen, slots, side, _ = dose_blocks.shape
    share = fluence_init.shape[0]
    parts = lax.axis_size("vox")
    beam_blocks = share * parts // side
    row_blocks = target.shape[0] // side
    scen_total = scen * lax.axis_size("scen")
    params = pltpu.CompilerParams(vmem_limit_bytes=16 * 2**20)
    passes = scen * slots * side * side
    dense = lambda *shape: jax.ShapeDtypeStruct(shape, F32)
    scratch = [pltpu.VMEM((scen, slots, side), F32)]

    target = target.reshape(row_blocks, side)
    fluence = fluence_init.reshape(share // side, side)
    row_hot, row_hot_t, col_hot, col_hot_t, mine = pl.pallas_call(
        hot_kernel,
        name="hot",
        out_shape=(
            jax.ShapeDtypeStruct((slots, row_blocks), BF16),
            jax.ShapeDtypeStruct((row_blocks, slots), BF16),
            jax.ShapeDtypeStruct((slots, beam_blocks), BF16),
            jax.ShapeDtypeStruct((beam_blocks, slots), BF16),
            dense(*fluence.shape),
        ),
        in_specs=[FAR, FAR, VMEM],
        out_specs=(VMEM,) * 5,
        scratch_shapes=[pltpu.VMEM((2, slots), jnp.int32), pltpu.SemaphoreType.DMA((2,))],
        compiler_params=params,
    )(far(block_map.T), far(fluence), block_counts.reshape(1, 1))

    for bit in bits("vox"):
        other = swap_both(fluence, bit)
        if bit == 1:
            fluence = mine
        rows_here = fluence.shape[0]
        fluence = pl.pallas_call(
            functools.partial(join_kernel, bit),
            name="join",
            out_shape=dense(2 * rows_here, side),
            in_specs=[VMEM] * 2,
            out_specs=VMEM,
            compiler_params=params,
        )(fluence, other)

    kept = slots * 2 // 5
    rest = slots - kept
    chunks = [(n * kept // 4, kept) for n in range(4)] + [(kept + n * rest // 6, rest) for n in range(6)]
    ends = [first for first, _ in chunks[1:]] + [slots]
    chunks = [(first, end - first, of) for (first, of), end in zip(chunks, ends) if end > first]
    chunks.sort(key=lambda chunk: (chunk[0] % kept if chunk[0] < kept else chunk[0] - kept) / chunk[2])
    chunks = [(first, size) for first, size, _ in chunks]
    near_blocks = pl.pallas_call(
        functools.partial(load_kernel, chunks),
        name="load",
        out_shape=(pltpu.VMEM((scen, kept, side, side), F32),) * 2
        + (pltpu.VMEM((scen, rest, 2 * side, side), BF16),) * 2
        + (pltpu.VMEM((rest, scen * side, side), BF16),) * 2,
        in_specs=[FAR],
        out_specs=(VMEM,) * 6,
        scratch_shapes=[
            pltpu.VMEM((scen, rest, side, side), F32),
            pltpu.SemaphoreType.DMA((len(chunks),)),
        ],
        compiler_params=params,
        cost_estimate=pl.CostEstimate(flops=0, bytes_accessed=8 * passes, transcendentals=0),
    )(far(dose_blocks))
    blocks = [near(x) for x in near_blocks[0::2]]
    flipped = [near(x) for x in near_blocks[1::2]]

    for outer_round in range(ROUNDS):
        excess, score_sum = pl.pallas_call(
            first_kernel,
            name="first",
            out_shape=(dense(scen, row_blocks, side), dense(row_blocks, side)),
            in_specs=[VMEM] * 7,
            out_specs=(VMEM,) * 2,
            scratch_shapes=scratch,
            compiler_params=params,
        )(*flipped, fluence, target, col_hot, row_hot_t)
        sum_a, sum_b = reduce_scen(score_sum, merge)
        weights, gradient = pl.pallas_call(
            second_kernel,
            name="second",
            out_shape=(dense(scen, row_blocks, side), dense(scen, beam_blocks, side)),
            in_specs=[VMEM] * 8,
            out_specs=(VMEM,) * 2,
            scratch_shapes=scratch,
            compiler_params=params,
        )(*blocks, excess, sum_a, sum_b, row_hot, col_hot_t)
        grad_a, grad_b = reduce_vox(gradient)
        last = outer_round == ROUNDS - 1
        form = (parts, scen, share // side, side) if last else (scen, beam_blocks, side)
        copies, gradient = pl.pallas_call(
            third_kernel,
            name="third",
            out_shape=(dense(scen, beam_blocks, side), dense(*form)),
            in_specs=[VMEM] * 15,
            out_specs=(VMEM,) * 2,
            scratch_shapes=scratch,
            compiler_params=params,
        )(
            *blocks, *flipped, fluence, grad_a, grad_b, weights, target,
            col_hot, col_hot_t, row_hot, row_hot_t,
        )
        if not last:
            grad_a, grad_b = reduce_vox(gradient)
        else:
            gradient = lax.all_to_all(gradient, "vox", split_axis=0, concat_axis=0, tiled=True)
            grad_a, grad_b = jnp.sum(gradient, axis=0), 0.0
            start = lax.axis_index("vox") * (share // side)
            copies = lax.dynamic_slice_in_dim(copies, start, share // side, 1)
        copies = jnp.maximum(copies - STEP_SIZE * (grad_a + grad_b), 0.0)
        mean_a, mean_b = reduce_scen(jnp.sum(copies, axis=0), jnp.add)
        fluence = (mean_a + mean_b) / scen_total
    return fluence.reshape(share), weights.reshape(scen, row_blocks * side)


def solution(mesh):
    placed = (P("scen", "vox", None, None), P("vox", None), P("vox"), P("vox"), P("vox"))
    return jax.shard_map(
        body, mesh=mesh, in_specs=placed, out_specs=(P("vox"), P("scen", "vox")), check_vma=False
    )
```

time: 126 us -> 117 us (0.929)
  waiting for transfers between devices: 70.1 us -> 64 us
  Pallas kernels: 26.2 us -> 23.7 us
  starting transfers between devices: 24.6 us -> 26 us
    ppermute x17 -> x8, waiting for transfers between devices: 59.8 us -> 13.4 us  [swap(): lax.ppermute(x, axis, [(i, i ^ bit) for i in range(lax.axis_size(axis))])]
    ppermute x0 -> x9, waiting for transfers between devices: none -> 41.8 us  [reduce_vox(): lax.ppermute(x, 'vox', [(v, v ^ pair[(v & steps[-2]) // steps[-2]]) for v...]
    ppermute x0 -> x9, starting transfers between devices: none -> 8.91 us  [reduce_vox(): lax.ppermute(x, 'vox', [(v, v ^ pair[(v & steps[-2]) // steps[-2]]) for v...]
    ppermute x17 -> x8, starting transfers between devices: 13.9 us -> 6.36 us  [swap(): lax.ppermute(x, axis, [(i, i ^ bit) for i in range(lax.axis_size(axis))])]
    pallas_call x2, Pallas kernels: 11.7 us -> 9.35 us  [body(): pl.pallas_call(third_kernel, name='third', out_shape=(dense(scen, beam_bl...]
    ppermute x3, waiting for transfers between devices: 3.02 us -> 1.47 us  [swap_both(): return lax.ppermute(x, ('scen', 'vox'), pairs)]
    pallas_call x2, Pallas kernels: 5.52 us -> 4.22 us  [body(): pl.pallas_call(second_kernel, name='second', out_shape=(dense(scen, row_b...]
    pallas_call x1 -> x4, Pallas kernels: 4.69 us -> 4.98 us  [the longest x1 4.96 us: body(): pl.pallas_call(functools.partial(load_kernel, chunks), name='load', out_s...]
  transfers between devices with their start and end apart: 21 -> 21, of which waited for: 20 -> 19; matrix products, arithmetic and copies ran while one was open for 1% -> 1% of each run, Pallas kernels for 4% -> 5%
where the time goes in v4:
time: 117 us
  waiting for transfers between devices  64 us (55%)
  starting transfers between devices  26 us (22%)
  Pallas kernels  23.7 us (20%)
  between operations  1.45 us (1%)
    ppermute x9, waiting for transfers between devices, reduce_vox(): lax.ppermute(x, 'vox', [(v, v ^ pair[(v & steps[-2]) // steps[-2]]) for v...  41.8 us
    ppermute x8, waiting for transfers between devices, swap(): lax.ppermute(x, axis, [(i, i ^ bit) for i in range(lax.axis_size(axis))])  13.4 us
    pallas_call x2, Pallas kernels, body(): pl.pallas_call(third_kernel, name='third', out_shape=(dense(scen, beam_bl...  9.35 us
    ppermute x9, starting transfers between devices, reduce_vox(): lax.ppermute(x, 'vox', [(v, v ^ pair[(v & steps[-2]) // steps[-2]]) for v...  8.91 us
    ppermute x3, starting transfers between devices, swap_both(): return lax.ppermute(x, ('scen', 'vox'), pairs)  7.36 us
    all_to_all x1, waiting for transfers between devices, body(): lax.all_to_all(gradient, 'vox', split_axis=0, concat_axis=0, tiled=True)  7.28 us
    ppermute x8, starting transfers between devices, swap(): lax.ppermute(x, axis, [(i, i ^ bit) for i in range(lax.axis_size(axis))])  6.36 us
    pallas_call x1, Pallas kernels, body(): pl.pallas_call(functools.partial(load_kernel, chunks), name='load', out_s...  4.96 us
  transfers between devices with their start and end apart: 21, of which 19 were waited for; matrix products, arithmetic and copies ran while one was open for 1% of the time, Pallas kernels for 5%

profile of v4, /device:TPU:0, one launch (start us, length us, event | category | flops | bytes accessed | tf_op | source)
XLA Modules:
  0.0 116.7 jit_solution(9660347403639250454)
XLA Ops:
  0.6 2.4 %collective-permute-start = (f32[16,128]{1,0:T(8,128)}, f32[16,128]{1,0:T(8,128)S(1)}, u32[]{:S(2)}, u32[]{:S(2)}) collective-permute-start(f32[16,128]{1,0:T(8,128)} %bitcast.17), channel_id=1, source_target_pairs={{0,9},{1,8},{2,11},{3,10},{4,13},{5,12},{6,15},{7,14},{8,1},{9,0},... | collective-permute-start | bytes 24584 | tf_op jit(solution)/shard_map/ppermute | solution.py:255
  3.7 0.9 hot.1
  4.7 2.1 %collective-permute-start.1 = (f32[32,128]{1,0:T(8,128)S(1)}, f32[32,128]{1,0:T(8,128)S(1)}, u32[]{:S(2)}, u32[]{:S(2)}) collective-permute-start(f32[32,128]{1,0:T(8,128)S(1)} %join.3.mine), channel_id=1, source_target_pairs={{0,10},{1,11},{2,8},{3,9},{4,14},{5,15},{6,12},{7,13},{8,2},{9,3},... | collective-permute-start | bytes 49160 | tf_op jit(solution)/shard_map/ppermute | solution.py:255
  6.8 1.4 %collective-permute-done.1.other = f32[32,128]{1,0:T(8,128)S(1)} collective-permute-done((f32[32,128]{1,0:T(8,128)S(1)}, f32[32,128]{1,0:T(8,128)S(1)}, u32[]{:S(2)}, u32[]{:S(2)}) %collective-permute-start.1) | collective-permute-done | bytes 16416 | tf_op jit(solution)/shard_map/ppermute | solution.py:255
  8.2 2.8 %collective-permute-start.2 = (f32[64,128]{1,0:T(8,128)S(1)}, f32[64,128]{1,0:T(8,128)S(1)}, u32[]{:S(2)}, u32[]{:S(2)}) collective-permute-start(f32[64,128]{1,0:T(8,128)S(1)} %join.4.mine), channel_id=1, source_target_pairs={{0,12},{1,13},{2,14},{3,15},{4,8},{5,9},{6,10},{7,11},{8,4},{9,5},... | collective-permute-start | bytes 98312 | tf_op jit(solution)/shard_map/ppermute | solution.py:255
  11.0 5.0 %load.1 = (f32[2,32,128,128]{3,2,1,0:T(8,128)S(1)}, f32[2,32,128,128]{3,2,1,0:T(8,128)S(1)}, bf16[2,48,256,128]{3,2,1,0:T(8,128)(2,1)S(1)}, bf16[2,48,256,128]{3...) custom-call(f32[2,80,128,128]{3,2,1,0:T(8,128)} %source.1), custom_call_target="tpu_custom_call" | custom-call | bytes 20971520 | tf_op jit(solution)/shard_map/load/pallas_call | solution.py:313
  16.0 2.0 %first.2 = (f32[2,128,128]{2,1,0:T(8,128)S(1)}, f32[128,128]{1,0:T(8,128)S(1)}) custom-call(f32[2,32,128,128]{3,2,1,0:T(8,128)S(1)} %get-tuple-element.28.whole.whole_t, bf16[2,48,256,128]{3,2,1,0:T(8,128)(2,1)S(1)} %get-tuple-element.29.upper.upper_t, bf16[48,256,128]{2,1,0:T(8,128)(2,1)S(1)} %get-tuple-element.30.lower.lower_t, ...), custom_call_target="tpu_custom_call" | custom-call | tf_op jit(solution)/shard_map/first/pallas_call | solution.py:332
  18.1 0.5 collective-permute-start.3
  18.5 0.9 collective-permute-done.3
  19.5 1.5 %collective-permute-start.4 = (f32[128,128]{1,0:T(8,128)S(1)}, f32[128,128]{1,0:T(8,128)S(1)}, u32[]{:S(2)}, u32[]{:S(2)}) collective-permute-start(f32[128,128]{1,0:T(8,128)S(1)} %log_add_fusion.1.sum_a), channel_id=1, source_target_pairs={{0,24},{8,16},{16,8},{24,0},{1,25},{9,17},{17,9},{25,1},{2,26},{10... | collective-permute-start | bytes 196616 | tf_op jit(solution)/shard_map/ppermute | solution.py:215
  21.0 2.5 %collective-permute-done.4.sum_b = f32[128,128]{1,0:T(8,128)S(1)} collective-permute-done((f32[128,128]{1,0:T(8,128)S(1)}, f32[128,128]{1,0:T(8,128)S(1)}, u32[]{:S(2)}, u32[]{:S(2)}) %collective-permute-start.4) | collective-permute-done | bytes 65568 | tf_op jit(solution)/shard_map/ppermute | solution.py:215
  23.5 2.1 %second.2 = (f32[2,128,128]{2,1,0:T(8,128)S(1)}, f32[2,128,128]{2,1,0:T(8,128)S(1)}) custom-call(f32[2,32,128,128]{3,2,1,0:T(8,128)S(1)} %get-tuple-element.25.whole, bf16[2,48,256,128]{3,2,1,0:T(8,128)(2,1)S(1)} %get-tuple-element.26.upper, bf16[48,256,128]{2,1,0:T(8,128)(2,1)S(1)} %get-tuple-element.27.lower, f32[2,128,128]{2,1,0:T(8,128)S(1)} %get-tuple-element.34.excess, ...), custom_call_target="tpu_custom_call" | custom-call | tf_op jit(solution)/shard_map/second/pallas_call | solution.py:342
  25.6 0.4 collective-permute-start.5
  26.0 6.2 %collective-permute-done.5 = f32[2,128,128]{2,1,0:T(8,128)S(1)} collective-permute-done((f32[2,128,128]{2,1,0:T(8,128)S(1)}, f32[2,128,128]{2,1,0:T(8,128)S(1)}, u32[]{:S(2)}, u32[]{:S(2)}) %collective-permute-start.5) | collective-permute-done | bytes 131104 | tf_op jit(solution)/shard_map/ppermute | solution.py:235
  32.2 1.6 %collective-permute-start.6 = (f32[2,128,128]{2,1,0:T(8,128)S(1)}, f32[2,128,128]{2,1,0:T(8,128)S(1)}, u32[]{:S(2)}, u32[]{:S(2)}) collective-permute-start(f32[2,128,128]{2,1,0:T(8,128)S(1)} %add.50), channel_id=1, source_target_pairs={{0,1},{1,0},{2,6},{3,7},{4,5},{5,4},{6,2},{7,3},{8,9},{9,8},{10,14... | collective-permute-start | bytes 393224 | tf_op jit(solution)/shard_map/ppermute | solution.py:235
  33.8 3.4 %collective-permute-done.6 = f32[2,128,128]{2,1,0:T(8,128)S(1)} collective-permute-done((f32[2,128,128]{2,1,0:T(8,128)S(1)}, f32[2,128,128]{2,1,0:T(8,128)S(1)}, u32[]{:S(2)}, u32[]{:S(2)}) %collective-permute-start.6) | collective-permute-done | bytes 131104 | tf_op jit(solution)/shard_map/ppermute | solution.py:235
  37.3 2.0 %collective-permute-start.7 = (f32[2,128,128]{2,1,0:T(8,128)S(1)}, f32[2,128,128]{2,1,0:T(8,128)S(1)}, u32[]{:S(2)}, u32[]{:S(2)}) collective-permute-start(f32[2,128,128]{2,1,0:T(8,128)S(1)} %add.51.grad_a), channel_id=1, source_target_pairs={{0,2},{1,3},{2,0},{3,1},{4,6},{5,7},{6,4},{7,5},{8,10},{9,11},{10,... | collective-permute-start | bytes 393224 | tf_op jit(solution)/shard_map/ppermute | solution.py:235
  39.3 3.0 %collective-permute-done.7.grad_b = f32[2,128,128]{2,1,0:T(8,128)S(1)} collective-permute-done((f32[2,128,128]{2,1,0:T(8,128)S(1)}, f32[2,128,128]{2,1,0:T(8,128)S(1)}, u32[]{:S(2)}, u32[]{:S(2)}) %collective-permute-start.7) | collective-permute-done | bytes 131104 | tf_op jit(solution)/shard_map/ppermute | solution.py:235
  42.3 4.4 %third.2 = (f32[2,128,128]{2,1,0:T(8,128)S(1)}, f32[2,128,128]{2,1,0:T(8,128)S(1)}) custom-call(f32[2,32,128,128]{3,2,1,0:T(8,128)S(1)} %get-tuple-element.25.whole, bf16[2,48,256,128]{3,2,1,0:T(8,128)(2,1)S(1)} %get-tuple-element.26.upper, bf16[48,256,128]{2,1,0:T(8,128)(2,1)S(1)} %get-tuple-element.27.lower, ...), custom_call_target="tpu_custom_call" | custom-call | tf_op jit(solution)/shard_map/third/pallas_call | solution.py:354
  46.7 0.4 collective-permute-start.8
  47.1 7.0 %collective-permute-done.8 = f32[2,128,128]{2,1,0:T(8,128)S(1)} collective-permute-done((f32[2,128,128]{2,1,0:T(8,128)S(1)}, f32[2,128,128]{2,1,0:T(8,128)S(1)}, u32[]{:S(2)}, u32[]{:S(2)}) %collective-permute-start.8) | collective-permute-done | bytes 131104 | tf_op jit(solution)/shard_map/ppermute | solution.py:235
  54.1 1.6 %collective-permute-start.9 = (f32[2,128,128]{2,1,0:T(8,128)S(1)}, f32[2,128,128]{2,1,0:T(8,128)S(1)}, u32[]{:S(2)}, u32[]{:S(2)}) collective-permute-start(f32[2,128,128]{2,1,0:T(8,128)S(1)} %add.52), channel_id=1, source_target_pairs={{0,1},{1,0},{2,6},{3,7},{4,5},{5,4},{6,2},{7,3},{8,9},{9,8},{10,14... | collective-permute-start | bytes 393224 | tf_op jit(solution)/shard_map/ppermute | solution.py:235
  55.7 3.4 %collective-permute-done.9 = f32[2,128,128]{2,1,0:T(8,128)S(1)} collective-permute-done((f32[2,128,128]{2,1,0:T(8,128)S(1)}, f32[2,128,128]{2,1,0:T(8,128)S(1)}, u32[]{:S(2)}, u32[]{:S(2)}) %collective-permute-start.9) | collective-permute-done | bytes 131104 | tf_op jit(solution)/shard_map/ppermute | solution.py:235
  59.1 0.6 collective-permute-start.10
  59.7 4.4 %collective-permute-done.10 = f32[2,128,128]{2,1,0:T(8,128)S(1)} collective-permute-done((f32[2,128,128]{2,1,0:T(8,128)S(1)}, f32[2,128,128]{2,1,0:T(8,128)S(1)}, u32[]{:S(2)}, u32[]{:S(2)}) %collective-permute-start.10) | collective-permute-done | bytes 131104 | tf_op jit(solution)/shard_map/ppermute | solution.py:235
  64.2 0.1 collective-permute-start.11
  64.3 1.2 %collective-permute-done.11 = f32[128,128]{1,0:T(8,128)S(1)} collective-permute-done((f32[128,128]{1,0:T(8,128)S(1)}, f32[128,128]{1,0:T(8,128)S(1)}, u32[]{:S(2)}, u32[]{:S(2)}) %collective-permute-start.11) | collective-permute-done | bytes 65568 | tf_op jit(solution)/shard_map/ppermute | solution.py:215
  65.5 1.3 %collective-permute-start.12 = (f32[128,128]{1,0:T(8,128)S(1)}, f32[128,128]{1,0:T(8,128)S(1)}, u32[]{:S(2)}, u32[]{:S(2)}) collective-permute-start(f32[128,128]{1,0:T(8,128)S(1)} %add.55), channel_id=1, source_target_pairs={{0,24},{8,16},{16,8},{24,0},{1,25},{9,17},{17,9},{25,1},{2,26},{10... | collective-permute-start | bytes 196616 | tf_op jit(solution)/shard_map/ppermute | solution.py:215
  66.9 2.8 %collective-permute-done.12 = f32[128,128]{1,0:T(8,128)S(1)} collective-permute-done((f32[128,128]{1,0:T(8,128)S(1)}, f32[128,128]{1,0:T(8,128)S(1)}, u32[]{:S(2)}, u32[]{:S(2)}) %collective-permute-start.12) | collective-permute-done | bytes 65568 | tf_op jit(solution)/shard_map/ppermute | solution.py:215
  69.6 2.2 %first.3 = (f32[2,128,128]{2,1,0:T(8,128)S(1)}, f32[128,128]{1,0:T(8,128)S(1)}) custom-call(f32[2,32,128,128]{3,2,1,0:T(8,128)S(1)} %get-tuple-element.28.whole.whole_t, bf16[2,48,256,128]{3,2,1,0:T(8,128)(2,1)S(1)} %get-tuple-element.29.upper.upper_t, bf16[48,256,128]{2,1,0:T(8,128)(2,1)S(1)} %get-tuple-element.30.lower.lower_t, ...), custom_call_target="tpu_custom_call" | custom-call | tf_op jit(solution)/shard_map/first/pallas_call | solution.py:332
  71.8 0.2 collective-permute-start.13
  72.1 1.1 collective-permute-done.13
  73.2 1.4 %collective-permute-start.14 = (f32[128,128]{1,0:T(8,128)S(1)}, f32[128,128]{1,0:T(8,128)S(1)}, u32[]{:S(2)}, u32[]{:S(2)}) collective-permute-start(f32[128,128]{1,0:T(8,128)S(1)} %log_add_fusion.sum_a), channel_id=1, source_target_pairs={{0,24},{8,16},{16,8},{24,0},{1,25},{9,17},{17,9},{25,1},{2,26},{10... | collective-permute-start | bytes 196616 | tf_op jit(solution)/shard_map/ppermute | solution.py:215
  74.6 2.8 %collective-permute-done.14.sum_b = f32[128,128]{1,0:T(8,128)S(1)} collective-permute-done((f32[128,128]{1,0:T(8,128)S(1)}, f32[128,128]{1,0:T(8,128)S(1)}, u32[]{:S(2)}, u32[]{:S(2)}) %collective-permute-start.14) | collective-permute-done | bytes 65568 | tf_op jit(solution)/shard_map/ppermute | solution.py:215
  77.3 2.1 %second.3 = (f32[2,128,128]{2,1,0:T(8,128)S(1)}, f32[2,128,128]{2,1,0:T(8,128)S(1)}) custom-call(f32[2,32,128,128]{3,2,1,0:T(8,128)S(1)} %get-tuple-element.25.whole, bf16[2,48,256,128]{3,2,1,0:T(8,128)(2,1)S(1)} %get-tuple-element.26.upper, bf16[48,256,128]{2,1,0:T(8,128)(2,1)S(1)} %get-tuple-element.27.lower, f32[2,128,128]{2,1,0:T(8,128)S(1)} %get-tuple-element.42.excess, ...), custom_call_target="tpu_custom_call" | custom-call | tf_op jit(solution)/shard_map/second/pallas_call | solution.py:342
  79.5 6.5 %collective-permute-done.15 = f32[2,128,128]{2,1,0:T(8,128)S(1)} collective-permute-done((f32[2,128,128]{2,1,0:T(8,128)S(1)}, f32[2,128,128]{2,1,0:T(8,128)S(1)}, u32[]{:S(2)}, u32[]{:S(2)}) %collective-permute-start.15) | collective-permute-done | bytes 131104 | tf_op jit(solution)/shard_map/ppermute | solution.py:235
  86.0 1.6 %collective-permute-start.16 = (f32[2,128,128]{2,1,0:T(8,128)S(1)}, f32[2,128,128]{2,1,0:T(8,128)S(1)}, u32[]{:S(2)}, u32[]{:S(2)}) collective-permute-start(f32[2,128,128]{2,1,0:T(8,128)S(1)} %add.59), channel_id=1, source_target_pairs={{0,1},{1,0},{2,6},{3,7},{4,5},{5,4},{6,2},{7,3},{8,9},{9,8},{10,14... | collective-permute-start | bytes 393224 | tf_op jit(solution)/shard_map/ppermute | solution.py:235
  87.6 3.4 %collective-permute-done.16 = f32[2,128,128]{2,1,0:T(8,128)S(1)} collective-permute-done((f32[2,128,128]{2,1,0:T(8,128)S(1)}, f32[2,128,128]{2,1,0:T(8,128)S(1)}, u32[]{:S(2)}, u32[]{:S(2)}) %collective-permute-start.16) | collective-permute-done | bytes 131104 | tf_op jit(solution)/shard_map/ppermute | solution.py:235
  91.0 0.6 collective-permute-start.17
  91.7 4.4 %collective-permute-done.17.grad_b = f32[2,128,128]{2,1,0:T(8,128)S(1)} collective-permute-done((f32[2,128,128]{2,1,0:T(8,128)S(1)}, f32[2,128,128]{2,1,0:T(8,128)S(1)}, u32[]{:S(2)}, u32[]{:S(2)}) %collective-permute-start.17) | collective-permute-done | bytes 131104 | tf_op jit(solution)/shard_map/ppermute | solution.py:235
  96.1 5.0 %third.3 = (f32[2,128,128]{2,1,0:T(8,128)S(1)}, f32[8,2,16,128]{3,2,1,0:T(8,128)}) custom-call(f32[2,32,128,128]{3,2,1,0:T(8,128)S(1)} %get-tuple-element.25.whole, bf16[2,48,256,128]{3,2,1,0:T(8,128)(2,1)S(1)} %get-tuple-element.26.upper, bf16[48,256,128]{2,1,0:T(8,128)(2,1)S(1)} %get-tuple-element.27.lower, ...), custom_call_target="tpu_custom_call" | custom-call | tf_op jit(solution)/shard_map/third/pallas_call | solution.py:354
  101.1 3.4 %all-to-all-start = ((f32[8,2,16,128]{3,2,1,0:T(8,128)}), f32[8,2,16,128]{3,2,1,0:T(8,128)S(1)}, u32[]{:S(2)}, u32[]{:S(2)}) async-start(f32[8,2,16,128]{3,2,1,0:T(8,128)} %get-tuple-element.47), calls=%async_computation | async-start | bytes 262144 | tf_op jit(solution)/shard_map/all_to_all | solution.py:369
  104.4 7.3 %all-to-all-done = f32[8,2,16,128]{3,2,1,0:T(8,128)S(1)} async-done(((f32[8,2,16,128]{3,2,1,0:T(8,128)}), f32[8,2,16,128]{3,2,1,0:T(8,128)S(1)}, u32[]{:S(2)}, u32[]{:S(2)}) %all-to-all-start) | async-done | bytes 131104 | tf_op jit(solution)/shard_map/all_to_all | solution.py:369
  111.8 1.2 collective-permute-done.18
  113.0 1.3 %collective-permute-start.19 = (f32[16,128]{1,0:T(8,128)S(1)}, f32[16,128]{1,0:T(8,128)S(1)}, u32[]{:S(2)}, u32[]{:S(2)}) collective-permute-start(f32[16,128]{1,0:T(8,128)S(1)} %add.62), channel_id=1, source_target_pairs={{0,24},{8,16},{16,8},{24,0},{1,25},{9,17},{17,9},{25,1},{2,26},{10... | collective-permute-start | bytes 24584 | tf_op jit(solution)/shard_map/ppermute | solution.py:215
  114.3 0.8 copy.9
  115.0 1.0 collective-permute-done.19
  116.1 0.6 multiply_bitcast_fusion
  (23 shorter events, 0.5 us)
Async XLA Ops:
  0.6 4.0 %collective-permute-start = (f32[16,128]{1,0:T(8,128)}, f32[16,128]{1,0:T(8,128)S(1)}, u32[]{:S(2)}, u32[]{:S(2)}) collective-permute-start(f32[16,128]{1,0:T(8,128)} %bitcast.17), channel_id=1, source_target_pairs={{0,9},{1,8},{2,11},{3,10},{4,13},{5,12},{6,15},{7,14},{8,1},{9,0},... | collective-permute-start | bytes 24584 | tf_op jit(solution)/shard_map/ppermute | solution.py:255
  4.7 3.6 %collective-permute-start.1 = (f32[32,128]{1,0:T(8,128)S(1)}, f32[32,128]{1,0:T(8,128)S(1)}, u32[]{:S(2)}, u32[]{:S(2)}) collective-permute-start(f32[32,128]{1,0:T(8,128)S(1)} %join.3.mine), channel_id=1, source_target_pairs={{0,10},{1,11},{2,8},{3,9},{4,14},{5,15},{6,12},{7,13},{8,2},{9,3},... | collective-permute-start | bytes 49160 | tf_op jit(solution)/shard_map/ppermute | solution.py:255
  8.2 7.8 %copy-start = (f32[16384]{0:T(1024)S(1)}, f32[16384]{0:T(1024)}, u32[]{:S(2)}) copy-start(f32[16384]{0:T(1024)} %param.8) | copy-start | bytes 196612
  8.2 7.8 %collective-permute-start.2 = (f32[64,128]{1,0:T(8,128)S(1)}, f32[64,128]{1,0:T(8,128)S(1)}, u32[]{:S(2)}, u32[]{:S(2)}) collective-permute-start(f32[64,128]{1,0:T(8,128)S(1)} %join.4.mine), channel_id=1, source_target_pairs={{0,12},{1,13},{2,14},{3,15},{4,8},{5,9},{6,10},{7,11},{8,4},{9,5},... | collective-permute-start | bytes 98312 | tf_op jit(solution)/shard_map/ppermute | solution.py:255
  18.1 1.4 %collective-permute-start.3 = (f32[128,128]{1,0:T(8,128)S(1)}, f32[128,128]{1,0:T(8,128)S(1)}, u32[]{:S(2)}, u32[]{:S(2)}) collective-permute-start(f32[128,128]{1,0:T(8,128)S(1)} %get-tuple-element.35), channel_id=1, source_target_pairs={{0,8},{8,0},{16,24},{24,16},{1,9},{9,1},{17,25},{25,17},{2,10},{10... | collective-permute-start | bytes 196616 | tf_op jit(solution)/shard_map/ppermute | solution.py:215
  19.5 4.0 %collective-permute-start.4 = (f32[128,128]{1,0:T(8,128)S(1)}, f32[128,128]{1,0:T(8,128)S(1)}, u32[]{:S(2)}, u32[]{:S(2)}) collective-permute-start(f32[128,128]{1,0:T(8,128)S(1)} %log_add_fusion.1.sum_a), channel_id=1, source_target_pairs={{0,24},{8,16},{16,8},{24,0},{1,25},{9,17},{17,9},{25,1},{2,26},{10... | collective-permute-start | bytes 196616 | tf_op jit(solution)/shard_map/ppermute | solution.py:215
  25.6 6.7 %collective-permute-start.5 = (f32[2,128,128]{2,1,0:T(8,128)S(1)}, f32[2,128,128]{2,1,0:T(8,128)S(1)}, u32[]{:S(2)}, u32[]{:S(2)}) collective-permute-start(f32[2,128,128]{2,1,0:T(8,128)S(1)} %get-tuple-element.38), channel_id=1, source_target_pairs={{0,4},{1,5},{2,3},{3,2},{4,0},{5,1},{6,7},{7,6},{8,12},{9,13},{10,... | collective-permute-start | bytes 393224 | tf_op jit(solution)/shard_map/ppermute | solution.py:235
  32.2 5.0 %collective-permute-start.6 = (f32[2,128,128]{2,1,0:T(8,128)S(1)}, f32[2,128,128]{2,1,0:T(8,128)S(1)}, u32[]{:S(2)}, u32[]{:S(2)}) collective-permute-start(f32[2,128,128]{2,1,0:T(8,128)S(1)} %add.50), channel_id=1, source_target_pairs={{0,1},{1,0},{2,6},{3,7},{4,5},{5,4},{6,2},{7,3},{8,9},{9,8},{10,14... | collective-permute-start | bytes 393224 | tf_op jit(solution)/shard_map/ppermute | solution.py:235
  37.3 5.0 %collective-permute-start.7 = (f32[2,128,128]{2,1,0:T(8,128)S(1)}, f32[2,128,128]{2,1,0:T(8,128)S(1)}, u32[]{:S(2)}, u32[]{:S(2)}) collective-permute-start(f32[2,128,128]{2,1,0:T(8,128)S(1)} %add.51.grad_a), channel_id=1, source_target_pairs={{0,2},{1,3},{2,0},{3,1},{4,6},{5,7},{6,4},{7,5},{8,10},{9,11},{10,... | collective-permute-start | bytes 393224 | tf_op jit(solution)/shard_map/ppermute | solution.py:235
  46.7 7.3 %collective-permute-start.8 = (f32[2,128,128]{2,1,0:T(8,128)S(1)}, f32[2,128,128]{2,1,0:T(8,128)S(1)}, u32[]{:S(2)}, u32[]{:S(2)}) collective-permute-start(f32[2,128,128]{2,1,0:T(8,128)S(1)} %get-tuple-element.41), channel_id=1, source_target_pairs={{0,4},{1,5},{2,3},{3,2},{4,0},{5,1},{6,7},{7,6},{8,12},{9,13},{10,... | collective-permute-start | bytes 393224 | tf_op jit(solution)/shard_map/ppermute | solution.py:235
  54.1 5.0 %collective-permute-start.9 = (f32[2,128,128]{2,1,0:T(8,128)S(1)}, f32[2,128,128]{2,1,0:T(8,128)S(1)}, u32[]{:S(2)}, u32[]{:S(2)}) collective-permute-start(f32[2,128,128]{2,1,0:T(8,128)S(1)} %add.52), channel_id=1, source_target_pairs={{0,1},{1,0},{2,6},{3,7},{4,5},{5,4},{6,2},{7,3},{8,9},{9,8},{10,14... | collective-permute-start | bytes 393224 | tf_op jit(solution)/shard_map/ppermute | solution.py:235
  59.1 5.0 %collective-permute-start.10 = (f32[2,128,128]{2,1,0:T(8,128)S(1)}, f32[2,128,128]{2,1,0:T(8,128)S(1)}, u32[]{:S(2)}, u32[]{:S(2)}) collective-permute-start(f32[2,128,128]{2,1,0:T(8,128)S(1)} %add.53), channel_id=1, source_target_pairs={{0,2},{1,3},{2,0},{3,1},{4,6},{5,7},{6,4},{7,5},{8,10},{9,11},{10,... | collective-permute-start | bytes 393224 | tf_op jit(solution)/shard_map/ppermute | solution.py:235
  64.2 1.3 %collective-permute-start.11 = (f32[128,128]{1,0:T(8,128)S(1)}, f32[128,128]{1,0:T(8,128)S(1)}, u32[]{:S(2)}, u32[]{:S(2)}) collective-permute-start(f32[128,128]{1,0:T(8,128)S(1)} %maximum_reduce_fusion), channel_id=1, source_target_pairs={{0,8},{8,0},{16,24},{24,16},{1,9},{9,1},{17,25},{25,17},{2,10},{10... | collective-permute-start | bytes 196616 | tf_op jit(solution)/shard_map/ppermute | solution.py:215
  65.5 4.1 %collective-permute-start.12 = (f32[128,128]{1,0:T(8,128)S(1)}, f32[128,128]{1,0:T(8,128)S(1)}, u32[]{:S(2)}, u32[]{:S(2)}) collective-permute-start(f32[128,128]{1,0:T(8,128)S(1)} %add.55), channel_id=1, source_target_pairs={{0,24},{8,16},{16,8},{24,0},{1,25},{9,17},{17,9},{25,1},{2,26},{10... | collective-permute-start | bytes 196616 | tf_op jit(solution)/shard_map/ppermute | solution.py:215
  71.8 1.3 %collective-permute-start.13 = (f32[128,128]{1,0:T(8,128)S(1)}, f32[128,128]{1,0:T(8,128)S(1)}, u32[]{:S(2)}, u32[]{:S(2)}) collective-permute-start(f32[128,128]{1,0:T(8,128)S(1)} %get-tuple-element.43), channel_id=1, source_target_pairs={{0,8},{8,0},{16,24},{24,16},{1,9},{9,1},{17,25},{25,17},{2,10},{10... | collective-permute-start | bytes 196616 | tf_op jit(solution)/shard_map/ppermute | solution.py:215
  73.2 4.1 %collective-permute-start.14 = (f32[128,128]{1,0:T(8,128)S(1)}, f32[128,128]{1,0:T(8,128)S(1)}, u32[]{:S(2)}, u32[]{:S(2)}) collective-permute-start(f32[128,128]{1,0:T(8,128)S(1)} %log_add_fusion.sum_a), channel_id=1, source_target_pairs={{0,24},{8,16},{16,8},{24,0},{1,25},{9,17},{17,9},{25,1},{2,26},{10... | collective-permute-start | bytes 196616 | tf_op jit(solution)/shard_map/ppermute | solution.py:215
  79.4 6.5 %collective-permute-start.15 = (f32[2,128,128]{2,1,0:T(8,128)S(1)}, f32[2,128,128]{2,1,0:T(8,128)S(1)}, u32[]{:S(2)}, u32[]{:S(2)}) collective-permute-start(f32[2,128,128]{2,1,0:T(8,128)S(1)} %get-tuple-element.44), channel_id=1, source_target_pairs={{0,4},{1,5},{2,3},{3,2},{4,0},{5,1},{6,7},{7,6},{8,12},{9,13},{10,... | collective-permute-start | bytes 393224 | tf_op jit(solution)/shard_map/ppermute | solution.py:235
  86.0 5.0 %collective-permute-start.16 = (f32[2,128,128]{2,1,0:T(8,128)S(1)}, f32[2,128,128]{2,1,0:T(8,128)S(1)}, u32[]{:S(2)}, u32[]{:S(2)}) collective-permute-start(f32[2,128,128]{2,1,0:T(8,128)S(1)} %add.59), channel_id=1, source_target_pairs={{0,1},{1,0},{2,6},{3,7},{4,5},{5,4},{6,2},{7,3},{8,9},{9,8},{10,14... | collective-permute-start | bytes 393224 | tf_op jit(solution)/shard_map/ppermute | solution.py:235
  91.0 5.0 %collective-permute-start.17 = (f32[2,128,128]{2,1,0:T(8,128)S(1)}, f32[2,128,128]{2,1,0:T(8,128)S(1)}, u32[]{:S(2)}, u32[]{:S(2)}) collective-permute-start(f32[2,128,128]{2,1,0:T(8,128)S(1)} %add.60.grad_a), channel_id=1, source_target_pairs={{0,2},{1,3},{2,0},{3,1},{4,6},{5,7},{6,4},{7,5},{8,10},{9,11},{10,... | collective-permute-start | bytes 393224 | tf_op jit(solution)/shard_map/ppermute | solution.py:235
  101.1 10.7 %all-to-all-start = ((f32[8,2,16,128]{3,2,1,0:T(8,128)}), f32[8,2,16,128]{3,2,1,0:T(8,128)S(1)}, u32[]{:S(2)}, u32[]{:S(2)}) async-start(f32[8,2,16,128]{3,2,1,0:T(8,128)} %get-tuple-element.47), calls=%async_computation | async-start | bytes 262144 | tf_op jit(solution)/shard_map/all_to_all | solution.py:369
  111.8 1.2 %collective-permute-start.18 = (f32[16,128]{1,0:T(8,128)S(1)}, f32[16,128]{1,0:T(8,128)S(1)}, u32[]{:S(2)}, u32[]{:S(2)}) collective-permute-start(f32[16,128]{1,0:T(8,128)S(1)} %maximum_reduce_fusion.1), channel_id=1, source_target_pairs={{0,8},{8,0},{16,24},{24,16},{1,9},{9,1},{17,25},{25,17},{2,10},{10... | collective-permute-start | bytes 24584 | tf_op jit(solution)/shard_map/ppermute | solution.py:215
  113.0 3.1 %collective-permute-start.19 = (f32[16,128]{1,0:T(8,128)S(1)}, f32[16,128]{1,0:T(8,128)S(1)}, u32[]{:S(2)}, u32[]{:S(2)}) collective-permute-start(f32[16,128]{1,0:T(8,128)S(1)} %add.62), channel_id=1, source_target_pairs={{0,24},{8,16},{16,8},{24,0},{1,25},{9,17},{17,9},{25,1},{2,26},{10... | collective-permute-start | bytes 24584 | tf_op jit(solution)/shard_map/ppermute | solution.py:215

commit v5 on v4

--- a/solution.py
+++ b/solution.py
@@ -90,30 +90,41 @@
     return top + jnp.log(jnp.exp(a - top) + jnp.exp(b - top))
 
 
-def load_kernel(chunks, source, whole, whole_t, upper, upper_t, lower, lower_t, held, sems):
-    scen, _, side, _ = source.shape
-    kept = whole.shape[1]
-    copies = []
-    for n, (first, size) in enumerate(chunks):
-        part = pl.ds(first, size)
-        to = whole.at[:, part] if first < kept else held.at[:, pl.ds(first - kept, size)]
-        copies.append(pltpu.make_async_copy(source.at[:, part], to, sems.at[n]))
-    for copy in copies:
+def bring(source, first, sizes, to, sems):
+    copies, done = [], 0
+    for n, size in enumerate(sizes):
+        copy = pltpu.make_async_copy(
+            source.at[:, pl.ds(first + done, size)], to.at[:, pl.ds(done, size)], sems.at[n]
+        )
         copy.start()
-    for copy, (first, size) in zip(copies, chunks):
+        copies.append((copy, range(done, done + size)))
+        done += size
+    for copy, slots in copies:
         copy.wait()
-        for k in range(first, first + size):
+        yield slots
+
+
+def whole_kernel(sizes, source, order, whole, whole_t, token, sems):
+    del order
+    token[...] = jnp.zeros_like(token)
+    for slots in bring(source, 0, sizes, whole, sems):
+        for k in slots:
+            for s in range(source.shape[0]):
+                whole_t[s, k] = whole[s, k].T
+
+
+def split_kernel(sizes, source, order, upper, upper_t, lower, lower_t, held, sems):
+    del order
+    scen, slots, side, _ = source.shape
+    for brought in bring(source, slots - held.shape[1], sizes, held, sems):
+        for k in brought:
             for s in range(scen):
-                if k < kept:
-                    whole_t[s, k] = whole[s, k].T
-                    continue
-                m = k - kept
-                block = held[s, m]
+                block = held[s, k]
                 for x, up, low in ((block, upper, lower), (block.T, upper_t, lower_t)):
                     high, mid, rest = pieces(x)
-                    up[s, m, :side] = high
-                    up[s, m, side:] = mid
-                    low[m, s * side : (s + 1) * side] = rest
+                    up[s, k, :side] = high
+                    up[s, k, side:] = mid
+                    low[k, s * side : (s + 1) * side] = rest
 
 
 def hot_kernel(
@@ -140,7 +151,8 @@
     col_hot[...] = flat(col).astype(BF16)
 
 
-def join_kernel(bit, mine, other, joined):
+def join_kernel(bit, mine, other, order, joined):
+    del order
     size = mine.shape[0]
     low = lax.axis_index("vox") & bit == 0
     joined[:size] = jnp.where(low, mine[...], other[...])
@@ -181,13 +193,16 @@
 
 def third_kernel(
     whole, upper, lower, whole_t, upper_t, lower_t, fluence, grad_a, grad_b, weights, target,
-    col_hot, col_hot_t, row_hot, row_hot_t, copies, gradient, rows
+    col_hot, col_hot_t, row_hot, row_hot_t, copies, gradient, rows, held
 ):
     scen = weights.shape[0]
+    share = copies.shape[1]
+    mine = pl.ds(0 if share == held.shape[1] else lax.axis_index("vox") * share, share)
     picked = []
     for s in range(scen):
         c = jnp.maximum(fluence[...] - STEP_SIZE * (grad_a[s] + grad_b[s]), 0.0)
-        copies[s] = c
+        held[s] = c
+        copies[s] = held[s, mine]
         picked.append(exact(col_hot[...], c))
     products(whole_t, upper_t, lower_t, picked, rows)
     picked = []
@@ -201,6 +216,11 @@
             gradient[s] = g
         else:
             gradient[:, s] = g.reshape(gradient.shape[0], *gradient.shape[2:])
+
+
+def place_kernel(weights, placed):
+    for s in range(weights.shape[0]):
+        placed[:, s] = weights[s]
 
 
 def near(x):
@@ -289,44 +309,56 @@
         compiler_params=params,
     )(far(block_map.T), far(fluence), block_counts.reshape(1, 1))
 
-    for bit in bits("vox"):
+    kept = slots * 2 // 5
+    rest = slots - kept
+    steps = bits("vox")
+    for n, bit in enumerate(steps):
         other = swap_both(fluence, bit)
-        if bit == 1:
+        if n == 0:
             fluence = mine
-        rows_here = fluence.shape[0]
+        token = fluence
+        if n == max(len(steps) - 2, 0):
+            sizes = split(kept, 4)
+            whole, whole_t, token = pl.pallas_call(
+                functools.partial(whole_kernel, sizes),
+                name="whole",
+                out_shape=(pltpu.VMEM((scen, kept, side, side), F32),) * 2 + (dense(8, 128),),
+                in_specs=[FAR, VMEM],
+                out_specs=(VMEM,) * 3,
+                scratch_shapes=[pltpu.SemaphoreType.DMA((len(sizes),))],
+                compiler_params=params,
+                cost_estimate=pl.CostEstimate(
+                    flops=0, bytes_accessed=3 * passes, transcendentals=0
+                ),
+            )(far(dose_blocks), token)
+        if n == len(steps) - 1:
+            sizes = split(rest, 6)
+            upper, upper_t, lower, lower_t = pl.pallas_call(
+                functools.partial(split_kernel, sizes),
+                name="split",
+                out_shape=(pltpu.VMEM((scen, rest, 2 * side, side), BF16),) * 2
+                + (pltpu.VMEM((rest, scen * side, side), BF16),) * 2,
+                in_specs=[FAR, VMEM],
+                out_specs=(VMEM,) * 4,
+                scratch_shapes=[
+                    pltpu.VMEM((scen, rest, side, side), F32),
+                    pltpu.SemaphoreType.DMA((len(sizes),)),
+                ],
+                compiler_params=params,
+                cost_estimate=pl.CostEstimate(
+                    flops=0, bytes_accessed=5 * passes, transcendentals=0
+                ),
+            )(far(dose_blocks), fluence)
         fluence = pl.pallas_call(
             functools.partial(join_kernel, bit),
             name="join",
-            out_shape=dense(2 * rows_here, side),
-            in_specs=[VMEM] * 2,
+            out_shape=dense(2 * fluence.shape[0], side),
+            in_specs=[VMEM] * 3,
             out_specs=VMEM,
             compiler_params=params,
-        )(fluence, other)
-
-    kept = slots * 2 // 5
-    rest = slots - kept
-    chunks = [(n * kept // 4, kept) for n in range(4)] + [(kept + n * rest // 6, rest) for n in range(6)]
-    ends = [first for first, _ in chunks[1:]] + [slots]
-    chunks = [(first, end - first, of) for (first, of), end in zip(chunks, ends) if end > first]
-    chunks.sort(key=lambda chunk: (chunk[0] % kept if chunk[0] < kept else chunk[0] - kept) / chunk[2])
-    chunks = [(first, size) for first, size, _ in chunks]
-    near_blocks = pl.pallas_call(
-        functools.partial(load_kernel, chunks),
-        name="load",
-        out_shape=(pltpu.VMEM((scen, kept, side, side), F32),) * 2
-        + (pltpu.VMEM((scen, rest, 2 * side, side), BF16),) * 2
-        + (pltpu.VMEM((rest, scen * side, side), BF16),) * 2,
-        in_specs=[FAR],
-        out_specs=(VMEM,) * 6,
-        scratch_shapes=[
-            pltpu.VMEM((scen, rest, side, side), F32),
-            pltpu.SemaphoreType.DMA((len(chunks),)),
-        ],
-        compiler_params=params,
-        cost_estimate=pl.CostEstimate(flops=0, bytes_accessed=8 * passes, transcendentals=0),
-    )(far(dose_blocks))
-    blocks = [near(x) for x in near_blocks[0::2]]
-    flipped = [near(x) for x in near_blocks[1::2]]
+        )(fluence, other, token)
+    blocks = [near(x) for x in (whole, upper, lower)]
+    flipped = [near(x) for x in (whole_t, upper_t, lower_t)]
 
     for outer_round in range(ROUNDS):
         excess, score_sum = pl.pallas_call(
@@ -339,6 +371,7 @@
             compiler_params=params,
         )(*flipped, fluence, target, col_hot, row_hot_t)
         sum_a, sum_b = reduce_scen(score_sum, merge)
+        last = outer_round == ROUNDS - 1
         weights, gradient = pl.pallas_call(
             second_kernel,
             name="second",
@@ -349,15 +382,14 @@
             compiler_params=params,
         )(*blocks, excess, sum_a, sum_b, row_hot, col_hot_t)
         grad_a, grad_b = reduce_vox(gradient)
-        last = outer_round == ROUNDS - 1
         form = (parts, scen, share // side, side) if last else (scen, beam_blocks, side)
         copies, gradient = pl.pallas_call(
             third_kernel,
             name="third",
-            out_shape=(dense(scen, beam_blocks, side), dense(*form)),
+            out_shape=(dense(scen, share // side if last else beam_blocks, side), dense(*form)),
             in_specs=[VMEM] * 15,
             out_specs=(VMEM,) * 2,
-            scratch_shapes=scratch,
+            scratch_shapes=scratch + [pltpu.VMEM((scen, beam_blocks, side), F32)],
             compiler_params=params,
         )(
             *blocks, *flipped, fluence, grad_a, grad_b, weights, target,
@@ -366,14 +398,25 @@
         if not last:
             grad_a, grad_b = reduce_vox(gradient)
         else:
+            weights = pl.pallas_call(
+                place_kernel,
+                name="place",
+                out_shape=dense(row_blocks, scen, side),
+                in_specs=[VMEM],
+                out_specs=VMEM,
+                compiler_params=params,
+                cost_estimate=pl.CostEstimate(
+                    flops=0, bytes_accessed=8 * weights.size, transcendentals=0
+                ),
+            )(near(weights))
+            weights = jnp.swapaxes(weights, 0, 1).reshape(scen, row_blocks * side)
+            gradient, copies, weights = lax.optimization_barrier((gradient, copies, weights))
             gradient = lax.all_to_all(gradient, "vox", split_axis=0, concat_axis=0, tiled=True)
             grad_a, grad_b = jnp.sum(gradient, axis=0), 0.0
-            start = lax.axis_index("vox") * (share // side)
-            copies = lax.dynamic_slice_in_dim(copies, start, share // side, 1)
         copies = jnp.maximum(copies - STEP_SIZE * (grad_a + grad_b), 0.0)
         mean_a, mean_b = reduce_scen(jnp.sum(copies, axis=0), jnp.add)
         fluence = (mean_a + mean_b) / scen_total
-    return fluence.reshape(share), weights.reshape(scen, row_blocks * side)
+    return fluence.reshape(share), weights
 
 
 def solution(mesh):

time: 117 us -> 115 us (0.983)
  blocking collectives: 0 us -> 9.94 us
  waiting for transfers between devices: 64 us -> 57.7 us
  starting transfers between devices: 26 us -> 20 us
    all_to_all x0 -> x1, blocking collectives: none -> 9.94 us  [body(): lax.all_to_all(gradient, 'vox', split_axis=0, concat_axis=0, tiled=True)]
    all_to_all x1 -> x0, waiting for transfers between devices: 7.28 us -> none  [body(): lax.all_to_all(gradient, 'vox', split_axis=0, concat_axis=0, tiled=True)]
    all_to_all x1 -> x0, starting transfers between devices: 3.37 us -> none  [body(): lax.all_to_all(gradient, 'vox', split_axis=0, concat_axis=0, tiled=True)]
    ppermute x9, starting transfers between devices: 8.91 us -> 6.94 us  [reduce_vox(): lax.ppermute(x, 'vox', [(v, v ^ pair[(v & steps[-2]) // steps[-2]]) for v...]
    ppermute x3, waiting for transfers between devices: 1.47 us -> 0.03 us  [swap_both(): return lax.ppermute(x, ('scen', 'vox'), pairs)]
    ppermute x8, waiting for transfers between devices: 13.4 us -> 14.7 us  [swap(): lax.ppermute(x, axis, [(i, i ^ bit) for i in range(lax.axis_size(axis))])]
    pallas_call x3 -> x5, Pallas kernels: 14.3 us -> 15.5 us  [the longest x2 8.61 us: body(): pl.pallas_call(third_kernel, name='third', out_shape=(dense(scen, share /...]
  transfers between devices with their start and end apart: 21 -> 20, of which waited for: 19 -> 17; matrix products, arithmetic and copies ran while one was open for 1% -> 0% of each run, Pallas kernels for 5% -> 7%
where the time goes in v5:
time: 115 us
  waiting for transfers between devices  57.7 us (50%)
  Pallas kernels  24.7 us (21%)
  starting transfers between devices  20 us (17%)
  blocking collectives  9.94 us (9%)
  between operations  1.49 us (1%)
    ppermute x9, waiting for transfers between devices, reduce_vox(): lax.ppermute(x, 'vox', [(v, v ^ pair[(v & steps[-2]) // steps[-2]]) for v...  42.9 us
    ppermute x8, waiting for transfers between devices, swap(): lax.ppermute(x, axis, [(i, i ^ bit) for i in range(lax.axis_size(axis))])  14.7 us
    all_to_all x1, blocking collectives, body(): lax.all_to_all(gradient, 'vox', split_axis=0, concat_axis=0, tiled=True)  9.94 us
    pallas_call x2, Pallas kernels, body(): pl.pallas_call(third_kernel, name='third', out_shape=(dense(scen, share /...  8.61 us
    ppermute x3, starting transfers between devices, swap_both(): return lax.ppermute(x, ('scen', 'vox'), pairs)  7.24 us
    ppermute x9, starting transfers between devices, reduce_vox(): lax.ppermute(x, 'vox', [(v, v ^ pair[(v & steps[-2]) // steps[-2]]) for v...  6.94 us
    ppermute x8, starting transfers between devices, swap(): lax.ppermute(x, axis, [(i, i ^ bit) for i in range(lax.axis_size(axis))])  5.86 us
    pallas_call x2, Pallas kernels, body(): pl.pallas_call(first_kernel, name='first', out_shape=(dense(scen, row_blo...  4.14 us
  transfers between devices with their start and end apart: 20, of which 17 were waited for; matrix products, arithmetic and copies ran while one was open for 0% of the time, Pallas kernels for 7%

profile of v5, /device:TPU:0, one launch (start us, length us, event | category | flops | bytes accessed | tf_op | source)
XLA Modules:
  0.0 114.7 jit_solution(15617509228017909986)
XLA Ops:
  0.6 2.4 %collective-permute-start = (f32[16,128]{1,0:T(8,128)}, f32[16,128]{1,0:T(8,128)S(1)}, u32[]{:S(2)}, u32[]{:S(2)}) collective-permute-start(f32[16,128]{1,0:T(8,128)} %bitcast.15), channel_id=1, source_target_pairs={{0,9},{1,8},{2,11},{3,10},{4,13},{5,12},{6,15},{7,14},{8,1},{9,0},... | collective-permute-start | bytes 24584 | tf_op jit(solution)/shard_map/ppermute | solution.py:275
  3.7 0.9 hot.1
  4.7 2.1 %collective-permute-start.1 = (f32[32,128]{1,0:T(8,128)S(1)}, f32[32,128]{1,0:T(8,128)S(1)}, u32[]{:S(2)}, u32[]{:S(2)}) collective-permute-start(f32[32,128]{1,0:T(8,128)S(1)} %join.3.order.mine), channel_id=1, source_target_pairs={{0,10},{1,11},{2,8},{3,9},{4,14},{5,15},{6,12},{7,13},{8,2},{9,3},... | collective-permute-start | bytes 49160 | tf_op jit(solution)/shard_map/ppermute | solution.py:275
  6.8 2.6 %whole.1 = (f32[2,32,128,128]{3,2,1,0:T(8,128)S(1)}, f32[2,32,128,128]{3,2,1,0:T(8,128)S(1)}, f32[8,128]{1,0:T(8,128)S(1)}) custom-call(f32[2,80,128,128]{3,2,1,0:T(8,128)} %source.3, f32[32,128]{1,0:T(8,128)S(1)} %join.3.order.mine), custom_call_target="tpu_custom_call" | custom-call | bytes 7864320 | tf_op jit(solution)/shard_map/whole/pallas_call | solution.py:322
  9.4 2.7 %collective-permute-start.2 = (f32[64,128]{1,0:T(8,128)S(1)}, f32[64,128]{1,0:T(8,128)S(1)}, u32[]{:S(2)}, u32[]{:S(2)}) collective-permute-start(f32[64,128]{1,0:T(8,128)S(1)} %join.4.order.mine), channel_id=1, source_target_pairs={{0,12},{1,13},{2,14},{3,15},{4,8},{5,9},{6,10},{7,11},{8,4},{9,5},... | collective-permute-start | bytes 98312 | tf_op jit(solution)/shard_map/ppermute | solution.py:275
  12.1 3.6 %split.1 = (bf16[2,48,256,128]{3,2,1,0:T(8,128)(2,1)S(1)}, bf16[2,48,256,128]{3,2,1,0:T(8,128)(2,1)S(1)}, bf16[48,256,128]{2,1,0:T(8,128)(2,1)S(1)}, bf16[48,256,128]{2,1,0:T(8,128)(2,1)S(1)}) custom-call(f32[2,80,128,128]{3,2,1,0:T(8,128)} %source.3, f32[64,128]{1,0:T(8,128)S(1)} %join.4.order.mine), custom_call_target="tpu_custom_call" | custom-call | bytes 13107200 | tf_op jit(solution)/shard_map/split/pallas_call | solution.py:336
  15.7 2.0 %first.2 = (f32[2,128,128]{2,1,0:T(8,128)S(1)}, f32[128,128]{1,0:T(8,128)S(1)}) custom-call(f32[2,32,128,128]{3,2,1,0:T(8,128)S(1)} %get-tuple-element.34.whole.whole_t, bf16[2,48,256,128]{3,2,1,0:T(8,128)(2,1)S(1)} %get-tuple-element.35.upper.upper_t, bf16[48,256,128]{2,1,0:T(8,128)(2,1)S(1)} %get-tuple-element.36.lower.lower_t, ...), custom_call_target="tpu_custom_call" | custom-call | tf_op jit(solution)/shard_map/first/pallas_call | solution.py:364
  17.7 0.1 collective-permute-start.3
  17.9 1.2 %collective-permute-done.3 = f32[128,128]{1,0:T(8,128)S(1)} collective-permute-done((f32[128,128]{1,0:T(8,128)S(1)}, f32[128,128]{1,0:T(8,128)S(1)}, u32[]{:S(2)}, u32[]{:S(2)}) %collective-permute-start.3) | collective-permute-done | bytes 65568 | tf_op jit(solution)/shard_map/ppermute | solution.py:235
  19.1 1.3 %collective-permute-start.4 = (f32[128,128]{1,0:T(8,128)S(1)}, f32[128,128]{1,0:T(8,128)S(1)}, u32[]{:S(2)}, u32[]{:S(2)}) collective-permute-start(f32[128,128]{1,0:T(8,128)S(1)} %log_add_fusion.1.sum_a), channel_id=1, source_target_pairs={{0,24},{8,16},{16,8},{24,0},{1,25},{9,17},{17,9},{25,1},{2,26},{10... | collective-permute-start | bytes 196616 | tf_op jit(solution)/shard_map/ppermute | solution.py:235
  20.4 2.8 %collective-permute-done.4.sum_b = f32[128,128]{1,0:T(8,128)S(1)} collective-permute-done((f32[128,128]{1,0:T(8,128)S(1)}, f32[128,128]{1,0:T(8,128)S(1)}, u32[]{:S(2)}, u32[]{:S(2)}) %collective-permute-start.4) | collective-permute-done | bytes 65568 | tf_op jit(solution)/shard_map/ppermute | solution.py:235
  23.2 2.0 %second.2 = (f32[2,128,128]{2,1,0:T(8,128)S(1)}, f32[2,128,128]{2,1,0:T(8,128)S(1)}) custom-call(f32[2,32,128,128]{3,2,1,0:T(8,128)S(1)} %get-tuple-element.30.whole, bf16[2,48,256,128]{3,2,1,0:T(8,128)(2,1)S(1)} %get-tuple-element.32.upper, bf16[48,256,128]{2,1,0:T(8,128)(2,1)S(1)} %get-tuple-element.33.lower, f32[2,128,128]{2,1,0:T(8,128)S(1)} %get-tuple-element.39.excess, ...), custom_call_target="tpu_custom_call" | custom-call | tf_op jit(solution)/shard_map/second/pallas_call | solution.py:375
  25.3 0.6 collective-permute-start.5
  25.9 5.9 %collective-permute-done.5 = f32[2,128,128]{2,1,0:T(8,128)S(1)} collective-permute-done((f32[2,128,128]{2,1,0:T(8,128)S(1)}, f32[2,128,128]{2,1,0:T(8,128)S(1)}, u32[]{:S(2)}, u32[]{:S(2)}) %collective-permute-start.5) | collective-permute-done | bytes 131104 | tf_op jit(solution)/shard_map/ppermute | solution.py:255
  31.8 1.6 %collective-permute-start.6 = (f32[2,128,128]{2,1,0:T(8,128)S(1)}, f32[2,128,128]{2,1,0:T(8,128)S(1)}, u32[]{:S(2)}, u32[]{:S(2)}) collective-permute-start(f32[2,128,128]{2,1,0:T(8,128)S(1)} %add.47), channel_id=1, source_target_pairs={{0,1},{1,0},{2,6},{3,7},{4,5},{5,4},{6,2},{7,3},{8,9},{9,8},{10,14... | collective-permute-start | bytes 393224 | tf_op jit(solution)/shard_map/ppermute | solution.py:255
  33.4 3.4 %collective-permute-done.6 = f32[2,128,128]{2,1,0:T(8,128)S(1)} collective-permute-done((f32[2,128,128]{2,1,0:T(8,128)S(1)}, f32[2,128,128]{2,1,0:T(8,128)S(1)}, u32[]{:S(2)}, u32[]{:S(2)}) %collective-permute-start.6) | collective-permute-done | bytes 131104 | tf_op jit(solution)/shard_map/ppermute | solution.py:255
  36.9 0.6 collective-permute-start.7
  37.5 4.4 %collective-permute-done.7.grad_b = f32[2,128,128]{2,1,0:T(8,128)S(1)} collective-permute-done((f32[2,128,128]{2,1,0:T(8,128)S(1)}, f32[2,128,128]{2,1,0:T(8,128)S(1)}, u32[]{:S(2)}, u32[]{:S(2)}) %collective-permute-start.7) | collective-permute-done | bytes 131104 | tf_op jit(solution)/shard_map/ppermute | solution.py:255
  41.9 4.3 %third.2 = (f32[2,128,128]{2,1,0:T(8,128)S(1)}, f32[2,128,128]{2,1,0:T(8,128)S(1)}) custom-call(f32[2,32,128,128]{3,2,1,0:T(8,128)S(1)} %get-tuple-element.30.whole, bf16[2,48,256,128]{3,2,1,0:T(8,128)(2,1)S(1)} %get-tuple-element.32.upper, bf16[48,256,128]{2,1,0:T(8,128)(2,1)S(1)} %get-tuple-element.33.lower, ...), custom_call_target="tpu_custom_call" | custom-call | tf_op jit(solution)/shard_map/third/pallas_call | solution.py:386
  46.2 0.7 collective-permute-start.8
  47.0 6.6 %collective-permute-done.8 = f32[2,128,128]{2,1,0:T(8,128)S(1)} collective-permute-done((f32[2,128,128]{2,1,0:T(8,128)S(1)}, f32[2,128,128]{2,1,0:T(8,128)S(1)}, u32[]{:S(2)}, u32[]{:S(2)}) %collective-permute-start.8) | collective-permute-done | bytes 131104 | tf_op jit(solution)/shard_map/ppermute | solution.py:255
  53.6 1.6 %collective-permute-start.9 = (f32[2,128,128]{2,1,0:T(8,128)S(1)}, f32[2,128,128]{2,1,0:T(8,128)S(1)}, u32[]{:S(2)}, u32[]{:S(2)}) collective-permute-start(f32[2,128,128]{2,1,0:T(8,128)S(1)} %add.49), channel_id=1, source_target_pairs={{0,1},{1,0},{2,6},{3,7},{4,5},{5,4},{6,2},{7,3},{8,9},{9,8},{10,14... | collective-permute-start | bytes 393224 | tf_op jit(solution)/shard_map/ppermute | solution.py:255
  55.2 3.4 %collective-permute-done.9 = f32[2,128,128]{2,1,0:T(8,128)S(1)} collective-permute-done((f32[2,128,128]{2,1,0:T(8,128)S(1)}, f32[2,128,128]{2,1,0:T(8,128)S(1)}, u32[]{:S(2)}, u32[]{:S(2)}) %collective-permute-start.9) | collective-permute-done | bytes 131104 | tf_op jit(solution)/shard_map/ppermute | solution.py:255
  58.6 0.1 collective-permute-start.10
  58.7 5.0 %collective-permute-done.10 = f32[2,128,128]{2,1,0:T(8,128)S(1)} collective-permute-done((f32[2,128,128]{2,1,0:T(8,128)S(1)}, f32[2,128,128]{2,1,0:T(8,128)S(1)}, u32[]{:S(2)}, u32[]{:S(2)}) %collective-permute-start.10) | collective-permute-done | bytes 131104 | tf_op jit(solution)/shard_map/ppermute | solution.py:255
  63.7 0.1 collective-permute-start.11
  63.8 1.2 %collective-permute-done.11 = f32[128,128]{1,0:T(8,128)S(1)} collective-permute-done((f32[128,128]{1,0:T(8,128)S(1)}, f32[128,128]{1,0:T(8,128)S(1)}, u32[]{:S(2)}, u32[]{:S(2)}) %collective-permute-start.11) | collective-permute-done | bytes 65568 | tf_op jit(solution)/shard_map/ppermute | solution.py:235
  65.0 1.3 %collective-permute-start.12 = (f32[128,128]{1,0:T(8,128)S(1)}, f32[128,128]{1,0:T(8,128)S(1)}, u32[]{:S(2)}, u32[]{:S(2)}) collective-permute-start(f32[128,128]{1,0:T(8,128)S(1)} %add.52), channel_id=1, source_target_pairs={{0,24},{8,16},{16,8},{24,0},{1,25},{9,17},{17,9},{25,1},{2,26},{10... | collective-permute-start | bytes 196616 | tf_op jit(solution)/shard_map/ppermute | solution.py:235
  66.4 2.8 %collective-permute-done.12 = f32[128,128]{1,0:T(8,128)S(1)} collective-permute-done((f32[128,128]{1,0:T(8,128)S(1)}, f32[128,128]{1,0:T(8,128)S(1)}, u32[]{:S(2)}, u32[]{:S(2)}) %collective-permute-start.12) | collective-permute-done | bytes 65568 | tf_op jit(solution)/shard_map/ppermute | solution.py:235
  69.1 2.2 %first.3 = (f32[2,128,128]{2,1,0:T(8,128)S(1)}, f32[128,128]{1,0:T(8,128)S(1)}) custom-call(f32[2,32,128,128]{3,2,1,0:T(8,128)S(1)} %get-tuple-element.34.whole.whole_t, bf16[2,48,256,128]{3,2,1,0:T(8,128)(2,1)S(1)} %get-tuple-element.35.upper.upper_t, bf16[48,256,128]{2,1,0:T(8,128)(2,1)S(1)} %get-tuple-element.36.lower.lower_t, ...), custom_call_target="tpu_custom_call" | custom-call | tf_op jit(solution)/shard_map/first/pallas_call | solution.py:364
  71.3 0.2 collective-permute-start.13
  71.5 1.1 collective-permute-done.13
  72.7 1.4 %collective-permute-start.14 = (f32[128,128]{1,0:T(8,128)S(1)}, f32[128,128]{1,0:T(8,128)S(1)}, u32[]{:S(2)}, u32[]{:S(2)}) collective-permute-start(f32[128,128]{1,0:T(8,128)S(1)} %log_add_fusion.sum_a), channel_id=1, source_target_pairs={{0,24},{8,16},{16,8},{24,0},{1,25},{9,17},{17,9},{25,1},{2,26},{10... | collective-permute-start | bytes 196616 | tf_op jit(solution)/shard_map/ppermute | solution.py:235
  74.0 2.8 %collective-permute-done.14.sum_b = f32[128,128]{1,0:T(8,128)S(1)} collective-permute-done((f32[128,128]{1,0:T(8,128)S(1)}, f32[128,128]{1,0:T(8,128)S(1)}, u32[]{:S(2)}, u32[]{:S(2)}) %collective-permute-start.14) | collective-permute-done | bytes 65568 | tf_op jit(solution)/shard_map/ppermute | solution.py:235
  76.8 2.0 %second.3 = (f32[2,128,128]{2,1,0:T(8,128)S(1)}, f32[2,128,128]{2,1,0:T(8,128)S(1)}) custom-call(f32[2,32,128,128]{3,2,1,0:T(8,128)S(1)} %get-tuple-element.30.whole, bf16[2,48,256,128]{3,2,1,0:T(8,128)(2,1)S(1)} %get-tuple-element.32.upper, bf16[48,256,128]{2,1,0:T(8,128)(2,1)S(1)} %get-tuple-element.33.lower, f32[2,128,128]{2,1,0:T(8,128)S(1)} %get-tuple-element.47.excess, ...), custom_call_target="tpu_custom_call" | custom-call | tf_op jit(solution)/shard_map/second/pallas_call | solution.py:375
  78.9 6.5 %collective-permute-done.15 = f32[2,128,128]{2,1,0:T(8,128)S(1)} collective-permute-done((f32[2,128,128]{2,1,0:T(8,128)S(1)}, f32[2,128,128]{2,1,0:T(8,128)S(1)}, u32[]{:S(2)}, u32[]{:S(2)}) %collective-permute-start.15) | collective-permute-done | bytes 131104 | tf_op jit(solution)/shard_map/ppermute | solution.py:255
  85.4 1.6 %collective-permute-start.16 = (f32[2,128,128]{2,1,0:T(8,128)S(1)}, f32[2,128,128]{2,1,0:T(8,128)S(1)}, u32[]{:S(2)}, u32[]{:S(2)}) collective-permute-start(f32[2,128,128]{2,1,0:T(8,128)S(1)} %add.56), channel_id=1, source_target_pairs={{0,1},{1,0},{2,6},{3,7},{4,5},{5,4},{6,2},{7,3},{8,9},{9,8},{10,14... | collective-permute-start | bytes 393224 | tf_op jit(solution)/shard_map/ppermute | solution.py:255
  87.0 3.4 %collective-permute-done.16 = f32[2,128,128]{2,1,0:T(8,128)S(1)} collective-permute-done((f32[2,128,128]{2,1,0:T(8,128)S(1)}, f32[2,128,128]{2,1,0:T(8,128)S(1)}, u32[]{:S(2)}, u32[]{:S(2)}) %collective-permute-start.16) | collective-permute-done | bytes 131104 | tf_op jit(solution)/shard_map/ppermute | solution.py:255
  90.4 0.1 collective-permute-start.17
  90.5 0.7 place.1
  91.3 4.2 %collective-permute-done.17.grad_b = f32[2,128,128]{2,1,0:T(8,128)S(1)} collective-permute-done((f32[2,128,128]{2,1,0:T(8,128)S(1)}, f32[2,128,128]{2,1,0:T(8,128)S(1)}, u32[]{:S(2)}, u32[]{:S(2)}) %collective-permute-start.17) | collective-permute-done | bytes 131104 | tf_op jit(solution)/shard_map/ppermute | solution.py:255
  95.5 4.3 %third.3 = (f32[2,16,128]{2,1,0:T(8,128)S(1)}, f32[8,2,16,128]{3,2,1,0:T(8,128)S(1)}) custom-call(f32[2,32,128,128]{3,2,1,0:T(8,128)S(1)} %get-tuple-element.30.whole, bf16[2,48,256,128]{3,2,1,0:T(8,128)(2,1)S(1)} %get-tuple-element.32.upper, bf16[48,256,128]{2,1,0:T(8,128)(2,1)S(1)} %get-tuple-element.33.lower, ...), custom_call_target="tpu_custom_call" | custom-call | tf_op jit(solution)/shard_map/third/pallas_call | solution.py:386
  99.8 9.9 %all_to_all.5 = f32[8,2,16,128]{3,2,1,0:T(8,128)S(1)} all-to-all(f32[8,2,16,128]{3,2,1,0:T(8,128)S(1)} %get-tuple-element.54), channel_id=1, replica_groups=mesh['scen'=4,'vox'=8] {'vox'}, dimensions={0} | all-to-all | bytes 262144 | tf_op jit(solution)/shard_map/all_to_all | solution.py:414
  109.8 0.1 collective-permute-start.18
  109.8 1.2 %collective-permute-done.18 = f32[16,128]{1,0:T(8,128)S(1)} collective-permute-done((f32[16,128]{1,0:T(8,128)S(1)}, f32[16,128]{1,0:T(8,128)S(1)}, u32[]{:S(2)}, u32[]{:S(2)}) %collective-permute-start.18) | collective-permute-done | bytes 8224 | tf_op jit(solution)/shard_map/ppermute | solution.py:235
  111.0 1.3 %collective-permute-start.19 = (f32[16,128]{1,0:T(8,128)S(1)}, f32[16,128]{1,0:T(8,128)S(1)}, u32[]{:S(2)}, u32[]{:S(2)}) collective-permute-start(f32[16,128]{1,0:T(8,128)S(1)} %add.58), channel_id=1, source_target_pairs={{0,24},{8,16},{16,8},{24,0},{1,25},{9,17},{17,9},{25,1},{2,26},{10... | collective-permute-start | bytes 24584 | tf_op jit(solution)/shard_map/ppermute | solution.py:235
  112.3 1.8 %collective-permute-done.19 = f32[16,128]{1,0:T(8,128)S(1)} collective-permute-done((f32[16,128]{1,0:T(8,128)S(1)}, f32[16,128]{1,0:T(8,128)S(1)}, u32[]{:S(2)}, u32[]{:S(2)}) %collective-permute-start.19) | collective-permute-done | bytes 8224 | tf_op jit(solution)/shard_map/ppermute | solution.py:235
  114.1 0.6 multiply_bitcast_fusion
  (23 shorter events, 0.4 us)
Async XLA Ops:
  0.6 4.0 %collective-permute-start = (f32[16,128]{1,0:T(8,128)}, f32[16,128]{1,0:T(8,128)S(1)}, u32[]{:S(2)}, u32[]{:S(2)}) collective-permute-start(f32[16,128]{1,0:T(8,128)} %bitcast.15), channel_id=1, source_target_pairs={{0,9},{1,8},{2,11},{3,10},{4,13},{5,12},{6,15},{7,14},{8,1},{9,0},... | collective-permute-start | bytes 24584 | tf_op jit(solution)/shard_map/ppermute | solution.py:275
  4.7 4.7 %collective-permute-start.1 = (f32[32,128]{1,0:T(8,128)S(1)}, f32[32,128]{1,0:T(8,128)S(1)}, u32[]{:S(2)}, u32[]{:S(2)}) collective-permute-start(f32[32,128]{1,0:T(8,128)S(1)} %join.3.order.mine), channel_id=1, source_target_pairs={{0,10},{1,11},{2,8},{3,9},{4,14},{5,15},{6,12},{7,13},{8,2},{9,3},... | collective-permute-start | bytes 49160 | tf_op jit(solution)/shard_map/ppermute | solution.py:275
  9.4 6.3 %copy-start = (f32[16384]{0:T(1024)S(1)}, f32[16384]{0:T(1024)}, u32[]{:S(2)}) copy-start(f32[16384]{0:T(1024)} %param.8) | copy-start | bytes 196612
  9.4 6.3 %collective-permute-start.2 = (f32[64,128]{1,0:T(8,128)S(1)}, f32[64,128]{1,0:T(8,128)S(1)}, u32[]{:S(2)}, u32[]{:S(2)}) collective-permute-start(f32[64,128]{1,0:T(8,128)S(1)} %join.4.order.mine), channel_id=1, source_target_pairs={{0,12},{1,13},{2,14},{3,15},{4,8},{5,9},{6,10},{7,11},{8,4},{9,5},... | collective-permute-start | bytes 98312 | tf_op jit(solution)/shard_map/ppermute | solution.py:275
  17.7 1.3 %collective-permute-start.3 = (f32[128,128]{1,0:T(8,128)S(1)}, f32[128,128]{1,0:T(8,128)S(1)}, u32[]{:S(2)}, u32[]{:S(2)}) collective-permute-start(f32[128,128]{1,0:T(8,128)S(1)} %get-tuple-element.40), channel_id=1, source_target_pairs={{0,8},{8,0},{16,24},{24,16},{1,9},{9,1},{17,25},{25,17},{2,10},{10... | collective-permute-start | bytes 196616 | tf_op jit(solution)/shard_map/ppermute | solution.py:235
  19.1 4.1 %collective-permute-start.4 = (f32[128,128]{1,0:T(8,128)S(1)}, f32[128,128]{1,0:T(8,128)S(1)}, u32[]{:S(2)}, u32[]{:S(2)}) collective-permute-start(f32[128,128]{1,0:T(8,128)S(1)} %log_add_fusion.1.sum_a), channel_id=1, source_target_pairs={{0,24},{8,16},{16,8},{24,0},{1,25},{9,17},{17,9},{25,1},{2,26},{10... | collective-permute-start | bytes 196616 | tf_op jit(solution)/shard_map/ppermute | solution.py:235
  25.3 6.5 %collective-permute-start.5 = (f32[2,128,128]{2,1,0:T(8,128)S(1)}, f32[2,128,128]{2,1,0:T(8,128)S(1)}, u32[]{:S(2)}, u32[]{:S(2)}) collective-permute-start(f32[2,128,128]{2,1,0:T(8,128)S(1)} %get-tuple-element.43), channel_id=1, source_target_pairs={{0,4},{1,5},{2,3},{3,2},{4,0},{5,1},{6,7},{7,6},{8,12},{9,13},{10,... | collective-permute-start | bytes 393224 | tf_op jit(solution)/shard_map/ppermute | solution.py:255
  31.8 5.0 %collective-permute-start.6 = (f32[2,128,128]{2,1,0:T(8,128)S(1)}, f32[2,128,128]{2,1,0:T(8,128)S(1)}, u32[]{:S(2)}, u32[]{:S(2)}) collective-permute-start(f32[2,128,128]{2,1,0:T(8,128)S(1)} %add.47), channel_id=1, source_target_pairs={{0,1},{1,0},{2,6},{3,7},{4,5},{5,4},{6,2},{7,3},{8,9},{9,8},{10,14... | collective-permute-start | bytes 393224 | tf_op jit(solution)/shard_map/ppermute | solution.py:255
  36.9 5.0 %collective-permute-start.7 = (f32[2,128,128]{2,1,0:T(8,128)S(1)}, f32[2,128,128]{2,1,0:T(8,128)S(1)}, u32[]{:S(2)}, u32[]{:S(2)}) collective-permute-start(f32[2,128,128]{2,1,0:T(8,128)S(1)} %add.48.grad_a), channel_id=1, source_target_pairs={{0,2},{1,3},{2,0},{3,1},{4,6},{5,7},{6,4},{7,5},{8,10},{9,11},{10,... | collective-permute-start | bytes 393224 | tf_op jit(solution)/shard_map/ppermute | solution.py:255
  46.2 7.3 %collective-permute-start.8 = (f32[2,128,128]{2,1,0:T(8,128)S(1)}, f32[2,128,128]{2,1,0:T(8,128)S(1)}, u32[]{:S(2)}, u32[]{:S(2)}) collective-permute-start(f32[2,128,128]{2,1,0:T(8,128)S(1)} %get-tuple-element.46), channel_id=1, source_target_pairs={{0,4},{1,5},{2,3},{3,2},{4,0},{5,1},{6,7},{7,6},{8,12},{9,13},{10,... | collective-permute-start | bytes 393224 | tf_op jit(solution)/shard_map/ppermute | solution.py:255
  53.6 5.0 %collective-permute-start.9 = (f32[2,128,128]{2,1,0:T(8,128)S(1)}, f32[2,128,128]{2,1,0:T(8,128)S(1)}, u32[]{:S(2)}, u32[]{:S(2)}) collective-permute-start(f32[2,128,128]{2,1,0:T(8,128)S(1)} %add.49), channel_id=1, source_target_pairs={{0,1},{1,0},{2,6},{3,7},{4,5},{5,4},{6,2},{7,3},{8,9},{9,8},{10,14... | collective-permute-start | bytes 393224 | tf_op jit(solution)/shard_map/ppermute | solution.py:255
  58.6 5.0 %collective-permute-start.10 = (f32[2,128,128]{2,1,0:T(8,128)S(1)}, f32[2,128,128]{2,1,0:T(8,128)S(1)}, u32[]{:S(2)}, u32[]{:S(2)}) collective-permute-start(f32[2,128,128]{2,1,0:T(8,128)S(1)} %add.50), channel_id=1, source_target_pairs={{0,2},{1,3},{2,0},{3,1},{4,6},{5,7},{6,4},{7,5},{8,10},{9,11},{10,... | collective-permute-start | bytes 393224 | tf_op jit(solution)/shard_map/ppermute | solution.py:255
  63.7 1.3 %collective-permute-start.11 = (f32[128,128]{1,0:T(8,128)S(1)}, f32[128,128]{1,0:T(8,128)S(1)}, u32[]{:S(2)}, u32[]{:S(2)}) collective-permute-start(f32[128,128]{1,0:T(8,128)S(1)} %maximum_reduce_fusion), channel_id=1, source_target_pairs={{0,8},{8,0},{16,24},{24,16},{1,9},{9,1},{17,25},{25,17},{2,10},{10... | collective-permute-start | bytes 196616 | tf_op jit(solution)/shard_map/ppermute | solution.py:235
  65.0 4.1 %collective-permute-start.12 = (f32[128,128]{1,0:T(8,128)S(1)}, f32[128,128]{1,0:T(8,128)S(1)}, u32[]{:S(2)}, u32[]{:S(2)}) collective-permute-start(f32[128,128]{1,0:T(8,128)S(1)} %add.52), channel_id=1, source_target_pairs={{0,24},{8,16},{16,8},{24,0},{1,25},{9,17},{17,9},{25,1},{2,26},{10... | collective-permute-start | bytes 196616 | tf_op jit(solution)/shard_map/ppermute | solution.py:235
  71.3 1.3 %collective-permute-start.13 = (f32[128,128]{1,0:T(8,128)S(1)}, f32[128,128]{1,0:T(8,128)S(1)}, u32[]{:S(2)}, u32[]{:S(2)}) collective-permute-start(f32[128,128]{1,0:T(8,128)S(1)} %get-tuple-element.48), channel_id=1, source_target_pairs={{0,8},{8,0},{16,24},{24,16},{1,9},{9,1},{17,25},{25,17},{2,10},{10... | collective-permute-start | bytes 196616 | tf_op jit(solution)/shard_map/ppermute | solution.py:235
  72.7 4.1 %collective-permute-start.14 = (f32[128,128]{1,0:T(8,128)S(1)}, f32[128,128]{1,0:T(8,128)S(1)}, u32[]{:S(2)}, u32[]{:S(2)}) collective-permute-start(f32[128,128]{1,0:T(8,128)S(1)} %log_add_fusion.sum_a), channel_id=1, source_target_pairs={{0,24},{8,16},{16,8},{24,0},{1,25},{9,17},{17,9},{25,1},{2,26},{10... | collective-permute-start | bytes 196616 | tf_op jit(solution)/shard_map/ppermute | solution.py:235
  78.8 6.5 %collective-permute-start.15 = (f32[2,128,128]{2,1,0:T(8,128)S(1)}, f32[2,128,128]{2,1,0:T(8,128)S(1)}, u32[]{:S(2)}, u32[]{:S(2)}) collective-permute-start(f32[2,128,128]{2,1,0:T(8,128)S(1)} %get-tuple-element.49), channel_id=1, source_target_pairs={{0,4},{1,5},{2,3},{3,2},{4,0},{5,1},{6,7},{7,6},{8,12},{9,13},{10,... | collective-permute-start | bytes 393224 | tf_op jit(solution)/shard_map/ppermute | solution.py:255
  85.4 5.0 %collective-permute-start.16 = (f32[2,128,128]{2,1,0:T(8,128)S(1)}, f32[2,128,128]{2,1,0:T(8,128)S(1)}, u32[]{:S(2)}, u32[]{:S(2)}) collective-permute-start(f32[2,128,128]{2,1,0:T(8,128)S(1)} %add.56), channel_id=1, source_target_pairs={{0,1},{1,0},{2,6},{3,7},{4,5},{5,4},{6,2},{7,3},{8,9},{9,8},{10,14... | collective-permute-start | bytes 393224 | tf_op jit(solution)/shard_map/ppermute | solution.py:255
  90.4 5.0 %collective-permute-start.17 = (f32[2,128,128]{2,1,0:T(8,128)S(1)}, f32[2,128,128]{2,1,0:T(8,128)S(1)}, u32[]{:S(2)}, u32[]{:S(2)}) collective-permute-start(f32[2,128,128]{2,1,0:T(8,128)S(1)} %add.57.grad_a), channel_id=1, source_target_pairs={{0,2},{1,3},{2,0},{3,1},{4,6},{5,7},{6,4},{7,5},{8,10},{9,11},{10,... | collective-permute-start | bytes 393224 | tf_op jit(solution)/shard_map/ppermute | solution.py:255
  109.8 1.2 %collective-permute-start.18 = (f32[16,128]{1,0:T(8,128)S(1)}, f32[16,128]{1,0:T(8,128)S(1)}, u32[]{:S(2)}, u32[]{:S(2)}) collective-permute-start(f32[16,128]{1,0:T(8,128)S(1)} %maximum_reduce_fusion.1), channel_id=1, source_target_pairs={{0,8},{8,0},{16,24},{24,16},{1,9},{9,1},{17,25},{25,17},{2,10},{10... | collective-permute-start | bytes 24584 | tf_op jit(solution)/shard_map/ppermute | solution.py:235
  111.0 3.1 %collective-permute-start.19 = (f32[16,128]{1,0:T(8,128)S(1)}, f32[16,128]{1,0:T(8,128)S(1)}, u32[]{:S(2)}, u32[]{:S(2)}) collective-permute-start(f32[16,128]{1,0:T(8,128)S(1)} %add.58), channel_id=1, source_target_pairs={{0,24},{8,16},{16,8},{24,0},{1,25},{9,17},{17,9},{25,1},{2,26},{10... | collective-permute-start | bytes 24584 | tf_op jit(solution)/shard_map/ppermute | solution.py:235

commit v6 on v5

--- a/solution.py
+++ b/solution.py
@@ -16,14 +16,12 @@
 FAR = pl.BlockSpec(memory_space=pltpu.HBM)
 
 
-def split3(x):
-    return jnp.concatenate(pieces(x), axis=-1)
-
-
-def exact(hot, x):
-    n = x.shape[1]
-    y = jnp.dot(hot, split3(x), preferred_element_type=F32)
-    return y[:, :n] + y[:, n : 2 * n] + y[:, 2 * n :]
+def exact(hot, xs):
+    n = xs[0].shape[1]
+    every = jnp.concatenate([y for x in xs for y in pieces(x)], axis=1)
+    y = jnp.dot(hot, every, preferred_element_type=F32)
+    parts = [y[:, m * n : (m + 1) * n] for m in range(3 * len(xs))]
+    return [parts[m] + parts[m + 1] + parts[m + 2] for m in range(0, len(parts), 3)]
 
 
 def columns(x):
@@ -128,27 +126,37 @@
 
 
 def hot_kernel(
-    map_far, fluence, counts, row_hot, row_hot_t, col_hot, col_hot_t, mine, block_map, sems
+    map_far, fluence, target_far, counts,
+    col_hot, col_hot_t, same, leads, target, mine, block_map, target_rows, sems
 ):
     copies = [
-        pltpu.make_async_copy(map_far, block_map, sems.at[0]),
-        pltpu.make_async_copy(fluence, mine, sems.at[1]),
+        pltpu.make_async_copy(x, y, sems.at[n])
+        for n, (x, y) in enumerate(
+            [(map_far, block_map), (fluence, mine), (target_far, target_rows)]
+        )
     ]
     for copy in copies:
         copy.start()
     for copy in copies:
         copy.wait()
-    row_blocks, slots = row_hot_t.shape
+    row_blocks, slots = leads.shape
     usable = lax.broadcasted_iota(jnp.int32, (row_blocks, slots), 1) < counts[...]
     rows = lax.broadcasted_iota(jnp.int32, (row_blocks, slots), 0) == block_map[0:1, :]
     row = jnp.where(rows & usable, 1.0, 0.0).astype(F32)
     beam_blocks = col_hot_t.shape[0]
     cols = lax.broadcasted_iota(jnp.int32, (beam_blocks, slots), 0) == block_map[1:2, :]
     col = jnp.where(cols, 1.0, 0.0).astype(F32)
-    row_hot_t[...] = row.astype(BF16)
     col_hot_t[...] = col.astype(BF16)
-    row_hot[...] = flat(row).astype(BF16)
     col_hot[...] = flat(col).astype(BF16)
+    row_hot = flat(row).astype(BF16)
+    shared = jnp.dot(row_hot, row.astype(BF16), preferred_element_type=F32)
+    same[...] = shared.astype(BF16)
+    before = lax.broadcasted_iota(jnp.int32, (slots, slots), 0) < lax.broadcasted_iota(
+        jnp.int32, (slots, slots), 1
+    )
+    earlier = jnp.sum(jnp.where(before, shared, 0.0), axis=0, keepdims=True)
+    leads[...] = jnp.where(earlier == 0.0, row, 0.0).astype(BF16)
+    target[...] = exact(row_hot, [target_rows[...]])[0]
 
 
 def join_kernel(bit, mine, other, order, joined):
@@ -159,15 +167,13 @@
     joined[size:] = jnp.where(low, other[...], mine[...])
 
 
-def first_kernel(
-    whole, upper, lower, fluence, target, col_hot, row_hot_t, excess, score_sum, rows
-):
+def first_kernel(whole, upper, lower, fluence, target, col_hot, same, excess, score_sum, rows):
     scen = whole.shape[0]
-    picked = exact(col_hot[...], fluence[...])
-    products(whole, upper, lower, [picked] * scen, rows)
+    picked = exact(col_hot[...], [fluence[...]])
+    products(whole, upper, lower, picked * scen, rows)
     scores = []
-    for s in range(scen):
-        e = exact(row_hot_t[...], rows[s]) - target[...]
+    for s, dose in enumerate(exact(same[...], [rows[s] for s in range(scen)])):
+        e = dose - target[...]
         excess[s] = e
         scores.append(SHARPNESS * e * e)
     top = functools.reduce(jnp.maximum, scores)
@@ -175,9 +181,7 @@
     score_sum[...] = top + jnp.log(total)
 
 
-def second_kernel(
-    whole, upper, lower, excess, sum_a, sum_b, row_hot, col_hot_t, weights, gradient, rows
-):
+def second_kernel(whole, upper, lower, excess, sum_a, sum_b, col_hot_t, weights, gradient, rows):
     scen = excess.shape[0]
     total = merge(sum_a[...], sum_b[...])
     picked = []
@@ -185,42 +189,42 @@
         e = excess[s]
         w = jnp.exp(SHARPNESS * e * e - total)
         weights[s] = w
-        picked.append(exact(row_hot[...], 2.0 * w * e))
+        picked.append(2.0 * w * e)
     products(whole, upper, lower, picked, rows)
-    for s in range(scen):
-        gradient[s] = exact(col_hot_t[...], rows[s])
+    put_gradient(col_hot_t, rows, gradient)
 
 
 def third_kernel(
     whole, upper, lower, whole_t, upper_t, lower_t, fluence, grad_a, grad_b, weights, target,
-    col_hot, col_hot_t, row_hot, row_hot_t, copies, gradient, rows, held
+    col_hot, col_hot_t, same, copies, gradient, rows, held
 ):
     scen = weights.shape[0]
     share = copies.shape[1]
     mine = pl.ds(0 if share == held.shape[1] else lax.axis_index("vox") * share, share)
-    picked = []
     for s in range(scen):
-        c = jnp.maximum(fluence[...] - STEP_SIZE * (grad_a[s] + grad_b[s]), 0.0)
-        held[s] = c
+        held[s] = jnp.maximum(fluence[...] - STEP_SIZE * (grad_a[s] + grad_b[s]), 0.0)
         copies[s] = held[s, mine]
-        picked.append(exact(col_hot[...], c))
+    picked = exact(col_hot[...], [held[s] for s in range(scen)])
     products(whole_t, upper_t, lower_t, picked, rows)
-    picked = []
-    for s in range(scen):
-        e = exact(row_hot_t[...], rows[s]) - target[...]
-        picked.append(exact(row_hot[...], 2.0 * weights[s] * e))
+    doses = exact(same[...], [rows[s] for s in range(scen)])
+    picked = [2.0 * weights[s] * (doses[s] - target[...]) for s in range(scen)]
     products(whole, upper, lower, picked, rows)
-    for s in range(scen):
-        g = exact(col_hot_t[...], rows[s])
+    put_gradient(col_hot_t, rows, gradient)
+
+
+def put_gradient(col_hot_t, rows, gradient):
+    for s, g in enumerate(exact(col_hot_t[...], [rows[s] for s in range(rows.shape[0])])):
         if len(gradient.shape) == 3:
             gradient[s] = g
         else:
             gradient[:, s] = g.reshape(gradient.shape[0], *gradient.shape[2:])
 
 
-def place_kernel(weights, placed):
-    for s in range(weights.shape[0]):
-        placed[:, s] = weights[s]
+def place_kernel(scen_total, weights, leads, placed):
+    used = jnp.sum(leads[...].astype(F32), axis=1, keepdims=True)
+    scen = weights.shape[0]
+    for s, w in enumerate(exact(leads[...], [weights[s] for s in range(scen)])):
+        placed[:, s] = jnp.where(used == 0.0, 1.0 / scen_total, w)
 
 
 def near(x):
@@ -291,23 +295,33 @@
     dense = lambda *shape: jax.ShapeDtypeStruct(shape, F32)
     scratch = [pltpu.VMEM((scen, slots, side), F32)]
 
-    target = target.reshape(row_blocks, side)
     fluence = fluence_init.reshape(share // side, side)
-    row_hot, row_hot_t, col_hot, col_hot_t, mine = pl.pallas_call(
+    half = lambda *shape: jax.ShapeDtypeStruct(shape, BF16)
+    col_hot, col_hot_t, same, leads, target, mine = pl.pallas_call(
         hot_kernel,
         name="hot",
         out_shape=(
-            jax.ShapeDtypeStruct((slots, row_blocks), BF16),
-            jax.ShapeDtypeStruct((row_blocks, slots), BF16),
-            jax.ShapeDtypeStruct((slots, beam_blocks), BF16),
-            jax.ShapeDtypeStruct((beam_blocks, slots), BF16),
+            half(slots, beam_blocks),
+            half(beam_blocks, slots),
+            half(slots, slots),
+            half(row_blocks, slots),
+            dense(slots, side),
             dense(*fluence.shape),
         ),
-        in_specs=[FAR, FAR, VMEM],
-        out_specs=(VMEM,) * 5,
-        scratch_shapes=[pltpu.VMEM((2, slots), jnp.int32), pltpu.SemaphoreType.DMA((2,))],
+        in_specs=[FAR] * 3 + [VMEM],
+        out_specs=(VMEM,) * 6,
+        scratch_shapes=[
+            pltpu.VMEM((2, slots), jnp.int32),
+            pltpu.VMEM((row_blocks, side), F32),
+            pltpu.SemaphoreType.DMA((3,)),
+        ],
         compiler_params=params,
-    )(far(block_map.T), far(fluence), block_counts.reshape(1, 1))
+    )(
+        far(block_map.T),
+        far(fluence),
+        far(target.reshape(row_blocks, side)),
+        block_counts.reshape(1, 1),
+    )
 
     kept = slots * 2 // 5
     rest = slots - kept
@@ -364,51 +378,51 @@
         excess, score_sum = pl.pallas_call(
             first_kernel,
             name="first",
-            out_shape=(dense(scen, row_blocks, side), dense(row_blocks, side)),
+            out_shape=(dense(scen, slots, side), dense(slots, side)),
             in_specs=[VMEM] * 7,
             out_specs=(VMEM,) * 2,
             scratch_shapes=scratch,
             compiler_params=params,
-        )(*flipped, fluence, target, col_hot, row_hot_t)
+        )(*flipped, fluence, target, col_hot, same)
         sum_a, sum_b = reduce_scen(score_sum, merge)
         last = outer_round == ROUNDS - 1
         weights, gradient = pl.pallas_call(
             second_kernel,
             name="second",
-            out_shape=(dense(scen, row_blocks, side), dense(scen, beam_blocks, side)),
-            in_specs=[VMEM] * 8,
+            out_shape=(dense(scen, slots, side), dense(scen, beam_blocks, side)),
+            in_specs=[VMEM] * 7,
             out_specs=(VMEM,) * 2,
             scratch_shapes=scratch,
             compiler_params=params,
-        )(*blocks, excess, sum_a, sum_b, row_hot, col_hot_t)
+        )(*blocks, excess, sum_a, sum_b, col_hot_t)
         grad_a, grad_b = reduce_vox(gradient)
         form = (parts, scen, share // side, side) if last else (scen, beam_blocks, side)
         copies, gradient = pl.pallas_call(
             third_kernel,
             name="third",
             out_shape=(dense(scen, share // side if last else beam_blocks, side), dense(*form)),
-            in_specs=[VMEM] * 15,
+            in_specs=[VMEM] * 14,
             out_specs=(VMEM,) * 2,
             scratch_shapes=scratch + [pltpu.VMEM((scen, beam_blocks, side), F32)],
             compiler_params=params,
         )(
             *blocks, *flipped, fluence, grad_a, grad_b, weights, target,
-            col_hot, col_hot_t, row_hot, row_hot_t,
+            col_hot, col_hot_t, same,
         )
         if not last:
             grad_a, grad_b = reduce_vox(gradient)
         else:
             weights = pl.pallas_call(
-                place_kernel,
+                functools.partial(place_kernel, scen_total),
                 name="place",
                 out_shape=dense(row_blocks, scen, side),
-                in_specs=[VMEM],
+                in_specs=[VMEM] * 2,
                 out_specs=VMEM,
                 compiler_params=params,
                 cost_estimate=pl.CostEstimate(
                     flops=0, bytes_accessed=8 * weights.size, transcendentals=0
                 ),
-            )(near(weights))
+            )(near(weights), leads)
             weights = jnp.swapaxes(weights, 0, 1).reshape(scen, row_blocks * side)
             gradient, copies, weights = lax.optimization_barrier((gradient, copies, weights))
             gradient = lax.all_to_all(gradient, "vox", split_axis=0, concat_axis=0, tiled=True)

time: 115 us -> 111 us (0.965)
  waiting for transfers between devices: 57.7 us -> 55.8 us
  Pallas kernels: 24.7 us -> 22.8 us
    pallas_call x2, Pallas kernels: 8.61 us -> 7.15 us  [body(): pl.pallas_call(third_kernel, name='third', out_shape=(dense(scen, share /...]
    ppermute x8, waiting for transfers between devices: 14.7 us -> 13.4 us  [swap(): lax.ppermute(x, axis, [(i, i ^ bit) for i in range(lax.axis_size(axis))])]
where the time goes in v6:
time: 111 us
  waiting for transfers between devices  55.8 us (50%)
  Pallas kernels  22.8 us (21%)
  starting transfers between devices  20.3 us (18%)
  blocking collectives  9.98 us (9%)
  between operations  1.49 us (1%)
    ppermute x9, waiting for transfers between devices, reduce_vox(): lax.ppermute(x, 'vox', [(v, v ^ pair[(v & steps[-2]) // steps[-2]]) for v...  42.4 us
    ppermute x8, waiting for transfers between devices, swap(): lax.ppermute(x, axis, [(i, i ^ bit) for i in range(lax.axis_size(axis))])  13.4 us
    all_to_all x1, blocking collectives, body(): lax.all_to_all(gradient, 'vox', split_axis=0, concat_axis=0, tiled=True)  9.98 us
    ppermute x9, starting transfers between devices, reduce_vox(): lax.ppermute(x, 'vox', [(v, v ^ pair[(v & steps[-2]) // steps[-2]]) for v...  7.31 us
    pallas_call x2, Pallas kernels, body(): pl.pallas_call(third_kernel, name='third', out_shape=(dense(scen, share /...  7.15 us
    ppermute x3, starting transfers between devices, swap_both(): return lax.ppermute(x, ('scen', 'vox'), pairs)  6.9 us
    ppermute x8, starting transfers between devices, swap(): lax.ppermute(x, axis, [(i, i ^ bit) for i in range(lax.axis_size(axis))])  6.08 us
    pallas_call x2, Pallas kernels, body(): pl.pallas_call(first_kernel, name='first', out_shape=(dense(scen, slots,...  3.81 us
  transfers between devices with their start and end apart: 20, of which 17 were waited for; matrix products, arithmetic and copies ran while one was open for 0% of the time, Pallas kernels for 7%

profile of v6, /device:TPU:0, one launch (start us, length us, event | category | flops | bytes accessed | tf_op | source)
XLA Modules:
  0.0 111.1 jit_solution(6174842999719468978)
XLA Ops:
  0.6 2.4 %collective-permute-start = (f32[16,128]{1,0:T(8,128)}, f32[16,128]{1,0:T(8,128)S(1)}, u32[]{:S(2)}, u32[]{:S(2)}) collective-permute-start(f32[16,128]{1,0:T(8,128)} %bitcast.12), channel_id=1, source_target_pairs={{0,9},{1,8},{2,11},{3,10},{4,13},{5,12},{6,15},{7,14},{8,1},{9,0},... | collective-permute-start | bytes 24584 | tf_op jit(solution)/shard_map/ppermute | solution.py:279
  3.7 1.2 %hot.1 = (bf16[80,128]{1,0:T(8,128)(2,1)S(1)}, bf16[128,80]{1,0:T(8,128)(2,1)S(1)}, bf16[80,80]{1,0:T(8,128)(2,1)S(1)}, bf16[128,80]{1,0:T(8,128)(2,1)S(1)}, f32...) custom-call(s32[2,80]{1,0:T(2,128)} %bitcast.14, f32[16,128]{1,0:T(8,128)} %bitcast.13, f32[128,128]{1,0:T(8,128)} %bitcast.11, ...), custom_call_target="tpu_custom_call" | custom-call | tf_op jit(solution)/shard_map/hot/pallas_call | solution.py:300
  5.0 1.9 %collective-permute-start.1 = (f32[32,128]{1,0:T(8,128)S(1)}, f32[32,128]{1,0:T(8,128)S(1)}, u32[]{:S(2)}, u32[]{:S(2)}) collective-permute-start(f32[32,128]{1,0:T(8,128)S(1)} %join.3.order.mine), channel_id=1, source_target_pairs={{0,10},{1,11},{2,8},{3,9},{4,14},{5,15},{6,12},{7,13},{8,2},{9,3},... | collective-permute-start | bytes 49160 | tf_op jit(solution)/shard_map/ppermute | solution.py:279
  6.9 2.6 %whole.1 = (f32[2,32,128,128]{3,2,1,0:T(8,128)S(1)}, f32[2,32,128,128]{3,2,1,0:T(8,128)S(1)}, f32[8,128]{1,0:T(8,128)S(1)}) custom-call(f32[2,80,128,128]{3,2,1,0:T(8,128)} %source.3, f32[32,128]{1,0:T(8,128)S(1)} %join.3.order.mine), custom_call_target="tpu_custom_call" | custom-call | bytes 7864320 | tf_op jit(solution)/shard_map/whole/pallas_call | solution.py:336
  9.5 2.5 %collective-permute-start.2 = (f32[64,128]{1,0:T(8,128)S(1)}, f32[64,128]{1,0:T(8,128)S(1)}, u32[]{:S(2)}, u32[]{:S(2)}) collective-permute-start(f32[64,128]{1,0:T(8,128)S(1)} %join.4.order.mine), channel_id=1, source_target_pairs={{0,12},{1,13},{2,14},{3,15},{4,8},{5,9},{6,10},{7,11},{8,4},{9,5},... | collective-permute-start | bytes 98312 | tf_op jit(solution)/shard_map/ppermute | solution.py:279
  12.1 3.6 %split.1 = (bf16[2,48,256,128]{3,2,1,0:T(8,128)(2,1)S(1)}, bf16[2,48,256,128]{3,2,1,0:T(8,128)(2,1)S(1)}, bf16[48,256,128]{2,1,0:T(8,128)(2,1)S(1)}, bf16[48,256,128]{2,1,0:T(8,128)(2,1)S(1)}) custom-call(f32[2,80,128,128]{3,2,1,0:T(8,128)} %source.3, f32[64,128]{1,0:T(8,128)S(1)} %join.4.order.mine), custom_call_target="tpu_custom_call" | custom-call | bytes 13107200 | tf_op jit(solution)/shard_map/split/pallas_call | solution.py:350
  15.7 1.8 %first.2 = (f32[2,80,128]{2,1,0:T(8,128)S(1)}, f32[80,128]{1,0:T(8,128)S(1)}) custom-call(f32[2,32,128,128]{3,2,1,0:T(8,128)S(1)} %get-tuple-element.35.whole.whole_t, bf16[2,48,256,128]{3,2,1,0:T(8,128)(2,1)S(1)} %get-tuple-element.36.upper.upper_t, bf16[48,256,128]{2,1,0:T(8,128)(2,1)S(1)} %get-tuple-element.37.lower.lower_t, f32[128,128]{1,0:T(8,128)S(1)} %join.5.fluence, ...), custom_call_target="tpu_custom_call" | custom-call | tf_op jit(solution)/shard_map/first/pallas_call | solution.py:378
  17.5 0.3 collective-permute-start.3
  17.8 1.0 collective-permute-done.3
  18.8 1.4 %collective-permute-start.4 = (f32[80,128]{1,0:T(8,128)S(1)}, f32[80,128]{1,0:T(8,128)S(1)}, u32[]{:S(2)}, u32[]{:S(2)}) collective-permute-start(f32[80,128]{1,0:T(8,128)S(1)} %log_add_fusion.1.sum_a), channel_id=1, source_target_pairs={{0,24},{8,16},{16,8},{24,0},{1,25},{9,17},{17,9},{25,1},{2,26},{10... | collective-permute-start | bytes 122888 | tf_op jit(solution)/shard_map/ppermute | solution.py:239
  20.3 2.2 %collective-permute-done.4.sum_b = f32[80,128]{1,0:T(8,128)S(1)} collective-permute-done((f32[80,128]{1,0:T(8,128)S(1)}, f32[80,128]{1,0:T(8,128)S(1)}, u32[]{:S(2)}, u32[]{:S(2)}) %collective-permute-start.4) | collective-permute-done | bytes 40992 | tf_op jit(solution)/shard_map/ppermute | solution.py:239
  22.4 1.7 %second.2 = (f32[2,80,128]{2,1,0:T(8,128)S(1)}, f32[2,128,128]{2,1,0:T(8,128)S(1)}) custom-call(f32[2,32,128,128]{3,2,1,0:T(8,128)S(1)} %get-tuple-element.31.whole, bf16[2,48,256,128]{3,2,1,0:T(8,128)(2,1)S(1)} %get-tuple-element.33.upper, bf16[48,256,128]{2,1,0:T(8,128)(2,1)S(1)} %get-tuple-element.34.lower, f32[2,80,128]{2,1,0:T(8,128)S(1)} %get-tuple-element.41.excess, ...), custom_call_target="tpu_custom_call" | custom-call | tf_op jit(solution)/shard_map/second/pallas_call | solution.py:389
  24.2 0.7 collective-permute-start.5
  24.9 5.8 %collective-permute-done.5 = f32[2,128,128]{2,1,0:T(8,128)S(1)} collective-permute-done((f32[2,128,128]{2,1,0:T(8,128)S(1)}, f32[2,128,128]{2,1,0:T(8,128)S(1)}, u32[]{:S(2)}, u32[]{:S(2)}) %collective-permute-start.5) | collective-permute-done | bytes 131104 | tf_op jit(solution)/shard_map/ppermute | solution.py:259
  30.7 1.6 %collective-permute-start.6 = (f32[2,128,128]{2,1,0:T(8,128)S(1)}, f32[2,128,128]{2,1,0:T(8,128)S(1)}, u32[]{:S(2)}, u32[]{:S(2)}) collective-permute-start(f32[2,128,128]{2,1,0:T(8,128)S(1)} %add.47), channel_id=1, source_target_pairs={{0,1},{1,0},{2,6},{3,7},{4,5},{5,4},{6,2},{7,3},{8,9},{9,8},{10,14... | collective-permute-start | bytes 393224 | tf_op jit(solution)/shard_map/ppermute | solution.py:259
  32.3 3.4 %collective-permute-done.6 = f32[2,128,128]{2,1,0:T(8,128)S(1)} collective-permute-done((f32[2,128,128]{2,1,0:T(8,128)S(1)}, f32[2,128,128]{2,1,0:T(8,128)S(1)}, u32[]{:S(2)}, u32[]{:S(2)}) %collective-permute-start.6) | collective-permute-done | bytes 131104 | tf_op jit(solution)/shard_map/ppermute | solution.py:259
  35.8 0.7 collective-permute-start.7
  36.4 4.4 %collective-permute-done.7.grad_b = f32[2,128,128]{2,1,0:T(8,128)S(1)} collective-permute-done((f32[2,128,128]{2,1,0:T(8,128)S(1)}, f32[2,128,128]{2,1,0:T(8,128)S(1)}, u32[]{:S(2)}, u32[]{:S(2)}) %collective-permute-start.7) | collective-permute-done | bytes 131104 | tf_op jit(solution)/shard_map/ppermute | solution.py:259
  40.8 3.6 %third.2 = (f32[2,128,128]{2,1,0:T(8,128)S(1)}, f32[2,128,128]{2,1,0:T(8,128)S(1)}) custom-call(f32[2,32,128,128]{3,2,1,0:T(8,128)S(1)} %get-tuple-element.31.whole, bf16[2,48,256,128]{3,2,1,0:T(8,128)(2,1)S(1)} %get-tuple-element.33.upper, bf16[48,256,128]{2,1,0:T(8,128)(2,1)S(1)} %get-tuple-element.34.lower, ...), custom_call_target="tpu_custom_call" | custom-call | tf_op jit(solution)/shard_map/third/pallas_call | solution.py:400
  44.4 0.8 collective-permute-start.8
  45.2 6.5 %collective-permute-done.8 = f32[2,128,128]{2,1,0:T(8,128)S(1)} collective-permute-done((f32[2,128,128]{2,1,0:T(8,128)S(1)}, f32[2,128,128]{2,1,0:T(8,128)S(1)}, u32[]{:S(2)}, u32[]{:S(2)}) %collective-permute-start.8) | collective-permute-done | bytes 131104 | tf_op jit(solution)/shard_map/ppermute | solution.py:259
  51.7 1.6 %collective-permute-start.9 = (f32[2,128,128]{2,1,0:T(8,128)S(1)}, f32[2,128,128]{2,1,0:T(8,128)S(1)}, u32[]{:S(2)}, u32[]{:S(2)}) collective-permute-start(f32[2,128,128]{2,1,0:T(8,128)S(1)} %add.49), channel_id=1, source_target_pairs={{0,1},{1,0},{2,6},{3,7},{4,5},{5,4},{6,2},{7,3},{8,9},{9,8},{10,14... | collective-permute-start | bytes 393224 | tf_op jit(solution)/shard_map/ppermute | solution.py:259
  53.4 3.4 %collective-permute-done.9 = f32[2,128,128]{2,1,0:T(8,128)S(1)} collective-permute-done((f32[2,128,128]{2,1,0:T(8,128)S(1)}, f32[2,128,128]{2,1,0:T(8,128)S(1)}, u32[]{:S(2)}, u32[]{:S(2)}) %collective-permute-start.9) | collective-permute-done | bytes 131104 | tf_op jit(solution)/shard_map/ppermute | solution.py:259
  56.8 0.1 collective-permute-start.10
  56.9 5.0 %collective-permute-done.10 = f32[2,128,128]{2,1,0:T(8,128)S(1)} collective-permute-done((f32[2,128,128]{2,1,0:T(8,128)S(1)}, f32[2,128,128]{2,1,0:T(8,128)S(1)}, u32[]{:S(2)}, u32[]{:S(2)}) %collective-permute-start.10) | collective-permute-done | bytes 131104 | tf_op jit(solution)/shard_map/ppermute | solution.py:259
  61.9 0.1 collective-permute-start.11
  61.9 1.2 %collective-permute-done.11 = f32[128,128]{1,0:T(8,128)S(1)} collective-permute-done((f32[128,128]{1,0:T(8,128)S(1)}, f32[128,128]{1,0:T(8,128)S(1)}, u32[]{:S(2)}, u32[]{:S(2)}) %collective-permute-start.11) | collective-permute-done | bytes 65568 | tf_op jit(solution)/shard_map/ppermute | solution.py:239
  63.2 1.3 %collective-permute-start.12 = (f32[128,128]{1,0:T(8,128)S(1)}, f32[128,128]{1,0:T(8,128)S(1)}, u32[]{:S(2)}, u32[]{:S(2)}) collective-permute-start(f32[128,128]{1,0:T(8,128)S(1)} %add.52), channel_id=1, source_target_pairs={{0,24},{8,16},{16,8},{24,0},{1,25},{9,17},{17,9},{25,1},{2,26},{10... | collective-permute-start | bytes 196616 | tf_op jit(solution)/shard_map/ppermute | solution.py:239
  64.5 2.8 %collective-permute-done.12 = f32[128,128]{1,0:T(8,128)S(1)} collective-permute-done((f32[128,128]{1,0:T(8,128)S(1)}, f32[128,128]{1,0:T(8,128)S(1)}, u32[]{:S(2)}, u32[]{:S(2)}) %collective-permute-start.12) | collective-permute-done | bytes 65568 | tf_op jit(solution)/shard_map/ppermute | solution.py:239
  67.3 2.0 %first.3 = (f32[2,80,128]{2,1,0:T(8,128)S(1)}, f32[80,128]{1,0:T(8,128)S(1)}) custom-call(f32[2,32,128,128]{3,2,1,0:T(8,128)S(1)} %get-tuple-element.35.whole.whole_t, bf16[2,48,256,128]{3,2,1,0:T(8,128)(2,1)S(1)} %get-tuple-element.36.upper.upper_t, bf16[48,256,128]{2,1,0:T(8,128)(2,1)S(1)} %get-tuple-element.37.lower.lower_t, ...), custom_call_target="tpu_custom_call" | custom-call | tf_op jit(solution)/shard_map/first/pallas_call | solution.py:378
  69.3 0.2 collective-permute-start.13
  69.5 1.1 collective-permute-done.13
  70.6 1.4 %collective-permute-start.14 = (f32[80,128]{1,0:T(8,128)S(1)}, f32[80,128]{1,0:T(8,128)S(1)}, u32[]{:S(2)}, u32[]{:S(2)}) collective-permute-start(f32[80,128]{1,0:T(8,128)S(1)} %log_add_fusion.sum_a), channel_id=1, source_target_pairs={{0,24},{8,16},{16,8},{24,0},{1,25},{9,17},{17,9},{25,1},{2,26},{10... | collective-permute-start | bytes 122888 | tf_op jit(solution)/shard_map/ppermute | solution.py:239
  72.0 2.2 %collective-permute-done.14.sum_b = f32[80,128]{1,0:T(8,128)S(1)} collective-permute-done((f32[80,128]{1,0:T(8,128)S(1)}, f32[80,128]{1,0:T(8,128)S(1)}, u32[]{:S(2)}, u32[]{:S(2)}) %collective-permute-start.14) | collective-permute-done | bytes 40992 | tf_op jit(solution)/shard_map/ppermute | solution.py:239
  74.2 1.7 %second.3 = (f32[2,80,128]{2,1,0:T(8,128)S(1)}, f32[2,128,128]{2,1,0:T(8,128)S(1)}) custom-call(f32[2,32,128,128]{3,2,1,0:T(8,128)S(1)} %get-tuple-element.31.whole, bf16[2,48,256,128]{3,2,1,0:T(8,128)(2,1)S(1)} %get-tuple-element.33.upper, bf16[48,256,128]{2,1,0:T(8,128)(2,1)S(1)} %get-tuple-element.34.lower, f32[2,80,128]{2,1,0:T(8,128)S(1)} %get-tuple-element.48.excess, ...), custom_call_target="tpu_custom_call" | custom-call | tf_op jit(solution)/shard_map/second/pallas_call | solution.py:389
  76.0 0.1 collective-permute-start.15
  76.1 6.5 %collective-permute-done.15 = f32[2,128,128]{2,1,0:T(8,128)S(1)} collective-permute-done((f32[2,128,128]{2,1,0:T(8,128)S(1)}, f32[2,128,128]{2,1,0:T(8,128)S(1)}, u32[]{:S(2)}, u32[]{:S(2)}) %collective-permute-start.15) | collective-permute-done | bytes 131104 | tf_op jit(solution)/shard_map/ppermute | solution.py:259
  82.5 1.6 %collective-permute-start.16 = (f32[2,128,128]{2,1,0:T(8,128)S(1)}, f32[2,128,128]{2,1,0:T(8,128)S(1)}, u32[]{:S(2)}, u32[]{:S(2)}) collective-permute-start(f32[2,128,128]{2,1,0:T(8,128)S(1)} %add.56), channel_id=1, source_target_pairs={{0,1},{1,0},{2,6},{3,7},{4,5},{5,4},{6,2},{7,3},{8,9},{9,8},{10,14... | collective-permute-start | bytes 393224 | tf_op jit(solution)/shard_map/ppermute | solution.py:259
  84.2 3.4 %collective-permute-done.16 = f32[2,128,128]{2,1,0:T(8,128)S(1)} collective-permute-done((f32[2,128,128]{2,1,0:T(8,128)S(1)}, f32[2,128,128]{2,1,0:T(8,128)S(1)}, u32[]{:S(2)}, u32[]{:S(2)}) %collective-permute-start.16) | collective-permute-done | bytes 131104 | tf_op jit(solution)/shard_map/ppermute | solution.py:259
  87.7 0.9 place.1
  88.6 4.1 %collective-permute-done.17.grad_b = f32[2,128,128]{2,1,0:T(8,128)S(1)} collective-permute-done((f32[2,128,128]{2,1,0:T(8,128)S(1)}, f32[2,128,128]{2,1,0:T(8,128)S(1)}, u32[]{:S(2)}, u32[]{:S(2)}) %collective-permute-start.17) | collective-permute-done | bytes 131104 | tf_op jit(solution)/shard_map/ppermute | solution.py:259
  92.6 3.6 %third.3 = (f32[2,16,128]{2,1,0:T(8,128)S(1)}, f32[8,2,16,128]{3,2,1,0:T(8,128)S(1)}) custom-call(f32[2,32,128,128]{3,2,1,0:T(8,128)S(1)} %get-tuple-element.31.whole, bf16[2,48,256,128]{3,2,1,0:T(8,128)(2,1)S(1)} %get-tuple-element.33.upper, bf16[48,256,128]{2,1,0:T(8,128)(2,1)S(1)} %get-tuple-element.34.lower, ...), custom_call_target="tpu_custom_call" | custom-call | tf_op jit(solution)/shard_map/third/pallas_call | solution.py:400
  96.2 10.0 %all_to_all.5 = f32[8,2,16,128]{3,2,1,0:T(8,128)S(1)} all-to-all(f32[8,2,16,128]{3,2,1,0:T(8,128)S(1)} %get-tuple-element.56), channel_id=1, replica_groups=mesh['scen'=4,'vox'=8] {'vox'}, dimensions={0} | all-to-all | bytes 262144 | tf_op jit(solution)/shard_map/all_to_all | solution.py:428
  106.2 0.1 collective-permute-start.18
  106.3 1.2 %collective-permute-done.18 = f32[16,128]{1,0:T(8,128)S(1)} collective-permute-done((f32[16,128]{1,0:T(8,128)S(1)}, f32[16,128]{1,0:T(8,128)S(1)}, u32[]{:S(2)}, u32[]{:S(2)}) %collective-permute-start.18) | collective-permute-done | bytes 8224 | tf_op jit(solution)/shard_map/ppermute | solution.py:239
  107.4 1.3 %collective-permute-start.19 = (f32[16,128]{1,0:T(8,128)S(1)}, f32[16,128]{1,0:T(8,128)S(1)}, u32[]{:S(2)}, u32[]{:S(2)}) collective-permute-start(f32[16,128]{1,0:T(8,128)S(1)} %add.58), channel_id=1, source_target_pairs={{0,24},{8,16},{16,8},{24,0},{1,25},{9,17},{17,9},{25,1},{2,26},{10... | collective-permute-start | bytes 24584 | tf_op jit(solution)/shard_map/ppermute | solution.py:239
  108.7 1.8 %collective-permute-done.19 = f32[16,128]{1,0:T(8,128)S(1)} collective-permute-done((f32[16,128]{1,0:T(8,128)S(1)}, f32[16,128]{1,0:T(8,128)S(1)}, u32[]{:S(2)}, u32[]{:S(2)}) %collective-permute-start.19) | collective-permute-done | bytes 8224 | tf_op jit(solution)/shard_map/ppermute | solution.py:239
  110.5 0.6 multiply_bitcast_fusion
  (21 shorter events, 0.4 us)
Async XLA Ops:
  0.6 4.3 %collective-permute-start = (f32[16,128]{1,0:T(8,128)}, f32[16,128]{1,0:T(8,128)S(1)}, u32[]{:S(2)}, u32[]{:S(2)}) collective-permute-start(f32[16,128]{1,0:T(8,128)} %bitcast.12), channel_id=1, source_target_pairs={{0,9},{1,8},{2,11},{3,10},{4,13},{5,12},{6,15},{7,14},{8,1},{9,0},... | collective-permute-start | bytes 24584 | tf_op jit(solution)/shard_map/ppermute | solution.py:279
  5.0 4.5 %collective-permute-start.1 = (f32[32,128]{1,0:T(8,128)S(1)}, f32[32,128]{1,0:T(8,128)S(1)}, u32[]{:S(2)}, u32[]{:S(2)}) collective-permute-start(f32[32,128]{1,0:T(8,128)S(1)} %join.3.order.mine), channel_id=1, source_target_pairs={{0,10},{1,11},{2,8},{3,9},{4,14},{5,15},{6,12},{7,13},{8,2},{9,3},... | collective-permute-start | bytes 49160 | tf_op jit(solution)/shard_map/ppermute | solution.py:279
  9.5 6.1 %collective-permute-start.2 = (f32[64,128]{1,0:T(8,128)S(1)}, f32[64,128]{1,0:T(8,128)S(1)}, u32[]{:S(2)}, u32[]{:S(2)}) collective-permute-start(f32[64,128]{1,0:T(8,128)S(1)} %join.4.order.mine), channel_id=1, source_target_pairs={{0,12},{1,13},{2,14},{3,15},{4,8},{5,9},{6,10},{7,11},{8,4},{9,5},... | collective-permute-start | bytes 98312 | tf_op jit(solution)/shard_map/ppermute | solution.py:279
  17.5 1.3 %collective-permute-start.3 = (f32[80,128]{1,0:T(8,128)S(1)}, f32[80,128]{1,0:T(8,128)S(1)}, u32[]{:S(2)}, u32[]{:S(2)}) collective-permute-start(f32[80,128]{1,0:T(8,128)S(1)} %get-tuple-element.42), channel_id=1, source_target_pairs={{0,8},{8,0},{16,24},{24,16},{1,9},{9,1},{17,25},{25,17},{2,10},{10... | collective-permute-start | bytes 122888 | tf_op jit(solution)/shard_map/ppermute | solution.py:239
  18.8 3.6 %collective-permute-start.4 = (f32[80,128]{1,0:T(8,128)S(1)}, f32[80,128]{1,0:T(8,128)S(1)}, u32[]{:S(2)}, u32[]{:S(2)}) collective-permute-start(f32[80,128]{1,0:T(8,128)S(1)} %log_add_fusion.1.sum_a), channel_id=1, source_target_pairs={{0,24},{8,16},{16,8},{24,0},{1,25},{9,17},{17,9},{25,1},{2,26},{10... | collective-permute-start | bytes 122888 | tf_op jit(solution)/shard_map/ppermute | solution.py:239
  24.2 6.5 %collective-permute-start.5 = (f32[2,128,128]{2,1,0:T(8,128)S(1)}, f32[2,128,128]{2,1,0:T(8,128)S(1)}, u32[]{:S(2)}, u32[]{:S(2)}) collective-permute-start(f32[2,128,128]{2,1,0:T(8,128)S(1)} %get-tuple-element.44), channel_id=1, source_target_pairs={{0,4},{1,5},{2,3},{3,2},{4,0},{5,1},{6,7},{7,6},{8,12},{9,13},{10,... | collective-permute-start | bytes 393224 | tf_op jit(solution)/shard_map/ppermute | solution.py:259
  30.7 5.0 %collective-permute-start.6 = (f32[2,128,128]{2,1,0:T(8,128)S(1)}, f32[2,128,128]{2,1,0:T(8,128)S(1)}, u32[]{:S(2)}, u32[]{:S(2)}) collective-permute-start(f32[2,128,128]{2,1,0:T(8,128)S(1)} %add.47), channel_id=1, source_target_pairs={{0,1},{1,0},{2,6},{3,7},{4,5},{5,4},{6,2},{7,3},{8,9},{9,8},{10,14... | collective-permute-start | bytes 393224 | tf_op jit(solution)/shard_map/ppermute | solution.py:259
  35.8 5.0 %collective-permute-start.7 = (f32[2,128,128]{2,1,0:T(8,128)S(1)}, f32[2,128,128]{2,1,0:T(8,128)S(1)}, u32[]{:S(2)}, u32[]{:S(2)}) collective-permute-start(f32[2,128,128]{2,1,0:T(8,128)S(1)} %add.48.grad_a), channel_id=1, source_target_pairs={{0,2},{1,3},{2,0},{3,1},{4,6},{5,7},{6,4},{7,5},{8,10},{9,11},{10,... | collective-permute-start | bytes 393224 | tf_op jit(solution)/shard_map/ppermute | solution.py:259
  44.4 7.3 %collective-permute-start.8 = (f32[2,128,128]{2,1,0:T(8,128)S(1)}, f32[2,128,128]{2,1,0:T(8,128)S(1)}, u32[]{:S(2)}, u32[]{:S(2)}) collective-permute-start(f32[2,128,128]{2,1,0:T(8,128)S(1)} %get-tuple-element.47), channel_id=1, source_target_pairs={{0,4},{1,5},{2,3},{3,2},{4,0},{5,1},{6,7},{7,6},{8,12},{9,13},{10,... | collective-permute-start | bytes 393224 | tf_op jit(solution)/shard_map/ppermute | solution.py:259
  51.7 5.0 %collective-permute-start.9 = (f32[2,128,128]{2,1,0:T(8,128)S(1)}, f32[2,128,128]{2,1,0:T(8,128)S(1)}, u32[]{:S(2)}, u32[]{:S(2)}) collective-permute-start(f32[2,128,128]{2,1,0:T(8,128)S(1)} %add.49), channel_id=1, source_target_pairs={{0,1},{1,0},{2,6},{3,7},{4,5},{5,4},{6,2},{7,3},{8,9},{9,8},{10,14... | collective-permute-start | bytes 393224 | tf_op jit(solution)/shard_map/ppermute | solution.py:259
  56.8 5.0 %collective-permute-start.10 = (f32[2,128,128]{2,1,0:T(8,128)S(1)}, f32[2,128,128]{2,1,0:T(8,128)S(1)}, u32[]{:S(2)}, u32[]{:S(2)}) collective-permute-start(f32[2,128,128]{2,1,0:T(8,128)S(1)} %add.50), channel_id=1, source_target_pairs={{0,2},{1,3},{2,0},{3,1},{4,6},{5,7},{6,4},{7,5},{8,10},{9,11},{10,... | collective-permute-start | bytes 393224 | tf_op jit(solution)/shard_map/ppermute | solution.py:259
  61.9 1.3 %collective-permute-start.11 = (f32[128,128]{1,0:T(8,128)S(1)}, f32[128,128]{1,0:T(8,128)S(1)}, u32[]{:S(2)}, u32[]{:S(2)}) collective-permute-start(f32[128,128]{1,0:T(8,128)S(1)} %maximum_reduce_fusion), channel_id=1, source_target_pairs={{0,8},{8,0},{16,24},{24,16},{1,9},{9,1},{17,25},{25,17},{2,10},{10... | collective-permute-start | bytes 196616 | tf_op jit(solution)/shard_map/ppermute | solution.py:239
  63.2 4.1 %collective-permute-start.12 = (f32[128,128]{1,0:T(8,128)S(1)}, f32[128,128]{1,0:T(8,128)S(1)}, u32[]{:S(2)}, u32[]{:S(2)}) collective-permute-start(f32[128,128]{1,0:T(8,128)S(1)} %add.52), channel_id=1, source_target_pairs={{0,24},{8,16},{16,8},{24,0},{1,25},{9,17},{17,9},{25,1},{2,26},{10... | collective-permute-start | bytes 196616 | tf_op jit(solution)/shard_map/ppermute | solution.py:239
  69.3 1.3 %collective-permute-start.13 = (f32[80,128]{1,0:T(8,128)S(1)}, f32[80,128]{1,0:T(8,128)S(1)}, u32[]{:S(2)}, u32[]{:S(2)}) collective-permute-start(f32[80,128]{1,0:T(8,128)S(1)} %get-tuple-element.49), channel_id=1, source_target_pairs={{0,8},{8,0},{16,24},{24,16},{1,9},{9,1},{17,25},{25,17},{2,10},{10... | collective-permute-start | bytes 122888 | tf_op jit(solution)/shard_map/ppermute | solution.py:239
  70.6 3.6 %collective-permute-start.14 = (f32[80,128]{1,0:T(8,128)S(1)}, f32[80,128]{1,0:T(8,128)S(1)}, u32[]{:S(2)}, u32[]{:S(2)}) collective-permute-start(f32[80,128]{1,0:T(8,128)S(1)} %log_add_fusion.sum_a), channel_id=1, source_target_pairs={{0,24},{8,16},{16,8},{24,0},{1,25},{9,17},{17,9},{25,1},{2,26},{10... | collective-permute-start | bytes 122888 | tf_op jit(solution)/shard_map/ppermute | solution.py:239
  76.0 6.5 %collective-permute-start.15 = (f32[2,128,128]{2,1,0:T(8,128)S(1)}, f32[2,128,128]{2,1,0:T(8,128)S(1)}, u32[]{:S(2)}, u32[]{:S(2)}) collective-permute-start(f32[2,128,128]{2,1,0:T(8,128)S(1)} %get-tuple-element.50), channel_id=1, source_target_pairs={{0,4},{1,5},{2,3},{3,2},{4,0},{5,1},{6,7},{7,6},{8,12},{9,13},{10,... | collective-permute-start | bytes 393224 | tf_op jit(solution)/shard_map/ppermute | solution.py:259
  82.5 5.0 %collective-permute-start.16 = (f32[2,128,128]{2,1,0:T(8,128)S(1)}, f32[2,128,128]{2,1,0:T(8,128)S(1)}, u32[]{:S(2)}, u32[]{:S(2)}) collective-permute-start(f32[2,128,128]{2,1,0:T(8,128)S(1)} %add.56), channel_id=1, source_target_pairs={{0,1},{1,0},{2,6},{3,7},{4,5},{5,4},{6,2},{7,3},{8,9},{9,8},{10,14... | collective-permute-start | bytes 393224 | tf_op jit(solution)/shard_map/ppermute | solution.py:259
  87.6 5.0 %collective-permute-start.17 = (f32[2,128,128]{2,1,0:T(8,128)S(1)}, f32[2,128,128]{2,1,0:T(8,128)S(1)}, u32[]{:S(2)}, u32[]{:S(2)}) collective-permute-start(f32[2,128,128]{2,1,0:T(8,128)S(1)} %add.57.grad_a), channel_id=1, source_target_pairs={{0,2},{1,3},{2,0},{3,1},{4,6},{5,7},{6,4},{7,5},{8,10},{9,11},{10,... | collective-permute-start | bytes 393224 | tf_op jit(solution)/shard_map/ppermute | solution.py:259
  106.2 1.2 %collective-permute-start.18 = (f32[16,128]{1,0:T(8,128)S(1)}, f32[16,128]{1,0:T(8,128)S(1)}, u32[]{:S(2)}, u32[]{:S(2)}) collective-permute-start(f32[16,128]{1,0:T(8,128)S(1)} %maximum_reduce_fusion.1), channel_id=1, source_target_pairs={{0,8},{8,0},{16,24},{24,16},{1,9},{9,1},{17,25},{25,17},{2,10},{10... | collective-permute-start | bytes 24584 | tf_op jit(solution)/shard_map/ppermute | solution.py:239
  107.4 3.1 %collective-permute-start.19 = (f32[16,128]{1,0:T(8,128)S(1)}, f32[16,128]{1,0:T(8,128)S(1)}, u32[]{:S(2)}, u32[]{:S(2)}) collective-permute-start(f32[16,128]{1,0:T(8,128)S(1)} %add.58), channel_id=1, source_target_pairs={{0,24},{8,16},{16,8},{24,0},{1,25},{9,17},{17,9},{25,1},{2,26},{10... | collective-permute-start | bytes 24584 | tf_op jit(solution)/shard_map/ppermute | solution.py:239

commit v7 on v6

--- a/solution.py
+++ b/solution.py
@@ -47,40 +47,47 @@
 
 
 def products(whole, upper, lower, picked, rows):
-    scen, kept, side, _ = whole.shape
-    split_slots = upper.shape[1]
+    _, kept, side, _ = whole.shape
+    pairs = lower.shape[1]
     turned, parts = {}, {}
-    for x in picked:
+    for _, x in picked:
         if id(x) not in turned:
             turned[id(x)] = columns(x[:kept])
             parts[id(x)] = [y.astype(F32) for y in pieces(x)]
-    depth = max(16, 8 * scen)
-    sub = lax.broadcasted_iota(jnp.int32, (depth, side), 0)
-    order = [(k + 0.5) / kept for k in range(kept)]
-    order += [(m + 0.5) / split_slots for m in range(split_slots)]
-    for k in sorted(range(kept + split_slots), key=lambda k: (order[k], k)):
-        if k < kept:
-            wide = {}
-            for s in range(scen):
-                key = id(picked[s])
-                if key not in wide:
-                    wide[key] = jnp.broadcast_to(turned[key][:, k : k + 1], (side, side))
-                rows[s, k : k + 1, :] = jnp.sum(whole[s, k] * wide[key], axis=0, keepdims=True)
-            continue
-        m = k - kept
-        firsts, stacks = [], {}
-        for s in range(scen):
-            key = id(picked[s])
-            high, mid, low = [x[k : k + 1, :] for x in parts[key]]
-            firsts.append(jnp.where(sub == 8 * s, high, 0.0).astype(BF16))
-            if key not in stacks:
-                stack = jnp.where(sub == 0, high, jnp.where(sub == 1, mid, jnp.where(sub == 2, low, 0.0)))
-                stacks[key] = jnp.concatenate([stack.astype(BF16)] * 2, axis=1)
-        rest = jnp.dot(jnp.concatenate(firsts, axis=1), lower[m], preferred_element_type=F32)
-        for s in range(scen):
-            main = jnp.dot(stacks[id(picked[s])], upper[s, m], preferred_element_type=F32)
-            total = main[:8] + rest[8 * s : 8 * s + 8]
-            rows[s, k : k + 1, :] = jnp.sum(total, axis=0, keepdims=True)
+    sub = lax.broadcasted_iota(jnp.int32, (16, side), 0)
+
+    def on_vector_unit(k):
+        wide = {}
+        for n, (s, x) in enumerate(picked):
+            if id(x) not in wide:
+                wide[id(x)] = jnp.broadcast_to(turned[id(x)][:, k : k + 1], (side, side))
+            rows[n, k : k + 1, :] = jnp.sum(whole[s, k] * wide[id(x)], axis=0, keepdims=True)
+
+    def on_matrix_unit(m):
+        left = {}
+        for n, (s, x) in enumerate(picked):
+            if id(x) not in left:
+                stacks, firsts = [], []
+                for u in range(2):
+                    k = kept + 2 * m + u
+                    high, mid, low = [y[k : k + 1, :] for y in parts[id(x)]]
+                    stack = jnp.where(sub == 1, mid, jnp.where(sub == 2, low, 0.0))
+                    stack = jnp.where(sub == 0, high, stack).astype(BF16)
+                    stacks.append(jnp.concatenate([stack] * 2, axis=1))
+                    firsts.append(jnp.where(sub == 8 * u, high, 0.0).astype(BF16))
+                left[id(x)] = stacks, jnp.concatenate(firsts, axis=1)
+            stacks, firsts = left[id(x)]
+            rest = jnp.dot(firsts, lower[s, m], preferred_element_type=F32)
+            for u in range(2):
+                k = kept + 2 * m + u
+                main = jnp.dot(stacks[u], upper[s, 2 * m + u], preferred_element_type=F32)
+                total = main[:8] + rest[8 * u : 8 * u + 8]
+                rows[n, k : k + 1, :] = jnp.sum(total, axis=0, keepdims=True)
+
+    order = [((k + 0.5) / kept, on_vector_unit, k) for k in range(kept)]
+    order += [((m + 0.5) / pairs, on_matrix_unit, m) for m in range(pairs)]
+    for _, work, k in sorted(order, key=lambda entry: entry[0]):
+        work(k)
 
 
 def merge(a, b):
@@ -122,7 +129,7 @@
                     high, mid, rest = pieces(x)
                     up[s, k, :side] = high
                     up[s, k, side:] = mid
-                    low[k, s * side : (s + 1) * side] = rest
+                    low[s, k // 2, k % 2 * side : (k % 2 + 1) * side] = rest
 
 
 def hot_kernel(
@@ -167,63 +174,75 @@
     joined[size:] = jnp.where(low, other[...], mine[...])
 
 
-def first_kernel(whole, upper, lower, fluence, target, col_hot, same, excess, score_sum, rows):
-    scen = whole.shape[0]
-    picked = exact(col_hot[...], [fluence[...]])
-    products(whole, upper, lower, picked * scen, rows)
+def first_kernel(whole, upper, lower, fluence, target, col_hot, same, *refs):
+    *excess, score_sum, rows = refs
+    scen = len(excess)
+    picked = exact(col_hot[...], [fluence[...]])[0]
+    products(whole, upper, lower, [(s, picked) for s in range(scen)], rows)
     scores = []
     for s, dose in enumerate(exact(same[...], [rows[s] for s in range(scen)])):
         e = dose - target[...]
-        excess[s] = e
+        excess[s][...] = e
         scores.append(SHARPNESS * e * e)
     top = functools.reduce(jnp.maximum, scores)
     total = functools.reduce(jnp.add, [jnp.exp(score - top) for score in scores])
     score_sum[...] = top + jnp.log(total)
 
 
-def second_kernel(whole, upper, lower, excess, sum_a, sum_b, col_hot_t, weights, gradient, rows):
-    scen = excess.shape[0]
+def second_kernel(scens, whole, upper, lower, sum_a, sum_b, col_hot_t, order, *refs):
+    del order
+    *refs, rows = refs
+    n = len(scens)
+    excess, weights, gradient = refs[:n], refs[n : 2 * n], refs[2 * n :]
     total = merge(sum_a[...], sum_b[...])
     picked = []
-    for s in range(scen):
-        e = excess[s]
+    for m, s in enumerate(scens):
+        e = excess[m][...]
         w = jnp.exp(SHARPNESS * e * e - total)
-        weights[s] = w
-        picked.append(2.0 * w * e)
+        weights[m][...] = w
+        picked.append((s, 2.0 * w * e))
     products(whole, upper, lower, picked, rows)
-    put_gradient(col_hot_t, rows, gradient)
+    for m, g in enumerate(exact(col_hot_t[...], [rows[m] for m in range(n)])):
+        gradient[m][...] = g
 
 
 def third_kernel(
-    whole, upper, lower, whole_t, upper_t, lower_t, fluence, grad_a, grad_b, weights, target,
-    col_hot, col_hot_t, same, copies, gradient, rows, held
+    scens, whole, upper, lower, whole_t, upper_t, lower_t, fluence, target,
+    col_hot, col_hot_t, same, *refs
 ):
-    scen = weights.shape[0]
-    share = copies.shape[1]
+    *refs, rows, held = refs
+    n = len(scens)
+    grad_a, grad_b, weights, refs = refs[:n], refs[n : 2 * n], refs[2 * n : 3 * n], refs[3 * n :]
+    together = len(refs[-1].shape) == 4
+    others = refs[: len(refs) - n - (1 if together else n)]
+    copies = refs[len(others) : len(others) + n]
+    gradient = refs[len(others) + n :]
+    share = copies[0].shape[0]
     mine = pl.ds(0 if share == held.shape[1] else lax.axis_index("vox") * share, share)
-    for s in range(scen):
-        held[s] = jnp.maximum(fluence[...] - STEP_SIZE * (grad_a[s] + grad_b[s]), 0.0)
-        copies[s] = held[s, mine]
-    picked = exact(col_hot[...], [held[s] for s in range(scen)])
-    products(whole_t, upper_t, lower_t, picked, rows)
-    doses = exact(same[...], [rows[s] for s in range(scen)])
-    picked = [2.0 * weights[s] * (doses[s] - target[...]) for s in range(scen)]
-    products(whole, upper, lower, picked, rows)
-    put_gradient(col_hot_t, rows, gradient)
-
-
-def put_gradient(col_hot_t, rows, gradient):
-    for s, g in enumerate(exact(col_hot_t[...], [rows[s] for s in range(rows.shape[0])])):
-        if len(gradient.shape) == 3:
-            gradient[s] = g
-        else:
-            gradient[:, s] = g.reshape(gradient.shape[0], *gradient.shape[2:])
-
-
-def place_kernel(scen_total, weights, leads, placed):
+    for m in range(n):
+        step = STEP_SIZE * (grad_a[m][...] + grad_b[m][...])
+        held[m] = jnp.maximum(fluence[...] - step, 0.0)
+        copies[m][...] = held[m, mine]
+    picked = exact(col_hot[...], [held[m] for m in range(n)])
+    products(whole_t, upper_t, lower_t, list(zip(scens, picked)), rows)
+    doses = exact(same[...], [rows[m] for m in range(n)])
+    picked = [2.0 * weights[m][...] * (doses[m] - target[...]) for m in range(n)]
+    products(whole, upper, lower, list(zip(scens, picked)), rows)
+    found = exact(col_hot_t[...], [rows[m] for m in range(n)])
+    if not together:
+        for m, g in enumerate(found):
+            gradient[m][...] = g
+        return
+    parts, _, *piece = gradient[0].shape
+    for m, g in enumerate([*(x[...] for x in others), *found]):
+        gradient[0][:, m] = g.reshape(parts, *piece)
+
+
+def place_kernel(scen_total, leads, order, *refs):
+    del order
     used = jnp.sum(leads[...].astype(F32), axis=1, keepdims=True)
-    scen = weights.shape[0]
-    for s, w in enumerate(exact(leads[...], [weights[s] for s in range(scen)])):
+    *weights, placed = refs
+    for s, w in enumerate(exact(leads[...], [x[...] for x in weights])):
         placed[:, s] = jnp.where(used == 0.0, 1.0 / scen_total, w)
 
 
@@ -293,7 +312,6 @@
     params = pltpu.CompilerParams(vmem_limit_bytes=16 * 2**20)
     passes = scen * slots * side * side
     dense = lambda *shape: jax.ShapeDtypeStruct(shape, F32)
-    scratch = [pltpu.VMEM((scen, slots, side), F32)]
 
     fluence = fluence_init.reshape(share // side, side)
     half = lambda *shape: jax.ShapeDtypeStruct(shape, BF16)
@@ -324,6 +342,7 @@
     )
 
     kept = slots * 2 // 5
+    kept += (slots - kept) % 2
     rest = slots - kept
     steps = bits("vox")
     for n, bit in enumerate(steps):
@@ -351,7 +370,7 @@
                 functools.partial(split_kernel, sizes),
                 name="split",
                 out_shape=(pltpu.VMEM((scen, rest, 2 * side, side), BF16),) * 2
-                + (pltpu.VMEM((rest, scen * side, side), BF16),) * 2,
+                + (pltpu.VMEM((scen, rest // 2, 2 * side, side), BF16),) * 2,
                 in_specs=[FAR, VMEM],
                 out_specs=(VMEM,) * 4,
                 scratch_shapes=[
@@ -375,61 +394,88 @@
     flipped = [near(x) for x in (whole_t, upper_t, lower_t)]
 
     for outer_round in range(ROUNDS):
-        excess, score_sum = pl.pallas_call(
+        last = outer_round == ROUNDS - 1
+        *excess, score_sum = pl.pallas_call(
             first_kernel,
             name="first",
-            out_shape=(dense(scen, slots, side), dense(slots, side)),
+            out_shape=(dense(slots, side),) * (scen + 1),
             in_specs=[VMEM] * 7,
-            out_specs=(VMEM,) * 2,
-            scratch_shapes=scratch,
+            out_specs=(VMEM,) * (scen + 1),
+            scratch_shapes=[pltpu.VMEM((scen, slots, side), F32)],
             compiler_params=params,
         )(*flipped, fluence, target, col_hot, same)
         sum_a, sum_b = reduce_scen(score_sum, merge)
-        last = outer_round == ROUNDS - 1
-        weights, gradient = pl.pallas_call(
-            second_kernel,
-            name="second",
-            out_shape=(dense(scen, slots, side), dense(scen, beam_blocks, side)),
-            in_specs=[VMEM] * 7,
-            out_specs=(VMEM,) * 2,
-            scratch_shapes=scratch,
-            compiler_params=params,
-        )(*blocks, excess, sum_a, sum_b, col_hot_t)
-        grad_a, grad_b = reduce_vox(gradient)
-        form = (parts, scen, share // side, side) if last else (scen, beam_blocks, side)
-        copies, gradient = pl.pallas_call(
-            third_kernel,
-            name="third",
-            out_shape=(dense(scen, share // side if last else beam_blocks, side), dense(*form)),
-            in_specs=[VMEM] * 14,
-            out_specs=(VMEM,) * 2,
-            scratch_shapes=scratch + [pltpu.VMEM((scen, beam_blocks, side), F32)],
-            compiler_params=params,
-        )(
-            *blocks, *flipped, fluence, grad_a, grad_b, weights, target,
-            col_hot, col_hot_t, same,
-        )
+
+        groups = [[s] for s in range(scen)] if last else [list(range(scen))]
+        weights, gradients, order = [], [], score_sum
+        for group in groups:
+            n = len(group)
+            found = pl.pallas_call(
+                functools.partial(second_kernel, group),
+                name="second",
+                out_shape=(dense(slots, side),) * n + (dense(beam_blocks, side),) * n,
+                in_specs=[VMEM] * (7 + n),
+                out_specs=(VMEM,) * (2 * n),
+                scratch_shapes=[pltpu.VMEM((n, slots, side), F32)],
+                compiler_params=params,
+            )(*blocks, sum_a, sum_b, col_hot_t, order, *[excess[s] for s in group])
+            order = found[-1]
+            weights += found[:n]
+            gradients += found[n:]
+        sums = [reduce_vox(gradient) for gradient in gradients]
+        copies, gradients = [], []
+        for group in groups:
+            n = len(group)
+            together = last and group is groups[-1]
+            others = gradients if together else []
+            form = [(parts, scen, share // side, side)] if together else [(beam_blocks, side)] * n
+            found = pl.pallas_call(
+                functools.partial(third_kernel, group),
+                name="third",
+                out_shape=(dense(share // side if last else beam_blocks, side),) * n
+                + tuple(dense(*shape) for shape in form),
+                in_specs=[VMEM] * (11 + 3 * n + len(others)),
+                out_specs=(VMEM,) * (n + len(form)),
+                scratch_shapes=[
+                    pltpu.VMEM((n, slots, side), F32),
+                    pltpu.VMEM((n, beam_blocks, side), F32),
+                ],
+                compiler_params=params,
+            )(
+                *blocks, *flipped, fluence, target, col_hot, col_hot_t, same,
+                *[sums[s][0] for s in group], *[sums[s][1] for s in group],
+                *[weights[s] for s in group], *others,
+            )
+            copies += found[:n]
+            gradients += found[n:]
         if not last:
-            grad_a, grad_b = reduce_vox(gradient)
+            sums = [reduce_vox(gradient) for gradient in gradients]
+            gradients = [a + b for a, b in sums]
         else:
-            weights = pl.pallas_call(
+            gradient, copies = lax.optimization_barrier((gradients[-1], copies))
+            gradient = lax.all_to_all(gradient, "vox", split_axis=0, concat_axis=0, tiled=True)
+            gradient = jnp.sum(gradient, axis=0)
+            gradients = [gradient[s] for s in range(scen)]
+        copies = [jnp.maximum(c - STEP_SIZE * g, 0.0) for c, g in zip(copies, gradients)]
+        total = functools.reduce(jnp.add, copies)
+        if last:
+            others = [swap(total, "scen", n) for n in range(1, lax.axis_size("scen"))]
+            placed = pl.pallas_call(
                 functools.partial(place_kernel, scen_total),
                 name="place",
                 out_shape=dense(row_blocks, scen, side),
-                in_specs=[VMEM] * 2,
+                in_specs=[VMEM] * (2 + scen),
                 out_specs=VMEM,
                 compiler_params=params,
                 cost_estimate=pl.CostEstimate(
-                    flops=0, bytes_accessed=8 * weights.size, transcendentals=0
+                    flops=0, bytes_accessed=8 * scen * row_blocks * side, transcendentals=0
                 ),
-            )(near(weights), leads)
-            weights = jnp.swapaxes(weights, 0, 1).reshape(scen, row_blocks * side)
-            gradient, copies, weights = lax.optimization_barrier((gradient, copies, weights))
-            gradient = lax.all_to_all(gradient, "vox", split_axis=0, concat_axis=0, tiled=True)
-            grad_a, grad_b = jnp.sum(gradient, axis=0), 0.0
-        copies = jnp.maximum(copies - STEP_SIZE * (grad_a + grad_b), 0.0)
-        mean_a, mean_b = reduce_scen(jnp.sum(copies, axis=0), jnp.add)
-        fluence = (mean_a + mean_b) / scen_total
+            )(leads, total, *weights)
+            weights = jnp.swapaxes(placed, 0, 1).reshape(scen, row_blocks * side)
+            total = functools.reduce(jnp.add, others, total)
+        else:
+            total = functools.reduce(jnp.add, reduce_scen(total, jnp.add))
+        fluence = total / scen_total
     return fluence.reshape(share), weights
 
 

time: 111 us -> 108 us (0.973)
  waiting for transfers between devices: 55.8 us -> 36.8 us
  starting transfers between devices: 20.3 us -> 33.6 us
  Pallas kernels: 22.8 us -> 24.6 us
    ppermute x9 -> x18, waiting for transfers between devices: 42.4 us -> 25.4 us  [reduce_vox(): lax.ppermute(x, 'vox', [(v, v ^ pair[(v & steps[-2]) // steps[-2]]) for v...]
    ppermute x9 -> x18, starting transfers between devices: 7.31 us -> 20.1 us  [reduce_vox(): lax.ppermute(x, 'vox', [(v, v ^ pair[(v & steps[-2]) // steps[-2]]) for v...]
    ppermute x8 -> x9, waiting for transfers between devices: 13.4 us -> 11.4 us  [swap(): lax.ppermute(x, axis, [(i, i ^ bit) for i in range(lax.axis_size(axis))])]
    pallas_call x6 -> x8, Pallas kernels: 14.4 us -> 16.3 us  [the longest x3 8.31 us: body(): pl.pallas_call(functools.partial(third_kernel, group), name='third', out_...]
    ppermute x8 -> x9, starting transfers between devices: 6.08 us -> 6.64 us  [swap(): lax.ppermute(x, axis, [(i, i ^ bit) for i in range(lax.axis_size(axis))])]
  transfers between devices with their start and end apart: 20 -> 30, of which waited for: 17 -> 25; matrix products, arithmetic and copies ran while one was open for 0% -> 0% of each run, Pallas kernels for 7% -> 11%
where the time goes in v7:
time: 108 us
  waiting for transfers between devices  36.8 us (34%)
  starting transfers between devices  33.6 us (31%)
  Pallas kernels  24.6 us (23%)
  blocking collectives  10.3 us (10%)
  between operations  1.52 us (1%)
    ppermute x18, waiting for transfers between devices, reduce_vox(): lax.ppermute(x, 'vox', [(v, v ^ pair[(v & steps[-2]) // steps[-2]]) for v...  25.4 us
    ppermute x18, starting transfers between devices, reduce_vox(): lax.ppermute(x, 'vox', [(v, v ^ pair[(v & steps[-2]) // steps[-2]]) for v...  20.1 us
    ppermute x9, waiting for transfers between devices, swap(): lax.ppermute(x, axis, [(i, i ^ bit) for i in range(lax.axis_size(axis))])  11.4 us
    all_to_all x1, blocking collectives, body(): lax.all_to_all(gradient, 'vox', split_axis=0, concat_axis=0, tiled=True)  10.3 us
    pallas_call x3, Pallas kernels, body(): pl.pallas_call(functools.partial(third_kernel, group), name='third', out_...  8.31 us
    ppermute x3, starting transfers between devices, swap_both(): return lax.ppermute(x, ('scen', 'vox'), pairs)  6.9 us
    ppermute x9, starting transfers between devices, swap(): lax.ppermute(x, axis, [(i, i ^ bit) for i in range(lax.axis_size(axis))])  6.64 us
    pallas_call x2, Pallas kernels, body(): pl.pallas_call(first_kernel, name='first', out_shape=(dense(slots, side),...  4.06 us
  transfers between devices with their start and end apart: 30, of which 25 were waited for; matrix products, arithmetic and copies ran while one was open for 0% of the time, Pallas kernels for 11%

profile of v7, /device:TPU:0, one launch (start us, length us, event | category | flops | bytes accessed | tf_op | source)
XLA Modules:
  0.0 107.7 jit_solution(14364984871453061839)
XLA Ops:
  0.6 2.4 %collective-permute-start = (f32[16,128]{1,0:T(8,128)}, f32[16,128]{1,0:T(8,128)S(1)}, u32[]{:S(2)}, u32[]{:S(2)}) collective-permute-start(f32[16,128]{1,0:T(8,128)} %bitcast.28), channel_id=1, source_target_pairs={{0,9},{1,8},{2,11},{3,10},{4,13},{5,12},{6,15},{7,14},{8,1},{9,0},... | collective-permute-start | bytes 24584 | tf_op jit(solution)/shard_map/ppermute | solution.py:298
  3.7 1.2 %hot.1 = (bf16[80,128]{1,0:T(8,128)(2,1)S(1)}, bf16[128,80]{1,0:T(8,128)(2,1)S(1)}, bf16[80,80]{1,0:T(8,128)(2,1)S(1)}, bf16[128,80]{1,0:T(8,128)(2,1)S(1)}, f32...) custom-call(s32[2,80]{1,0:T(2,128)} %bitcast.30, f32[16,128]{1,0:T(8,128)} %bitcast.29, f32[128,128]{1,0:T(8,128)} %bitcast.27, ...), custom_call_target="tpu_custom_call" | custom-call | tf_op jit(solution)/shard_map/hot/pallas_call | solution.py:318
  5.0 1.9 %collective-permute-start.1 = (f32[32,128]{1,0:T(8,128)S(1)}, f32[32,128]{1,0:T(8,128)S(1)}, u32[]{:S(2)}, u32[]{:S(2)}) collective-permute-start(f32[32,128]{1,0:T(8,128)S(1)} %join.3.order.mine), channel_id=1, source_target_pairs={{0,10},{1,11},{2,8},{3,9},{4,14},{5,15},{6,12},{7,13},{8,2},{9,3},... | collective-permute-start | bytes 49160 | tf_op jit(solution)/shard_map/ppermute | solution.py:298
  6.9 2.6 %whole.1 = (f32[2,32,128,128]{3,2,1,0:T(8,128)S(1)}, f32[2,32,128,128]{3,2,1,0:T(8,128)S(1)}, f32[8,128]{1,0:T(8,128)S(1)}) custom-call(f32[2,80,128,128]{3,2,1,0:T(8,128)} %source.3, f32[32,128]{1,0:T(8,128)S(1)} %join.3.order.mine), custom_call_target="tpu_custom_call" | custom-call | bytes 7864320 | tf_op jit(solution)/shard_map/whole/pallas_call | solution.py:355
  9.5 2.5 %collective-permute-start.2 = (f32[64,128]{1,0:T(8,128)S(1)}, f32[64,128]{1,0:T(8,128)S(1)}, u32[]{:S(2)}, u32[]{:S(2)}) collective-permute-start(f32[64,128]{1,0:T(8,128)S(1)} %join.4.order.mine), channel_id=1, source_target_pairs={{0,12},{1,13},{2,14},{3,15},{4,8},{5,9},{6,10},{7,11},{8,4},{9,5},... | collective-permute-start | bytes 98312 | tf_op jit(solution)/shard_map/ppermute | solution.py:298
  12.1 3.6 %split.1 = (bf16[2,48,256,128]{3,2,1,0:T(8,128)(2,1)S(1)}, bf16[2,48,256,128]{3,2,1,0:T(8,128)(2,1)S(1)}, bf16[2,24,256,128]{3,2,1,0:T(8,128)(2,1)S(1)}, bf16[2,24,256,128]{3,2,1,0:T(8,128)(2,1)S(1)}) custom-call(f32[2,80,128,128]{3,2,1,0:T(8,128)} %source.3, f32[64,128]{1,0:T(8,128)S(1)} %join.4.order.mine), custom_call_target="tpu_custom_call" | custom-call | bytes 13107200 | tf_op jit(solution)/shard_map/split/pallas_call | solution.py:369
  15.7 1.9 %first.2 = (f32[80,128]{1,0:T(8,128)S(1)}, f32[80,128]{1,0:T(8,128)S(1)}, f32[80,128]{1,0:T(8,128)S(1)}) custom-call(f32[2,32,128,128]{3,2,1,0:T(8,128)S(1)} %get-tuple-element.45.whole.whole_t, bf16[2,48,256,128]{3,2,1,0:T(8,128)(2,1)S(1)} %get-tuple-element.46.upper.upper_t, bf16[2,24,256,128]{3,2,1,0:T(8,128)(2,1)S(1)} %get-tuple-element.47.lower.lower_t, ...), custom_call_target="tpu_custom_call" | custom-call | tf_op jit(solution)/shard_map/first/pallas_call | solution.py:398
  17.9 1.0 collective-permute-done.3
  19.0 1.4 %collective-permute-start.4 = (f32[80,128]{1,0:T(8,128)S(1)}, f32[80,128]{1,0:T(8,128)S(1)}, u32[]{:S(2)}, u32[]{:S(2)}) collective-permute-start(f32[80,128]{1,0:T(8,128)S(1)} %log_add_fusion.1.sum_a), channel_id=1, source_target_pairs={{0,24},{8,16},{16,8},{24,0},{1,25},{9,17},{17,9},{25,1},{2,26},{10... | collective-permute-start | bytes 122888 | tf_op jit(solution)/shard_map/ppermute | solution.py:258
  20.4 2.2 %collective-permute-done.4.sum_b = f32[80,128]{1,0:T(8,128)S(1)} collective-permute-done((f32[80,128]{1,0:T(8,128)S(1)}, f32[80,128]{1,0:T(8,128)S(1)}, u32[]{:S(2)}, u32[]{:S(2)}) %collective-permute-start.4) | collective-permute-done | bytes 40992 | tf_op jit(solution)/shard_map/ppermute | solution.py:258
  22.6 1.7 %second.3 = (f32[80,128]{1,0:T(8,128)S(1)}, f32[80,128]{1,0:T(8,128)S(1)}, f32[128,128]{1,0:T(8,128)S(1)}, f32[128,128]{1,0:T(8,128)S(1)}) custom-call(f32[2,32,128,128]{3,2,1,0:T(8,128)S(1)} %get-tuple-element.41.whole, bf16[2,48,256,128]{3,2,1,0:T(8,128)(2,1)S(1)} %get-tuple-element.43.upper, bf16[2,24,256,128]{3,2,1,0:T(8,128)(2,1)S(1)} %get-tuple-element.44.lower, ...), custom_call_target="tpu_custom_call" | custom-call | tf_op jit(solution)/shard_map/second/pallas_call | solution.py:413
  25.0 2.3 %collective-permute-start.7 = (f32[128,128]{1,0:T(8,128)S(1)}, f32[128,128]{1,0:T(8,128)S(1)}, u32[]{:S(2)}, u32[]{:S(2)}) collective-permute-start(f32[128,128]{1,0:T(8,128)S(1)} %get-tuple-element.56), channel_id=1, source_target_pairs={{0,4},{1,5},{2,3},{3,2},{4,0},{5,1},{6,7},{7,6},{8,12},{9,13},{10,... | collective-permute-start | bytes 196616 | tf_op jit(solution)/shard_map/ppermute | solution.py:278
  27.3 2.8 %collective-permute-done.5 = f32[128,128]{1,0:T(8,128)S(1)} collective-permute-done((f32[128,128]{1,0:T(8,128)S(1)}, f32[128,128]{1,0:T(8,128)S(1)}, u32[]{:S(2)}, u32[]{:S(2)}) %collective-permute-start.5) | collective-permute-done | bytes 65568 | tf_op jit(solution)/shard_map/ppermute | solution.py:278
  30.1 1.6 %collective-permute-start.6 = (f32[128,128]{1,0:T(8,128)S(1)}, f32[128,128]{1,0:T(8,128)S(1)}, u32[]{:S(2)}, u32[]{:S(2)}) collective-permute-start(f32[128,128]{1,0:T(8,128)S(1)} %add.77), channel_id=1, source_target_pairs={{0,1},{1,0},{2,6},{3,7},{4,5},{5,4},{6,2},{7,3},{8,9},{9,8},{10,14... | collective-permute-start | bytes 196616 | tf_op jit(solution)/shard_map/ppermute | solution.py:278
  32.5 2.0 %collective-permute-done.6 = f32[128,128]{1,0:T(8,128)S(1)} collective-permute-done((f32[128,128]{1,0:T(8,128)S(1)}, f32[128,128]{1,0:T(8,128)S(1)}, u32[]{:S(2)}, u32[]{:S(2)}) %collective-permute-start.6) | collective-permute-done | bytes 65568 | tf_op jit(solution)/shard_map/ppermute | solution.py:278
  34.7 1.4 %collective-permute-done.8 = f32[128,128]{1,0:T(8,128)S(1)} collective-permute-done((f32[128,128]{1,0:T(8,128)S(1)}, f32[128,128]{1,0:T(8,128)S(1)}, u32[]{:S(2)}, u32[]{:S(2)}) %collective-permute-start.8) | collective-permute-done | bytes 65568 | tf_op jit(solution)/shard_map/ppermute | solution.py:278
  36.6 2.2 %collective-permute-done.9.refs_2_ = f32[128,128]{1,0:T(8,128)S(1)} collective-permute-done((f32[128,128]{1,0:T(8,128)S(1)}, f32[128,128]{1,0:T(8,128)S(1)}, u32[]{:S(2)}, u32[]{:S(2)}) %collective-permute-start.9) | collective-permute-done | bytes 65568 | tf_op jit(solution)/shard_map/ppermute | solution.py:278
  38.8 1.6 %collective-permute-done.10.refs_3_ = f32[128,128]{1,0:T(8,128)S(1)} collective-permute-done((f32[128,128]{1,0:T(8,128)S(1)}, f32[128,128]{1,0:T(8,128)S(1)}, u32[]{:S(2)}, u32[]{:S(2)}) %collective-permute-start.10) | collective-permute-done | bytes 65568 | tf_op jit(solution)/shard_map/ppermute | solution.py:278
  40.4 3.7 %third.3 = (f32[128,128]{1,0:T(8,128)S(1)}, f32[128,128]{1,0:T(8,128)S(1)}, f32[128,128]{1,0:T(8,128)S(1)}, f32[128,128]{1,0:T(8,128)S(1)}) custom-call(f32[2,32,128,128]{3,2,1,0:T(8,128)S(1)} %get-tuple-element.41.whole, bf16[2,48,256,128]{3,2,1,0:T(8,128)(2,1)S(1)} %get-tuple-element.43.upper, bf16[2,24,256,128]{3,2,1,0:T(8,128)(2,1)S(1)} %get-tuple-element.44.lower, ...), custom_call_target="tpu_custom_call" | custom-call | tf_op jit(solution)/shard_map/third/pallas_call | solution.py:432
  44.1 0.8 collective-permute-start.11
  44.9 2.2 %collective-permute-start.14 = (f32[128,128]{1,0:T(8,128)S(1)}, f32[128,128]{1,0:T(8,128)S(1)}, u32[]{:S(2)}, u32[]{:S(2)}) collective-permute-start(f32[128,128]{1,0:T(8,128)S(1)} %get-tuple-element.62), channel_id=1, source_target_pairs={{0,4},{1,5},{2,3},{3,2},{4,0},{5,1},{6,7},{7,6},{8,12},{9,13},{10,... | collective-permute-start | bytes 196616 | tf_op jit(solution)/shard_map/ppermute | solution.py:278
  47.1 2.9 %collective-permute-done.11 = f32[128,128]{1,0:T(8,128)S(1)} collective-permute-done((f32[128,128]{1,0:T(8,128)S(1)}, f32[128,128]{1,0:T(8,128)S(1)}, u32[]{:S(2)}, u32[]{:S(2)}) %collective-permute-start.11) | collective-permute-done | bytes 65568 | tf_op jit(solution)/shard_map/ppermute | solution.py:278
  50.8 1.4 %collective-permute-start.15 = (f32[128,128]{1,0:T(8,128)S(1)}, f32[128,128]{1,0:T(8,128)S(1)}, u32[]{:S(2)}, u32[]{:S(2)}) collective-permute-start(f32[128,128]{1,0:T(8,128)S(1)} %add.84), channel_id=1, source_target_pairs={{0,1},{1,0},{2,6},{3,7},{4,5},{5,4},{6,2},{7,3},{8,9},{9,8},{10,14... | collective-permute-start | bytes 196616 | tf_op jit(solution)/shard_map/ppermute | solution.py:278
  52.2 2.2 %collective-permute-done.12 = f32[128,128]{1,0:T(8,128)S(1)} collective-permute-done((f32[128,128]{1,0:T(8,128)S(1)}, f32[128,128]{1,0:T(8,128)S(1)}, u32[]{:S(2)}, u32[]{:S(2)}) %collective-permute-start.12) | collective-permute-done | bytes 65568 | tf_op jit(solution)/shard_map/ppermute | solution.py:278
  55.2 1.4 %collective-permute-start.16 = (f32[128,128]{1,0:T(8,128)S(1)}, f32[128,128]{1,0:T(8,128)S(1)}, u32[]{:S(2)}, u32[]{:S(2)}) collective-permute-start(f32[128,128]{1,0:T(8,128)S(1)} %add.85), channel_id=1, source_target_pairs={{0,2},{1,3},{2,0},{3,1},{4,6},{5,7},{6,4},{7,5},{8,10},{9,11},{10,... | collective-permute-start | bytes 196616 | tf_op jit(solution)/shard_map/ppermute | solution.py:278
  56.6 2.2 %collective-permute-done.13 = f32[128,128]{1,0:T(8,128)S(1)} collective-permute-done((f32[128,128]{1,0:T(8,128)S(1)}, f32[128,128]{1,0:T(8,128)S(1)}, u32[]{:S(2)}, u32[]{:S(2)}) %collective-permute-start.13) | collective-permute-done | bytes 65568 | tf_op jit(solution)/shard_map/ppermute | solution.py:278
  59.6 1.2 %collective-permute-done.17 = f32[128,128]{1,0:T(8,128)S(1)} collective-permute-done((f32[128,128]{1,0:T(8,128)S(1)}, f32[128,128]{1,0:T(8,128)S(1)}, u32[]{:S(2)}, u32[]{:S(2)}) %collective-permute-start.17) | collective-permute-done | bytes 65568 | tf_op jit(solution)/shard_map/ppermute | solution.py:258
  60.8 1.3 %collective-permute-start.18 = (f32[128,128]{1,0:T(8,128)S(1)}, f32[128,128]{1,0:T(8,128)S(1)}, u32[]{:S(2)}, u32[]{:S(2)}) collective-permute-start(f32[128,128]{1,0:T(8,128)S(1)} %add.88), channel_id=1, source_target_pairs={{0,24},{8,16},{16,8},{24,0},{1,25},{9,17},{17,9},{25,1},{2,26},{10... | collective-permute-start | bytes 196616 | tf_op jit(solution)/shard_map/ppermute | solution.py:258
  62.2 2.8 %collective-permute-done.18 = f32[128,128]{1,0:T(8,128)S(1)} collective-permute-done((f32[128,128]{1,0:T(8,128)S(1)}, f32[128,128]{1,0:T(8,128)S(1)}, u32[]{:S(2)}, u32[]{:S(2)}) %collective-permute-start.18) | collective-permute-done | bytes 65568 | tf_op jit(solution)/shard_map/ppermute | solution.py:258
  65.0 2.1 %first.3 = (f32[80,128]{1,0:T(8,128)S(1)}, f32[80,128]{1,0:T(8,128)S(1)}, f32[80,128]{1,0:T(8,128)S(1)}) custom-call(f32[2,32,128,128]{3,2,1,0:T(8,128)S(1)} %get-tuple-element.45.whole.whole_t, bf16[2,48,256,128]{3,2,1,0:T(8,128)(2,1)S(1)} %get-tuple-element.46.upper.upper_t, bf16[2,24,256,128]{3,2,1,0:T(8,128)(2,1)S(1)} %get-tuple-element.47.lower.lower_t, ...), custom_call_target="tpu_custom_call" | custom-call | tf_op jit(solution)/shard_map/first/pallas_call | solution.py:398
  67.3 1.1 collective-permute-done.19
  68.4 1.4 %collective-permute-start.20 = (f32[80,128]{1,0:T(8,128)S(1)}, f32[80,128]{1,0:T(8,128)S(1)}, u32[]{:S(2)}, u32[]{:S(2)}) collective-permute-start(f32[80,128]{1,0:T(8,128)S(1)} %log_add_fusion.sum_a), channel_id=1, source_target_pairs={{0,24},{8,16},{16,8},{24,0},{1,25},{9,17},{17,9},{25,1},{2,26},{10... | collective-permute-start | bytes 122888 | tf_op jit(solution)/shard_map/ppermute | solution.py:258
  69.8 2.2 %collective-permute-done.20.sum_b = f32[80,128]{1,0:T(8,128)S(1)} collective-permute-done((f32[80,128]{1,0:T(8,128)S(1)}, f32[80,128]{1,0:T(8,128)S(1)}, u32[]{:S(2)}, u32[]{:S(2)}) %collective-permute-start.20) | collective-permute-done | bytes 40992 | tf_op jit(solution)/shard_map/ppermute | solution.py:258
  72.0 1.1 %second.4 = (f32[80,128]{1,0:T(8,128)S(1)}, f32[128,128]{1,0:T(8,128)S(1)}) custom-call(f32[2,32,128,128]{3,2,1,0:T(8,128)S(1)} %get-tuple-element.41.whole, bf16[2,48,256,128]{3,2,1,0:T(8,128)(2,1)S(1)} %get-tuple-element.43.upper, bf16[2,24,256,128]{3,2,1,0:T(8,128)(2,1)S(1)} %get-tuple-element.44.lower, f32[80,128]{1,0:T(8,128)S(1)} %log_add_fusion.sum_a, ...), custom_call_target="tpu_custom_call" | custom-call | tf_op jit(solution)/shard_map/second/pallas_call | solution.py:413
  73.1 1.8 %collective-permute-start.24 = (f32[128,128]{1,0:T(8,128)S(1)}, f32[128,128]{1,0:T(8,128)S(1)}, u32[]{:S(2)}, u32[]{:S(2)}) collective-permute-start(f32[128,128]{1,0:T(8,128)S(1)} %get-tuple-element.65.order), channel_id=1, source_target_pairs={{0,4},{1,5},{2,3},{3,2},{4,0},{5,1},{6,7},{7,6},{8,12},{9,13},{10,... | collective-permute-start | bytes 196616 | tf_op jit(solution)/shard_map/ppermute | solution.py:278
  74.9 1.1 %second.5 = (f32[80,128]{1,0:T(8,128)S(1)}, f32[128,128]{1,0:T(8,128)S(1)}) custom-call(f32[2,32,128,128]{3,2,1,0:T(8,128)S(1)} %get-tuple-element.41.whole, bf16[2,48,256,128]{3,2,1,0:T(8,128)(2,1)S(1)} %get-tuple-element.43.upper, bf16[2,24,256,128]{3,2,1,0:T(8,128)(2,1)S(1)} %get-tuple-element.44.lower, f32[80,128]{1,0:T(8,128)S(1)} %log_add_fusion.sum_a, ...), custom_call_target="tpu_custom_call" | custom-call | tf_op jit(solution)/shard_map/second/pallas_call | solution.py:413
  76.0 1.3 %collective-permute-start.21 = (f32[128,128]{1,0:T(8,128)S(1)}, f32[128,128]{1,0:T(8,128)S(1)}, u32[]{:S(2)}, u32[]{:S(2)}) collective-permute-start(f32[128,128]{1,0:T(8,128)S(1)} %get-tuple-element.67), channel_id=1, source_target_pairs={{0,4},{1,5},{2,3},{3,2},{4,0},{5,1},{6,7},{7,6},{8,12},{9,13},{10,... | collective-permute-start | bytes 196616 | tf_op jit(solution)/shard_map/ppermute | solution.py:278
  77.3 1.1 collective-permute-done.24
  78.4 1.4 %collective-permute-start.25 = (f32[128,128]{1,0:T(8,128)S(1)}, f32[128,128]{1,0:T(8,128)S(1)}, u32[]{:S(2)}, u32[]{:S(2)}) collective-permute-start(f32[128,128]{1,0:T(8,128)S(1)} %add.94), channel_id=1, source_target_pairs={{0,1},{1,0},{2,6},{3,7},{4,5},{5,4},{6,2},{7,3},{8,9},{9,8},{10,14... | collective-permute-start | bytes 196616 | tf_op jit(solution)/shard_map/ppermute | solution.py:278
  79.8 2.2 %collective-permute-done.21 = f32[128,128]{1,0:T(8,128)S(1)} collective-permute-done((f32[128,128]{1,0:T(8,128)S(1)}, f32[128,128]{1,0:T(8,128)S(1)}, u32[]{:S(2)}, u32[]{:S(2)}) %collective-permute-start.21) | collective-permute-done | bytes 65568 | tf_op jit(solution)/shard_map/ppermute | solution.py:278
  82.8 1.7 %collective-permute-start.26 = (f32[128,128]{1,0:T(8,128)S(1)}, f32[128,128]{1,0:T(8,128)S(1)}, u32[]{:S(2)}, u32[]{:S(2)}) collective-permute-start(f32[128,128]{1,0:T(8,128)S(1)} %add.95.refs_0_), channel_id=1, source_target_pairs={{0,2},{1,3},{2,0},{3,1},{4,6},{5,7},{6,4},{7,5},{8,10},{9,11},{10,... | collective-permute-start | bytes 196616 | tf_op jit(solution)/shard_map/ppermute | solution.py:278
  84.5 1.8 %collective-permute-done.22 = f32[128,128]{1,0:T(8,128)S(1)} collective-permute-done((f32[128,128]{1,0:T(8,128)S(1)}, f32[128,128]{1,0:T(8,128)S(1)}, u32[]{:S(2)}, u32[]{:S(2)}) %collective-permute-start.22) | collective-permute-done | bytes 65568 | tf_op jit(solution)/shard_map/ppermute | solution.py:278
  87.3 2.3 %third.4 = (f32[16,128]{1,0:T(8,128)S(1)}, f32[128,128]{1,0:T(8,128)S(1)}) custom-call(f32[2,32,128,128]{3,2,1,0:T(8,128)S(1)} %get-tuple-element.41.whole, bf16[2,48,256,128]{3,2,1,0:T(8,128)(2,1)S(1)} %get-tuple-element.43.upper, bf16[2,24,256,128]{3,2,1,0:T(8,128)(2,1)S(1)} %get-tuple-element.44.lower, ...), custom_call_target="tpu_custom_call" | custom-call | tf_op jit(solution)/shard_map/third/pallas_call | solution.py:432
  89.6 1.0 collective-permute-done.23.refs_1_
  90.6 2.3 %third.5 = (f32[16,128]{1,0:T(8,128)S(1)}, f32[8,2,16,128]{3,2,1,0:T(8,128)S(1)}) custom-call(f32[2,32,128,128]{3,2,1,0:T(8,128)S(1)} %get-tuple-element.41.whole, bf16[2,48,256,128]{3,2,1,0:T(8,128)(2,1)S(1)} %get-tuple-element.43.upper, bf16[2,24,256,128]{3,2,1,0:T(8,128)(2,1)S(1)} %get-tuple-element.44.lower, ...), custom_call_target="tpu_custom_call" | custom-call | tf_op jit(solution)/shard_map/third/pallas_call | solution.py:432
  93.0 10.3 %all_to_all.5 = f32[8,2,16,128]{3,2,1,0:T(8,128)S(1)} all-to-all(f32[8,2,16,128]{3,2,1,0:T(8,128)S(1)} %get-tuple-element.75), channel_id=1, replica_groups=mesh['scen'=4,'vox'=8] {'vox'}, dimensions={0} | all-to-all | bytes 262144 | tf_op jit(solution)/shard_map/all_to_all | solution.py:456
  103.4 1.6 %collective-permute-start.28 = (f32[16,128]{1,0:T(8,128)S(1)}, f32[16,128]{1,0:T(8,128)S(1)}, u32[]{:S(2)}, u32[]{:S(2)}) collective-permute-start(f32[16,128]{1,0:T(8,128)S(1)} %fusion.5.order), channel_id=1, source_target_pairs={{0,16},{8,24},{16,0},{24,8},{1,17},{9,25},{17,1},{25,9},{2,18},{10... | collective-permute-start | bytes 24584 | tf_op jit(solution)/shard_map/ppermute | solution.py:258
  105.3 0.9 place.1
  (48 shorter events, 9.1 us)
Async XLA Ops:
  0.6 4.3 %collective-permute-start = (f32[16,128]{1,0:T(8,128)}, f32[16,128]{1,0:T(8,128)S(1)}, u32[]{:S(2)}, u32[]{:S(2)}) collective-permute-start(f32[16,128]{1,0:T(8,128)} %bitcast.28), channel_id=1, source_target_pairs={{0,9},{1,8},{2,11},{3,10},{4,13},{5,12},{6,15},{7,14},{8,1},{9,0},... | collective-permute-start | bytes 24584 | tf_op jit(solution)/shard_map/ppermute | solution.py:298
  5.0 4.5 %collective-permute-start.1 = (f32[32,128]{1,0:T(8,128)S(1)}, f32[32,128]{1,0:T(8,128)S(1)}, u32[]{:S(2)}, u32[]{:S(2)}) collective-permute-start(f32[32,128]{1,0:T(8,128)S(1)} %join.3.order.mine), channel_id=1, source_target_pairs={{0,10},{1,11},{2,8},{3,9},{4,14},{5,15},{6,12},{7,13},{8,2},{9,3},... | collective-permute-start | bytes 49160 | tf_op jit(solution)/shard_map/ppermute | solution.py:298
  9.5 6.1 %collective-permute-start.2 = (f32[64,128]{1,0:T(8,128)S(1)}, f32[64,128]{1,0:T(8,128)S(1)}, u32[]{:S(2)}, u32[]{:S(2)}) collective-permute-start(f32[64,128]{1,0:T(8,128)S(1)} %join.4.order.mine), channel_id=1, source_target_pairs={{0,12},{1,13},{2,14},{3,15},{4,8},{5,9},{6,10},{7,11},{8,4},{9,5},... | collective-permute-start | bytes 98312 | tf_op jit(solution)/shard_map/ppermute | solution.py:298
  17.6 1.3 %collective-permute-start.3 = (f32[80,128]{1,0:T(8,128)S(1)}, f32[80,128]{1,0:T(8,128)S(1)}, u32[]{:S(2)}, u32[]{:S(2)}) collective-permute-start(f32[80,128]{1,0:T(8,128)S(1)} %get-tuple-element.52.order), channel_id=1, source_target_pairs={{0,8},{8,0},{16,24},{24,16},{1,9},{9,1},{17,25},{25,17},{2,10},{10... | collective-permute-start | bytes 122888 | tf_op jit(solution)/shard_map/ppermute | solution.py:258
  19.0 3.6 %collective-permute-start.4 = (f32[80,128]{1,0:T(8,128)S(1)}, f32[80,128]{1,0:T(8,128)S(1)}, u32[]{:S(2)}, u32[]{:S(2)}) collective-permute-start(f32[80,128]{1,0:T(8,128)S(1)} %log_add_fusion.1.sum_a), channel_id=1, source_target_pairs={{0,24},{8,16},{16,8},{24,0},{1,25},{9,17},{17,9},{25,1},{2,26},{10... | collective-permute-start | bytes 122888 | tf_op jit(solution)/shard_map/ppermute | solution.py:258
  24.3 5.8 %collective-permute-start.5 = (f32[128,128]{1,0:T(8,128)S(1)}, f32[128,128]{1,0:T(8,128)S(1)}, u32[]{:S(2)}, u32[]{:S(2)}) collective-permute-start(f32[128,128]{1,0:T(8,128)S(1)} %get-tuple-element.55), channel_id=1, source_target_pairs={{0,4},{1,5},{2,3},{3,2},{4,0},{5,1},{6,7},{7,6},{8,12},{9,13},{10,... | collective-permute-start | bytes 196616 | tf_op jit(solution)/shard_map/ppermute | solution.py:278
  25.0 6.7 %collective-permute-start.7 = (f32[128,128]{1,0:T(8,128)S(1)}, f32[128,128]{1,0:T(8,128)S(1)}, u32[]{:S(2)}, u32[]{:S(2)}) collective-permute-start(f32[128,128]{1,0:T(8,128)S(1)} %get-tuple-element.56), channel_id=1, source_target_pairs={{0,4},{1,5},{2,3},{3,2},{4,0},{5,1},{6,7},{7,6},{8,12},{9,13},{10,... | collective-permute-start | bytes 196616 | tf_op jit(solution)/shard_map/ppermute | solution.py:278
  30.1 4.3 %collective-permute-start.6 = (f32[128,128]{1,0:T(8,128)S(1)}, f32[128,128]{1,0:T(8,128)S(1)}, u32[]{:S(2)}, u32[]{:S(2)}) collective-permute-start(f32[128,128]{1,0:T(8,128)S(1)} %add.77), channel_id=1, source_target_pairs={{0,1},{1,0},{2,6},{3,7},{4,5},{5,4},{6,2},{7,3},{8,9},{9,8},{10,14... | collective-permute-start | bytes 196616 | tf_op jit(solution)/shard_map/ppermute | solution.py:278
  31.8 4.3 %collective-permute-start.8 = (f32[128,128]{1,0:T(8,128)S(1)}, f32[128,128]{1,0:T(8,128)S(1)}, u32[]{:S(2)}, u32[]{:S(2)}) collective-permute-start(f32[128,128]{1,0:T(8,128)S(1)} %add.79), channel_id=1, source_target_pairs={{0,1},{1,0},{2,6},{3,7},{4,5},{5,4},{6,2},{7,3},{8,9},{9,8},{10,14... | collective-permute-start | bytes 196616 | tf_op jit(solution)/shard_map/ppermute | solution.py:278
  34.5 4.3 %collective-permute-start.9 = (f32[128,128]{1,0:T(8,128)S(1)}, f32[128,128]{1,0:T(8,128)S(1)}, u32[]{:S(2)}, u32[]{:S(2)}) collective-permute-start(f32[128,128]{1,0:T(8,128)S(1)} %add.78.refs_0_), channel_id=1, source_target_pairs={{0,2},{1,3},{2,0},{3,1},{4,6},{5,7},{6,4},{7,5},{8,10},{9,11},{10,... | collective-permute-start | bytes 196616 | tf_op jit(solution)/shard_map/ppermute | solution.py:278
  36.1 4.3 %collective-permute-start.10 = (f32[128,128]{1,0:T(8,128)S(1)}, f32[128,128]{1,0:T(8,128)S(1)}, u32[]{:S(2)}, u32[]{:S(2)}) collective-permute-start(f32[128,128]{1,0:T(8,128)S(1)} %add.80.refs_1_), channel_id=1, source_target_pairs={{0,2},{1,3},{2,0},{3,1},{4,6},{5,7},{6,4},{7,5},{8,10},{9,11},{10,... | collective-permute-start | bytes 196616 | tf_op jit(solution)/shard_map/ppermute | solution.py:278
  44.1 5.9 %collective-permute-start.11 = (f32[128,128]{1,0:T(8,128)S(1)}, f32[128,128]{1,0:T(8,128)S(1)}, u32[]{:S(2)}, u32[]{:S(2)}) collective-permute-start(f32[128,128]{1,0:T(8,128)S(1)} %get-tuple-element.60), channel_id=1, source_target_pairs={{0,4},{1,5},{2,3},{3,2},{4,0},{5,1},{6,7},{7,6},{8,12},{9,13},{10,... | collective-permute-start | bytes 196616 | tf_op jit(solution)/shard_map/ppermute | solution.py:278
  44.9 5.9 %collective-permute-start.14 = (f32[128,128]{1,0:T(8,128)S(1)}, f32[128,128]{1,0:T(8,128)S(1)}, u32[]{:S(2)}, u32[]{:S(2)}) collective-permute-start(f32[128,128]{1,0:T(8,128)S(1)} %get-tuple-element.62), channel_id=1, source_target_pairs={{0,4},{1,5},{2,3},{3,2},{4,0},{5,1},{6,7},{7,6},{8,12},{9,13},{10,... | collective-permute-start | bytes 196616 | tf_op jit(solution)/shard_map/ppermute | solution.py:278
  50.0 4.3 %collective-permute-start.12 = (f32[128,128]{1,0:T(8,128)S(1)}, f32[128,128]{1,0:T(8,128)S(1)}, u32[]{:S(2)}, u32[]{:S(2)}) collective-permute-start(f32[128,128]{1,0:T(8,128)S(1)} %add.81), channel_id=1, source_target_pairs={{0,1},{1,0},{2,6},{3,7},{4,5},{5,4},{6,2},{7,3},{8,9},{9,8},{10,14... | collective-permute-start | bytes 196616 | tf_op jit(solution)/shard_map/ppermute | solution.py:278
  50.8 4.3 %collective-permute-start.15 = (f32[128,128]{1,0:T(8,128)S(1)}, f32[128,128]{1,0:T(8,128)S(1)}, u32[]{:S(2)}, u32[]{:S(2)}) collective-permute-start(f32[128,128]{1,0:T(8,128)S(1)} %add.84), channel_id=1, source_target_pairs={{0,1},{1,0},{2,6},{3,7},{4,5},{5,4},{6,2},{7,3},{8,9},{9,8},{10,14... | collective-permute-start | bytes 196616 | tf_op jit(solution)/shard_map/ppermute | solution.py:278
  54.4 4.3 %collective-permute-start.13 = (f32[128,128]{1,0:T(8,128)S(1)}, f32[128,128]{1,0:T(8,128)S(1)}, u32[]{:S(2)}, u32[]{:S(2)}) collective-permute-start(f32[128,128]{1,0:T(8,128)S(1)} %add.82), channel_id=1, source_target_pairs={{0,2},{1,3},{2,0},{3,1},{4,6},{5,7},{6,4},{7,5},{8,10},{9,11},{10,... | collective-permute-start | bytes 196616 | tf_op jit(solution)/shard_map/ppermute | solution.py:278
  55.2 4.3 %collective-permute-start.16 = (f32[128,128]{1,0:T(8,128)S(1)}, f32[128,128]{1,0:T(8,128)S(1)}, u32[]{:S(2)}, u32[]{:S(2)}) collective-permute-start(f32[128,128]{1,0:T(8,128)S(1)} %add.85), channel_id=1, source_target_pairs={{0,2},{1,3},{2,0},{3,1},{4,6},{5,7},{6,4},{7,5},{8,10},{9,11},{10,... | collective-permute-start | bytes 196616 | tf_op jit(solution)/shard_map/ppermute | solution.py:278
  59.5 1.3 %collective-permute-start.17 = (f32[128,128]{1,0:T(8,128)S(1)}, f32[128,128]{1,0:T(8,128)S(1)}, u32[]{:S(2)}, u32[]{:S(2)}) collective-permute-start(f32[128,128]{1,0:T(8,128)S(1)} %maximum_add_fusion), channel_id=1, source_target_pairs={{0,8},{8,0},{16,24},{24,16},{1,9},{9,1},{17,25},{25,17},{2,10},{10... | collective-permute-start | bytes 196616 | tf_op jit(solution)/shard_map/ppermute | solution.py:258
  60.8 4.1 %collective-permute-start.18 = (f32[128,128]{1,0:T(8,128)S(1)}, f32[128,128]{1,0:T(8,128)S(1)}, u32[]{:S(2)}, u32[]{:S(2)}) collective-permute-start(f32[128,128]{1,0:T(8,128)S(1)} %add.88), channel_id=1, source_target_pairs={{0,24},{8,16},{16,8},{24,0},{1,25},{9,17},{17,9},{25,1},{2,26},{10... | collective-permute-start | bytes 196616 | tf_op jit(solution)/shard_map/ppermute | solution.py:258
  67.1 1.3 %collective-permute-start.19 = (f32[80,128]{1,0:T(8,128)S(1)}, f32[80,128]{1,0:T(8,128)S(1)}, u32[]{:S(2)}, u32[]{:S(2)}) collective-permute-start(f32[80,128]{1,0:T(8,128)S(1)} %get-tuple-element.63.order), channel_id=1, source_target_pairs={{0,8},{8,0},{16,24},{24,16},{1,9},{9,1},{17,25},{25,17},{2,10},{10... | collective-permute-start | bytes 122888 | tf_op jit(solution)/shard_map/ppermute | solution.py:258
  68.4 3.6 %collective-permute-start.20 = (f32[80,128]{1,0:T(8,128)S(1)}, f32[80,128]{1,0:T(8,128)S(1)}, u32[]{:S(2)}, u32[]{:S(2)}) collective-permute-start(f32[80,128]{1,0:T(8,128)S(1)} %log_add_fusion.sum_a), channel_id=1, source_target_pairs={{0,24},{8,16},{16,8},{24,0},{1,25},{9,17},{17,9},{25,1},{2,26},{10... | collective-permute-start | bytes 122888 | tf_op jit(solution)/shard_map/ppermute | solution.py:258
  73.1 5.2 %collective-permute-start.24 = (f32[128,128]{1,0:T(8,128)S(1)}, f32[128,128]{1,0:T(8,128)S(1)}, u32[]{:S(2)}, u32[]{:S(2)}) collective-permute-start(f32[128,128]{1,0:T(8,128)S(1)} %get-tuple-element.65.order), channel_id=1, source_target_pairs={{0,4},{1,5},{2,3},{3,2},{4,0},{5,1},{6,7},{7,6},{8,12},{9,13},{10,... | collective-permute-start | bytes 196616 | tf_op jit(solution)/shard_map/ppermute | solution.py:278
  76.0 5.9 %collective-permute-start.21 = (f32[128,128]{1,0:T(8,128)S(1)}, f32[128,128]{1,0:T(8,128)S(1)}, u32[]{:S(2)}, u32[]{:S(2)}) collective-permute-start(f32[128,128]{1,0:T(8,128)S(1)} %get-tuple-element.67), channel_id=1, source_target_pairs={{0,4},{1,5},{2,3},{3,2},{4,0},{5,1},{6,7},{7,6},{8,12},{9,13},{10,... | collective-permute-start | bytes 196616 | tf_op jit(solution)/shard_map/ppermute | solution.py:278
  78.4 4.4 %collective-permute-start.25 = (f32[128,128]{1,0:T(8,128)S(1)}, f32[128,128]{1,0:T(8,128)S(1)}, u32[]{:S(2)}, u32[]{:S(2)}) collective-permute-start(f32[128,128]{1,0:T(8,128)S(1)} %add.94), channel_id=1, source_target_pairs={{0,1},{1,0},{2,6},{3,7},{4,5},{5,4},{6,2},{7,3},{8,9},{9,8},{10,14... | collective-permute-start | bytes 196616 | tf_op jit(solution)/shard_map/ppermute | solution.py:278
  81.9 4.3 %collective-permute-start.22 = (f32[128,128]{1,0:T(8,128)S(1)}, f32[128,128]{1,0:T(8,128)S(1)}, u32[]{:S(2)}, u32[]{:S(2)}) collective-permute-start(f32[128,128]{1,0:T(8,128)S(1)} %add.92), channel_id=1, source_target_pairs={{0,1},{1,0},{2,6},{3,7},{4,5},{5,4},{6,2},{7,3},{8,9},{9,8},{10,14... | collective-permute-start | bytes 196616 | tf_op jit(solution)/shard_map/ppermute | solution.py:278
  82.8 4.5 %collective-permute-start.26 = (f32[128,128]{1,0:T(8,128)S(1)}, f32[128,128]{1,0:T(8,128)S(1)}, u32[]{:S(2)}, u32[]{:S(2)}) collective-permute-start(f32[128,128]{1,0:T(8,128)S(1)} %add.95.refs_0_), channel_id=1, source_target_pairs={{0,2},{1,3},{2,0},{3,1},{4,6},{5,7},{6,4},{7,5},{8,10},{9,11},{10,... | collective-permute-start | bytes 196616 | tf_op jit(solution)/shard_map/ppermute | solution.py:278
  86.3 4.3 %collective-permute-start.23 = (f32[128,128]{1,0:T(8,128)S(1)}, f32[128,128]{1,0:T(8,128)S(1)}, u32[]{:S(2)}, u32[]{:S(2)}) collective-permute-start(f32[128,128]{1,0:T(8,128)S(1)} %add.93.refs_0_), channel_id=1, source_target_pairs={{0,2},{1,3},{2,0},{3,1},{4,6},{5,7},{6,4},{7,5},{8,10},{9,11},{10,... | collective-permute-start | bytes 196616 | tf_op jit(solution)/shard_map/ppermute | solution.py:278
  103.3 3.1 %collective-permute-start.29 = (f32[16,128]{1,0:T(8,128)S(1)}, f32[16,128]{1,0:T(8,128)S(1)}, u32[]{:S(2)}, u32[]{:S(2)}) collective-permute-start(f32[16,128]{1,0:T(8,128)S(1)} %fusion.5.order), channel_id=1, source_target_pairs={{0,24},{8,16},{16,8},{24,0},{1,25},{9,17},{17,9},{25,1},{2,26},{10... | collective-permute-start | bytes 24584 | tf_op jit(solution)/shard_map/ppermute | solution.py:258
  103.4 3.7 %collective-permute-start.28 = (f32[16,128]{1,0:T(8,128)S(1)}, f32[16,128]{1,0:T(8,128)S(1)}, u32[]{:S(2)}, u32[]{:S(2)}) collective-permute-start(f32[16,128]{1,0:T(8,128)S(1)} %fusion.5.order), channel_id=1, source_target_pairs={{0,16},{8,24},{16,0},{24,8},{1,17},{9,25},{17,1},{25,9},{2,18},{10... | collective-permute-start | bytes 24584 | tf_op jit(solution)/shard_map/ppermute | solution.py:258
  105.0 2.1 %collective-permute-start.27 = (f32[16,128]{1,0:T(8,128)S(1)}, f32[16,128]{1,0:T(8,128)S(1)}, u32[]{:S(2)}, u32[]{:S(2)}) collective-permute-start(f32[16,128]{1,0:T(8,128)S(1)} %fusion.5.order), channel_id=1, source_target_pairs={{0,8},{8,0},{16,24},{24,16},{1,9},{9,1},{17,25},{25,17},{2,10},{10... | collective-permute-start | bytes 24584 | tf_op jit(solution)/shard_map/ppermute | solution.py:258

commit v8 on v7

--- a/solution.py
+++ b/solution.py
@@ -90,9 +90,9 @@
         work(k)
 
 
-def merge(a, b):
-    top = jnp.maximum(a, b)
-    return top + jnp.log(jnp.exp(a - top) + jnp.exp(b - top))
+def log_sum_exp(xs):
+    top = functools.reduce(jnp.maximum, xs)
+    return top + jnp.log(functools.reduce(jnp.add, [jnp.exp(x - top) for x in xs]))
 
 
 def bring(source, first, sizes, to, sems):
@@ -184,17 +184,16 @@
         e = dose - target[...]
         excess[s][...] = e
         scores.append(SHARPNESS * e * e)
-    top = functools.reduce(jnp.maximum, scores)
-    total = functools.reduce(jnp.add, [jnp.exp(score - top) for score in scores])
-    score_sum[...] = top + jnp.log(total)
-
-
-def second_kernel(scens, whole, upper, lower, sum_a, sum_b, col_hot_t, order, *refs):
+    score_sum[...] = log_sum_exp(scores)
+
+
+def second_kernel(scens, whole, upper, lower, col_hot_t, order, *refs):
     del order
     *refs, rows = refs
     n = len(scens)
+    sums, refs = refs[: -3 * n], refs[-3 * n :]
     excess, weights, gradient = refs[:n], refs[n : 2 * n], refs[2 * n :]
-    total = merge(sum_a[...], sum_b[...])
+    total = log_sum_exp([x[...] for x in sums])
     picked = []
     for m, s in enumerate(scens):
         e = excess[m][...]
@@ -283,13 +282,8 @@
     return x, other
 
 
-def reduce_scen(x, combine):
-    steps = bits("scen")
-    x = [x, swap(x, "scen", steps[0])]
-    for bit in steps[1:]:
-        both = combine(*x)
-        x = [both, swap(both, "scen", bit ^ 1)]
-    return x
+def spread_scen(x):
+    return [x] + [swap(x, "scen", n) for n in range(1, lax.axis_size("scen"))]
 
 
 def swap_both(x, bit):
@@ -404,7 +398,7 @@
             scratch_shapes=[pltpu.VMEM((scen, slots, side), F32)],
             compiler_params=params,
         )(*flipped, fluence, target, col_hot, same)
-        sum_a, sum_b = reduce_scen(score_sum, merge)
+        score_sums = spread_scen(score_sum)
 
         groups = [[s] for s in range(scen)] if last else [list(range(scen))]
         weights, gradients, order = [], [], score_sum
@@ -414,11 +408,11 @@
                 functools.partial(second_kernel, group),
                 name="second",
                 out_shape=(dense(slots, side),) * n + (dense(beam_blocks, side),) * n,
-                in_specs=[VMEM] * (7 + n),
+                in_specs=[VMEM] * (5 + len(score_sums) + n),
                 out_specs=(VMEM,) * (2 * n),
                 scratch_shapes=[pltpu.VMEM((n, slots, side), F32)],
                 compiler_params=params,
-            )(*blocks, sum_a, sum_b, col_hot_t, order, *[excess[s] for s in group])
+            )(*blocks, col_hot_t, order, *score_sums, *[excess[s] for s in group])
             order = found[-1]
             weights += found[:n]
             gradients += found[n:]
@@ -458,8 +452,8 @@
             gradients = [gradient[s] for s in range(scen)]
         copies = [jnp.maximum(c - STEP_SIZE * g, 0.0) for c, g in zip(copies, gradients)]
         total = functools.reduce(jnp.add, copies)
+        totals = spread_scen(total)
         if last:
-            others = [swap(total, "scen", n) for n in range(1, lax.axis_size("scen"))]
             placed = pl.pallas_call(
                 functools.partial(place_kernel, scen_total),
                 name="place",
@@ -472,10 +466,7 @@
                 ),
             )(leads, total, *weights)
             weights = jnp.swapaxes(placed, 0, 1).reshape(scen, row_blocks * side)
-            total = functools.reduce(jnp.add, others, total)
-        else:
-            total = functools.reduce(jnp.add, reduce_scen(total, jnp.add))
-        fluence = total / scen_total
+        fluence = functools.reduce(jnp.add, totals) / scen_total
     return fluence.reshape(share), weights
 
 

time: 108 us -> 108 us (level)
  waiting for transfers between devices: 36.8 us -> 33.5 us
  starting transfers between devices: 33.6 us -> 36.5 us
    ppermute x18, waiting for transfers between devices: 25.4 us -> 23 us  [reduce_vox(): lax.ppermute(x, 'vox', [(v, v ^ pair[(v & steps[-2]) // steps[-2]]) for v...]
    ppermute x18, starting transfers between devices: 20.1 us -> 21.8 us  [reduce_vox(): lax.ppermute(x, 'vox', [(v, v ^ pair[(v & steps[-2]) // steps[-2]]) for v...]
    ppermute x9 -> x12, starting transfers between devices: 6.64 us -> 7.73 us  [swap(): lax.ppermute(x, axis, [(i, i ^ bit) for i in range(lax.axis_size(axis))])]
    ppermute x9 -> x12, waiting for transfers between devices: 11.4 us -> 10.5 us  [swap(): lax.ppermute(x, axis, [(i, i ^ bit) for i in range(lax.axis_size(axis))])]
  transfers between devices with their start and end apart: 30 -> 33, of which waited for: 25 -> 23; matrix products, arithmetic and copies ran while one was open for 0% -> 0% of each run, Pallas kernels for 11% -> 11%
where the time goes in v8:
time: 108 us; the launch traced here: 107 us
  starting transfers between devices  36.5 us (34%)
  waiting for transfers between devices  33.5 us (31%)
  Pallas kernels  24.3 us (22%)
  blocking collectives  10.9 us (10%)
  between operations  1.52 us (1%)
    ppermute x18, waiting for transfers between devices, reduce_vox(): lax.ppermute(x, 'vox', [(v, v ^ pair[(v & steps[-2]) // steps[-2]]) for v...  23 us
    ppermute x18, starting transfers between devices, reduce_vox(): lax.ppermute(x, 'vox', [(v, v ^ pair[(v & steps[-2]) // steps[-2]]) for v...  21.8 us
    all_to_all x1, blocking collectives, body(): lax.all_to_all(gradient, 'vox', split_axis=0, concat_axis=0, tiled=True)  10.9 us
    ppermute x12, waiting for transfers between devices, swap(): lax.ppermute(x, axis, [(i, i ^ bit) for i in range(lax.axis_size(axis))])  10.5 us
    pallas_call x3, Pallas kernels, body(): pl.pallas_call(functools.partial(third_kernel, group), name='third', out_...  8.19 us
    ppermute x12, starting transfers between devices, swap(): lax.ppermute(x, axis, [(i, i ^ bit) for i in range(lax.axis_size(axis))])  7.73 us
    ppermute x3, starting transfers between devices, swap_both(): return lax.ppermute(x, ('scen', 'vox'), pairs)  6.9 us
    pallas_call x3, Pallas kernels, body(): pl.pallas_call(functools.partial(second_kernel, group), name='second', ou...  3.97 us
  transfers between devices with their start and end apart: 33, of which 23 were waited for; matrix products, arithmetic and copies ran while one was open for 0% of the time, Pallas kernels for 11%

profile of v8, /device:TPU:0, one launch (start us, length us, event | category | flops | bytes accessed | tf_op | source)
XLA Modules:
  0.0 107.4 jit_solution(6069230765201930593)
XLA Ops:
  0.6 2.4 %collective-permute-start = (f32[16,128]{1,0:T(8,128)}, f32[16,128]{1,0:T(8,128)S(1)}, u32[]{:S(2)}, u32[]{:S(2)}) collective-permute-start(f32[16,128]{1,0:T(8,128)} %bitcast.28), channel_id=1, source_target_pairs={{0,9},{1,8},{2,11},{3,10},{4,13},{5,12},{6,15},{7,14},{8,1},{9,0},... | collective-permute-start | bytes 24584 | tf_op jit(solution)/shard_map/ppermute | solution.py:292
  3.7 1.2 %hot.1 = (bf16[80,128]{1,0:T(8,128)(2,1)S(1)}, bf16[128,80]{1,0:T(8,128)(2,1)S(1)}, bf16[80,80]{1,0:T(8,128)(2,1)S(1)}, bf16[128,80]{1,0:T(8,128)(2,1)S(1)}, f32...) custom-call(s32[2,80]{1,0:T(2,128)} %bitcast.30, f32[16,128]{1,0:T(8,128)} %bitcast.29, f32[128,128]{1,0:T(8,128)} %bitcast.27, ...), custom_call_target="tpu_custom_call" | custom-call | tf_op jit(solution)/shard_map/hot/pallas_call | solution.py:312
  5.0 1.9 %collective-permute-start.1 = (f32[32,128]{1,0:T(8,128)S(1)}, f32[32,128]{1,0:T(8,128)S(1)}, u32[]{:S(2)}, u32[]{:S(2)}) collective-permute-start(f32[32,128]{1,0:T(8,128)S(1)} %join.3.order.mine), channel_id=1, source_target_pairs={{0,10},{1,11},{2,8},{3,9},{4,14},{5,15},{6,12},{7,13},{8,2},{9,3},... | collective-permute-start | bytes 49160 | tf_op jit(solution)/shard_map/ppermute | solution.py:292
  6.9 2.6 %whole.1 = (f32[2,32,128,128]{3,2,1,0:T(8,128)S(1)}, f32[2,32,128,128]{3,2,1,0:T(8,128)S(1)}, f32[8,128]{1,0:T(8,128)S(1)}) custom-call(f32[2,80,128,128]{3,2,1,0:T(8,128)} %source.3, f32[32,128]{1,0:T(8,128)S(1)} %join.3.order.mine), custom_call_target="tpu_custom_call" | custom-call | bytes 7864320 | tf_op jit(solution)/shard_map/whole/pallas_call | solution.py:349
  9.5 2.5 %collective-permute-start.2 = (f32[64,128]{1,0:T(8,128)S(1)}, f32[64,128]{1,0:T(8,128)S(1)}, u32[]{:S(2)}, u32[]{:S(2)}) collective-permute-start(f32[64,128]{1,0:T(8,128)S(1)} %join.4.order.mine), channel_id=1, source_target_pairs={{0,12},{1,13},{2,14},{3,15},{4,8},{5,9},{6,10},{7,11},{8,4},{9,5},... | collective-permute-start | bytes 98312 | tf_op jit(solution)/shard_map/ppermute | solution.py:292
  12.1 3.6 %split.1 = (bf16[2,48,256,128]{3,2,1,0:T(8,128)(2,1)S(1)}, bf16[2,48,256,128]{3,2,1,0:T(8,128)(2,1)S(1)}, bf16[2,24,256,128]{3,2,1,0:T(8,128)(2,1)S(1)}, bf16[2,24,256,128]{3,2,1,0:T(8,128)(2,1)S(1)}) custom-call(f32[2,80,128,128]{3,2,1,0:T(8,128)} %source.3, f32[64,128]{1,0:T(8,128)S(1)} %join.4.order.mine), custom_call_target="tpu_custom_call" | custom-call | bytes 13107200 | tf_op jit(solution)/shard_map/split/pallas_call | solution.py:363
  15.7 1.9 %first.2 = (f32[80,128]{1,0:T(8,128)S(1)}, f32[80,128]{1,0:T(8,128)S(1)}, f32[80,128]{1,0:T(8,128)S(1)}) custom-call(f32[2,32,128,128]{3,2,1,0:T(8,128)S(1)} %get-tuple-element.45.whole.whole_t, bf16[2,48,256,128]{3,2,1,0:T(8,128)(2,1)S(1)} %get-tuple-element.46.upper.upper_t, bf16[2,24,256,128]{3,2,1,0:T(8,128)(2,1)S(1)} %get-tuple-element.47.lower.lower_t, ...), custom_call_target="tpu_custom_call" | custom-call | tf_op jit(solution)/shard_map/first/pallas_call | solution.py:392
  17.6 1.4 %collective-permute-start.5 = (f32[80,128]{1,0:T(8,128)S(1)}, f32[80,128]{1,0:T(8,128)S(1)}, u32[]{:S(2)}, u32[]{:S(2)}) collective-permute-start(f32[80,128]{1,0:T(8,128)S(1)} %get-tuple-element.52.order.refs_0_), channel_id=1, source_target_pairs={{0,24},{8,16},{16,8},{24,0},{1,25},{9,17},{17,9},{25,1},{2,26},{10... | collective-permute-start | bytes 122888 | tf_op jit(solution)/shard_map/ppermute | solution.py:257
  19.5 1.7 %collective-permute-done.5.refs_3_ = f32[80,128]{1,0:T(8,128)S(1)} collective-permute-done((f32[80,128]{1,0:T(8,128)S(1)}, f32[80,128]{1,0:T(8,128)S(1)}, u32[]{:S(2)}, u32[]{:S(2)}) %collective-permute-start.5) | collective-permute-done | bytes 40992 | tf_op jit(solution)/shard_map/ppermute | solution.py:257
  21.2 1.8 %collective-permute-done.4.refs_2_ = f32[80,128]{1,0:T(8,128)S(1)} collective-permute-done((f32[80,128]{1,0:T(8,128)S(1)}, f32[80,128]{1,0:T(8,128)S(1)}, u32[]{:S(2)}, u32[]{:S(2)}) %collective-permute-start.4) | collective-permute-done | bytes 40992 | tf_op jit(solution)/shard_map/ppermute | solution.py:257
  23.0 1.7 %second.3 = (f32[80,128]{1,0:T(8,128)S(1)}, f32[80,128]{1,0:T(8,128)S(1)}, f32[128,128]{1,0:T(8,128)S(1)}, f32[128,128]{1,0:T(8,128)S(1)}) custom-call(f32[2,32,128,128]{3,2,1,0:T(8,128)S(1)} %get-tuple-element.41.whole, bf16[2,48,256,128]{3,2,1,0:T(8,128)(2,1)S(1)} %get-tuple-element.43.upper, bf16[2,24,256,128]{3,2,1,0:T(8,128)(2,1)S(1)} %get-tuple-element.44.lower, ...), custom_call_target="tpu_custom_call" | custom-call | tf_op jit(solution)/shard_map/second/pallas_call | solution.py:407
  25.6 2.1 %collective-permute-start.8 = (f32[128,128]{1,0:T(8,128)S(1)}, f32[128,128]{1,0:T(8,128)S(1)}, u32[]{:S(2)}, u32[]{:S(2)}) collective-permute-start(f32[128,128]{1,0:T(8,128)S(1)} %get-tuple-element.56), channel_id=1, source_target_pairs={{0,4},{1,5},{2,3},{3,2},{4,0},{5,1},{6,7},{7,6},{8,12},{9,13},{10,... | collective-permute-start | bytes 196616 | tf_op jit(solution)/shard_map/ppermute | solution.py:277
  27.7 2.2 %collective-permute-done.6 = f32[128,128]{1,0:T(8,128)S(1)} collective-permute-done((f32[128,128]{1,0:T(8,128)S(1)}, f32[128,128]{1,0:T(8,128)S(1)}, u32[]{:S(2)}, u32[]{:S(2)}) %collective-permute-start.6) | collective-permute-done | bytes 65568 | tf_op jit(solution)/shard_map/ppermute | solution.py:277
  30.0 1.5 %collective-permute-start.7 = (f32[128,128]{1,0:T(8,128)S(1)}, f32[128,128]{1,0:T(8,128)S(1)}, u32[]{:S(2)}, u32[]{:S(2)}) collective-permute-start(f32[128,128]{1,0:T(8,128)S(1)} %add.66), channel_id=1, source_target_pairs={{0,1},{1,0},{2,6},{3,7},{4,5},{5,4},{6,2},{7,3},{8,9},{9,8},{10,14... | collective-permute-start | bytes 196616 | tf_op jit(solution)/shard_map/ppermute | solution.py:277
  31.5 2.3 %collective-permute-start.9 = (f32[128,128]{1,0:T(8,128)S(1)}, f32[128,128]{1,0:T(8,128)S(1)}, u32[]{:S(2)}, u32[]{:S(2)}) collective-permute-start(f32[128,128]{1,0:T(8,128)S(1)} %add.68), channel_id=1, source_target_pairs={{0,1},{1,0},{2,6},{3,7},{4,5},{5,4},{6,2},{7,3},{8,9},{9,8},{10,14... | collective-permute-start | bytes 196616 | tf_op jit(solution)/shard_map/ppermute | solution.py:277
  35.0 1.1 collective-permute-done.9
  36.1 1.0 collective-permute-start.11
  37.1 1.5 %collective-permute-done.10.refs_2_ = f32[128,128]{1,0:T(8,128)S(1)} collective-permute-done((f32[128,128]{1,0:T(8,128)S(1)}, f32[128,128]{1,0:T(8,128)S(1)}, u32[]{:S(2)}, u32[]{:S(2)}) %collective-permute-start.10) | collective-permute-done | bytes 65568 | tf_op jit(solution)/shard_map/ppermute | solution.py:277
  38.7 1.8 %collective-permute-done.11.refs_3_ = f32[128,128]{1,0:T(8,128)S(1)} collective-permute-done((f32[128,128]{1,0:T(8,128)S(1)}, f32[128,128]{1,0:T(8,128)S(1)}, u32[]{:S(2)}, u32[]{:S(2)}) %collective-permute-start.11) | collective-permute-done | bytes 65568 | tf_op jit(solution)/shard_map/ppermute | solution.py:277
  40.4 3.6 %third.3 = (f32[128,128]{1,0:T(8,128)S(1)}, f32[128,128]{1,0:T(8,128)S(1)}, f32[128,128]{1,0:T(8,128)S(1)}, f32[128,128]{1,0:T(8,128)S(1)}) custom-call(f32[2,32,128,128]{3,2,1,0:T(8,128)S(1)} %get-tuple-element.41.whole, bf16[2,48,256,128]{3,2,1,0:T(8,128)(2,1)S(1)} %get-tuple-element.43.upper, bf16[2,24,256,128]{3,2,1,0:T(8,128)(2,1)S(1)} %get-tuple-element.44.lower, ...), custom_call_target="tpu_custom_call" | custom-call | tf_op jit(solution)/shard_map/third/pallas_call | solution.py:426
  44.0 1.6 %collective-permute-start.12 = (f32[128,128]{1,0:T(8,128)S(1)}, f32[128,128]{1,0:T(8,128)S(1)}, u32[]{:S(2)}, u32[]{:S(2)}) collective-permute-start(f32[128,128]{1,0:T(8,128)S(1)} %get-tuple-element.60), channel_id=1, source_target_pairs={{0,4},{1,5},{2,3},{3,2},{4,0},{5,1},{6,7},{7,6},{8,12},{9,13},{10,... | collective-permute-start | bytes 196616 | tf_op jit(solution)/shard_map/ppermute | solution.py:277
  45.6 1.4 %collective-permute-start.15 = (f32[128,128]{1,0:T(8,128)S(1)}, f32[128,128]{1,0:T(8,128)S(1)}, u32[]{:S(2)}, u32[]{:S(2)}) collective-permute-start(f32[128,128]{1,0:T(8,128)S(1)} %get-tuple-element.62), channel_id=1, source_target_pairs={{0,4},{1,5},{2,3},{3,2},{4,0},{5,1},{6,7},{7,6},{8,12},{9,13},{10,... | collective-permute-start | bytes 196616 | tf_op jit(solution)/shard_map/ppermute | solution.py:277
  47.0 2.6 %collective-permute-done.12 = f32[128,128]{1,0:T(8,128)S(1)} collective-permute-done((f32[128,128]{1,0:T(8,128)S(1)}, f32[128,128]{1,0:T(8,128)S(1)}, u32[]{:S(2)}, u32[]{:S(2)}) %collective-permute-start.12) | collective-permute-done | bytes 65568 | tf_op jit(solution)/shard_map/ppermute | solution.py:277
  49.6 1.9 %collective-permute-start.13 = (f32[128,128]{1,0:T(8,128)S(1)}, f32[128,128]{1,0:T(8,128)S(1)}, u32[]{:S(2)}, u32[]{:S(2)}) collective-permute-start(f32[128,128]{1,0:T(8,128)S(1)} %add.70), channel_id=1, source_target_pairs={{0,1},{1,0},{2,6},{3,7},{4,5},{5,4},{6,2},{7,3},{8,9},{9,8},{10,14... | collective-permute-start | bytes 196616 | tf_op jit(solution)/shard_map/ppermute | solution.py:277
  52.2 1.7 %collective-permute-done.13 = f32[128,128]{1,0:T(8,128)S(1)} collective-permute-done((f32[128,128]{1,0:T(8,128)S(1)}, f32[128,128]{1,0:T(8,128)S(1)}, u32[]{:S(2)}, u32[]{:S(2)}) %collective-permute-start.13) | collective-permute-done | bytes 65568 | tf_op jit(solution)/shard_map/ppermute | solution.py:277
  54.7 1.2 %collective-permute-done.16 = f32[128,128]{1,0:T(8,128)S(1)} collective-permute-done((f32[128,128]{1,0:T(8,128)S(1)}, f32[128,128]{1,0:T(8,128)S(1)}, u32[]{:S(2)}, u32[]{:S(2)}) %collective-permute-start.16) | collective-permute-done | bytes 65568 | tf_op jit(solution)/shard_map/ppermute | solution.py:277
  56.1 2.2 %collective-permute-done.14 = f32[128,128]{1,0:T(8,128)S(1)} collective-permute-done((f32[128,128]{1,0:T(8,128)S(1)}, f32[128,128]{1,0:T(8,128)S(1)}, u32[]{:S(2)}, u32[]{:S(2)}) %collective-permute-start.14) | collective-permute-done | bytes 65568 | tf_op jit(solution)/shard_map/ppermute | solution.py:277
  58.3 1.9 %collective-permute-done.17 = f32[128,128]{1,0:T(8,128)S(1)} collective-permute-done((f32[128,128]{1,0:T(8,128)S(1)}, f32[128,128]{1,0:T(8,128)S(1)}, u32[]{:S(2)}, u32[]{:S(2)}) %collective-permute-start.17) | collective-permute-done | bytes 65568 | tf_op jit(solution)/shard_map/ppermute | solution.py:277
  61.2 0.9 collective-permute-start.18
  62.2 2.1 %collective-permute-done.20 = f32[128,128]{1,0:T(8,128)S(1)} collective-permute-done((f32[128,128]{1,0:T(8,128)S(1)}, f32[128,128]{1,0:T(8,128)S(1)}, u32[]{:S(2)}, u32[]{:S(2)}) %collective-permute-start.20) | collective-permute-done | bytes 65568 | tf_op jit(solution)/shard_map/ppermute | solution.py:257
  64.3 1.0 collective-permute-done.19
  65.3 1.9 %first.3 = (f32[80,128]{1,0:T(8,128)S(1)}, f32[80,128]{1,0:T(8,128)S(1)}, f32[80,128]{1,0:T(8,128)S(1)}) custom-call(f32[2,32,128,128]{3,2,1,0:T(8,128)S(1)} %get-tuple-element.45.whole.whole_t, bf16[2,48,256,128]{3,2,1,0:T(8,128)(2,1)S(1)} %get-tuple-element.46.upper.upper_t, bf16[2,24,256,128]{3,2,1,0:T(8,128)(2,1)S(1)} %get-tuple-element.47.lower.lower_t, ...), custom_call_target="tpu_custom_call" | custom-call | tf_op jit(solution)/shard_map/first/pallas_call | solution.py:392
  68.1 0.9 collective-permute-start.22
  69.2 1.7 %collective-permute-done.23.refs_3_ = f32[80,128]{1,0:T(8,128)S(1)} collective-permute-done((f32[80,128]{1,0:T(8,128)S(1)}, f32[80,128]{1,0:T(8,128)S(1)}, u32[]{:S(2)}, u32[]{:S(2)}) %collective-permute-start.23) | collective-permute-done | bytes 40992 | tf_op jit(solution)/shard_map/ppermute | solution.py:257
  70.8 1.3 %collective-permute-done.22.refs_2_ = f32[80,128]{1,0:T(8,128)S(1)} collective-permute-done((f32[80,128]{1,0:T(8,128)S(1)}, f32[80,128]{1,0:T(8,128)S(1)}, u32[]{:S(2)}, u32[]{:S(2)}) %collective-permute-start.22) | collective-permute-done | bytes 40992 | tf_op jit(solution)/shard_map/ppermute | solution.py:257
  72.1 1.1 %second.4 = (f32[80,128]{1,0:T(8,128)S(1)}, f32[128,128]{1,0:T(8,128)S(1)}) custom-call(f32[2,32,128,128]{3,2,1,0:T(8,128)S(1)} %get-tuple-element.41.whole, bf16[2,48,256,128]{3,2,1,0:T(8,128)(2,1)S(1)} %get-tuple-element.43.upper, bf16[2,24,256,128]{3,2,1,0:T(8,128)(2,1)S(1)} %get-tuple-element.44.lower, bf16[128,80]{1,0:T(8,128)(2,1)S(1)} %get-tuple-element.50.col_hot_t, ...), custom_call_target="tpu_custom_call" | custom-call | tf_op jit(solution)/shard_map/second/pallas_call | solution.py:407
  73.2 1.3 %collective-permute-start.27 = (f32[128,128]{1,0:T(8,128)S(1)}, f32[128,128]{1,0:T(8,128)S(1)}, u32[]{:S(2)}, u32[]{:S(2)}) collective-permute-start(f32[128,128]{1,0:T(8,128)S(1)} %get-tuple-element.65.order), channel_id=1, source_target_pairs={{0,4},{1,5},{2,3},{3,2},{4,0},{5,1},{6,7},{7,6},{8,12},{9,13},{10,... | collective-permute-start | bytes 196616 | tf_op jit(solution)/shard_map/ppermute | solution.py:277
  74.5 1.1 %second.5 = (f32[80,128]{1,0:T(8,128)S(1)}, f32[128,128]{1,0:T(8,128)S(1)}) custom-call(f32[2,32,128,128]{3,2,1,0:T(8,128)S(1)} %get-tuple-element.41.whole, bf16[2,48,256,128]{3,2,1,0:T(8,128)(2,1)S(1)} %get-tuple-element.43.upper, bf16[2,24,256,128]{3,2,1,0:T(8,128)(2,1)S(1)} %get-tuple-element.44.lower, bf16[128,80]{1,0:T(8,128)(2,1)S(1)} %get-tuple-element.50.col_hot_t, ...), custom_call_target="tpu_custom_call" | custom-call | tf_op jit(solution)/shard_map/second/pallas_call | solution.py:407
  75.6 1.8 %collective-permute-start.24 = (f32[128,128]{1,0:T(8,128)S(1)}, f32[128,128]{1,0:T(8,128)S(1)}, u32[]{:S(2)}, u32[]{:S(2)}) collective-permute-start(f32[128,128]{1,0:T(8,128)S(1)} %get-tuple-element.67), channel_id=1, source_target_pairs={{0,4},{1,5},{2,3},{3,2},{4,0},{5,1},{6,7},{7,6},{8,12},{9,13},{10,... | collective-permute-start | bytes 196616 | tf_op jit(solution)/shard_map/ppermute | solution.py:277
  77.4 1.1 collective-permute-done.27
  79.1 1.7 %collective-permute-done.24 = f32[128,128]{1,0:T(8,128)S(1)} collective-permute-done((f32[128,128]{1,0:T(8,128)S(1)}, f32[128,128]{1,0:T(8,128)S(1)}, u32[]{:S(2)}, u32[]{:S(2)}) %collective-permute-start.24) | collective-permute-done | bytes 65568 | tf_op jit(solution)/shard_map/ppermute | solution.py:277
  80.9 1.5 %collective-permute-start.25 = (f32[128,128]{1,0:T(8,128)S(1)}, f32[128,128]{1,0:T(8,128)S(1)}, u32[]{:S(2)}, u32[]{:S(2)}) collective-permute-start(f32[128,128]{1,0:T(8,128)S(1)} %add.80), channel_id=1, source_target_pairs={{0,1},{1,0},{2,6},{3,7},{4,5},{5,4},{6,2},{7,3},{8,9},{9,8},{10,14... | collective-permute-start | bytes 196616 | tf_op jit(solution)/shard_map/ppermute | solution.py:277
  83.7 1.5 %collective-permute-done.25 = f32[128,128]{1,0:T(8,128)S(1)} collective-permute-done((f32[128,128]{1,0:T(8,128)S(1)}, f32[128,128]{1,0:T(8,128)S(1)}, u32[]{:S(2)}, u32[]{:S(2)}) %collective-permute-start.25) | collective-permute-done | bytes 65568 | tf_op jit(solution)/shard_map/ppermute | solution.py:277
  86.1 1.3 %collective-permute-done.29.refs_1_ = f32[128,128]{1,0:T(8,128)S(1)} collective-permute-done((f32[128,128]{1,0:T(8,128)S(1)}, f32[128,128]{1,0:T(8,128)S(1)}, u32[]{:S(2)}, u32[]{:S(2)}) %collective-permute-start.29) | collective-permute-done | bytes 65568 | tf_op jit(solution)/shard_map/ppermute | solution.py:277
  87.4 2.3 %third.4 = (f32[16,128]{1,0:T(8,128)S(1)}, f32[128,128]{1,0:T(8,128)S(1)}) custom-call(f32[2,32,128,128]{3,2,1,0:T(8,128)S(1)} %get-tuple-element.41.whole, bf16[2,48,256,128]{3,2,1,0:T(8,128)(2,1)S(1)} %get-tuple-element.43.upper, bf16[2,24,256,128]{3,2,1,0:T(8,128)(2,1)S(1)} %get-tuple-element.44.lower, ...), custom_call_target="tpu_custom_call" | custom-call | tf_op jit(solution)/shard_map/third/pallas_call | solution.py:426
  89.8 2.3 %third.5 = (f32[16,128]{1,0:T(8,128)S(1)}, f32[8,2,16,128]{3,2,1,0:T(8,128)S(1)}) custom-call(f32[2,32,128,128]{3,2,1,0:T(8,128)S(1)} %get-tuple-element.41.whole, bf16[2,48,256,128]{3,2,1,0:T(8,128)(2,1)S(1)} %get-tuple-element.43.upper, bf16[2,24,256,128]{3,2,1,0:T(8,128)(2,1)S(1)} %get-tuple-element.44.lower, ...), custom_call_target="tpu_custom_call" | custom-call | tf_op jit(solution)/shard_map/third/pallas_call | solution.py:426
  92.1 10.9 %all_to_all.5 = f32[8,2,16,128]{3,2,1,0:T(8,128)S(1)} all-to-all(f32[8,2,16,128]{3,2,1,0:T(8,128)S(1)} %get-tuple-element.75), channel_id=1, replica_groups=mesh['scen'=4,'vox'=8] {'vox'}, dimensions={0} | all-to-all | bytes 262144 | tf_op jit(solution)/shard_map/all_to_all | solution.py:450
  103.8 1.1 collective-permute-start.30
  (51 shorter events, 12.7 us)
Async XLA Ops:
  0.6 4.3 %collective-permute-start = (f32[16,128]{1,0:T(8,128)}, f32[16,128]{1,0:T(8,128)S(1)}, u32[]{:S(2)}, u32[]{:S(2)}) collective-permute-start(f32[16,128]{1,0:T(8,128)} %bitcast.28), channel_id=1, source_target_pairs={{0,9},{1,8},{2,11},{3,10},{4,13},{5,12},{6,15},{7,14},{8,1},{9,0},... | collective-permute-start | bytes 24584 | tf_op jit(solution)/shard_map/ppermute | solution.py:292
  5.0 4.5 %collective-permute-start.1 = (f32[32,128]{1,0:T(8,128)S(1)}, f32[32,128]{1,0:T(8,128)S(1)}, u32[]{:S(2)}, u32[]{:S(2)}) collective-permute-start(f32[32,128]{1,0:T(8,128)S(1)} %join.3.order.mine), channel_id=1, source_target_pairs={{0,10},{1,11},{2,8},{3,9},{4,14},{5,15},{6,12},{7,13},{8,2},{9,3},... | collective-permute-start | bytes 49160 | tf_op jit(solution)/shard_map/ppermute | solution.py:292
  9.5 6.1 %collective-permute-start.2 = (f32[64,128]{1,0:T(8,128)S(1)}, f32[64,128]{1,0:T(8,128)S(1)}, u32[]{:S(2)}, u32[]{:S(2)}) collective-permute-start(f32[64,128]{1,0:T(8,128)S(1)} %join.4.order.mine), channel_id=1, source_target_pairs={{0,12},{1,13},{2,14},{3,15},{4,8},{5,9},{6,10},{7,11},{8,4},{9,5},... | collective-permute-start | bytes 98312 | tf_op jit(solution)/shard_map/ppermute | solution.py:292
  17.6 3.6 %collective-permute-start.5 = (f32[80,128]{1,0:T(8,128)S(1)}, f32[80,128]{1,0:T(8,128)S(1)}, u32[]{:S(2)}, u32[]{:S(2)}) collective-permute-start(f32[80,128]{1,0:T(8,128)S(1)} %get-tuple-element.52.order.refs_0_), channel_id=1, source_target_pairs={{0,24},{8,16},{16,8},{24,0},{1,25},{9,17},{17,9},{25,1},{2,26},{10... | collective-permute-start | bytes 122888 | tf_op jit(solution)/shard_map/ppermute | solution.py:257
  19.0 4.0 %collective-permute-start.4 = (f32[80,128]{1,0:T(8,128)S(1)}, f32[80,128]{1,0:T(8,128)S(1)}, u32[]{:S(2)}, u32[]{:S(2)}) collective-permute-start(f32[80,128]{1,0:T(8,128)S(1)} %get-tuple-element.52.order.refs_0_), channel_id=1, source_target_pairs={{0,16},{8,24},{16,0},{24,8},{1,17},{9,25},{17,1},{25,9},{2,18},{10... | collective-permute-start | bytes 122888 | tf_op jit(solution)/shard_map/ppermute | solution.py:257
  19.5 3.5 %collective-permute-start.3 = (f32[80,128]{1,0:T(8,128)S(1)}, f32[80,128]{1,0:T(8,128)S(1)}, u32[]{:S(2)}, u32[]{:S(2)}) collective-permute-start(f32[80,128]{1,0:T(8,128)S(1)} %get-tuple-element.52.order.refs_0_), channel_id=1, source_target_pairs={{0,8},{8,0},{16,24},{24,16},{1,9},{9,1},{17,25},{25,17},{2,10},{10... | collective-permute-start | bytes 122888 | tf_op jit(solution)/shard_map/ppermute | solution.py:257
  24.8 5.2 %collective-permute-start.6 = (f32[128,128]{1,0:T(8,128)S(1)}, f32[128,128]{1,0:T(8,128)S(1)}, u32[]{:S(2)}, u32[]{:S(2)}) collective-permute-start(f32[128,128]{1,0:T(8,128)S(1)} %get-tuple-element.55), channel_id=1, source_target_pairs={{0,4},{1,5},{2,3},{3,2},{4,0},{5,1},{6,7},{7,6},{8,12},{9,13},{10,... | collective-permute-start | bytes 196616 | tf_op jit(solution)/shard_map/ppermute | solution.py:277
  25.6 5.9 %collective-permute-start.8 = (f32[128,128]{1,0:T(8,128)S(1)}, f32[128,128]{1,0:T(8,128)S(1)}, u32[]{:S(2)}, u32[]{:S(2)}) collective-permute-start(f32[128,128]{1,0:T(8,128)S(1)} %get-tuple-element.56), channel_id=1, source_target_pairs={{0,4},{1,5},{2,3},{3,2},{4,0},{5,1},{6,7},{7,6},{8,12},{9,13},{10,... | collective-permute-start | bytes 196616 | tf_op jit(solution)/shard_map/ppermute | solution.py:277
  30.0 4.3 %collective-permute-start.7 = (f32[128,128]{1,0:T(8,128)S(1)}, f32[128,128]{1,0:T(8,128)S(1)}, u32[]{:S(2)}, u32[]{:S(2)}) collective-permute-start(f32[128,128]{1,0:T(8,128)S(1)} %add.66), channel_id=1, source_target_pairs={{0,1},{1,0},{2,6},{3,7},{4,5},{5,4},{6,2},{7,3},{8,9},{9,8},{10,14... | collective-permute-start | bytes 196616 | tf_op jit(solution)/shard_map/ppermute | solution.py:277
  31.5 4.6 %collective-permute-start.9 = (f32[128,128]{1,0:T(8,128)S(1)}, f32[128,128]{1,0:T(8,128)S(1)}, u32[]{:S(2)}, u32[]{:S(2)}) collective-permute-start(f32[128,128]{1,0:T(8,128)S(1)} %add.68), channel_id=1, source_target_pairs={{0,1},{1,0},{2,6},{3,7},{4,5},{5,4},{6,2},{7,3},{8,9},{9,8},{10,14... | collective-permute-start | bytes 196616 | tf_op jit(solution)/shard_map/ppermute | solution.py:277
  34.3 4.3 %collective-permute-start.10 = (f32[128,128]{1,0:T(8,128)S(1)}, f32[128,128]{1,0:T(8,128)S(1)}, u32[]{:S(2)}, u32[]{:S(2)}) collective-permute-start(f32[128,128]{1,0:T(8,128)S(1)} %add.67.refs_0_), channel_id=1, source_target_pairs={{0,2},{1,3},{2,0},{3,1},{4,6},{5,7},{6,4},{7,5},{8,10},{9,11},{10,... | collective-permute-start | bytes 196616 | tf_op jit(solution)/shard_map/ppermute | solution.py:277
  36.1 4.3 %collective-permute-start.11 = (f32[128,128]{1,0:T(8,128)S(1)}, f32[128,128]{1,0:T(8,128)S(1)}, u32[]{:S(2)}, u32[]{:S(2)}) collective-permute-start(f32[128,128]{1,0:T(8,128)S(1)} %add.69.refs_1_), channel_id=1, source_target_pairs={{0,2},{1,3},{2,0},{3,1},{4,6},{5,7},{6,4},{7,5},{8,10},{9,11},{10,... | collective-permute-start | bytes 196616 | tf_op jit(solution)/shard_map/ppermute | solution.py:277
  44.0 5.6 %collective-permute-start.12 = (f32[128,128]{1,0:T(8,128)S(1)}, f32[128,128]{1,0:T(8,128)S(1)}, u32[]{:S(2)}, u32[]{:S(2)}) collective-permute-start(f32[128,128]{1,0:T(8,128)S(1)} %get-tuple-element.60), channel_id=1, source_target_pairs={{0,4},{1,5},{2,3},{3,2},{4,0},{5,1},{6,7},{7,6},{8,12},{9,13},{10,... | collective-permute-start | bytes 196616 | tf_op jit(solution)/shard_map/ppermute | solution.py:277
  45.6 5.9 %collective-permute-start.15 = (f32[128,128]{1,0:T(8,128)S(1)}, f32[128,128]{1,0:T(8,128)S(1)}, u32[]{:S(2)}, u32[]{:S(2)}) collective-permute-start(f32[128,128]{1,0:T(8,128)S(1)} %get-tuple-element.62), channel_id=1, source_target_pairs={{0,4},{1,5},{2,3},{3,2},{4,0},{5,1},{6,7},{7,6},{8,12},{9,13},{10,... | collective-permute-start | bytes 196616 | tf_op jit(solution)/shard_map/ppermute | solution.py:277
  49.6 4.3 %collective-permute-start.13 = (f32[128,128]{1,0:T(8,128)S(1)}, f32[128,128]{1,0:T(8,128)S(1)}, u32[]{:S(2)}, u32[]{:S(2)}) collective-permute-start(f32[128,128]{1,0:T(8,128)S(1)} %add.70), channel_id=1, source_target_pairs={{0,1},{1,0},{2,6},{3,7},{4,5},{5,4},{6,2},{7,3},{8,9},{9,8},{10,14... | collective-permute-start | bytes 196616 | tf_op jit(solution)/shard_map/ppermute | solution.py:277
  51.5 4.3 %collective-permute-start.16 = (f32[128,128]{1,0:T(8,128)S(1)}, f32[128,128]{1,0:T(8,128)S(1)}, u32[]{:S(2)}, u32[]{:S(2)}) collective-permute-start(f32[128,128]{1,0:T(8,128)S(1)} %add.73), channel_id=1, source_target_pairs={{0,1},{1,0},{2,6},{3,7},{4,5},{5,4},{6,2},{7,3},{8,9},{9,8},{10,14... | collective-permute-start | bytes 196616 | tf_op jit(solution)/shard_map/ppermute | solution.py:277
  53.9 4.3 %collective-permute-start.14 = (f32[128,128]{1,0:T(8,128)S(1)}, f32[128,128]{1,0:T(8,128)S(1)}, u32[]{:S(2)}, u32[]{:S(2)}) collective-permute-start(f32[128,128]{1,0:T(8,128)S(1)} %add.71), channel_id=1, source_target_pairs={{0,2},{1,3},{2,0},{3,1},{4,6},{5,7},{6,4},{7,5},{8,10},{9,11},{10,... | collective-permute-start | bytes 196616 | tf_op jit(solution)/shard_map/ppermute | solution.py:277
  55.9 4.3 %collective-permute-start.17 = (f32[128,128]{1,0:T(8,128)S(1)}, f32[128,128]{1,0:T(8,128)S(1)}, u32[]{:S(2)}, u32[]{:S(2)}) collective-permute-start(f32[128,128]{1,0:T(8,128)S(1)} %add.74), channel_id=1, source_target_pairs={{0,2},{1,3},{2,0},{3,1},{4,6},{5,7},{6,4},{7,5},{8,10},{9,11},{10,... | collective-permute-start | bytes 196616 | tf_op jit(solution)/shard_map/ppermute | solution.py:277
  60.2 4.1 %collective-permute-start.20 = (f32[128,128]{1,0:T(8,128)S(1)}, f32[128,128]{1,0:T(8,128)S(1)}, u32[]{:S(2)}, u32[]{:S(2)}) collective-permute-start(f32[128,128]{1,0:T(8,128)S(1)} %maximum_add_fusion), channel_id=1, source_target_pairs={{0,24},{8,16},{16,8},{24,0},{1,25},{9,17},{17,9},{25,1},{2,26},{10... | collective-permute-start | bytes 196616 | tf_op jit(solution)/shard_map/ppermute | solution.py:257
  60.3 5.0 %collective-permute-start.19 = (f32[128,128]{1,0:T(8,128)S(1)}, f32[128,128]{1,0:T(8,128)S(1)}, u32[]{:S(2)}, u32[]{:S(2)}) collective-permute-start(f32[128,128]{1,0:T(8,128)S(1)} %maximum_add_fusion), channel_id=1, source_target_pairs={{0,16},{8,24},{16,0},{24,8},{1,17},{9,25},{17,1},{25,9},{2,18},{10... | collective-permute-start | bytes 196616 | tf_op jit(solution)/shard_map/ppermute | solution.py:257
  61.2 4.1 %collective-permute-start.18 = (f32[128,128]{1,0:T(8,128)S(1)}, f32[128,128]{1,0:T(8,128)S(1)}, u32[]{:S(2)}, u32[]{:S(2)}) collective-permute-start(f32[128,128]{1,0:T(8,128)S(1)} %maximum_add_fusion), channel_id=1, source_target_pairs={{0,8},{8,0},{16,24},{24,16},{1,9},{9,1},{17,25},{25,17},{2,10},{10... | collective-permute-start | bytes 196616 | tf_op jit(solution)/shard_map/ppermute | solution.py:257
  67.2 3.6 %collective-permute-start.23 = (f32[80,128]{1,0:T(8,128)S(1)}, f32[80,128]{1,0:T(8,128)S(1)}, u32[]{:S(2)}, u32[]{:S(2)}) collective-permute-start(f32[80,128]{1,0:T(8,128)S(1)} %get-tuple-element.63.order.refs_0_), channel_id=1, source_target_pairs={{0,24},{8,16},{16,8},{24,0},{1,25},{9,17},{17,9},{25,1},{2,26},{10... | collective-permute-start | bytes 122888 | tf_op jit(solution)/shard_map/ppermute | solution.py:257
  68.1 4.0 %collective-permute-start.22 = (f32[80,128]{1,0:T(8,128)S(1)}, f32[80,128]{1,0:T(8,128)S(1)}, u32[]{:S(2)}, u32[]{:S(2)}) collective-permute-start(f32[80,128]{1,0:T(8,128)S(1)} %get-tuple-element.63.order.refs_0_), channel_id=1, source_target_pairs={{0,16},{8,24},{16,0},{24,8},{1,17},{9,25},{17,1},{25,9},{2,18},{10... | collective-permute-start | bytes 122888 | tf_op jit(solution)/shard_map/ppermute | solution.py:257
  69.0 3.1 %collective-permute-start.21 = (f32[80,128]{1,0:T(8,128)S(1)}, f32[80,128]{1,0:T(8,128)S(1)}, u32[]{:S(2)}, u32[]{:S(2)}) collective-permute-start(f32[80,128]{1,0:T(8,128)S(1)} %get-tuple-element.63.order.refs_0_), channel_id=1, source_target_pairs={{0,8},{8,0},{16,24},{24,16},{1,9},{9,1},{17,25},{25,17},{2,10},{10... | collective-permute-start | bytes 122888 | tf_op jit(solution)/shard_map/ppermute | solution.py:257
  73.2 5.2 %collective-permute-start.27 = (f32[128,128]{1,0:T(8,128)S(1)}, f32[128,128]{1,0:T(8,128)S(1)}, u32[]{:S(2)}, u32[]{:S(2)}) collective-permute-start(f32[128,128]{1,0:T(8,128)S(1)} %get-tuple-element.65.order), channel_id=1, source_target_pairs={{0,4},{1,5},{2,3},{3,2},{4,0},{5,1},{6,7},{7,6},{8,12},{9,13},{10,... | collective-permute-start | bytes 196616 | tf_op jit(solution)/shard_map/ppermute | solution.py:277
  75.6 5.2 %collective-permute-start.24 = (f32[128,128]{1,0:T(8,128)S(1)}, f32[128,128]{1,0:T(8,128)S(1)}, u32[]{:S(2)}, u32[]{:S(2)}) collective-permute-start(f32[128,128]{1,0:T(8,128)S(1)} %get-tuple-element.67), channel_id=1, source_target_pairs={{0,4},{1,5},{2,3},{3,2},{4,0},{5,1},{6,7},{7,6},{8,12},{9,13},{10,... | collective-permute-start | bytes 196616 | tf_op jit(solution)/shard_map/ppermute | solution.py:277
  78.5 4.6 %collective-permute-start.28 = (f32[128,128]{1,0:T(8,128)S(1)}, f32[128,128]{1,0:T(8,128)S(1)}, u32[]{:S(2)}, u32[]{:S(2)}) collective-permute-start(f32[128,128]{1,0:T(8,128)S(1)} %add.82), channel_id=1, source_target_pairs={{0,1},{1,0},{2,6},{3,7},{4,5},{5,4},{6,2},{7,3},{8,9},{9,8},{10,14... | collective-permute-start | bytes 196616 | tf_op jit(solution)/shard_map/ppermute | solution.py:277
  80.9 4.3 %collective-permute-start.25 = (f32[128,128]{1,0:T(8,128)S(1)}, f32[128,128]{1,0:T(8,128)S(1)}, u32[]{:S(2)}, u32[]{:S(2)}) collective-permute-start(f32[128,128]{1,0:T(8,128)S(1)} %add.80), channel_id=1, source_target_pairs={{0,1},{1,0},{2,6},{3,7},{4,5},{5,4},{6,2},{7,3},{8,9},{9,8},{10,14... | collective-permute-start | bytes 196616 | tf_op jit(solution)/shard_map/ppermute | solution.py:277
  83.1 4.3 %collective-permute-start.29 = (f32[128,128]{1,0:T(8,128)S(1)}, f32[128,128]{1,0:T(8,128)S(1)}, u32[]{:S(2)}, u32[]{:S(2)}) collective-permute-start(f32[128,128]{1,0:T(8,128)S(1)} %add.83.refs_0_), channel_id=1, source_target_pairs={{0,2},{1,3},{2,0},{3,1},{4,6},{5,7},{6,4},{7,5},{8,10},{9,11},{10,... | collective-permute-start | bytes 196616 | tf_op jit(solution)/shard_map/ppermute | solution.py:277
  85.2 4.5 %collective-permute-start.26 = (f32[128,128]{1,0:T(8,128)S(1)}, f32[128,128]{1,0:T(8,128)S(1)}, u32[]{:S(2)}, u32[]{:S(2)}) collective-permute-start(f32[128,128]{1,0:T(8,128)S(1)} %add.81.refs_0_), channel_id=1, source_target_pairs={{0,2},{1,3},{2,0},{3,1},{4,6},{5,7},{6,4},{7,5},{8,10},{9,11},{10,... | collective-permute-start | bytes 196616 | tf_op jit(solution)/shard_map/ppermute | solution.py:277
  103.0 3.1 %collective-permute-start.32 = (f32[16,128]{1,0:T(8,128)S(1)}, f32[16,128]{1,0:T(8,128)S(1)}, u32[]{:S(2)}, u32[]{:S(2)}) collective-permute-start(f32[16,128]{1,0:T(8,128)S(1)} %fusion.3.order), channel_id=1, source_target_pairs={{0,24},{8,16},{16,8},{24,0},{1,25},{9,17},{17,9},{25,1},{2,26},{10... | collective-permute-start | bytes 24584 | tf_op jit(solution)/shard_map/ppermute | solution.py:257
  103.0 3.7 %collective-permute-start.31 = (f32[16,128]{1,0:T(8,128)S(1)}, f32[16,128]{1,0:T(8,128)S(1)}, u32[]{:S(2)}, u32[]{:S(2)}) collective-permute-start(f32[16,128]{1,0:T(8,128)S(1)} %fusion.3.order), channel_id=1, source_target_pairs={{0,16},{8,24},{16,0},{24,8},{1,17},{9,25},{17,1},{25,9},{2,18},{10... | collective-permute-start | bytes 24584 | tf_op jit(solution)/shard_map/ppermute | solution.py:257
  103.8 2.9 %collective-permute-start.30 = (f32[16,128]{1,0:T(8,128)S(1)}, f32[16,128]{1,0:T(8,128)S(1)}, u32[]{:S(2)}, u32[]{:S(2)}) collective-permute-start(f32[16,128]{1,0:T(8,128)S(1)} %fusion.3.order), channel_id=1, source_target_pairs={{0,8},{8,0},{16,24},{24,16},{1,9},{9,1},{17,25},{25,17},{2,10},{10... | collective-permute-start | bytes 24584 | tf_op jit(solution)/shard_map/ppermute | solution.py:257

commit v9 on v8

--- a/solution.py
+++ b/solution.py
@@ -104,25 +104,17 @@
         copy.start()
         copies.append((copy, range(done, done + size)))
         done += size
+    yield range(0)
     for copy, slots in copies:
         copy.wait()
         yield slots
 
 
-def whole_kernel(sizes, source, order, whole, whole_t, token, sems):
-    del order
-    token[...] = jnp.zeros_like(token)
-    for slots in bring(source, 0, sizes, whole, sems):
-        for k in slots:
-            for s in range(source.shape[0]):
-                whole_t[s, k] = whole[s, k].T
-
-
 def split_kernel(sizes, source, order, upper, upper_t, lower, lower_t, held, sems):
     del order
     scen, slots, side, _ = source.shape
-    for brought in bring(source, slots - held.shape[1], sizes, held, sems):
-        for k in brought:
+    for ready in bring(source, slots - held.shape[1], sizes, held, sems):
+        for k in ready:
             for s in range(scen):
                 block = held[s, k]
                 for x, up, low in ((block, upper, lower), (block.T, upper_t, lower_t)):
@@ -133,8 +125,8 @@
 
 
 def hot_kernel(
-    map_far, fluence, target_far, counts,
-    col_hot, col_hot_t, same, leads, target, mine, block_map, target_rows, sems
+    sizes, map_far, fluence, target_far, counts, source,
+    col_hot, col_hot_t, same, leads, target, mine, whole, whole_t, block_map, target_rows, sems
 ):
     copies = [
         pltpu.make_async_copy(x, y, sems.at[n])
@@ -144,6 +136,8 @@
     ]
     for copy in copies:
         copy.start()
+    brought = bring(source, 0, sizes, whole, sems.at[pl.ds(len(copies), len(sizes))])
+    next(brought)
     for copy in copies:
         copy.wait()
     row_blocks, slots = leads.shape
@@ -164,14 +158,26 @@
     earlier = jnp.sum(jnp.where(before, shared, 0.0), axis=0, keepdims=True)
     leads[...] = jnp.where(earlier == 0.0, row, 0.0).astype(BF16)
     target[...] = exact(row_hot, [target_rows[...]])[0]
-
-
-def join_kernel(bit, mine, other, order, joined):
-    del order
+    for ready in brought:
+        for k in ready:
+            for s in range(source.shape[0]):
+                whole_t[s, k] = whole[s, k].T
+
+
+def join_kernel(bit, mine, other, joined):
     size = mine.shape[0]
     low = lax.axis_index("vox") & bit == 0
     joined[:size] = jnp.where(low, mine[...], other[...])
     joined[size:] = jnp.where(low, other[...], mine[...])
+
+
+def collect_kernel(*refs):
+    *found, collected = refs
+    count, size = len(found), found[0].shape[0]
+    here = lax.axis_index("vox") & (count - 1)
+    for offset, piece in enumerate(found):
+        at = pl.multiple_of((here ^ offset) * size, size)
+        collected[pl.ds(at, size)] = piece[...]
 
 
 def first_kernel(whole, upper, lower, fluence, target, col_hot, same, *refs):
@@ -309,8 +315,12 @@
 
     fluence = fluence_init.reshape(share // side, side)
     half = lambda *shape: jax.ShapeDtypeStruct(shape, BF16)
-    col_hot, col_hot_t, same, leads, target, mine = pl.pallas_call(
-        hot_kernel,
+    kept = slots * 2 // 5
+    kept += (slots - kept) % 2
+    rest = slots - kept
+    sizes = split(kept, 4)
+    col_hot, col_hot_t, same, leads, target, mine, whole, whole_t = pl.pallas_call(
+        functools.partial(hot_kernel, sizes),
         name="hot",
         out_shape=(
             half(slots, beam_blocks),
@@ -319,71 +329,65 @@
             half(row_blocks, slots),
             dense(slots, side),
             dense(*fluence.shape),
+            pltpu.VMEM((scen, kept, side, side), F32),
+            pltpu.VMEM((scen, kept, side, side), F32),
         ),
-        in_specs=[FAR] * 3 + [VMEM],
-        out_specs=(VMEM,) * 6,
+        in_specs=[FAR] * 3 + [VMEM, FAR],
+        out_specs=(VMEM,) * 8,
         scratch_shapes=[
             pltpu.VMEM((2, slots), jnp.int32),
             pltpu.VMEM((row_blocks, side), F32),
-            pltpu.SemaphoreType.DMA((3,)),
+            pltpu.SemaphoreType.DMA((3 + len(sizes),)),
         ],
         compiler_params=params,
+        cost_estimate=pl.CostEstimate(flops=0, bytes_accessed=3 * passes, transcendentals=0),
     )(
         far(block_map.T),
         far(fluence),
         far(target.reshape(row_blocks, side)),
         block_counts.reshape(1, 1),
+        far(dose_blocks),
     )
 
-    kept = slots * 2 // 5
-    kept += (slots - kept) % 2
-    rest = slots - kept
-    steps = bits("vox")
-    for n, bit in enumerate(steps):
+    neighbours = min(4, parts)
+    order = fluence
+    found = [mine] + [swap_both(fluence, n) for n in range(1, neighbours)]
+    fluence = pl.pallas_call(
+        collect_kernel,
+        name="collect",
+        out_shape=dense(neighbours * mine.shape[0], side),
+        in_specs=[VMEM] * neighbours,
+        out_specs=VMEM,
+        compiler_params=params,
+    )(*found)
+    for bit in bits("vox"):
+        if bit < neighbours:
+            continue
         other = swap_both(fluence, bit)
-        if n == 0:
-            fluence = mine
-        token = fluence
-        if n == max(len(steps) - 2, 0):
-            sizes = split(kept, 4)
-            whole, whole_t, token = pl.pallas_call(
-                functools.partial(whole_kernel, sizes),
-                name="whole",
-                out_shape=(pltpu.VMEM((scen, kept, side, side), F32),) * 2 + (dense(8, 128),),
-                in_specs=[FAR, VMEM],
-                out_specs=(VMEM,) * 3,
-                scratch_shapes=[pltpu.SemaphoreType.DMA((len(sizes),))],
-                compiler_params=params,
-                cost_estimate=pl.CostEstimate(
-                    flops=0, bytes_accessed=3 * passes, transcendentals=0
-                ),
-            )(far(dose_blocks), token)
-        if n == len(steps) - 1:
-            sizes = split(rest, 6)
-            upper, upper_t, lower, lower_t = pl.pallas_call(
-                functools.partial(split_kernel, sizes),
-                name="split",
-                out_shape=(pltpu.VMEM((scen, rest, 2 * side, side), BF16),) * 2
-                + (pltpu.VMEM((scen, rest // 2, 2 * side, side), BF16),) * 2,
-                in_specs=[FAR, VMEM],
-                out_specs=(VMEM,) * 4,
-                scratch_shapes=[
-                    pltpu.VMEM((scen, rest, side, side), F32),
-                    pltpu.SemaphoreType.DMA((len(sizes),)),
-                ],
-                compiler_params=params,
-                cost_estimate=pl.CostEstimate(
-                    flops=0, bytes_accessed=5 * passes, transcendentals=0
-                ),
-            )(far(dose_blocks), fluence)
+        order = fluence
         fluence = pl.pallas_call(
             functools.partial(join_kernel, bit),
             name="join",
             out_shape=dense(2 * fluence.shape[0], side),
-            in_specs=[VMEM] * 3,
+            in_specs=[VMEM] * 2,
             out_specs=VMEM,
             compiler_params=params,
-        )(fluence, other, token)
+        )(fluence, other)
+    sizes = split(rest, 6)
+    upper, upper_t, lower, lower_t = pl.pallas_call(
+        functools.partial(split_kernel, sizes),
+        name="split",
+        out_shape=(pltpu.VMEM((scen, rest, 2 * side, side), BF16),) * 2
+        + (pltpu.VMEM((scen, rest // 2, 2 * side, side), BF16),) * 2,
+        in_specs=[FAR, VMEM],
+        out_specs=(VMEM,) * 4,
+        scratch_shapes=[
+            pltpu.VMEM((scen, rest, side, side), F32),
+            pltpu.SemaphoreType.DMA((len(sizes),)),
+        ],
+        compiler_params=params,
+        cost_estimate=pl.CostEstimate(flops=0, bytes_accessed=5 * passes, transcendentals=0),
+    )(far(dose_blocks), order)
     blocks = [near(x) for x in (whole, upper, lower)]
     flipped = [near(x) for x in (whole_t, upper_t, lower_t)]
 

time: 108 us -> 107 us (level)
  Pallas kernels: 24.3 us -> 23.1 us
    pallas_call x2, Pallas kernels: 3.81 us -> 2.72 us  [the longest x1 2.71 us: body(): pl.pallas_call(functools.partial(hot_kernel, sizes), name='hot', out_shap...]
    ppermute x3 -> x4, starting transfers between devices: 6.9 us -> 7.1 us  [swap_both(): return lax.ppermute(x, ('scen', 'vox'), pairs)]
  transfers between devices with their start and end apart: 33 -> 34, of which waited for: 23 -> 22; matrix products, arithmetic and copies ran while one was open for 0% -> 0% of each run, Pallas kernels for 11% -> 10%
where the time goes in v9:
time: 107 us
  starting transfers between devices  36.7 us (34%)
  waiting for transfers between devices  34.4 us (32%)
  Pallas kernels  23.1 us (22%)
  blocking collectives  10.7 us (10%)
  between operations  1.52 us (1%)
    ppermute x18, waiting for transfers between devices, reduce_vox(): lax.ppermute(x, 'vox', [(v, v ^ pair[(v & steps[-2]) // steps[-2]]) for v...  23.8 us
    ppermute x18, starting transfers between devices, reduce_vox(): lax.ppermute(x, 'vox', [(v, v ^ pair[(v & steps[-2]) // steps[-2]]) for v...  21.9 us
    all_to_all x1, blocking collectives, body(): lax.all_to_all(gradient, 'vox', split_axis=0, concat_axis=0, tiled=True)  10.7 us
    ppermute x12, waiting for transfers between devices, swap(): lax.ppermute(x, axis, [(i, i ^ bit) for i in range(lax.axis_size(axis))])  10.6 us
    pallas_call x3, Pallas kernels, body(): pl.pallas_call(functools.partial(third_kernel, group), name='third', out_...  8.18 us
    ppermute x12, starting transfers between devices, swap(): lax.ppermute(x, axis, [(i, i ^ bit) for i in range(lax.axis_size(axis))])  7.69 us
    ppermute x4, starting transfers between devices, swap_both(): return lax.ppermute(x, ('scen', 'vox'), pairs)  7.1 us
    pallas_call x3, Pallas kernels, body(): pl.pallas_call(functools.partial(second_kernel, group), name='second', ou...  3.97 us
  transfers between devices with their start and end apart: 34, of which 22 were waited for; matrix products, arithmetic and copies ran while one was open for 0% of the time, Pallas kernels for 10%

profile of v9, /device:TPU:0, one launch (start us, length us, event | category | flops | bytes accessed | tf_op | source)
XLA Modules:
  0.0 107.3 jit_solution(3394919577408545456)
XLA Ops:
  0.6 3.5 %collective-permute-start.2 = (f32[16,128]{1,0:T(8,128)}, f32[16,128]{1,0:T(8,128)S(1)}, u32[]{:S(2)}, u32[]{:S(2)}) collective-permute-start(f32[16,128]{1,0:T(8,128)} %bitcast.28), channel_id=1, source_target_pairs={{0,11},{1,10},{2,9},{3,8},{4,15},{5,14},{6,13},{7,12},{8,3},{9,2},... | collective-permute-start | bytes 24584 | tf_op jit(solution)/shard_map/ppermute | solution.py:298
  5.7 2.7 %hot.1 = (bf16[80,128]{1,0:T(8,128)(2,1)S(1)}, bf16[128,80]{1,0:T(8,128)(2,1)S(1)}, bf16[80,80]{1,0:T(8,128)(2,1)S(1)}, bf16[128,80]{1,0:T(8,128)(2,1)S(1)}, f32...) custom-call(s32[2,80]{1,0:T(2,128)} %bitcast.32, ...), custom_call_target="tpu_custom_call" | custom-call | bytes 7864320 | tf_op jit(solution)/shard_map/hot/pallas_call | solution.py:322
  8.4 2.7 %collective-permute-start.3 = (f32[64,128]{1,0:T(8,128)S(1)}, f32[64,128]{1,0:T(8,128)S(1)}, u32[]{:S(2)}, u32[]{:S(2)}) collective-permute-start(f32[64,128]{1,0:T(8,128)S(1)} %collect.1.order.mine), channel_id=1, source_target_pairs={{0,12},{1,13},{2,14},{3,15},{4,8},{5,9},{6,10},{7,11},{8,4},{9,5},... | collective-permute-start | bytes 98312 | tf_op jit(solution)/shard_map/ppermute | solution.py:298
  11.2 3.6 %split.1 = (bf16[2,48,256,128]{3,2,1,0:T(8,128)(2,1)S(1)}, bf16[2,48,256,128]{3,2,1,0:T(8,128)(2,1)S(1)}, bf16[2,24,256,128]{3,2,1,0:T(8,128)(2,1)S(1)}, bf16[2,24,256,128]{3,2,1,0:T(8,128)(2,1)S(1)}) custom-call(f32[2,80,128,128]{3,2,1,0:T(8,128)} %source.3, f32[64,128]{1,0:T(8,128)S(1)} %collect.1.order.mine), custom_call_target="tpu_custom_call" | custom-call | bytes 13107200 | tf_op jit(solution)/shard_map/split/pallas_call | solution.py:377
  14.8 1.9 %first.2 = (f32[80,128]{1,0:T(8,128)S(1)}, f32[80,128]{1,0:T(8,128)S(1)}, f32[80,128]{1,0:T(8,128)S(1)}) custom-call(f32[2,32,128,128]{3,2,1,0:T(8,128)S(1)} %get-tuple-element.43.whole.whole_t, bf16[2,48,256,128]{3,2,1,0:T(8,128)(2,1)S(1)} %get-tuple-element.44.upper.upper_t, bf16[2,24,256,128]{3,2,1,0:T(8,128)(2,1)S(1)} %get-tuple-element.45.lower.lower_t, ...), custom_call_target="tpu_custom_call" | custom-call | tf_op jit(solution)/shard_map/first/pallas_call | solution.py:396
  16.7 1.2 %collective-permute-start.6 = (f32[80,128]{1,0:T(8,128)S(1)}, f32[80,128]{1,0:T(8,128)S(1)}, u32[]{:S(2)}, u32[]{:S(2)}) collective-permute-start(f32[80,128]{1,0:T(8,128)S(1)} %get-tuple-element.50.order.refs_0_), channel_id=1, source_target_pairs={{0,24},{8,16},{16,8},{24,0},{1,25},{9,17},{17,9},{25,1},{2,26},{10... | collective-permute-start | bytes 122888 | tf_op jit(solution)/shard_map/ppermute | solution.py:263
  18.6 1.8 %collective-permute-done.6.refs_3_ = f32[80,128]{1,0:T(8,128)S(1)} collective-permute-done((f32[80,128]{1,0:T(8,128)S(1)}, f32[80,128]{1,0:T(8,128)S(1)}, u32[]{:S(2)}, u32[]{:S(2)}) %collective-permute-start.6) | collective-permute-done | bytes 40992 | tf_op jit(solution)/shard_map/ppermute | solution.py:263
  20.3 1.5 %collective-permute-done.5.refs_2_ = f32[80,128]{1,0:T(8,128)S(1)} collective-permute-done((f32[80,128]{1,0:T(8,128)S(1)}, f32[80,128]{1,0:T(8,128)S(1)}, u32[]{:S(2)}, u32[]{:S(2)}) %collective-permute-start.5) | collective-permute-done | bytes 40992 | tf_op jit(solution)/shard_map/ppermute | solution.py:263
  21.9 1.7 %second.3 = (f32[80,128]{1,0:T(8,128)S(1)}, f32[80,128]{1,0:T(8,128)S(1)}, f32[128,128]{1,0:T(8,128)S(1)}, f32[128,128]{1,0:T(8,128)S(1)}) custom-call(f32[2,32,128,128]{3,2,1,0:T(8,128)S(1)} %get-tuple-element.39.whole, bf16[2,48,256,128]{3,2,1,0:T(8,128)(2,1)S(1)} %get-tuple-element.41.upper, bf16[2,24,256,128]{3,2,1,0:T(8,128)(2,1)S(1)} %get-tuple-element.42.lower, ...), custom_call_target="tpu_custom_call" | custom-call | tf_op jit(solution)/shard_map/second/pallas_call | solution.py:411
  23.7 1.1 collective-permute-start.7
  24.7 1.9 %collective-permute-start.9 = (f32[128,128]{1,0:T(8,128)S(1)}, f32[128,128]{1,0:T(8,128)S(1)}, u32[]{:S(2)}, u32[]{:S(2)}) collective-permute-start(f32[128,128]{1,0:T(8,128)S(1)} %get-tuple-element.54), channel_id=1, source_target_pairs={{0,4},{1,5},{2,3},{3,2},{4,0},{5,1},{6,7},{7,6},{8,12},{9,13},{10,... | collective-permute-start | bytes 196616 | tf_op jit(solution)/shard_map/ppermute | solution.py:283
  26.6 2.2 %collective-permute-done.7 = f32[128,128]{1,0:T(8,128)S(1)} collective-permute-done((f32[128,128]{1,0:T(8,128)S(1)}, f32[128,128]{1,0:T(8,128)S(1)}, u32[]{:S(2)}, u32[]{:S(2)}) %collective-permute-start.7) | collective-permute-done | bytes 65568 | tf_op jit(solution)/shard_map/ppermute | solution.py:283
  28.9 1.7 %collective-permute-start.8 = (f32[128,128]{1,0:T(8,128)S(1)}, f32[128,128]{1,0:T(8,128)S(1)}, u32[]{:S(2)}, u32[]{:S(2)}) collective-permute-start(f32[128,128]{1,0:T(8,128)S(1)} %add.66), channel_id=1, source_target_pairs={{0,1},{1,0},{2,6},{3,7},{4,5},{5,4},{6,2},{7,3},{8,9},{9,8},{10,14... | collective-permute-start | bytes 196616 | tf_op jit(solution)/shard_map/ppermute | solution.py:283
  31.4 1.8 %collective-permute-done.8 = f32[128,128]{1,0:T(8,128)S(1)} collective-permute-done((f32[128,128]{1,0:T(8,128)S(1)}, f32[128,128]{1,0:T(8,128)S(1)}, u32[]{:S(2)}, u32[]{:S(2)}) %collective-permute-start.8) | collective-permute-done | bytes 65568 | tf_op jit(solution)/shard_map/ppermute | solution.py:283
  33.2 2.8 %collective-permute-start.11 = (f32[128,128]{1,0:T(8,128)S(1)}, f32[128,128]{1,0:T(8,128)S(1)}, u32[]{:S(2)}, u32[]{:S(2)}) collective-permute-start(f32[128,128]{1,0:T(8,128)S(1)} %add.67.refs_0_), channel_id=1, source_target_pairs={{0,2},{1,3},{2,0},{3,1},{4,6},{5,7},{6,4},{7,5},{8,10},{9,11},{10,... | collective-permute-start | bytes 196616 | tf_op jit(solution)/shard_map/ppermute | solution.py:283
  36.7 1.5 %collective-permute-done.11.refs_2_ = f32[128,128]{1,0:T(8,128)S(1)} collective-permute-done((f32[128,128]{1,0:T(8,128)S(1)}, f32[128,128]{1,0:T(8,128)S(1)}, u32[]{:S(2)}, u32[]{:S(2)}) %collective-permute-start.11) | collective-permute-done | bytes 65568 | tf_op jit(solution)/shard_map/ppermute | solution.py:283
  38.2 2.1 %collective-permute-done.12.refs_3_ = f32[128,128]{1,0:T(8,128)S(1)} collective-permute-done((f32[128,128]{1,0:T(8,128)S(1)}, f32[128,128]{1,0:T(8,128)S(1)}, u32[]{:S(2)}, u32[]{:S(2)}) %collective-permute-start.12) | collective-permute-done | bytes 65568 | tf_op jit(solution)/shard_map/ppermute | solution.py:283
  40.3 3.6 %third.3 = (f32[128,128]{1,0:T(8,128)S(1)}, f32[128,128]{1,0:T(8,128)S(1)}, f32[128,128]{1,0:T(8,128)S(1)}, f32[128,128]{1,0:T(8,128)S(1)}) custom-call(f32[2,32,128,128]{3,2,1,0:T(8,128)S(1)} %get-tuple-element.39.whole, bf16[2,48,256,128]{3,2,1,0:T(8,128)(2,1)S(1)} %get-tuple-element.41.upper, bf16[2,24,256,128]{3,2,1,0:T(8,128)(2,1)S(1)} %get-tuple-element.42.lower, ...), custom_call_target="tpu_custom_call" | custom-call | tf_op jit(solution)/shard_map/third/pallas_call | solution.py:430
  44.4 2.5 %collective-permute-start.16 = (f32[128,128]{1,0:T(8,128)S(1)}, f32[128,128]{1,0:T(8,128)S(1)}, u32[]{:S(2)}, u32[]{:S(2)}) collective-permute-start(f32[128,128]{1,0:T(8,128)S(1)} %get-tuple-element.60), channel_id=1, source_target_pairs={{0,4},{1,5},{2,3},{3,2},{4,0},{5,1},{6,7},{7,6},{8,12},{9,13},{10,... | collective-permute-start | bytes 196616 | tf_op jit(solution)/shard_map/ppermute | solution.py:283
  46.9 3.0 %collective-permute-done.13 = f32[128,128]{1,0:T(8,128)S(1)} collective-permute-done((f32[128,128]{1,0:T(8,128)S(1)}, f32[128,128]{1,0:T(8,128)S(1)}, u32[]{:S(2)}, u32[]{:S(2)}) %collective-permute-start.13) | collective-permute-done | bytes 65568 | tf_op jit(solution)/shard_map/ppermute | solution.py:283
  49.9 1.3 %collective-permute-start.14 = (f32[128,128]{1,0:T(8,128)S(1)}, f32[128,128]{1,0:T(8,128)S(1)}, u32[]{:S(2)}, u32[]{:S(2)}) collective-permute-start(f32[128,128]{1,0:T(8,128)S(1)} %add.70), channel_id=1, source_target_pairs={{0,1},{1,0},{2,6},{3,7},{4,5},{5,4},{6,2},{7,3},{8,9},{9,8},{10,14... | collective-permute-start | bytes 196616 | tf_op jit(solution)/shard_map/ppermute | solution.py:283
  51.2 0.9 collective-permute-start.17
  52.0 2.2 %collective-permute-done.14 = f32[128,128]{1,0:T(8,128)S(1)} collective-permute-done((f32[128,128]{1,0:T(8,128)S(1)}, f32[128,128]{1,0:T(8,128)S(1)}, u32[]{:S(2)}, u32[]{:S(2)}) %collective-permute-start.14) | collective-permute-done | bytes 65568 | tf_op jit(solution)/shard_map/ppermute | solution.py:283
  54.3 1.2 %collective-permute-done.17 = f32[128,128]{1,0:T(8,128)S(1)} collective-permute-done((f32[128,128]{1,0:T(8,128)S(1)}, f32[128,128]{1,0:T(8,128)S(1)}, u32[]{:S(2)}, u32[]{:S(2)}) %collective-permute-start.17) | collective-permute-done | bytes 65568 | tf_op jit(solution)/shard_map/ppermute | solution.py:283
  56.4 2.2 %collective-permute-done.15 = f32[128,128]{1,0:T(8,128)S(1)} collective-permute-done((f32[128,128]{1,0:T(8,128)S(1)}, f32[128,128]{1,0:T(8,128)S(1)}, u32[]{:S(2)}, u32[]{:S(2)}) %collective-permute-start.15) | collective-permute-done | bytes 65568 | tf_op jit(solution)/shard_map/ppermute | solution.py:283
  58.5 1.3 %collective-permute-done.18 = f32[128,128]{1,0:T(8,128)S(1)} collective-permute-done((f32[128,128]{1,0:T(8,128)S(1)}, f32[128,128]{1,0:T(8,128)S(1)}, u32[]{:S(2)}, u32[]{:S(2)}) %collective-permute-start.18) | collective-permute-done | bytes 65568 | tf_op jit(solution)/shard_map/ppermute | solution.py:283
  60.0 0.9 collective-permute-start.20
  60.9 0.9 collective-permute-start.19
  61.8 1.8 %collective-permute-done.21 = f32[128,128]{1,0:T(8,128)S(1)} collective-permute-done((f32[128,128]{1,0:T(8,128)S(1)}, f32[128,128]{1,0:T(8,128)S(1)}, u32[]{:S(2)}, u32[]{:S(2)}) %collective-permute-start.21) | collective-permute-done | bytes 65568 | tf_op jit(solution)/shard_map/ppermute | solution.py:263
  63.6 1.4 %collective-permute-done.20 = f32[128,128]{1,0:T(8,128)S(1)} collective-permute-done((f32[128,128]{1,0:T(8,128)S(1)}, f32[128,128]{1,0:T(8,128)S(1)}, u32[]{:S(2)}, u32[]{:S(2)}) %collective-permute-start.20) | collective-permute-done | bytes 65568 | tf_op jit(solution)/shard_map/ppermute | solution.py:263
  65.1 1.9 %first.3 = (f32[80,128]{1,0:T(8,128)S(1)}, f32[80,128]{1,0:T(8,128)S(1)}, f32[80,128]{1,0:T(8,128)S(1)}) custom-call(f32[2,32,128,128]{3,2,1,0:T(8,128)S(1)} %get-tuple-element.43.whole.whole_t, bf16[2,48,256,128]{3,2,1,0:T(8,128)(2,1)S(1)} %get-tuple-element.44.upper.upper_t, bf16[2,24,256,128]{3,2,1,0:T(8,128)(2,1)S(1)} %get-tuple-element.45.lower.lower_t, ...), custom_call_target="tpu_custom_call" | custom-call | tf_op jit(solution)/shard_map/first/pallas_call | solution.py:396
  67.0 1.0 collective-permute-start.24
  68.9 1.8 %collective-permute-done.24.refs_3_ = f32[80,128]{1,0:T(8,128)S(1)} collective-permute-done((f32[80,128]{1,0:T(8,128)S(1)}, f32[80,128]{1,0:T(8,128)S(1)}, u32[]{:S(2)}, u32[]{:S(2)}) %collective-permute-start.24) | collective-permute-done | bytes 40992 | tf_op jit(solution)/shard_map/ppermute | solution.py:263
  70.7 1.2 %collective-permute-done.23.refs_2_ = f32[80,128]{1,0:T(8,128)S(1)} collective-permute-done((f32[80,128]{1,0:T(8,128)S(1)}, f32[80,128]{1,0:T(8,128)S(1)}, u32[]{:S(2)}, u32[]{:S(2)}) %collective-permute-start.23) | collective-permute-done | bytes 40992 | tf_op jit(solution)/shard_map/ppermute | solution.py:263
  71.9 1.1 %second.4 = (f32[80,128]{1,0:T(8,128)S(1)}, f32[128,128]{1,0:T(8,128)S(1)}) custom-call(f32[2,32,128,128]{3,2,1,0:T(8,128)S(1)} %get-tuple-element.39.whole, bf16[2,48,256,128]{3,2,1,0:T(8,128)(2,1)S(1)} %get-tuple-element.41.upper, bf16[2,24,256,128]{3,2,1,0:T(8,128)(2,1)S(1)} %get-tuple-element.42.lower, bf16[128,80]{1,0:T(8,128)(2,1)S(1)} %get-tuple-element.48.col_hot_t, ...), custom_call_target="tpu_custom_call" | custom-call | tf_op jit(solution)/shard_map/second/pallas_call | solution.py:411
  73.1 1.2 %collective-permute-start.28 = (f32[128,128]{1,0:T(8,128)S(1)}, f32[128,128]{1,0:T(8,128)S(1)}, u32[]{:S(2)}, u32[]{:S(2)}) collective-permute-start(f32[128,128]{1,0:T(8,128)S(1)} %get-tuple-element.63.order), channel_id=1, source_target_pairs={{0,4},{1,5},{2,3},{3,2},{4,0},{5,1},{6,7},{7,6},{8,12},{9,13},{10,... | collective-permute-start | bytes 196616 | tf_op jit(solution)/shard_map/ppermute | solution.py:283
  74.2 1.1 %second.5 = (f32[80,128]{1,0:T(8,128)S(1)}, f32[128,128]{1,0:T(8,128)S(1)}) custom-call(f32[2,32,128,128]{3,2,1,0:T(8,128)S(1)} %get-tuple-element.39.whole, bf16[2,48,256,128]{3,2,1,0:T(8,128)(2,1)S(1)} %get-tuple-element.41.upper, bf16[2,24,256,128]{3,2,1,0:T(8,128)(2,1)S(1)} %get-tuple-element.42.lower, bf16[128,80]{1,0:T(8,128)(2,1)S(1)} %get-tuple-element.48.col_hot_t, ...), custom_call_target="tpu_custom_call" | custom-call | tf_op jit(solution)/shard_map/second/pallas_call | solution.py:411
  75.3 1.9 %collective-permute-start.25 = (f32[128,128]{1,0:T(8,128)S(1)}, f32[128,128]{1,0:T(8,128)S(1)}, u32[]{:S(2)}, u32[]{:S(2)}) collective-permute-start(f32[128,128]{1,0:T(8,128)S(1)} %get-tuple-element.65), channel_id=1, source_target_pairs={{0,4},{1,5},{2,3},{3,2},{4,0},{5,1},{6,7},{7,6},{8,12},{9,13},{10,... | collective-permute-start | bytes 196616 | tf_op jit(solution)/shard_map/ppermute | solution.py:283
  77.2 1.5 %collective-permute-done.28 = f32[128,128]{1,0:T(8,128)S(1)} collective-permute-done((f32[128,128]{1,0:T(8,128)S(1)}, f32[128,128]{1,0:T(8,128)S(1)}, u32[]{:S(2)}, u32[]{:S(2)}) %collective-permute-start.28) | collective-permute-done | bytes 65568 | tf_op jit(solution)/shard_map/ppermute | solution.py:283
  79.3 1.5 %collective-permute-done.25 = f32[128,128]{1,0:T(8,128)S(1)} collective-permute-done((f32[128,128]{1,0:T(8,128)S(1)}, f32[128,128]{1,0:T(8,128)S(1)}, u32[]{:S(2)}, u32[]{:S(2)}) %collective-permute-start.25) | collective-permute-done | bytes 65568 | tf_op jit(solution)/shard_map/ppermute | solution.py:283
  80.8 1.7 %collective-permute-start.26 = (f32[128,128]{1,0:T(8,128)S(1)}, f32[128,128]{1,0:T(8,128)S(1)}, u32[]{:S(2)}, u32[]{:S(2)}) collective-permute-start(f32[128,128]{1,0:T(8,128)S(1)} %add.80), channel_id=1, source_target_pairs={{0,1},{1,0},{2,6},{3,7},{4,5},{5,4},{6,2},{7,3},{8,9},{9,8},{10,14... | collective-permute-start | bytes 196616 | tf_op jit(solution)/shard_map/ppermute | solution.py:283
  84.0 1.2 %collective-permute-done.26 = f32[128,128]{1,0:T(8,128)S(1)} collective-permute-done((f32[128,128]{1,0:T(8,128)S(1)}, f32[128,128]{1,0:T(8,128)S(1)}, u32[]{:S(2)}, u32[]{:S(2)}) %collective-permute-start.26) | collective-permute-done | bytes 65568 | tf_op jit(solution)/shard_map/ppermute | solution.py:283
  85.9 1.6 %collective-permute-done.30.refs_1_ = f32[128,128]{1,0:T(8,128)S(1)} collective-permute-done((f32[128,128]{1,0:T(8,128)S(1)}, f32[128,128]{1,0:T(8,128)S(1)}, u32[]{:S(2)}, u32[]{:S(2)}) %collective-permute-start.30) | collective-permute-done | bytes 65568 | tf_op jit(solution)/shard_map/ppermute | solution.py:283
  87.4 2.3 %third.4 = (f32[16,128]{1,0:T(8,128)S(1)}, f32[128,128]{1,0:T(8,128)S(1)}) custom-call(f32[2,32,128,128]{3,2,1,0:T(8,128)S(1)} %get-tuple-element.39.whole, bf16[2,48,256,128]{3,2,1,0:T(8,128)(2,1)S(1)} %get-tuple-element.41.upper, bf16[2,24,256,128]{3,2,1,0:T(8,128)(2,1)S(1)} %get-tuple-element.42.lower, ...), custom_call_target="tpu_custom_call" | custom-call | tf_op jit(solution)/shard_map/third/pallas_call | solution.py:430
  89.7 2.3 %third.5 = (f32[16,128]{1,0:T(8,128)S(1)}, f32[8,2,16,128]{3,2,1,0:T(8,128)S(1)}) custom-call(f32[2,32,128,128]{3,2,1,0:T(8,128)S(1)} %get-tuple-element.39.whole, bf16[2,48,256,128]{3,2,1,0:T(8,128)(2,1)S(1)} %get-tuple-element.41.upper, bf16[2,24,256,128]{3,2,1,0:T(8,128)(2,1)S(1)} %get-tuple-element.42.lower, ...), custom_call_target="tpu_custom_call" | custom-call | tf_op jit(solution)/shard_map/third/pallas_call | solution.py:430
  92.1 10.7 %all_to_all.5 = f32[8,2,16,128]{3,2,1,0:T(8,128)S(1)} all-to-all(f32[8,2,16,128]{3,2,1,0:T(8,128)S(1)} %get-tuple-element.73), channel_id=1, replica_groups=mesh['scen'=4,'vox'=8] {'vox'}, dimensions={0} | all-to-all | bytes 262144 | tf_op jit(solution)/shard_map/all_to_all | solution.py:454
  102.9 1.0 collective-permute-start.32
  104.7 0.9 place.1
  (51 shorter events, 11.1 us)
Async XLA Ops:
  0.6 7.8 %collective-permute-start.2 = (f32[16,128]{1,0:T(8,128)}, f32[16,128]{1,0:T(8,128)S(1)}, u32[]{:S(2)}, u32[]{:S(2)}) collective-permute-start(f32[16,128]{1,0:T(8,128)} %bitcast.28), channel_id=1, source_target_pairs={{0,11},{1,10},{2,9},{3,8},{4,15},{5,14},{6,13},{7,12},{8,3},{9,2},... | collective-permute-start | bytes 24584 | tf_op jit(solution)/shard_map/ppermute | solution.py:298
  4.1 4.3 %collective-permute-start.1 = (f32[16,128]{1,0:T(8,128)}, f32[16,128]{1,0:T(8,128)S(1)}, u32[]{:S(2)}, u32[]{:S(2)}) collective-permute-start(f32[16,128]{1,0:T(8,128)} %bitcast.29), channel_id=1, source_target_pairs={{0,10},{1,11},{2,8},{3,9},{4,14},{5,15},{6,12},{7,13},{8,2},{9,3},... | collective-permute-start | bytes 24584 | tf_op jit(solution)/shard_map/ppermute | solution.py:298
  4.8 3.6 %collective-permute-start = (f32[16,128]{1,0:T(8,128)}, f32[16,128]{1,0:T(8,128)S(1)}, u32[]{:S(2)}, u32[]{:S(2)}) collective-permute-start(f32[16,128]{1,0:T(8,128)} %bitcast.30), channel_id=1, source_target_pairs={{0,9},{1,8},{2,11},{3,10},{4,13},{5,12},{6,15},{7,14},{8,1},{9,0},... | collective-permute-start | bytes 24584 | tf_op jit(solution)/shard_map/ppermute | solution.py:298
  8.4 6.3 %collective-permute-start.3 = (f32[64,128]{1,0:T(8,128)S(1)}, f32[64,128]{1,0:T(8,128)S(1)}, u32[]{:S(2)}, u32[]{:S(2)}) collective-permute-start(f32[64,128]{1,0:T(8,128)S(1)} %collect.1.order.mine), channel_id=1, source_target_pairs={{0,12},{1,13},{2,14},{3,15},{4,8},{5,9},{6,10},{7,11},{8,4},{9,5},... | collective-permute-start | bytes 98312 | tf_op jit(solution)/shard_map/ppermute | solution.py:298
  16.7 3.7 %collective-permute-start.6 = (f32[80,128]{1,0:T(8,128)S(1)}, f32[80,128]{1,0:T(8,128)S(1)}, u32[]{:S(2)}, u32[]{:S(2)}) collective-permute-start(f32[80,128]{1,0:T(8,128)S(1)} %get-tuple-element.50.order.refs_0_), channel_id=1, source_target_pairs={{0,24},{8,16},{16,8},{24,0},{1,25},{9,17},{17,9},{25,1},{2,26},{10... | collective-permute-start | bytes 122888 | tf_op jit(solution)/shard_map/ppermute | solution.py:263
  17.9 4.0 %collective-permute-start.5 = (f32[80,128]{1,0:T(8,128)S(1)}, f32[80,128]{1,0:T(8,128)S(1)}, u32[]{:S(2)}, u32[]{:S(2)}) collective-permute-start(f32[80,128]{1,0:T(8,128)S(1)} %get-tuple-element.50.order.refs_0_), channel_id=1, source_target_pairs={{0,16},{8,24},{16,0},{24,8},{1,17},{9,25},{17,1},{25,9},{2,18},{10... | collective-permute-start | bytes 122888 | tf_op jit(solution)/shard_map/ppermute | solution.py:263
  18.4 3.5 %collective-permute-start.4 = (f32[80,128]{1,0:T(8,128)S(1)}, f32[80,128]{1,0:T(8,128)S(1)}, u32[]{:S(2)}, u32[]{:S(2)}) collective-permute-start(f32[80,128]{1,0:T(8,128)S(1)} %get-tuple-element.50.order.refs_0_), channel_id=1, source_target_pairs={{0,8},{8,0},{16,24},{24,16},{1,9},{9,1},{17,25},{25,17},{2,10},{10... | collective-permute-start | bytes 122888 | tf_op jit(solution)/shard_map/ppermute | solution.py:263
  23.7 5.2 %collective-permute-start.7 = (f32[128,128]{1,0:T(8,128)S(1)}, f32[128,128]{1,0:T(8,128)S(1)}, u32[]{:S(2)}, u32[]{:S(2)}) collective-permute-start(f32[128,128]{1,0:T(8,128)S(1)} %get-tuple-element.53), channel_id=1, source_target_pairs={{0,4},{1,5},{2,3},{3,2},{4,0},{5,1},{6,7},{7,6},{8,12},{9,13},{10,... | collective-permute-start | bytes 196616 | tf_op jit(solution)/shard_map/ppermute | solution.py:283
  24.7 5.9 %collective-permute-start.9 = (f32[128,128]{1,0:T(8,128)S(1)}, f32[128,128]{1,0:T(8,128)S(1)}, u32[]{:S(2)}, u32[]{:S(2)}) collective-permute-start(f32[128,128]{1,0:T(8,128)S(1)} %get-tuple-element.54), channel_id=1, source_target_pairs={{0,4},{1,5},{2,3},{3,2},{4,0},{5,1},{6,7},{7,6},{8,12},{9,13},{10,... | collective-permute-start | bytes 196616 | tf_op jit(solution)/shard_map/ppermute | solution.py:283
  28.9 4.3 %collective-permute-start.8 = (f32[128,128]{1,0:T(8,128)S(1)}, f32[128,128]{1,0:T(8,128)S(1)}, u32[]{:S(2)}, u32[]{:S(2)}) collective-permute-start(f32[128,128]{1,0:T(8,128)S(1)} %add.66), channel_id=1, source_target_pairs={{0,1},{1,0},{2,6},{3,7},{4,5},{5,4},{6,2},{7,3},{8,9},{9,8},{10,14... | collective-permute-start | bytes 196616 | tf_op jit(solution)/shard_map/ppermute | solution.py:283
  30.6 5.4 %collective-permute-start.10 = (f32[128,128]{1,0:T(8,128)S(1)}, f32[128,128]{1,0:T(8,128)S(1)}, u32[]{:S(2)}, u32[]{:S(2)}) collective-permute-start(f32[128,128]{1,0:T(8,128)S(1)} %add.68), channel_id=1, source_target_pairs={{0,1},{1,0},{2,6},{3,7},{4,5},{5,4},{6,2},{7,3},{8,9},{9,8},{10,14... | collective-permute-start | bytes 196616 | tf_op jit(solution)/shard_map/ppermute | solution.py:283
  33.2 5.0 %collective-permute-start.11 = (f32[128,128]{1,0:T(8,128)S(1)}, f32[128,128]{1,0:T(8,128)S(1)}, u32[]{:S(2)}, u32[]{:S(2)}) collective-permute-start(f32[128,128]{1,0:T(8,128)S(1)} %add.67.refs_0_), channel_id=1, source_target_pairs={{0,2},{1,3},{2,0},{3,1},{4,6},{5,7},{6,4},{7,5},{8,10},{9,11},{10,... | collective-permute-start | bytes 196616 | tf_op jit(solution)/shard_map/ppermute | solution.py:283
  36.0 4.3 %collective-permute-start.12 = (f32[128,128]{1,0:T(8,128)S(1)}, f32[128,128]{1,0:T(8,128)S(1)}, u32[]{:S(2)}, u32[]{:S(2)}) collective-permute-start(f32[128,128]{1,0:T(8,128)S(1)} %add.69.refs_1_), channel_id=1, source_target_pairs={{0,2},{1,3},{2,0},{3,1},{4,6},{5,7},{6,4},{7,5},{8,10},{9,11},{10,... | collective-permute-start | bytes 196616 | tf_op jit(solution)/shard_map/ppermute | solution.py:283
  43.9 5.9 %collective-permute-start.13 = (f32[128,128]{1,0:T(8,128)S(1)}, f32[128,128]{1,0:T(8,128)S(1)}, u32[]{:S(2)}, u32[]{:S(2)}) collective-permute-start(f32[128,128]{1,0:T(8,128)S(1)} %get-tuple-element.58), channel_id=1, source_target_pairs={{0,4},{1,5},{2,3},{3,2},{4,0},{5,1},{6,7},{7,6},{8,12},{9,13},{10,... | collective-permute-start | bytes 196616 | tf_op jit(solution)/shard_map/ppermute | solution.py:283
  44.4 6.7 %collective-permute-start.16 = (f32[128,128]{1,0:T(8,128)S(1)}, f32[128,128]{1,0:T(8,128)S(1)}, u32[]{:S(2)}, u32[]{:S(2)}) collective-permute-start(f32[128,128]{1,0:T(8,128)S(1)} %get-tuple-element.60), channel_id=1, source_target_pairs={{0,4},{1,5},{2,3},{3,2},{4,0},{5,1},{6,7},{7,6},{8,12},{9,13},{10,... | collective-permute-start | bytes 196616 | tf_op jit(solution)/shard_map/ppermute | solution.py:283
  49.9 4.3 %collective-permute-start.14 = (f32[128,128]{1,0:T(8,128)S(1)}, f32[128,128]{1,0:T(8,128)S(1)}, u32[]{:S(2)}, u32[]{:S(2)}) collective-permute-start(f32[128,128]{1,0:T(8,128)S(1)} %add.70), channel_id=1, source_target_pairs={{0,1},{1,0},{2,6},{3,7},{4,5},{5,4},{6,2},{7,3},{8,9},{9,8},{10,14... | collective-permute-start | bytes 196616 | tf_op jit(solution)/shard_map/ppermute | solution.py:283
  51.2 4.3 %collective-permute-start.17 = (f32[128,128]{1,0:T(8,128)S(1)}, f32[128,128]{1,0:T(8,128)S(1)}, u32[]{:S(2)}, u32[]{:S(2)}) collective-permute-start(f32[128,128]{1,0:T(8,128)S(1)} %add.73), channel_id=1, source_target_pairs={{0,1},{1,0},{2,6},{3,7},{4,5},{5,4},{6,2},{7,3},{8,9},{9,8},{10,14... | collective-permute-start | bytes 196616 | tf_op jit(solution)/shard_map/ppermute | solution.py:283
  54.2 4.3 %collective-permute-start.15 = (f32[128,128]{1,0:T(8,128)S(1)}, f32[128,128]{1,0:T(8,128)S(1)}, u32[]{:S(2)}, u32[]{:S(2)}) collective-permute-start(f32[128,128]{1,0:T(8,128)S(1)} %add.71), channel_id=1, source_target_pairs={{0,2},{1,3},{2,0},{3,1},{4,6},{5,7},{6,4},{7,5},{8,10},{9,11},{10,... | collective-permute-start | bytes 196616 | tf_op jit(solution)/shard_map/ppermute | solution.py:283
  55.5 4.3 %collective-permute-start.18 = (f32[128,128]{1,0:T(8,128)S(1)}, f32[128,128]{1,0:T(8,128)S(1)}, u32[]{:S(2)}, u32[]{:S(2)}) collective-permute-start(f32[128,128]{1,0:T(8,128)S(1)} %add.74), channel_id=1, source_target_pairs={{0,2},{1,3},{2,0},{3,1},{4,6},{5,7},{6,4},{7,5},{8,10},{9,11},{10,... | collective-permute-start | bytes 196616 | tf_op jit(solution)/shard_map/ppermute | solution.py:283
  59.9 3.8 %collective-permute-start.21 = (f32[128,128]{1,0:T(8,128)S(1)}, f32[128,128]{1,0:T(8,128)S(1)}, u32[]{:S(2)}, u32[]{:S(2)}) collective-permute-start(f32[128,128]{1,0:T(8,128)S(1)} %maximum_add_fusion), channel_id=1, source_target_pairs={{0,24},{8,16},{16,8},{24,0},{1,25},{9,17},{17,9},{25,1},{2,26},{10... | collective-permute-start | bytes 196616 | tf_op jit(solution)/shard_map/ppermute | solution.py:263
  60.0 5.1 %collective-permute-start.20 = (f32[128,128]{1,0:T(8,128)S(1)}, f32[128,128]{1,0:T(8,128)S(1)}, u32[]{:S(2)}, u32[]{:S(2)}) collective-permute-start(f32[128,128]{1,0:T(8,128)S(1)} %maximum_add_fusion), channel_id=1, source_target_pairs={{0,16},{8,24},{16,0},{24,8},{1,17},{9,25},{17,1},{25,9},{2,18},{10... | collective-permute-start | bytes 196616 | tf_op jit(solution)/shard_map/ppermute | solution.py:263
  60.9 4.2 %collective-permute-start.19 = (f32[128,128]{1,0:T(8,128)S(1)}, f32[128,128]{1,0:T(8,128)S(1)}, u32[]{:S(2)}, u32[]{:S(2)}) collective-permute-start(f32[128,128]{1,0:T(8,128)S(1)} %maximum_add_fusion), channel_id=1, source_target_pairs={{0,8},{8,0},{16,24},{24,16},{1,9},{9,1},{17,25},{25,17},{2,10},{10... | collective-permute-start | bytes 196616 | tf_op jit(solution)/shard_map/ppermute | solution.py:263
  67.0 3.7 %collective-permute-start.24 = (f32[80,128]{1,0:T(8,128)S(1)}, f32[80,128]{1,0:T(8,128)S(1)}, u32[]{:S(2)}, u32[]{:S(2)}) collective-permute-start(f32[80,128]{1,0:T(8,128)S(1)} %get-tuple-element.61.order.refs_0_), channel_id=1, source_target_pairs={{0,24},{8,16},{16,8},{24,0},{1,25},{9,17},{17,9},{25,1},{2,26},{10... | collective-permute-start | bytes 122888 | tf_op jit(solution)/shard_map/ppermute | solution.py:263
  67.9 4.0 %collective-permute-start.23 = (f32[80,128]{1,0:T(8,128)S(1)}, f32[80,128]{1,0:T(8,128)S(1)}, u32[]{:S(2)}, u32[]{:S(2)}) collective-permute-start(f32[80,128]{1,0:T(8,128)S(1)} %get-tuple-element.61.order.refs_0_), channel_id=1, source_target_pairs={{0,16},{8,24},{16,0},{24,8},{1,17},{9,25},{17,1},{25,9},{2,18},{10... | collective-permute-start | bytes 122888 | tf_op jit(solution)/shard_map/ppermute | solution.py:263
  68.7 3.3 %collective-permute-start.22 = (f32[80,128]{1,0:T(8,128)S(1)}, f32[80,128]{1,0:T(8,128)S(1)}, u32[]{:S(2)}, u32[]{:S(2)}) collective-permute-start(f32[80,128]{1,0:T(8,128)S(1)} %get-tuple-element.61.order.refs_0_), channel_id=1, source_target_pairs={{0,8},{8,0},{16,24},{24,16},{1,9},{9,1},{17,25},{25,17},{2,10},{10... | collective-permute-start | bytes 122888 | tf_op jit(solution)/shard_map/ppermute | solution.py:263
  73.1 5.7 %collective-permute-start.28 = (f32[128,128]{1,0:T(8,128)S(1)}, f32[128,128]{1,0:T(8,128)S(1)}, u32[]{:S(2)}, u32[]{:S(2)}) collective-permute-start(f32[128,128]{1,0:T(8,128)S(1)} %get-tuple-element.63.order), channel_id=1, source_target_pairs={{0,4},{1,5},{2,3},{3,2},{4,0},{5,1},{6,7},{7,6},{8,12},{9,13},{10,... | collective-permute-start | bytes 196616 | tf_op jit(solution)/shard_map/ppermute | solution.py:283
  75.3 5.4 %collective-permute-start.25 = (f32[128,128]{1,0:T(8,128)S(1)}, f32[128,128]{1,0:T(8,128)S(1)}, u32[]{:S(2)}, u32[]{:S(2)}) collective-permute-start(f32[128,128]{1,0:T(8,128)S(1)} %get-tuple-element.65), channel_id=1, source_target_pairs={{0,4},{1,5},{2,3},{3,2},{4,0},{5,1},{6,7},{7,6},{8,12},{9,13},{10,... | collective-permute-start | bytes 196616 | tf_op jit(solution)/shard_map/ppermute | solution.py:283
  78.7 4.3 %collective-permute-start.29 = (f32[128,128]{1,0:T(8,128)S(1)}, f32[128,128]{1,0:T(8,128)S(1)}, u32[]{:S(2)}, u32[]{:S(2)}) collective-permute-start(f32[128,128]{1,0:T(8,128)S(1)} %add.82), channel_id=1, source_target_pairs={{0,1},{1,0},{2,6},{3,7},{4,5},{5,4},{6,2},{7,3},{8,9},{9,8},{10,14... | collective-permute-start | bytes 196616 | tf_op jit(solution)/shard_map/ppermute | solution.py:283
  80.8 4.3 %collective-permute-start.26 = (f32[128,128]{1,0:T(8,128)S(1)}, f32[128,128]{1,0:T(8,128)S(1)}, u32[]{:S(2)}, u32[]{:S(2)}) collective-permute-start(f32[128,128]{1,0:T(8,128)S(1)} %add.80), channel_id=1, source_target_pairs={{0,1},{1,0},{2,6},{3,7},{4,5},{5,4},{6,2},{7,3},{8,9},{9,8},{10,14... | collective-permute-start | bytes 196616 | tf_op jit(solution)/shard_map/ppermute | solution.py:283
  83.1 4.3 %collective-permute-start.30 = (f32[128,128]{1,0:T(8,128)S(1)}, f32[128,128]{1,0:T(8,128)S(1)}, u32[]{:S(2)}, u32[]{:S(2)}) collective-permute-start(f32[128,128]{1,0:T(8,128)S(1)} %add.83.refs_0_), channel_id=1, source_target_pairs={{0,2},{1,3},{2,0},{3,1},{4,6},{5,7},{6,4},{7,5},{8,10},{9,11},{10,... | collective-permute-start | bytes 196616 | tf_op jit(solution)/shard_map/ppermute | solution.py:283
  85.1 4.6 %collective-permute-start.27 = (f32[128,128]{1,0:T(8,128)S(1)}, f32[128,128]{1,0:T(8,128)S(1)}, u32[]{:S(2)}, u32[]{:S(2)}) collective-permute-start(f32[128,128]{1,0:T(8,128)S(1)} %add.81.refs_0_), channel_id=1, source_target_pairs={{0,2},{1,3},{2,0},{3,1},{4,6},{5,7},{6,4},{7,5},{8,10},{9,11},{10,... | collective-permute-start | bytes 196616 | tf_op jit(solution)/shard_map/ppermute | solution.py:283
  102.8 3.1 %collective-permute-start.33 = (f32[16,128]{1,0:T(8,128)S(1)}, f32[16,128]{1,0:T(8,128)S(1)}, u32[]{:S(2)}, u32[]{:S(2)}) collective-permute-start(f32[16,128]{1,0:T(8,128)S(1)} %fusion.3.order), channel_id=1, source_target_pairs={{0,24},{8,16},{16,8},{24,0},{1,25},{9,17},{17,9},{25,1},{2,26},{10... | collective-permute-start | bytes 24584 | tf_op jit(solution)/shard_map/ppermute | solution.py:263
  102.9 3.8 %collective-permute-start.32 = (f32[16,128]{1,0:T(8,128)S(1)}, f32[16,128]{1,0:T(8,128)S(1)}, u32[]{:S(2)}, u32[]{:S(2)}) collective-permute-start(f32[16,128]{1,0:T(8,128)S(1)} %fusion.3.order), channel_id=1, source_target_pairs={{0,16},{8,24},{16,0},{24,8},{1,17},{9,25},{17,1},{25,9},{2,18},{10... | collective-permute-start | bytes 24584 | tf_op jit(solution)/shard_map/ppermute | solution.py:263
  103.9 2.8 %collective-permute-start.31 = (f32[16,128]{1,0:T(8,128)S(1)}, f32[16,128]{1,0:T(8,128)S(1)}, u32[]{:S(2)}, u32[]{:S(2)}) collective-permute-start(f32[16,128]{1,0:T(8,128)S(1)} %fusion.3.order), channel_id=1, source_target_pairs={{0,8},{8,0},{16,24},{24,16},{1,9},{9,1},{17,25},{25,17},{2,10},{10... | collective-permute-start | bytes 24584 | tf_op jit(solution)/shard_map/ppermute | solution.py:263

commit v10 on v9

--- a/solution.py
+++ b/solution.py
@@ -286,6 +286,15 @@
             [(v, v ^ pair[(v & steps[-2]) // steps[-2]]) for v in range(lax.axis_size("vox"))],
         )
     return x, other
+
+
+def reduce_scen(x, combine):
+    steps = bits("scen")
+    x = [x, swap(x, "scen", steps[0])]
+    for bit in steps[1:]:
+        both = combine(x)
+        x = [both, swap(both, "scen", bit ^ 1)]
+    return x
 
 
 def spread_scen(x):
@@ -421,6 +430,7 @@
             weights += found[:n]
             gradients += found[n:]
         sums = [reduce_vox(gradient) for gradient in gradients]
+        groups = [[s] for s in range(scen)]
         copies, gradients = [], []
         for group in groups:
             n = len(group)
@@ -456,7 +466,7 @@
             gradients = [gradient[s] for s in range(scen)]
         copies = [jnp.maximum(c - STEP_SIZE * g, 0.0) for c, g in zip(copies, gradients)]
         total = functools.reduce(jnp.add, copies)
-        totals = spread_scen(total)
+        totals = spread_scen(total) if last else reduce_scen(total, sum)
         if last:
             placed = pl.pallas_call(
                 functools.partial(place_kernel, scen_total),

time: 107 us -> 107 us (level)
  waiting for transfers between devices: 34.4 us -> 29.3 us
  starting transfers between devices: 36.7 us -> 40.2 us
  Pallas kernels: 23.1 us -> 24.3 us
    ppermute x18, waiting for transfers between devices: 23.8 us -> 17.6 us  [reduce_vox(): lax.ppermute(x, 'vox', [(v, v ^ pair[(v & steps[-2]) // steps[-2]]) for v...]
    ppermute x18, starting transfers between devices: 21.9 us -> 26.1 us  [reduce_vox(): lax.ppermute(x, 'vox', [(v, v ^ pair[(v & steps[-2]) // steps[-2]]) for v...]
    pallas_call x3 -> x4, Pallas kernels: 8.18 us -> 9.36 us  [body(): pl.pallas_call(functools.partial(third_kernel, group), name='third', out_...]
    ppermute x12 -> x11, waiting for transfers between devices: 10.6 us -> 11.7 us  [swap(): lax.ppermute(x, axis, [(i, i ^ bit) for i in range(lax.axis_size(axis))])]
    ppermute x12 -> x11, starting transfers between devices: 7.69 us -> 7.08 us  [swap(): lax.ppermute(x, axis, [(i, i ^ bit) for i in range(lax.axis_size(axis))])]
  transfers between devices with their start and end apart: 34 -> 33, of which waited for: 22 -> 22; matrix products, arithmetic and copies ran while one was open for 0% -> 0% of each run, Pallas kernels for 10% -> 14%
where the time goes in v10:
time: 107 us; the launch traced here: 106 us
  starting transfers between devices  40.2 us (38%)
  waiting for transfers between devices  29.3 us (27%)
  Pallas kernels  24.3 us (23%)
  blocking collectives  10.3 us (10%)
  between operations  1.51 us (1%)
    ppermute x18, starting transfers between devices, reduce_vox(): lax.ppermute(x, 'vox', [(v, v ^ pair[(v & steps[-2]) // steps[-2]]) for v...  26.1 us
    ppermute x18, waiting for transfers between devices, reduce_vox(): lax.ppermute(x, 'vox', [(v, v ^ pair[(v & steps[-2]) // steps[-2]]) for v...  17.6 us
    ppermute x11, waiting for transfers between devices, swap(): lax.ppermute(x, axis, [(i, i ^ bit) for i in range(lax.axis_size(axis))])  11.7 us
    all_to_all x1, blocking collectives, body(): lax.all_to_all(gradient, 'vox', split_axis=0, concat_axis=0, tiled=True)  10.3 us
    pallas_call x4, Pallas kernels, body(): pl.pallas_call(functools.partial(third_kernel, group), name='third', out_...  9.36 us
    ppermute x4, starting transfers between devices, swap_both(): return lax.ppermute(x, ('scen', 'vox'), pairs)  7.1 us
    ppermute x11, starting transfers between devices, swap(): lax.ppermute(x, axis, [(i, i ^ bit) for i in range(lax.axis_size(axis))])  7.08 us
    pallas_call x3, Pallas kernels, body(): pl.pallas_call(functools.partial(second_kernel, group), name='second', ou...  3.97 us
  transfers between devices with their start and end apart: 33, of which 22 were waited for; matrix products, arithmetic and copies ran while one was open for 0% of the time, Pallas kernels for 14%

profile of v10, /device:TPU:0, one launch (start us, length us, event | category | flops | bytes accessed | tf_op | source)
XLA Modules:
  0.0 106.4 jit_solution(15249620519543337607)
XLA Ops:
  0.6 3.5 %collective-permute-start.2 = (f32[16,128]{1,0:T(8,128)}, f32[16,128]{1,0:T(8,128)S(1)}, u32[]{:S(2)}, u32[]{:S(2)}) collective-permute-start(f32[16,128]{1,0:T(8,128)} %bitcast.28), channel_id=1, source_target_pairs={{0,11},{1,10},{2,9},{3,8},{4,15},{5,14},{6,13},{7,12},{8,3},{9,2},... | collective-permute-start | bytes 24584 | tf_op jit(solution)/shard_map/ppermute | solution.py:307
  5.7 2.7 %hot.1 = (bf16[80,128]{1,0:T(8,128)(2,1)S(1)}, bf16[128,80]{1,0:T(8,128)(2,1)S(1)}, bf16[80,80]{1,0:T(8,128)(2,1)S(1)}, bf16[128,80]{1,0:T(8,128)(2,1)S(1)}, f32...) custom-call(s32[2,80]{1,0:T(2,128)} %bitcast.32, ...), custom_call_target="tpu_custom_call" | custom-call | bytes 7864320 | tf_op jit(solution)/shard_map/hot/pallas_call | solution.py:331
  8.4 2.7 %collective-permute-start.3 = (f32[64,128]{1,0:T(8,128)S(1)}, f32[64,128]{1,0:T(8,128)S(1)}, u32[]{:S(2)}, u32[]{:S(2)}) collective-permute-start(f32[64,128]{1,0:T(8,128)S(1)} %collect.1.order.mine), channel_id=1, source_target_pairs={{0,12},{1,13},{2,14},{3,15},{4,8},{5,9},{6,10},{7,11},{8,4},{9,5},... | collective-permute-start | bytes 98312 | tf_op jit(solution)/shard_map/ppermute | solution.py:307
  11.2 3.6 %split.1 = (bf16[2,48,256,128]{3,2,1,0:T(8,128)(2,1)S(1)}, bf16[2,48,256,128]{3,2,1,0:T(8,128)(2,1)S(1)}, bf16[2,24,256,128]{3,2,1,0:T(8,128)(2,1)S(1)}, bf16[2,24,256,128]{3,2,1,0:T(8,128)(2,1)S(1)}) custom-call(f32[2,80,128,128]{3,2,1,0:T(8,128)} %source.3, f32[64,128]{1,0:T(8,128)S(1)} %collect.1.order.mine), custom_call_target="tpu_custom_call" | custom-call | bytes 13107200 | tf_op jit(solution)/shard_map/split/pallas_call | solution.py:386
  14.8 1.9 %first.2 = (f32[80,128]{1,0:T(8,128)S(1)}, f32[80,128]{1,0:T(8,128)S(1)}, f32[80,128]{1,0:T(8,128)S(1)}) custom-call(f32[2,32,128,128]{3,2,1,0:T(8,128)S(1)} %get-tuple-element.43.whole.whole_t, bf16[2,48,256,128]{3,2,1,0:T(8,128)(2,1)S(1)} %get-tuple-element.44.upper.upper_t, bf16[2,24,256,128]{3,2,1,0:T(8,128)(2,1)S(1)} %get-tuple-element.45.lower.lower_t, ...), custom_call_target="tpu_custom_call" | custom-call | tf_op jit(solution)/shard_map/first/pallas_call | solution.py:405
  16.7 1.2 %collective-permute-start.6 = (f32[80,128]{1,0:T(8,128)S(1)}, f32[80,128]{1,0:T(8,128)S(1)}, u32[]{:S(2)}, u32[]{:S(2)}) collective-permute-start(f32[80,128]{1,0:T(8,128)S(1)} %get-tuple-element.50.order.refs_0_), channel_id=1, source_target_pairs={{0,24},{8,16},{16,8},{24,0},{1,25},{9,17},{17,9},{25,1},{2,26},{10... | collective-permute-start | bytes 122888 | tf_op jit(solution)/shard_map/ppermute | solution.py:263
  18.6 1.8 %collective-permute-done.6.refs_3_ = f32[80,128]{1,0:T(8,128)S(1)} collective-permute-done((f32[80,128]{1,0:T(8,128)S(1)}, f32[80,128]{1,0:T(8,128)S(1)}, u32[]{:S(2)}, u32[]{:S(2)}) %collective-permute-start.6) | collective-permute-done | bytes 40992 | tf_op jit(solution)/shard_map/ppermute | solution.py:263
  20.3 1.5 %collective-permute-done.5.refs_2_ = f32[80,128]{1,0:T(8,128)S(1)} collective-permute-done((f32[80,128]{1,0:T(8,128)S(1)}, f32[80,128]{1,0:T(8,128)S(1)}, u32[]{:S(2)}, u32[]{:S(2)}) %collective-permute-start.5) | collective-permute-done | bytes 40992 | tf_op jit(solution)/shard_map/ppermute | solution.py:263
  21.9 1.7 %second.3 = (f32[80,128]{1,0:T(8,128)S(1)}, f32[80,128]{1,0:T(8,128)S(1)}, f32[128,128]{1,0:T(8,128)S(1)}, f32[128,128]{1,0:T(8,128)S(1)}) custom-call(f32[2,32,128,128]{3,2,1,0:T(8,128)S(1)} %get-tuple-element.39.whole, bf16[2,48,256,128]{3,2,1,0:T(8,128)(2,1)S(1)} %get-tuple-element.41.upper, bf16[2,24,256,128]{3,2,1,0:T(8,128)(2,1)S(1)} %get-tuple-element.42.lower, ...), custom_call_target="tpu_custom_call" | custom-call | tf_op jit(solution)/shard_map/second/pallas_call | solution.py:420
  23.7 1.1 collective-permute-start.7
  24.7 1.9 %collective-permute-start.13 = (f32[128,128]{1,0:T(8,128)S(1)}, f32[128,128]{1,0:T(8,128)S(1)}, u32[]{:S(2)}, u32[]{:S(2)}) collective-permute-start(f32[128,128]{1,0:T(8,128)S(1)} %get-tuple-element.57), channel_id=1, source_target_pairs={{0,4},{1,5},{2,3},{3,2},{4,0},{5,1},{6,7},{7,6},{8,12},{9,13},{10,... | collective-permute-start | bytes 196616 | tf_op jit(solution)/shard_map/ppermute | solution.py:283
  26.6 2.2 %collective-permute-done.7 = f32[128,128]{1,0:T(8,128)S(1)} collective-permute-done((f32[128,128]{1,0:T(8,128)S(1)}, f32[128,128]{1,0:T(8,128)S(1)}, u32[]{:S(2)}, u32[]{:S(2)}) %collective-permute-start.7) | collective-permute-done | bytes 65568 | tf_op jit(solution)/shard_map/ppermute | solution.py:283
  28.9 1.7 %collective-permute-start.8 = (f32[128,128]{1,0:T(8,128)S(1)}, f32[128,128]{1,0:T(8,128)S(1)}, u32[]{:S(2)}, u32[]{:S(2)}) collective-permute-start(f32[128,128]{1,0:T(8,128)S(1)} %add.63), channel_id=1, source_target_pairs={{0,1},{1,0},{2,6},{3,7},{4,5},{5,4},{6,2},{7,3},{8,9},{9,8},{10,14... | collective-permute-start | bytes 196616 | tf_op jit(solution)/shard_map/ppermute | solution.py:283
  30.6 0.8 collective-permute-start.14
  31.4 1.8 %collective-permute-done.8 = f32[128,128]{1,0:T(8,128)S(1)} collective-permute-done((f32[128,128]{1,0:T(8,128)S(1)}, f32[128,128]{1,0:T(8,128)S(1)}, u32[]{:S(2)}, u32[]{:S(2)}) %collective-permute-start.8) | collective-permute-done | bytes 65568 | tf_op jit(solution)/shard_map/ppermute | solution.py:283
  33.2 2.8 %collective-permute-start.9 = (f32[128,128]{1,0:T(8,128)S(1)}, f32[128,128]{1,0:T(8,128)S(1)}, u32[]{:S(2)}, u32[]{:S(2)}) collective-permute-start(f32[128,128]{1,0:T(8,128)S(1)} %add.64.refs_0_), channel_id=1, source_target_pairs={{0,2},{1,3},{2,0},{3,1},{4,6},{5,7},{6,4},{7,5},{8,10},{9,11},{10,... | collective-permute-start | bytes 196616 | tf_op jit(solution)/shard_map/ppermute | solution.py:283
  36.7 1.5 %collective-permute-done.9.refs_1_ = f32[128,128]{1,0:T(8,128)S(1)} collective-permute-done((f32[128,128]{1,0:T(8,128)S(1)}, f32[128,128]{1,0:T(8,128)S(1)}, u32[]{:S(2)}, u32[]{:S(2)}) %collective-permute-start.9) | collective-permute-done | bytes 65568 | tf_op jit(solution)/shard_map/ppermute | solution.py:283
  38.2 2.3 %third.4 = (f32[128,128]{1,0:T(8,128)S(1)}, f32[128,128]{1,0:T(8,128)S(1)}) custom-call(f32[2,32,128,128]{3,2,1,0:T(8,128)S(1)} %get-tuple-element.39.whole, bf16[2,48,256,128]{3,2,1,0:T(8,128)(2,1)S(1)} %get-tuple-element.41.upper, bf16[2,24,256,128]{3,2,1,0:T(8,128)(2,1)S(1)} %get-tuple-element.42.lower, ...), custom_call_target="tpu_custom_call" | custom-call | tf_op jit(solution)/shard_map/third/pallas_call | solution.py:440
  40.6 1.1 %collective-permute-start.10 = (f32[128,128]{1,0:T(8,128)S(1)}, f32[128,128]{1,0:T(8,128)S(1)}, u32[]{:S(2)}, u32[]{:S(2)}) collective-permute-start(f32[128,128]{1,0:T(8,128)S(1)} %get-tuple-element.56), channel_id=1, source_target_pairs={{0,4},{1,5},{2,3},{3,2},{4,0},{5,1},{6,7},{7,6},{8,12},{9,13},{10,... | collective-permute-start | bytes 196616 | tf_op jit(solution)/shard_map/ppermute | solution.py:283
  41.6 2.4 %third.5 = (f32[128,128]{1,0:T(8,128)S(1)}, f32[128,128]{1,0:T(8,128)S(1)}) custom-call(f32[2,32,128,128]{3,2,1,0:T(8,128)S(1)} %get-tuple-element.39.whole, bf16[2,48,256,128]{3,2,1,0:T(8,128)(2,1)S(1)} %get-tuple-element.41.upper, bf16[2,24,256,128]{3,2,1,0:T(8,128)(2,1)S(1)} %get-tuple-element.42.lower, ...), custom_call_target="tpu_custom_call" | custom-call | tf_op jit(solution)/shard_map/third/pallas_call | solution.py:440
  44.1 2.0 %collective-permute-start.16 = (f32[128,128]{1,0:T(8,128)S(1)}, f32[128,128]{1,0:T(8,128)S(1)}, u32[]{:S(2)}, u32[]{:S(2)}) collective-permute-start(f32[128,128]{1,0:T(8,128)S(1)} %get-tuple-element.60), channel_id=1, source_target_pairs={{0,4},{1,5},{2,3},{3,2},{4,0},{5,1},{6,7},{7,6},{8,12},{9,13},{10,... | collective-permute-start | bytes 196616 | tf_op jit(solution)/shard_map/ppermute | solution.py:283
  46.5 1.2 %collective-permute-start.11 = (f32[128,128]{1,0:T(8,128)S(1)}, f32[128,128]{1,0:T(8,128)S(1)}, u32[]{:S(2)}, u32[]{:S(2)}) collective-permute-start(f32[128,128]{1,0:T(8,128)S(1)} %add.65), channel_id=1, source_target_pairs={{0,1},{1,0},{2,6},{3,7},{4,5},{5,4},{6,2},{7,3},{8,9},{9,8},{10,14... | collective-permute-start | bytes 196616 | tf_op jit(solution)/shard_map/ppermute | solution.py:283
  47.7 1.7 %collective-permute-done.16 = f32[128,128]{1,0:T(8,128)S(1)} collective-permute-done((f32[128,128]{1,0:T(8,128)S(1)}, f32[128,128]{1,0:T(8,128)S(1)}, u32[]{:S(2)}, u32[]{:S(2)}) %collective-permute-start.16) | collective-permute-done | bytes 65568 | tf_op jit(solution)/shard_map/ppermute | solution.py:283
  49.5 1.1 %collective-permute-start.17 = (f32[128,128]{1,0:T(8,128)S(1)}, f32[128,128]{1,0:T(8,128)S(1)}, u32[]{:S(2)}, u32[]{:S(2)}) collective-permute-start(f32[128,128]{1,0:T(8,128)S(1)} %add.70), channel_id=1, source_target_pairs={{0,1},{1,0},{2,6},{3,7},{4,5},{5,4},{6,2},{7,3},{8,9},{9,8},{10,14... | collective-permute-start | bytes 196616 | tf_op jit(solution)/shard_map/ppermute | solution.py:283
  50.8 2.4 %collective-permute-start.12 = (f32[128,128]{1,0:T(8,128)S(1)}, f32[128,128]{1,0:T(8,128)S(1)}, u32[]{:S(2)}, u32[]{:S(2)}) collective-permute-start(f32[128,128]{1,0:T(8,128)S(1)} %add.66), channel_id=1, source_target_pairs={{0,2},{1,3},{2,0},{3,1},{4,6},{5,7},{6,4},{7,5},{8,10},{9,11},{10,... | collective-permute-start | bytes 196616 | tf_op jit(solution)/shard_map/ppermute | solution.py:283
  53.8 2.1 %collective-permute-start.18 = (f32[128,128]{1,0:T(8,128)S(1)}, f32[128,128]{1,0:T(8,128)S(1)}, u32[]{:S(2)}, u32[]{:S(2)}) collective-permute-start(f32[128,128]{1,0:T(8,128)S(1)} %add.71), channel_id=1, source_target_pairs={{0,2},{1,3},{2,0},{3,1},{4,6},{5,7},{6,4},{7,5},{8,10},{9,11},{10,... | collective-permute-start | bytes 196616 | tf_op jit(solution)/shard_map/ppermute | solution.py:283
  55.9 2.3 %collective-permute-done.18 = f32[128,128]{1,0:T(8,128)S(1)} collective-permute-done((f32[128,128]{1,0:T(8,128)S(1)}, f32[128,128]{1,0:T(8,128)S(1)}, u32[]{:S(2)}, u32[]{:S(2)}) %collective-permute-start.18) | collective-permute-done | bytes 65568 | tf_op jit(solution)/shard_map/ppermute | solution.py:283
  58.3 1.2 %collective-permute-done.19 = f32[128,128]{1,0:T(8,128)S(1)} collective-permute-done((f32[128,128]{1,0:T(8,128)S(1)}, f32[128,128]{1,0:T(8,128)S(1)}, u32[]{:S(2)}, u32[]{:S(2)}) %collective-permute-start.19) | collective-permute-done | bytes 65568 | tf_op jit(solution)/shard_map/ppermute | solution.py:263
  59.5 1.2 %collective-permute-start.20 = (f32[128,128]{1,0:T(8,128)S(1)}, f32[128,128]{1,0:T(8,128)S(1)}, u32[]{:S(2)}, u32[]{:S(2)}) collective-permute-start(f32[128,128]{1,0:T(8,128)S(1)} %add.74), channel_id=1, source_target_pairs={{0,24},{8,16},{16,8},{24,0},{1,25},{9,17},{17,9},{25,1},{2,26},{10... | collective-permute-start | bytes 196616 | tf_op jit(solution)/shard_map/ppermute | solution.py:263
  60.8 2.9 %collective-permute-done.20 = f32[128,128]{1,0:T(8,128)S(1)} collective-permute-done((f32[128,128]{1,0:T(8,128)S(1)}, f32[128,128]{1,0:T(8,128)S(1)}, u32[]{:S(2)}, u32[]{:S(2)}) %collective-permute-start.20) | collective-permute-done | bytes 65568 | tf_op jit(solution)/shard_map/ppermute | solution.py:263
  63.7 1.9 %first.3 = (f32[80,128]{1,0:T(8,128)S(1)}, f32[80,128]{1,0:T(8,128)S(1)}, f32[80,128]{1,0:T(8,128)S(1)}) custom-call(f32[2,32,128,128]{3,2,1,0:T(8,128)S(1)} %get-tuple-element.43.whole.whole_t, bf16[2,48,256,128]{3,2,1,0:T(8,128)(2,1)S(1)} %get-tuple-element.44.upper.upper_t, bf16[2,24,256,128]{3,2,1,0:T(8,128)(2,1)S(1)} %get-tuple-element.45.lower.lower_t, ...), custom_call_target="tpu_custom_call" | custom-call | tf_op jit(solution)/shard_map/first/pallas_call | solution.py:405
  65.6 1.2 %collective-permute-start.23 = (f32[80,128]{1,0:T(8,128)S(1)}, f32[80,128]{1,0:T(8,128)S(1)}, u32[]{:S(2)}, u32[]{:S(2)}) collective-permute-start(f32[80,128]{1,0:T(8,128)S(1)} %get-tuple-element.61.order.refs_0_), channel_id=1, source_target_pairs={{0,24},{8,16},{16,8},{24,0},{1,25},{9,17},{17,9},{25,1},{2,26},{10... | collective-permute-start | bytes 122888 | tf_op jit(solution)/shard_map/ppermute | solution.py:263
  67.5 1.7 %collective-permute-done.23.refs_3_ = f32[80,128]{1,0:T(8,128)S(1)} collective-permute-done((f32[80,128]{1,0:T(8,128)S(1)}, f32[80,128]{1,0:T(8,128)S(1)}, u32[]{:S(2)}, u32[]{:S(2)}) %collective-permute-start.23) | collective-permute-done | bytes 40992 | tf_op jit(solution)/shard_map/ppermute | solution.py:263
  69.1 1.7 %collective-permute-done.22.refs_2_ = f32[80,128]{1,0:T(8,128)S(1)} collective-permute-done((f32[80,128]{1,0:T(8,128)S(1)}, f32[80,128]{1,0:T(8,128)S(1)}, u32[]{:S(2)}, u32[]{:S(2)}) %collective-permute-start.22) | collective-permute-done | bytes 40992 | tf_op jit(solution)/shard_map/ppermute | solution.py:263
  70.8 1.1 %second.4 = (f32[80,128]{1,0:T(8,128)S(1)}, f32[128,128]{1,0:T(8,128)S(1)}) custom-call(f32[2,32,128,128]{3,2,1,0:T(8,128)S(1)} %get-tuple-element.39.whole, bf16[2,48,256,128]{3,2,1,0:T(8,128)(2,1)S(1)} %get-tuple-element.41.upper, bf16[2,24,256,128]{3,2,1,0:T(8,128)(2,1)S(1)} %get-tuple-element.42.lower, bf16[128,80]{1,0:T(8,128)(2,1)S(1)} %get-tuple-element.48.col_hot_t, ...), custom_call_target="tpu_custom_call" | custom-call | tf_op jit(solution)/shard_map/second/pallas_call | solution.py:420
  71.9 2.0 %collective-permute-start.27 = (f32[128,128]{1,0:T(8,128)S(1)}, f32[128,128]{1,0:T(8,128)S(1)}, u32[]{:S(2)}, u32[]{:S(2)}) collective-permute-start(f32[128,128]{1,0:T(8,128)S(1)} %get-tuple-element.63.order), channel_id=1, source_target_pairs={{0,4},{1,5},{2,3},{3,2},{4,0},{5,1},{6,7},{7,6},{8,12},{9,13},{10,... | collective-permute-start | bytes 196616 | tf_op jit(solution)/shard_map/ppermute | solution.py:283
  73.9 1.1 %second.5 = (f32[80,128]{1,0:T(8,128)S(1)}, f32[128,128]{1,0:T(8,128)S(1)}) custom-call(f32[2,32,128,128]{3,2,1,0:T(8,128)S(1)} %get-tuple-element.39.whole, bf16[2,48,256,128]{3,2,1,0:T(8,128)(2,1)S(1)} %get-tuple-element.41.upper, bf16[2,24,256,128]{3,2,1,0:T(8,128)(2,1)S(1)} %get-tuple-element.42.lower, bf16[128,80]{1,0:T(8,128)(2,1)S(1)} %get-tuple-element.48.col_hot_t, ...), custom_call_target="tpu_custom_call" | custom-call | tf_op jit(solution)/shard_map/second/pallas_call | solution.py:420
  75.0 1.1 %collective-permute-start.24 = (f32[128,128]{1,0:T(8,128)S(1)}, f32[128,128]{1,0:T(8,128)S(1)}, u32[]{:S(2)}, u32[]{:S(2)}) collective-permute-start(f32[128,128]{1,0:T(8,128)S(1)} %get-tuple-element.65), channel_id=1, source_target_pairs={{0,4},{1,5},{2,3},{3,2},{4,0},{5,1},{6,7},{7,6},{8,12},{9,13},{10,... | collective-permute-start | bytes 196616 | tf_op jit(solution)/shard_map/ppermute | solution.py:283
  76.1 1.1 collective-permute-done.27
  77.9 2.9 %collective-permute-done.24 = f32[128,128]{1,0:T(8,128)S(1)} collective-permute-done((f32[128,128]{1,0:T(8,128)S(1)}, f32[128,128]{1,0:T(8,128)S(1)}, u32[]{:S(2)}, u32[]{:S(2)}) %collective-permute-start.24) | collective-permute-done | bytes 65568 | tf_op jit(solution)/shard_map/ppermute | solution.py:283
  80.7 1.1 %collective-permute-start.25 = (f32[128,128]{1,0:T(8,128)S(1)}, f32[128,128]{1,0:T(8,128)S(1)}, u32[]{:S(2)}, u32[]{:S(2)}) collective-permute-start(f32[128,128]{1,0:T(8,128)S(1)} %add.76), channel_id=1, source_target_pairs={{0,1},{1,0},{2,6},{3,7},{4,5},{5,4},{6,2},{7,3},{8,9},{9,8},{10,14... | collective-permute-start | bytes 196616 | tf_op jit(solution)/shard_map/ppermute | solution.py:283
  82.1 2.4 %collective-permute-start.29 = (f32[128,128]{1,0:T(8,128)S(1)}, f32[128,128]{1,0:T(8,128)S(1)}, u32[]{:S(2)}, u32[]{:S(2)}) collective-permute-start(f32[128,128]{1,0:T(8,128)S(1)} %add.79.refs_0_), channel_id=1, source_target_pairs={{0,2},{1,3},{2,0},{3,1},{4,6},{5,7},{6,4},{7,5},{8,10},{9,11},{10,... | collective-permute-start | bytes 196616 | tf_op jit(solution)/shard_map/ppermute | solution.py:283
  85.2 1.5 %collective-permute-done.29.refs_1_ = f32[128,128]{1,0:T(8,128)S(1)} collective-permute-done((f32[128,128]{1,0:T(8,128)S(1)}, f32[128,128]{1,0:T(8,128)S(1)}, u32[]{:S(2)}, u32[]{:S(2)}) %collective-permute-start.29) | collective-permute-done | bytes 65568 | tf_op jit(solution)/shard_map/ppermute | solution.py:283
  86.7 2.3 %third.6 = (f32[16,128]{1,0:T(8,128)S(1)}, f32[128,128]{1,0:T(8,128)S(1)}) custom-call(f32[2,32,128,128]{3,2,1,0:T(8,128)S(1)} %get-tuple-element.39.whole, bf16[2,48,256,128]{3,2,1,0:T(8,128)(2,1)S(1)} %get-tuple-element.41.upper, bf16[2,24,256,128]{3,2,1,0:T(8,128)(2,1)S(1)} %get-tuple-element.42.lower, ...), custom_call_target="tpu_custom_call" | custom-call | tf_op jit(solution)/shard_map/third/pallas_call | solution.py:440
  89.4 2.3 %third.7 = (f32[16,128]{1,0:T(8,128)S(1)}, f32[8,2,16,128]{3,2,1,0:T(8,128)S(1)}) custom-call(f32[2,32,128,128]{3,2,1,0:T(8,128)S(1)} %get-tuple-element.39.whole, bf16[2,48,256,128]{3,2,1,0:T(8,128)(2,1)S(1)} %get-tuple-element.41.upper, bf16[2,24,256,128]{3,2,1,0:T(8,128)(2,1)S(1)} %get-tuple-element.42.lower, ...), custom_call_target="tpu_custom_call" | custom-call | tf_op jit(solution)/shard_map/third/pallas_call | solution.py:440
  91.7 10.3 %all_to_all.5 = f32[8,2,16,128]{3,2,1,0:T(8,128)S(1)} all-to-all(f32[8,2,16,128]{3,2,1,0:T(8,128)S(1)} %get-tuple-element.73), channel_id=1, replica_groups=mesh['scen'=4,'vox'=8] {'vox'}, dimensions={0} | all-to-all | bytes 262144 | tf_op jit(solution)/shard_map/all_to_all | solution.py:464
  102.1 1.6 %collective-permute-start.31 = (f32[16,128]{1,0:T(8,128)S(1)}, f32[16,128]{1,0:T(8,128)S(1)}, u32[]{:S(2)}, u32[]{:S(2)}) collective-permute-start(f32[16,128]{1,0:T(8,128)S(1)} %fusion.3.order), channel_id=1, source_target_pairs={{0,16},{8,24},{16,0},{24,8},{1,17},{9,25},{17,1},{25,9},{2,18},{10... | collective-permute-start | bytes 24584 | tf_op jit(solution)/shard_map/ppermute | solution.py:263
  104.0 0.9 place.1
  (51 shorter events, 8.7 us)
Async XLA Ops:
  0.6 7.8 %collective-permute-start.2 = (f32[16,128]{1,0:T(8,128)}, f32[16,128]{1,0:T(8,128)S(1)}, u32[]{:S(2)}, u32[]{:S(2)}) collective-permute-start(f32[16,128]{1,0:T(8,128)} %bitcast.28), channel_id=1, source_target_pairs={{0,11},{1,10},{2,9},{3,8},{4,15},{5,14},{6,13},{7,12},{8,3},{9,2},... | collective-permute-start | bytes 24584 | tf_op jit(solution)/shard_map/ppermute | solution.py:307
  4.1 4.3 %collective-permute-start.1 = (f32[16,128]{1,0:T(8,128)}, f32[16,128]{1,0:T(8,128)S(1)}, u32[]{:S(2)}, u32[]{:S(2)}) collective-permute-start(f32[16,128]{1,0:T(8,128)} %bitcast.29), channel_id=1, source_target_pairs={{0,10},{1,11},{2,8},{3,9},{4,14},{5,15},{6,12},{7,13},{8,2},{9,3},... | collective-permute-start | bytes 24584 | tf_op jit(solution)/shard_map/ppermute | solution.py:307
  4.8 3.6 %collective-permute-start = (f32[16,128]{1,0:T(8,128)}, f32[16,128]{1,0:T(8,128)S(1)}, u32[]{:S(2)}, u32[]{:S(2)}) collective-permute-start(f32[16,128]{1,0:T(8,128)} %bitcast.30), channel_id=1, source_target_pairs={{0,9},{1,8},{2,11},{3,10},{4,13},{5,12},{6,15},{7,14},{8,1},{9,0},... | collective-permute-start | bytes 24584 | tf_op jit(solution)/shard_map/ppermute | solution.py:307
  8.4 6.3 %collective-permute-start.3 = (f32[64,128]{1,0:T(8,128)S(1)}, f32[64,128]{1,0:T(8,128)S(1)}, u32[]{:S(2)}, u32[]{:S(2)}) collective-permute-start(f32[64,128]{1,0:T(8,128)S(1)} %collect.1.order.mine), channel_id=1, source_target_pairs={{0,12},{1,13},{2,14},{3,15},{4,8},{5,9},{6,10},{7,11},{8,4},{9,5},... | collective-permute-start | bytes 98312 | tf_op jit(solution)/shard_map/ppermute | solution.py:307
  16.7 3.7 %collective-permute-start.6 = (f32[80,128]{1,0:T(8,128)S(1)}, f32[80,128]{1,0:T(8,128)S(1)}, u32[]{:S(2)}, u32[]{:S(2)}) collective-permute-start(f32[80,128]{1,0:T(8,128)S(1)} %get-tuple-element.50.order.refs_0_), channel_id=1, source_target_pairs={{0,24},{8,16},{16,8},{24,0},{1,25},{9,17},{17,9},{25,1},{2,26},{10... | collective-permute-start | bytes 122888 | tf_op jit(solution)/shard_map/ppermute | solution.py:263
  17.9 4.0 %collective-permute-start.5 = (f32[80,128]{1,0:T(8,128)S(1)}, f32[80,128]{1,0:T(8,128)S(1)}, u32[]{:S(2)}, u32[]{:S(2)}) collective-permute-start(f32[80,128]{1,0:T(8,128)S(1)} %get-tuple-element.50.order.refs_0_), channel_id=1, source_target_pairs={{0,16},{8,24},{16,0},{24,8},{1,17},{9,25},{17,1},{25,9},{2,18},{10... | collective-permute-start | bytes 122888 | tf_op jit(solution)/shard_map/ppermute | solution.py:263
  18.4 3.5 %collective-permute-start.4 = (f32[80,128]{1,0:T(8,128)S(1)}, f32[80,128]{1,0:T(8,128)S(1)}, u32[]{:S(2)}, u32[]{:S(2)}) collective-permute-start(f32[80,128]{1,0:T(8,128)S(1)} %get-tuple-element.50.order.refs_0_), channel_id=1, source_target_pairs={{0,8},{8,0},{16,24},{24,16},{1,9},{9,1},{17,25},{25,17},{2,10},{10... | collective-permute-start | bytes 122888 | tf_op jit(solution)/shard_map/ppermute | solution.py:263
  23.7 5.2 %collective-permute-start.7 = (f32[128,128]{1,0:T(8,128)S(1)}, f32[128,128]{1,0:T(8,128)S(1)}, u32[]{:S(2)}, u32[]{:S(2)}) collective-permute-start(f32[128,128]{1,0:T(8,128)S(1)} %get-tuple-element.53), channel_id=1, source_target_pairs={{0,4},{1,5},{2,3},{3,2},{4,0},{5,1},{6,7},{7,6},{8,12},{9,13},{10,... | collective-permute-start | bytes 196616 | tf_op jit(solution)/shard_map/ppermute | solution.py:283
  24.7 5.9 %collective-permute-start.13 = (f32[128,128]{1,0:T(8,128)S(1)}, f32[128,128]{1,0:T(8,128)S(1)}, u32[]{:S(2)}, u32[]{:S(2)}) collective-permute-start(f32[128,128]{1,0:T(8,128)S(1)} %get-tuple-element.57), channel_id=1, source_target_pairs={{0,4},{1,5},{2,3},{3,2},{4,0},{5,1},{6,7},{7,6},{8,12},{9,13},{10,... | collective-permute-start | bytes 196616 | tf_op jit(solution)/shard_map/ppermute | solution.py:283
  28.9 4.3 %collective-permute-start.8 = (f32[128,128]{1,0:T(8,128)S(1)}, f32[128,128]{1,0:T(8,128)S(1)}, u32[]{:S(2)}, u32[]{:S(2)}) collective-permute-start(f32[128,128]{1,0:T(8,128)S(1)} %add.63), channel_id=1, source_target_pairs={{0,1},{1,0},{2,6},{3,7},{4,5},{5,4},{6,2},{7,3},{8,9},{9,8},{10,14... | collective-permute-start | bytes 196616 | tf_op jit(solution)/shard_map/ppermute | solution.py:283
  30.6 5.4 %collective-permute-start.14 = (f32[128,128]{1,0:T(8,128)S(1)}, f32[128,128]{1,0:T(8,128)S(1)}, u32[]{:S(2)}, u32[]{:S(2)}) collective-permute-start(f32[128,128]{1,0:T(8,128)S(1)} %add.68), channel_id=1, source_target_pairs={{0,1},{1,0},{2,6},{3,7},{4,5},{5,4},{6,2},{7,3},{8,9},{9,8},{10,14... | collective-permute-start | bytes 196616 | tf_op jit(solution)/shard_map/ppermute | solution.py:283
  33.2 5.0 %collective-permute-start.9 = (f32[128,128]{1,0:T(8,128)S(1)}, f32[128,128]{1,0:T(8,128)S(1)}, u32[]{:S(2)}, u32[]{:S(2)}) collective-permute-start(f32[128,128]{1,0:T(8,128)S(1)} %add.64.refs_0_), channel_id=1, source_target_pairs={{0,2},{1,3},{2,0},{3,1},{4,6},{5,7},{6,4},{7,5},{8,10},{9,11},{10,... | collective-permute-start | bytes 196616 | tf_op jit(solution)/shard_map/ppermute | solution.py:283
  36.0 5.6 %collective-permute-start.15 = (f32[128,128]{1,0:T(8,128)S(1)}, f32[128,128]{1,0:T(8,128)S(1)}, u32[]{:S(2)}, u32[]{:S(2)}) collective-permute-start(f32[128,128]{1,0:T(8,128)S(1)} %add.69.refs_0_), channel_id=1, source_target_pairs={{0,2},{1,3},{2,0},{3,1},{4,6},{5,7},{6,4},{7,5},{8,10},{9,11},{10,... | collective-permute-start | bytes 196616 | tf_op jit(solution)/shard_map/ppermute | solution.py:283
  40.6 5.9 %collective-permute-start.10 = (f32[128,128]{1,0:T(8,128)S(1)}, f32[128,128]{1,0:T(8,128)S(1)}, u32[]{:S(2)}, u32[]{:S(2)}) collective-permute-start(f32[128,128]{1,0:T(8,128)S(1)} %get-tuple-element.56), channel_id=1, source_target_pairs={{0,4},{1,5},{2,3},{3,2},{4,0},{5,1},{6,7},{7,6},{8,12},{9,13},{10,... | collective-permute-start | bytes 196616 | tf_op jit(solution)/shard_map/ppermute | solution.py:283
  44.1 5.4 %collective-permute-start.16 = (f32[128,128]{1,0:T(8,128)S(1)}, f32[128,128]{1,0:T(8,128)S(1)}, u32[]{:S(2)}, u32[]{:S(2)}) collective-permute-start(f32[128,128]{1,0:T(8,128)S(1)} %get-tuple-element.60), channel_id=1, source_target_pairs={{0,4},{1,5},{2,3},{3,2},{4,0},{5,1},{6,7},{7,6},{8,12},{9,13},{10,... | collective-permute-start | bytes 196616 | tf_op jit(solution)/shard_map/ppermute | solution.py:283
  46.5 4.3 %collective-permute-start.11 = (f32[128,128]{1,0:T(8,128)S(1)}, f32[128,128]{1,0:T(8,128)S(1)}, u32[]{:S(2)}, u32[]{:S(2)}) collective-permute-start(f32[128,128]{1,0:T(8,128)S(1)} %add.65), channel_id=1, source_target_pairs={{0,1},{1,0},{2,6},{3,7},{4,5},{5,4},{6,2},{7,3},{8,9},{9,8},{10,14... | collective-permute-start | bytes 196616 | tf_op jit(solution)/shard_map/ppermute | solution.py:283
  49.5 4.3 %collective-permute-start.17 = (f32[128,128]{1,0:T(8,128)S(1)}, f32[128,128]{1,0:T(8,128)S(1)}, u32[]{:S(2)}, u32[]{:S(2)}) collective-permute-start(f32[128,128]{1,0:T(8,128)S(1)} %add.70), channel_id=1, source_target_pairs={{0,1},{1,0},{2,6},{3,7},{4,5},{5,4},{6,2},{7,3},{8,9},{9,8},{10,14... | collective-permute-start | bytes 196616 | tf_op jit(solution)/shard_map/ppermute | solution.py:283
  50.8 5.1 %collective-permute-start.12 = (f32[128,128]{1,0:T(8,128)S(1)}, f32[128,128]{1,0:T(8,128)S(1)}, u32[]{:S(2)}, u32[]{:S(2)}) collective-permute-start(f32[128,128]{1,0:T(8,128)S(1)} %add.66), channel_id=1, source_target_pairs={{0,2},{1,3},{2,0},{3,1},{4,6},{5,7},{6,4},{7,5},{8,10},{9,11},{10,... | collective-permute-start | bytes 196616 | tf_op jit(solution)/shard_map/ppermute | solution.py:283
  53.8 4.3 %collective-permute-start.18 = (f32[128,128]{1,0:T(8,128)S(1)}, f32[128,128]{1,0:T(8,128)S(1)}, u32[]{:S(2)}, u32[]{:S(2)}) collective-permute-start(f32[128,128]{1,0:T(8,128)S(1)} %add.71), channel_id=1, source_target_pairs={{0,2},{1,3},{2,0},{3,1},{4,6},{5,7},{6,4},{7,5},{8,10},{9,11},{10,... | collective-permute-start | bytes 196616 | tf_op jit(solution)/shard_map/ppermute | solution.py:283
  58.2 1.3 %collective-permute-start.19 = (f32[128,128]{1,0:T(8,128)S(1)}, f32[128,128]{1,0:T(8,128)S(1)}, u32[]{:S(2)}, u32[]{:S(2)}) collective-permute-start(f32[128,128]{1,0:T(8,128)S(1)} %maximum_add_fusion), channel_id=1, source_target_pairs={{0,8},{8,0},{16,24},{24,16},{1,9},{9,1},{17,25},{25,17},{2,10},{10... | collective-permute-start | bytes 196616 | tf_op jit(solution)/shard_map/ppermute | solution.py:263
  59.5 4.1 %collective-permute-start.20 = (f32[128,128]{1,0:T(8,128)S(1)}, f32[128,128]{1,0:T(8,128)S(1)}, u32[]{:S(2)}, u32[]{:S(2)}) collective-permute-start(f32[128,128]{1,0:T(8,128)S(1)} %add.74), channel_id=1, source_target_pairs={{0,24},{8,16},{16,8},{24,0},{1,25},{9,17},{17,9},{25,1},{2,26},{10... | collective-permute-start | bytes 196616 | tf_op jit(solution)/shard_map/ppermute | solution.py:263
  65.6 3.6 %collective-permute-start.23 = (f32[80,128]{1,0:T(8,128)S(1)}, f32[80,128]{1,0:T(8,128)S(1)}, u32[]{:S(2)}, u32[]{:S(2)}) collective-permute-start(f32[80,128]{1,0:T(8,128)S(1)} %get-tuple-element.61.order.refs_0_), channel_id=1, source_target_pairs={{0,24},{8,16},{16,8},{24,0},{1,25},{9,17},{17,9},{25,1},{2,26},{10... | collective-permute-start | bytes 122888 | tf_op jit(solution)/shard_map/ppermute | solution.py:263
  66.8 4.0 %collective-permute-start.22 = (f32[80,128]{1,0:T(8,128)S(1)}, f32[80,128]{1,0:T(8,128)S(1)}, u32[]{:S(2)}, u32[]{:S(2)}) collective-permute-start(f32[80,128]{1,0:T(8,128)S(1)} %get-tuple-element.61.order.refs_0_), channel_id=1, source_target_pairs={{0,16},{8,24},{16,0},{24,8},{1,17},{9,25},{17,1},{25,9},{2,18},{10... | collective-permute-start | bytes 122888 | tf_op jit(solution)/shard_map/ppermute | solution.py:263
  67.4 3.4 %collective-permute-start.21 = (f32[80,128]{1,0:T(8,128)S(1)}, f32[80,128]{1,0:T(8,128)S(1)}, u32[]{:S(2)}, u32[]{:S(2)}) collective-permute-start(f32[80,128]{1,0:T(8,128)S(1)} %get-tuple-element.61.order.refs_0_), channel_id=1, source_target_pairs={{0,8},{8,0},{16,24},{24,16},{1,9},{9,1},{17,25},{25,17},{2,10},{10... | collective-permute-start | bytes 122888 | tf_op jit(solution)/shard_map/ppermute | solution.py:263
  71.9 5.2 %collective-permute-start.27 = (f32[128,128]{1,0:T(8,128)S(1)}, f32[128,128]{1,0:T(8,128)S(1)}, u32[]{:S(2)}, u32[]{:S(2)}) collective-permute-start(f32[128,128]{1,0:T(8,128)S(1)} %get-tuple-element.63.order), channel_id=1, source_target_pairs={{0,4},{1,5},{2,3},{3,2},{4,0},{5,1},{6,7},{7,6},{8,12},{9,13},{10,... | collective-permute-start | bytes 196616 | tf_op jit(solution)/shard_map/ppermute | solution.py:283
  75.0 5.7 %collective-permute-start.24 = (f32[128,128]{1,0:T(8,128)S(1)}, f32[128,128]{1,0:T(8,128)S(1)}, u32[]{:S(2)}, u32[]{:S(2)}) collective-permute-start(f32[128,128]{1,0:T(8,128)S(1)} %get-tuple-element.65), channel_id=1, source_target_pairs={{0,4},{1,5},{2,3},{3,2},{4,0},{5,1},{6,7},{7,6},{8,12},{9,13},{10,... | collective-permute-start | bytes 196616 | tf_op jit(solution)/shard_map/ppermute | solution.py:283
  77.2 4.9 %collective-permute-start.28 = (f32[128,128]{1,0:T(8,128)S(1)}, f32[128,128]{1,0:T(8,128)S(1)}, u32[]{:S(2)}, u32[]{:S(2)}) collective-permute-start(f32[128,128]{1,0:T(8,128)S(1)} %add.78), channel_id=1, source_target_pairs={{0,1},{1,0},{2,6},{3,7},{4,5},{5,4},{6,2},{7,3},{8,9},{9,8},{10,14... | collective-permute-start | bytes 196616 | tf_op jit(solution)/shard_map/ppermute | solution.py:283
  80.7 4.3 %collective-permute-start.25 = (f32[128,128]{1,0:T(8,128)S(1)}, f32[128,128]{1,0:T(8,128)S(1)}, u32[]{:S(2)}, u32[]{:S(2)}) collective-permute-start(f32[128,128]{1,0:T(8,128)S(1)} %add.76), channel_id=1, source_target_pairs={{0,1},{1,0},{2,6},{3,7},{4,5},{5,4},{6,2},{7,3},{8,9},{9,8},{10,14... | collective-permute-start | bytes 196616 | tf_op jit(solution)/shard_map/ppermute | solution.py:283
  82.1 4.6 %collective-permute-start.29 = (f32[128,128]{1,0:T(8,128)S(1)}, f32[128,128]{1,0:T(8,128)S(1)}, u32[]{:S(2)}, u32[]{:S(2)}) collective-permute-start(f32[128,128]{1,0:T(8,128)S(1)} %add.79.refs_0_), channel_id=1, source_target_pairs={{0,2},{1,3},{2,0},{3,1},{4,6},{5,7},{6,4},{7,5},{8,10},{9,11},{10,... | collective-permute-start | bytes 196616 | tf_op jit(solution)/shard_map/ppermute | solution.py:283
  85.1 4.3 %collective-permute-start.26 = (f32[128,128]{1,0:T(8,128)S(1)}, f32[128,128]{1,0:T(8,128)S(1)}, u32[]{:S(2)}, u32[]{:S(2)}) collective-permute-start(f32[128,128]{1,0:T(8,128)S(1)} %add.77.refs_0_), channel_id=1, source_target_pairs={{0,2},{1,3},{2,0},{3,1},{4,6},{5,7},{6,4},{7,5},{8,10},{9,11},{10,... | collective-permute-start | bytes 196616 | tf_op jit(solution)/shard_map/ppermute | solution.py:283
  102.0 3.2 %collective-permute-start.32 = (f32[16,128]{1,0:T(8,128)S(1)}, f32[16,128]{1,0:T(8,128)S(1)}, u32[]{:S(2)}, u32[]{:S(2)}) collective-permute-start(f32[16,128]{1,0:T(8,128)S(1)} %fusion.3.order), channel_id=1, source_target_pairs={{0,24},{8,16},{16,8},{24,0},{1,25},{9,17},{17,9},{25,1},{2,26},{10... | collective-permute-start | bytes 24584 | tf_op jit(solution)/shard_map/ppermute | solution.py:263
  102.1 3.7 %collective-permute-start.31 = (f32[16,128]{1,0:T(8,128)S(1)}, f32[16,128]{1,0:T(8,128)S(1)}, u32[]{:S(2)}, u32[]{:S(2)}) collective-permute-start(f32[16,128]{1,0:T(8,128)S(1)} %fusion.3.order), channel_id=1, source_target_pairs={{0,16},{8,24},{16,0},{24,8},{1,17},{9,25},{17,1},{25,9},{2,18},{10... | collective-permute-start | bytes 24584 | tf_op jit(solution)/shard_map/ppermute | solution.py:263
  103.7 2.1 %collective-permute-start.30 = (f32[16,128]{1,0:T(8,128)S(1)}, f32[16,128]{1,0:T(8,128)S(1)}, u32[]{:S(2)}, u32[]{:S(2)}) collective-permute-start(f32[16,128]{1,0:T(8,128)S(1)} %fusion.3.order), channel_id=1, source_target_pairs={{0,8},{8,0},{16,24},{24,16},{1,9},{9,1},{17,25},{25,17},{2,10},{10... | collective-permute-start | bytes 24584 | tf_op jit(solution)/shard_map/ppermute | solution.py:263

commit v11 on v10

--- a/solution.py
+++ b/solution.py
@@ -411,7 +411,7 @@
             scratch_shapes=[pltpu.VMEM((scen, slots, side), F32)],
             compiler_params=params,
         )(*flipped, fluence, target, col_hot, same)
-        score_sums = spread_scen(score_sum)
+        score_sums = spread_scen(score_sum) if last else reduce_scen(score_sum, log_sum_exp)
 
         groups = [[s] for s in range(scen)] if last else [list(range(scen))]
         weights, gradients, order = [], [], score_sum

time: 107 us -> 107 us (level)
  waiting for transfers between devices: 29.3 us -> 31.1 us
  starting transfers between devices: 40.2 us -> 38.5 us
    ppermute x18, waiting for transfers between devices: 17.6 us -> 19.3 us  [reduce_vox(): lax.ppermute(x, 'vox', [(v, v ^ pair[(v & steps[-2]) // steps[-2]]) for v...]
    ppermute x18, starting transfers between devices: 26.1 us -> 24.7 us  [reduce_vox(): lax.ppermute(x, 'vox', [(v, v ^ pair[(v & steps[-2]) // steps[-2]]) for v...]
    ppermute x11 -> x10, starting transfers between devices: 7.08 us -> 6.73 us  [swap(): lax.ppermute(x, axis, [(i, i ^ bit) for i in range(lax.axis_size(axis))])]
    ppermute x11 -> x10, waiting for transfers between devices: 11.7 us -> 11.8 us  [swap(): lax.ppermute(x, axis, [(i, i ^ bit) for i in range(lax.axis_size(axis))])]
  transfers between devices with their start and end apart: 33 -> 32, of which waited for: 22 -> 21; matrix products, arithmetic and copies ran while one was open for 0% -> 0% of each run, Pallas kernels for 14% -> 14%
where the time goes in v11:
time: 107 us
  starting transfers between devices  38.5 us (36%)
  waiting for transfers between devices  31.1 us (29%)
  Pallas kernels  24.4 us (23%)
  blocking collectives  10.5 us (10%)
  between operations  1.52 us (1%)
    ppermute x18, starting transfers between devices, reduce_vox(): lax.ppermute(x, 'vox', [(v, v ^ pair[(v & steps[-2]) // steps[-2]]) for v...  24.7 us
    ppermute x18, waiting for transfers between devices, reduce_vox(): lax.ppermute(x, 'vox', [(v, v ^ pair[(v & steps[-2]) // steps[-2]]) for v...  19.3 us
    ppermute x10, waiting for transfers between devices, swap(): lax.ppermute(x, axis, [(i, i ^ bit) for i in range(lax.axis_size(axis))])  11.8 us
    all_to_all x1, blocking collectives, body(): lax.all_to_all(gradient, 'vox', split_axis=0, concat_axis=0, tiled=True)  10.5 us
    pallas_call x4, Pallas kernels, body(): pl.pallas_call(functools.partial(third_kernel, group), name='third', out_...  9.32 us
    ppermute x4, starting transfers between devices, swap_both(): return lax.ppermute(x, ('scen', 'vox'), pairs)  7.1 us
    ppermute x10, starting transfers between devices, swap(): lax.ppermute(x, axis, [(i, i ^ bit) for i in range(lax.axis_size(axis))])  6.73 us
    pallas_call x3, Pallas kernels, body(): pl.pallas_call(functools.partial(second_kernel, group), name='second', ou...  3.96 us
  transfers between devices with their start and end apart: 32, of which 21 were waited for; matrix products, arithmetic and copies ran while one was open for 0% of the time, Pallas kernels for 14%

profile of v11, /device:TPU:0, one launch (start us, length us, event | category | flops | bytes accessed | tf_op | source)
XLA Modules:
  0.0 106.9 jit_solution(2691038515818795939)
XLA Ops:
  0.6 3.5 %collective-permute-start.2 = (f32[16,128]{1,0:T(8,128)}, f32[16,128]{1,0:T(8,128)S(1)}, u32[]{:S(2)}, u32[]{:S(2)}) collective-permute-start(f32[16,128]{1,0:T(8,128)} %bitcast.28), channel_id=1, source_target_pairs={{0,11},{1,10},{2,9},{3,8},{4,15},{5,14},{6,13},{7,12},{8,3},{9,2},... | collective-permute-start | bytes 24584 | tf_op jit(solution)/shard_map/ppermute | solution.py:307
  5.7 2.7 %hot.1 = (bf16[80,128]{1,0:T(8,128)(2,1)S(1)}, bf16[128,80]{1,0:T(8,128)(2,1)S(1)}, bf16[80,80]{1,0:T(8,128)(2,1)S(1)}, bf16[128,80]{1,0:T(8,128)(2,1)S(1)}, f32...) custom-call(s32[2,80]{1,0:T(2,128)} %bitcast.32, ...), custom_call_target="tpu_custom_call" | custom-call | bytes 7864320 | tf_op jit(solution)/shard_map/hot/pallas_call | solution.py:331
  8.4 2.7 %collective-permute-start.3 = (f32[64,128]{1,0:T(8,128)S(1)}, f32[64,128]{1,0:T(8,128)S(1)}, u32[]{:S(2)}, u32[]{:S(2)}) collective-permute-start(f32[64,128]{1,0:T(8,128)S(1)} %collect.1.order.mine), channel_id=1, source_target_pairs={{0,12},{1,13},{2,14},{3,15},{4,8},{5,9},{6,10},{7,11},{8,4},{9,5},... | collective-permute-start | bytes 98312 | tf_op jit(solution)/shard_map/ppermute | solution.py:307
  11.2 3.6 %split.1 = (bf16[2,48,256,128]{3,2,1,0:T(8,128)(2,1)S(1)}, bf16[2,48,256,128]{3,2,1,0:T(8,128)(2,1)S(1)}, bf16[2,24,256,128]{3,2,1,0:T(8,128)(2,1)S(1)}, bf16[2,24,256,128]{3,2,1,0:T(8,128)(2,1)S(1)}) custom-call(f32[2,80,128,128]{3,2,1,0:T(8,128)} %source.3, f32[64,128]{1,0:T(8,128)S(1)} %collect.1.order.mine), custom_call_target="tpu_custom_call" | custom-call | bytes 13107200 | tf_op jit(solution)/shard_map/split/pallas_call | solution.py:386
  14.8 1.9 %first.2 = (f32[80,128]{1,0:T(8,128)S(1)}, f32[80,128]{1,0:T(8,128)S(1)}, f32[80,128]{1,0:T(8,128)S(1)}) custom-call(f32[2,32,128,128]{3,2,1,0:T(8,128)S(1)} %get-tuple-element.43.whole.whole_t, bf16[2,48,256,128]{3,2,1,0:T(8,128)(2,1)S(1)} %get-tuple-element.44.upper.upper_t, bf16[2,24,256,128]{3,2,1,0:T(8,128)(2,1)S(1)} %get-tuple-element.45.lower.lower_t, ...), custom_call_target="tpu_custom_call" | custom-call | tf_op jit(solution)/shard_map/first/pallas_call | solution.py:405
  16.8 1.2 %collective-permute-done.4 = f32[80,128]{1,0:T(8,128)S(1)} collective-permute-done((f32[80,128]{1,0:T(8,128)S(1)}, f32[80,128]{1,0:T(8,128)S(1)}, u32[]{:S(2)}, u32[]{:S(2)}) %collective-permute-start.4) | collective-permute-done | bytes 40992 | tf_op jit(solution)/shard_map/ppermute | solution.py:263
  18.0 1.4 %collective-permute-start.5 = (f32[80,128]{1,0:T(8,128)S(1)}, f32[80,128]{1,0:T(8,128)S(1)}, u32[]{:S(2)}, u32[]{:S(2)}) collective-permute-start(f32[80,128]{1,0:T(8,128)S(1)} %log_add_fusion.refs_0_), channel_id=1, source_target_pairs={{0,24},{8,16},{16,8},{24,0},{1,25},{9,17},{17,9},{25,1},{2,26},{10... | collective-permute-start | bytes 122888 | tf_op jit(solution)/shard_map/ppermute | solution.py:263
  19.4 2.2 %collective-permute-done.5.refs_1_ = f32[80,128]{1,0:T(8,128)S(1)} collective-permute-done((f32[80,128]{1,0:T(8,128)S(1)}, f32[80,128]{1,0:T(8,128)S(1)}, u32[]{:S(2)}, u32[]{:S(2)}) %collective-permute-start.5) | collective-permute-done | bytes 40992 | tf_op jit(solution)/shard_map/ppermute | solution.py:263
  21.6 1.7 %second.3 = (f32[80,128]{1,0:T(8,128)S(1)}, f32[80,128]{1,0:T(8,128)S(1)}, f32[128,128]{1,0:T(8,128)S(1)}, f32[128,128]{1,0:T(8,128)S(1)}) custom-call(f32[2,32,128,128]{3,2,1,0:T(8,128)S(1)} %get-tuple-element.39.whole, bf16[2,48,256,128]{3,2,1,0:T(8,128)(2,1)S(1)} %get-tuple-element.41.upper, bf16[2,24,256,128]{3,2,1,0:T(8,128)(2,1)S(1)} %get-tuple-element.42.lower, ...), custom_call_target="tpu_custom_call" | custom-call | tf_op jit(solution)/shard_map/second/pallas_call | solution.py:420
  24.0 2.3 %collective-permute-start.12 = (f32[128,128]{1,0:T(8,128)S(1)}, f32[128,128]{1,0:T(8,128)S(1)}, u32[]{:S(2)}, u32[]{:S(2)}) collective-permute-start(f32[128,128]{1,0:T(8,128)S(1)} %get-tuple-element.57), channel_id=1, source_target_pairs={{0,4},{1,5},{2,3},{3,2},{4,0},{5,1},{6,7},{7,6},{8,12},{9,13},{10,... | collective-permute-start | bytes 196616 | tf_op jit(solution)/shard_map/ppermute | solution.py:283
  26.3 2.8 %collective-permute-done.6 = f32[128,128]{1,0:T(8,128)S(1)} collective-permute-done((f32[128,128]{1,0:T(8,128)S(1)}, f32[128,128]{1,0:T(8,128)S(1)}, u32[]{:S(2)}, u32[]{:S(2)}) %collective-permute-start.6) | collective-permute-done | bytes 65568 | tf_op jit(solution)/shard_map/ppermute | solution.py:283
  29.2 1.6 %collective-permute-start.7 = (f32[128,128]{1,0:T(8,128)S(1)}, f32[128,128]{1,0:T(8,128)S(1)}, u32[]{:S(2)}, u32[]{:S(2)}) collective-permute-start(f32[128,128]{1,0:T(8,128)S(1)} %add.71), channel_id=1, source_target_pairs={{0,1},{1,0},{2,6},{3,7},{4,5},{5,4},{6,2},{7,3},{8,9},{9,8},{10,14... | collective-permute-start | bytes 196616 | tf_op jit(solution)/shard_map/ppermute | solution.py:283
  31.5 2.1 %collective-permute-done.7 = f32[128,128]{1,0:T(8,128)S(1)} collective-permute-done((f32[128,128]{1,0:T(8,128)S(1)}, f32[128,128]{1,0:T(8,128)S(1)}, u32[]{:S(2)}, u32[]{:S(2)}) %collective-permute-start.7) | collective-permute-done | bytes 65568 | tf_op jit(solution)/shard_map/ppermute | solution.py:283
  33.5 1.6 %collective-permute-start.8 = (f32[128,128]{1,0:T(8,128)S(1)}, f32[128,128]{1,0:T(8,128)S(1)}, u32[]{:S(2)}, u32[]{:S(2)}) collective-permute-start(f32[128,128]{1,0:T(8,128)S(1)} %add.72.refs_0_), channel_id=1, source_target_pairs={{0,2},{1,3},{2,0},{3,1},{4,6},{5,7},{6,4},{7,5},{8,10},{9,11},{10,... | collective-permute-start | bytes 196616 | tf_op jit(solution)/shard_map/ppermute | solution.py:283
  35.2 1.2 %collective-permute-start.14 = (f32[128,128]{1,0:T(8,128)S(1)}, f32[128,128]{1,0:T(8,128)S(1)}, u32[]{:S(2)}, u32[]{:S(2)}) collective-permute-start(f32[128,128]{1,0:T(8,128)S(1)} %add.77.refs_0_), channel_id=1, source_target_pairs={{0,2},{1,3},{2,0},{3,1},{4,6},{5,7},{6,4},{7,5},{8,10},{9,11},{10,... | collective-permute-start | bytes 196616 | tf_op jit(solution)/shard_map/ppermute | solution.py:283
  36.4 1.5 %collective-permute-done.8.refs_1_ = f32[128,128]{1,0:T(8,128)S(1)} collective-permute-done((f32[128,128]{1,0:T(8,128)S(1)}, f32[128,128]{1,0:T(8,128)S(1)}, u32[]{:S(2)}, u32[]{:S(2)}) %collective-permute-start.8) | collective-permute-done | bytes 65568 | tf_op jit(solution)/shard_map/ppermute | solution.py:283
  37.9 2.3 %third.4 = (f32[128,128]{1,0:T(8,128)S(1)}, f32[128,128]{1,0:T(8,128)S(1)}) custom-call(f32[2,32,128,128]{3,2,1,0:T(8,128)S(1)} %get-tuple-element.39.whole, bf16[2,48,256,128]{3,2,1,0:T(8,128)(2,1)S(1)} %get-tuple-element.41.upper, bf16[2,24,256,128]{3,2,1,0:T(8,128)(2,1)S(1)} %get-tuple-element.42.lower, ...), custom_call_target="tpu_custom_call" | custom-call | tf_op jit(solution)/shard_map/third/pallas_call | solution.py:440
  41.0 2.3 %third.5 = (f32[128,128]{1,0:T(8,128)S(1)}, f32[128,128]{1,0:T(8,128)S(1)}) custom-call(f32[2,32,128,128]{3,2,1,0:T(8,128)S(1)} %get-tuple-element.39.whole, bf16[2,48,256,128]{3,2,1,0:T(8,128)(2,1)S(1)} %get-tuple-element.41.upper, bf16[2,24,256,128]{3,2,1,0:T(8,128)(2,1)S(1)} %get-tuple-element.42.lower, ...), custom_call_target="tpu_custom_call" | custom-call | tf_op jit(solution)/shard_map/third/pallas_call | solution.py:440
  43.4 2.4 %collective-permute-start.15 = (f32[128,128]{1,0:T(8,128)S(1)}, f32[128,128]{1,0:T(8,128)S(1)}, u32[]{:S(2)}, u32[]{:S(2)}) collective-permute-start(f32[128,128]{1,0:T(8,128)S(1)} %get-tuple-element.60), channel_id=1, source_target_pairs={{0,4},{1,5},{2,3},{3,2},{4,0},{5,1},{6,7},{7,6},{8,12},{9,13},{10,... | collective-permute-start | bytes 196616 | tf_op jit(solution)/shard_map/ppermute | solution.py:283
  46.3 1.6 %collective-permute-start.10 = (f32[128,128]{1,0:T(8,128)S(1)}, f32[128,128]{1,0:T(8,128)S(1)}, u32[]{:S(2)}, u32[]{:S(2)}) collective-permute-start(f32[128,128]{1,0:T(8,128)S(1)} %add.73), channel_id=1, source_target_pairs={{0,1},{1,0},{2,6},{3,7},{4,5},{5,4},{6,2},{7,3},{8,9},{9,8},{10,14... | collective-permute-start | bytes 196616 | tf_op jit(solution)/shard_map/ppermute | solution.py:283
  47.9 1.6 %collective-permute-done.15 = f32[128,128]{1,0:T(8,128)S(1)} collective-permute-done((f32[128,128]{1,0:T(8,128)S(1)}, f32[128,128]{1,0:T(8,128)S(1)}, u32[]{:S(2)}, u32[]{:S(2)}) %collective-permute-start.15) | collective-permute-done | bytes 65568 | tf_op jit(solution)/shard_map/ppermute | solution.py:283
  50.7 1.6 %collective-permute-start.11 = (f32[128,128]{1,0:T(8,128)S(1)}, f32[128,128]{1,0:T(8,128)S(1)}, u32[]{:S(2)}, u32[]{:S(2)}) collective-permute-start(f32[128,128]{1,0:T(8,128)S(1)} %add.74), channel_id=1, source_target_pairs={{0,2},{1,3},{2,0},{3,1},{4,6},{5,7},{6,4},{7,5},{8,10},{9,11},{10,... | collective-permute-start | bytes 196616 | tf_op jit(solution)/shard_map/ppermute | solution.py:283
  52.3 1.6 %collective-permute-done.16 = f32[128,128]{1,0:T(8,128)S(1)} collective-permute-done((f32[128,128]{1,0:T(8,128)S(1)}, f32[128,128]{1,0:T(8,128)S(1)}, u32[]{:S(2)}, u32[]{:S(2)}) %collective-permute-start.16) | collective-permute-done | bytes 65568 | tf_op jit(solution)/shard_map/ppermute | solution.py:283
  53.9 2.0 %collective-permute-start.17 = (f32[128,128]{1,0:T(8,128)S(1)}, f32[128,128]{1,0:T(8,128)S(1)}, u32[]{:S(2)}, u32[]{:S(2)}) collective-permute-start(f32[128,128]{1,0:T(8,128)S(1)} %add.79), channel_id=1, source_target_pairs={{0,2},{1,3},{2,0},{3,1},{4,6},{5,7},{6,4},{7,5},{8,10},{9,11},{10,... | collective-permute-start | bytes 196616 | tf_op jit(solution)/shard_map/ppermute | solution.py:283
  55.9 2.3 %collective-permute-done.17 = f32[128,128]{1,0:T(8,128)S(1)} collective-permute-done((f32[128,128]{1,0:T(8,128)S(1)}, f32[128,128]{1,0:T(8,128)S(1)}, u32[]{:S(2)}, u32[]{:S(2)}) %collective-permute-start.17) | collective-permute-done | bytes 65568 | tf_op jit(solution)/shard_map/ppermute | solution.py:283
  58.3 1.2 %collective-permute-done.18 = f32[128,128]{1,0:T(8,128)S(1)} collective-permute-done((f32[128,128]{1,0:T(8,128)S(1)}, f32[128,128]{1,0:T(8,128)S(1)}, u32[]{:S(2)}, u32[]{:S(2)}) %collective-permute-start.18) | collective-permute-done | bytes 65568 | tf_op jit(solution)/shard_map/ppermute | solution.py:263
  59.6 1.3 %collective-permute-start.19 = (f32[128,128]{1,0:T(8,128)S(1)}, f32[128,128]{1,0:T(8,128)S(1)}, u32[]{:S(2)}, u32[]{:S(2)}) collective-permute-start(f32[128,128]{1,0:T(8,128)S(1)} %add.82), channel_id=1, source_target_pairs={{0,24},{8,16},{16,8},{24,0},{1,25},{9,17},{17,9},{25,1},{2,26},{10... | collective-permute-start | bytes 196616 | tf_op jit(solution)/shard_map/ppermute | solution.py:263
  60.9 2.8 %collective-permute-done.19 = f32[128,128]{1,0:T(8,128)S(1)} collective-permute-done((f32[128,128]{1,0:T(8,128)S(1)}, f32[128,128]{1,0:T(8,128)S(1)}, u32[]{:S(2)}, u32[]{:S(2)}) %collective-permute-start.19) | collective-permute-done | bytes 65568 | tf_op jit(solution)/shard_map/ppermute | solution.py:263
  63.7 1.9 %first.3 = (f32[80,128]{1,0:T(8,128)S(1)}, f32[80,128]{1,0:T(8,128)S(1)}, f32[80,128]{1,0:T(8,128)S(1)}) custom-call(f32[2,32,128,128]{3,2,1,0:T(8,128)S(1)} %get-tuple-element.43.whole.whole_t, bf16[2,48,256,128]{3,2,1,0:T(8,128)(2,1)S(1)} %get-tuple-element.44.upper.upper_t, bf16[2,24,256,128]{3,2,1,0:T(8,128)(2,1)S(1)} %get-tuple-element.45.lower.lower_t, ...), custom_call_target="tpu_custom_call" | custom-call | tf_op jit(solution)/shard_map/first/pallas_call | solution.py:405
  65.7 1.3 %collective-permute-start.22 = (f32[80,128]{1,0:T(8,128)S(1)}, f32[80,128]{1,0:T(8,128)S(1)}, u32[]{:S(2)}, u32[]{:S(2)}) collective-permute-start(f32[80,128]{1,0:T(8,128)S(1)} %get-tuple-element.61.order.refs_0_), channel_id=1, source_target_pairs={{0,24},{8,16},{16,8},{24,0},{1,25},{9,17},{17,9},{25,1},{2,26},{10... | collective-permute-start | bytes 122888 | tf_op jit(solution)/shard_map/ppermute | solution.py:263
  67.6 1.7 %collective-permute-done.22.refs_3_ = f32[80,128]{1,0:T(8,128)S(1)} collective-permute-done((f32[80,128]{1,0:T(8,128)S(1)}, f32[80,128]{1,0:T(8,128)S(1)}, u32[]{:S(2)}, u32[]{:S(2)}) %collective-permute-start.22) | collective-permute-done | bytes 40992 | tf_op jit(solution)/shard_map/ppermute | solution.py:263
  69.3 1.8 %collective-permute-done.21.refs_2_ = f32[80,128]{1,0:T(8,128)S(1)} collective-permute-done((f32[80,128]{1,0:T(8,128)S(1)}, f32[80,128]{1,0:T(8,128)S(1)}, u32[]{:S(2)}, u32[]{:S(2)}) %collective-permute-start.21) | collective-permute-done | bytes 40992 | tf_op jit(solution)/shard_map/ppermute | solution.py:263
  71.0 1.1 %second.4 = (f32[80,128]{1,0:T(8,128)S(1)}, f32[128,128]{1,0:T(8,128)S(1)}) custom-call(f32[2,32,128,128]{3,2,1,0:T(8,128)S(1)} %get-tuple-element.39.whole, bf16[2,48,256,128]{3,2,1,0:T(8,128)(2,1)S(1)} %get-tuple-element.41.upper, bf16[2,24,256,128]{3,2,1,0:T(8,128)(2,1)S(1)} %get-tuple-element.42.lower, bf16[128,80]{1,0:T(8,128)(2,1)S(1)} %get-tuple-element.48.col_hot_t, ...), custom_call_target="tpu_custom_call" | custom-call | tf_op jit(solution)/shard_map/second/pallas_call | solution.py:420
  72.1 2.1 %collective-permute-start.26 = (f32[128,128]{1,0:T(8,128)S(1)}, f32[128,128]{1,0:T(8,128)S(1)}, u32[]{:S(2)}, u32[]{:S(2)}) collective-permute-start(f32[128,128]{1,0:T(8,128)S(1)} %get-tuple-element.63.order), channel_id=1, source_target_pairs={{0,4},{1,5},{2,3},{3,2},{4,0},{5,1},{6,7},{7,6},{8,12},{9,13},{10,... | collective-permute-start | bytes 196616 | tf_op jit(solution)/shard_map/ppermute | solution.py:283
  74.2 1.1 %second.5 = (f32[80,128]{1,0:T(8,128)S(1)}, f32[128,128]{1,0:T(8,128)S(1)}) custom-call(f32[2,32,128,128]{3,2,1,0:T(8,128)S(1)} %get-tuple-element.39.whole, bf16[2,48,256,128]{3,2,1,0:T(8,128)(2,1)S(1)} %get-tuple-element.41.upper, bf16[2,24,256,128]{3,2,1,0:T(8,128)(2,1)S(1)} %get-tuple-element.42.lower, bf16[128,80]{1,0:T(8,128)(2,1)S(1)} %get-tuple-element.48.col_hot_t, ...), custom_call_target="tpu_custom_call" | custom-call | tf_op jit(solution)/shard_map/second/pallas_call | solution.py:420
  75.3 1.0 collective-permute-start.23
  76.3 1.1 collective-permute-done.26
  77.4 0.9 collective-permute-start.27
  78.3 2.6 %collective-permute-done.23 = f32[128,128]{1,0:T(8,128)S(1)} collective-permute-done((f32[128,128]{1,0:T(8,128)S(1)}, f32[128,128]{1,0:T(8,128)S(1)}, u32[]{:S(2)}, u32[]{:S(2)}) %collective-permute-start.23) | collective-permute-done | bytes 65568 | tf_op jit(solution)/shard_map/ppermute | solution.py:283
  80.9 1.3 %collective-permute-start.24 = (f32[128,128]{1,0:T(8,128)S(1)}, f32[128,128]{1,0:T(8,128)S(1)}, u32[]{:S(2)}, u32[]{:S(2)}) collective-permute-start(f32[128,128]{1,0:T(8,128)S(1)} %add.84), channel_id=1, source_target_pairs={{0,1},{1,0},{2,6},{3,7},{4,5},{5,4},{6,2},{7,3},{8,9},{9,8},{10,14... | collective-permute-start | bytes 196616 | tf_op jit(solution)/shard_map/ppermute | solution.py:283
  82.2 2.0 %collective-permute-start.28 = (f32[128,128]{1,0:T(8,128)S(1)}, f32[128,128]{1,0:T(8,128)S(1)}, u32[]{:S(2)}, u32[]{:S(2)}) collective-permute-start(f32[128,128]{1,0:T(8,128)S(1)} %add.87.refs_0_), channel_id=1, source_target_pairs={{0,2},{1,3},{2,0},{3,1},{4,6},{5,7},{6,4},{7,5},{8,10},{9,11},{10,... | collective-permute-start | bytes 196616 | tf_op jit(solution)/shard_map/ppermute | solution.py:283
  84.2 1.0 collective-permute-done.24
  85.3 1.2 %collective-permute-done.28.refs_1_ = f32[128,128]{1,0:T(8,128)S(1)} collective-permute-done((f32[128,128]{1,0:T(8,128)S(1)}, f32[128,128]{1,0:T(8,128)S(1)}, u32[]{:S(2)}, u32[]{:S(2)}) %collective-permute-start.28) | collective-permute-done | bytes 65568 | tf_op jit(solution)/shard_map/ppermute | solution.py:283
  86.5 2.3 %third.6 = (f32[16,128]{1,0:T(8,128)S(1)}, f32[128,128]{1,0:T(8,128)S(1)}) custom-call(f32[2,32,128,128]{3,2,1,0:T(8,128)S(1)} %get-tuple-element.39.whole, bf16[2,48,256,128]{3,2,1,0:T(8,128)(2,1)S(1)} %get-tuple-element.41.upper, bf16[2,24,256,128]{3,2,1,0:T(8,128)(2,1)S(1)} %get-tuple-element.42.lower, ...), custom_call_target="tpu_custom_call" | custom-call | tf_op jit(solution)/shard_map/third/pallas_call | solution.py:440
  89.6 2.3 %third.7 = (f32[16,128]{1,0:T(8,128)S(1)}, f32[8,2,16,128]{3,2,1,0:T(8,128)S(1)}) custom-call(f32[2,32,128,128]{3,2,1,0:T(8,128)S(1)} %get-tuple-element.39.whole, bf16[2,48,256,128]{3,2,1,0:T(8,128)(2,1)S(1)} %get-tuple-element.41.upper, bf16[2,24,256,128]{3,2,1,0:T(8,128)(2,1)S(1)} %get-tuple-element.42.lower, ...), custom_call_target="tpu_custom_call" | custom-call | tf_op jit(solution)/shard_map/third/pallas_call | solution.py:440
  91.9 10.5 %all_to_all.5 = f32[8,2,16,128]{3,2,1,0:T(8,128)S(1)} all-to-all(f32[8,2,16,128]{3,2,1,0:T(8,128)S(1)} %get-tuple-element.73), channel_id=1, replica_groups=mesh['scen'=4,'vox'=8] {'vox'}, dimensions={0} | all-to-all | bytes 262144 | tf_op jit(solution)/shard_map/all_to_all | solution.py:464
  102.5 1.6 %collective-permute-start.30 = (f32[16,128]{1,0:T(8,128)S(1)}, f32[16,128]{1,0:T(8,128)S(1)}, u32[]{:S(2)}, u32[]{:S(2)}) collective-permute-start(f32[16,128]{1,0:T(8,128)S(1)} %fusion.4.order), channel_id=1, source_target_pairs={{0,16},{8,24},{16,0},{24,8},{1,17},{9,25},{17,1},{25,9},{2,18},{10... | collective-permute-start | bytes 24584 | tf_op jit(solution)/shard_map/ppermute | solution.py:263
  104.4 0.9 place.1
  (50 shorter events, 8.4 us)
Async XLA Ops:
  0.6 7.8 %collective-permute-start.2 = (f32[16,128]{1,0:T(8,128)}, f32[16,128]{1,0:T(8,128)S(1)}, u32[]{:S(2)}, u32[]{:S(2)}) collective-permute-start(f32[16,128]{1,0:T(8,128)} %bitcast.28), channel_id=1, source_target_pairs={{0,11},{1,10},{2,9},{3,8},{4,15},{5,14},{6,13},{7,12},{8,3},{9,2},... | collective-permute-start | bytes 24584 | tf_op jit(solution)/shard_map/ppermute | solution.py:307
  4.1 4.3 %collective-permute-start.1 = (f32[16,128]{1,0:T(8,128)}, f32[16,128]{1,0:T(8,128)S(1)}, u32[]{:S(2)}, u32[]{:S(2)}) collective-permute-start(f32[16,128]{1,0:T(8,128)} %bitcast.29), channel_id=1, source_target_pairs={{0,10},{1,11},{2,8},{3,9},{4,14},{5,15},{6,12},{7,13},{8,2},{9,3},... | collective-permute-start | bytes 24584 | tf_op jit(solution)/shard_map/ppermute | solution.py:307
  4.8 3.6 %collective-permute-start = (f32[16,128]{1,0:T(8,128)}, f32[16,128]{1,0:T(8,128)S(1)}, u32[]{:S(2)}, u32[]{:S(2)}) collective-permute-start(f32[16,128]{1,0:T(8,128)} %bitcast.30), channel_id=1, source_target_pairs={{0,9},{1,8},{2,11},{3,10},{4,13},{5,12},{6,15},{7,14},{8,1},{9,0},... | collective-permute-start | bytes 24584 | tf_op jit(solution)/shard_map/ppermute | solution.py:307
  8.4 6.3 %collective-permute-start.3 = (f32[64,128]{1,0:T(8,128)S(1)}, f32[64,128]{1,0:T(8,128)S(1)}, u32[]{:S(2)}, u32[]{:S(2)}) collective-permute-start(f32[64,128]{1,0:T(8,128)S(1)} %collect.1.order.mine), channel_id=1, source_target_pairs={{0,12},{1,13},{2,14},{3,15},{4,8},{5,9},{6,10},{7,11},{8,4},{9,5},... | collective-permute-start | bytes 98312 | tf_op jit(solution)/shard_map/ppermute | solution.py:307
  16.7 1.3 %collective-permute-start.4 = (f32[80,128]{1,0:T(8,128)S(1)}, f32[80,128]{1,0:T(8,128)S(1)}, u32[]{:S(2)}, u32[]{:S(2)}) collective-permute-start(f32[80,128]{1,0:T(8,128)S(1)} %get-tuple-element.50.order), channel_id=1, source_target_pairs={{0,8},{8,0},{16,24},{24,16},{1,9},{9,1},{17,25},{25,17},{2,10},{10... | collective-permute-start | bytes 122888 | tf_op jit(solution)/shard_map/ppermute | solution.py:263
  18.0 3.6 %collective-permute-start.5 = (f32[80,128]{1,0:T(8,128)S(1)}, f32[80,128]{1,0:T(8,128)S(1)}, u32[]{:S(2)}, u32[]{:S(2)}) collective-permute-start(f32[80,128]{1,0:T(8,128)S(1)} %log_add_fusion.refs_0_), channel_id=1, source_target_pairs={{0,24},{8,16},{16,8},{24,0},{1,25},{9,17},{17,9},{25,1},{2,26},{10... | collective-permute-start | bytes 122888 | tf_op jit(solution)/shard_map/ppermute | solution.py:263
  23.4 5.8 %collective-permute-start.6 = (f32[128,128]{1,0:T(8,128)S(1)}, f32[128,128]{1,0:T(8,128)S(1)}, u32[]{:S(2)}, u32[]{:S(2)}) collective-permute-start(f32[128,128]{1,0:T(8,128)S(1)} %get-tuple-element.53), channel_id=1, source_target_pairs={{0,4},{1,5},{2,3},{3,2},{4,0},{5,1},{6,7},{7,6},{8,12},{9,13},{10,... | collective-permute-start | bytes 196616 | tf_op jit(solution)/shard_map/ppermute | solution.py:283
  24.0 6.7 %collective-permute-start.12 = (f32[128,128]{1,0:T(8,128)S(1)}, f32[128,128]{1,0:T(8,128)S(1)}, u32[]{:S(2)}, u32[]{:S(2)}) collective-permute-start(f32[128,128]{1,0:T(8,128)S(1)} %get-tuple-element.57), channel_id=1, source_target_pairs={{0,4},{1,5},{2,3},{3,2},{4,0},{5,1},{6,7},{7,6},{8,12},{9,13},{10,... | collective-permute-start | bytes 196616 | tf_op jit(solution)/shard_map/ppermute | solution.py:283
  29.2 4.3 %collective-permute-start.7 = (f32[128,128]{1,0:T(8,128)S(1)}, f32[128,128]{1,0:T(8,128)S(1)}, u32[]{:S(2)}, u32[]{:S(2)}) collective-permute-start(f32[128,128]{1,0:T(8,128)S(1)} %add.71), channel_id=1, source_target_pairs={{0,1},{1,0},{2,6},{3,7},{4,5},{5,4},{6,2},{7,3},{8,9},{9,8},{10,14... | collective-permute-start | bytes 196616 | tf_op jit(solution)/shard_map/ppermute | solution.py:283
  30.8 4.4 %collective-permute-start.13 = (f32[128,128]{1,0:T(8,128)S(1)}, f32[128,128]{1,0:T(8,128)S(1)}, u32[]{:S(2)}, u32[]{:S(2)}) collective-permute-start(f32[128,128]{1,0:T(8,128)S(1)} %add.76), channel_id=1, source_target_pairs={{0,1},{1,0},{2,6},{3,7},{4,5},{5,4},{6,2},{7,3},{8,9},{9,8},{10,14... | collective-permute-start | bytes 196616 | tf_op jit(solution)/shard_map/ppermute | solution.py:283
  33.5 4.3 %collective-permute-start.8 = (f32[128,128]{1,0:T(8,128)S(1)}, f32[128,128]{1,0:T(8,128)S(1)}, u32[]{:S(2)}, u32[]{:S(2)}) collective-permute-start(f32[128,128]{1,0:T(8,128)S(1)} %add.72.refs_0_), channel_id=1, source_target_pairs={{0,2},{1,3},{2,0},{3,1},{4,6},{5,7},{6,4},{7,5},{8,10},{9,11},{10,... | collective-permute-start | bytes 196616 | tf_op jit(solution)/shard_map/ppermute | solution.py:283
  35.2 5.9 %collective-permute-start.14 = (f32[128,128]{1,0:T(8,128)S(1)}, f32[128,128]{1,0:T(8,128)S(1)}, u32[]{:S(2)}, u32[]{:S(2)}) collective-permute-start(f32[128,128]{1,0:T(8,128)S(1)} %add.77.refs_0_), channel_id=1, source_target_pairs={{0,2},{1,3},{2,0},{3,1},{4,6},{5,7},{6,4},{7,5},{8,10},{9,11},{10,... | collective-permute-start | bytes 196616 | tf_op jit(solution)/shard_map/ppermute | solution.py:283
  40.2 6.1 %collective-permute-start.9 = (f32[128,128]{1,0:T(8,128)S(1)}, f32[128,128]{1,0:T(8,128)S(1)}, u32[]{:S(2)}, u32[]{:S(2)}) collective-permute-start(f32[128,128]{1,0:T(8,128)S(1)} %get-tuple-element.56), channel_id=1, source_target_pairs={{0,4},{1,5},{2,3},{3,2},{4,0},{5,1},{6,7},{7,6},{8,12},{9,13},{10,... | collective-permute-start | bytes 196616 | tf_op jit(solution)/shard_map/ppermute | solution.py:283
  43.4 6.1 %collective-permute-start.15 = (f32[128,128]{1,0:T(8,128)S(1)}, f32[128,128]{1,0:T(8,128)S(1)}, u32[]{:S(2)}, u32[]{:S(2)}) collective-permute-start(f32[128,128]{1,0:T(8,128)S(1)} %get-tuple-element.60), channel_id=1, source_target_pairs={{0,4},{1,5},{2,3},{3,2},{4,0},{5,1},{6,7},{7,6},{8,12},{9,13},{10,... | collective-permute-start | bytes 196616 | tf_op jit(solution)/shard_map/ppermute | solution.py:283
  46.3 4.3 %collective-permute-start.10 = (f32[128,128]{1,0:T(8,128)S(1)}, f32[128,128]{1,0:T(8,128)S(1)}, u32[]{:S(2)}, u32[]{:S(2)}) collective-permute-start(f32[128,128]{1,0:T(8,128)S(1)} %add.73), channel_id=1, source_target_pairs={{0,1},{1,0},{2,6},{3,7},{4,5},{5,4},{6,2},{7,3},{8,9},{9,8},{10,14... | collective-permute-start | bytes 196616 | tf_op jit(solution)/shard_map/ppermute | solution.py:283
  49.5 4.3 %collective-permute-start.16 = (f32[128,128]{1,0:T(8,128)S(1)}, f32[128,128]{1,0:T(8,128)S(1)}, u32[]{:S(2)}, u32[]{:S(2)}) collective-permute-start(f32[128,128]{1,0:T(8,128)S(1)} %add.78), channel_id=1, source_target_pairs={{0,1},{1,0},{2,6},{3,7},{4,5},{5,4},{6,2},{7,3},{8,9},{9,8},{10,14... | collective-permute-start | bytes 196616 | tf_op jit(solution)/shard_map/ppermute | solution.py:283
  50.7 5.2 %collective-permute-start.11 = (f32[128,128]{1,0:T(8,128)S(1)}, f32[128,128]{1,0:T(8,128)S(1)}, u32[]{:S(2)}, u32[]{:S(2)}) collective-permute-start(f32[128,128]{1,0:T(8,128)S(1)} %add.74), channel_id=1, source_target_pairs={{0,2},{1,3},{2,0},{3,1},{4,6},{5,7},{6,4},{7,5},{8,10},{9,11},{10,... | collective-permute-start | bytes 196616 | tf_op jit(solution)/shard_map/ppermute | solution.py:283
  53.9 4.3 %collective-permute-start.17 = (f32[128,128]{1,0:T(8,128)S(1)}, f32[128,128]{1,0:T(8,128)S(1)}, u32[]{:S(2)}, u32[]{:S(2)}) collective-permute-start(f32[128,128]{1,0:T(8,128)S(1)} %add.79), channel_id=1, source_target_pairs={{0,2},{1,3},{2,0},{3,1},{4,6},{5,7},{6,4},{7,5},{8,10},{9,11},{10,... | collective-permute-start | bytes 196616 | tf_op jit(solution)/shard_map/ppermute | solution.py:283
  58.2 1.3 %collective-permute-start.18 = (f32[128,128]{1,0:T(8,128)S(1)}, f32[128,128]{1,0:T(8,128)S(1)}, u32[]{:S(2)}, u32[]{:S(2)}) collective-permute-start(f32[128,128]{1,0:T(8,128)S(1)} %maximum_add_fusion), channel_id=1, source_target_pairs={{0,8},{8,0},{16,24},{24,16},{1,9},{9,1},{17,25},{25,17},{2,10},{10... | collective-permute-start | bytes 196616 | tf_op jit(solution)/shard_map/ppermute | solution.py:263
  59.6 4.1 %collective-permute-start.19 = (f32[128,128]{1,0:T(8,128)S(1)}, f32[128,128]{1,0:T(8,128)S(1)}, u32[]{:S(2)}, u32[]{:S(2)}) collective-permute-start(f32[128,128]{1,0:T(8,128)S(1)} %add.82), channel_id=1, source_target_pairs={{0,24},{8,16},{16,8},{24,0},{1,25},{9,17},{17,9},{25,1},{2,26},{10... | collective-permute-start | bytes 196616 | tf_op jit(solution)/shard_map/ppermute | solution.py:263
  65.7 3.6 %collective-permute-start.22 = (f32[80,128]{1,0:T(8,128)S(1)}, f32[80,128]{1,0:T(8,128)S(1)}, u32[]{:S(2)}, u32[]{:S(2)}) collective-permute-start(f32[80,128]{1,0:T(8,128)S(1)} %get-tuple-element.61.order.refs_0_), channel_id=1, source_target_pairs={{0,24},{8,16},{16,8},{24,0},{1,25},{9,17},{17,9},{25,1},{2,26},{10... | collective-permute-start | bytes 122888 | tf_op jit(solution)/shard_map/ppermute | solution.py:263
  67.0 4.0 %collective-permute-start.21 = (f32[80,128]{1,0:T(8,128)S(1)}, f32[80,128]{1,0:T(8,128)S(1)}, u32[]{:S(2)}, u32[]{:S(2)}) collective-permute-start(f32[80,128]{1,0:T(8,128)S(1)} %get-tuple-element.61.order.refs_0_), channel_id=1, source_target_pairs={{0,16},{8,24},{16,0},{24,8},{1,17},{9,25},{17,1},{25,9},{2,18},{10... | collective-permute-start | bytes 122888 | tf_op jit(solution)/shard_map/ppermute | solution.py:263
  67.5 3.5 %collective-permute-start.20 = (f32[80,128]{1,0:T(8,128)S(1)}, f32[80,128]{1,0:T(8,128)S(1)}, u32[]{:S(2)}, u32[]{:S(2)}) collective-permute-start(f32[80,128]{1,0:T(8,128)S(1)} %get-tuple-element.61.order.refs_0_), channel_id=1, source_target_pairs={{0,8},{8,0},{16,24},{24,16},{1,9},{9,1},{17,25},{25,17},{2,10},{10... | collective-permute-start | bytes 122888 | tf_op jit(solution)/shard_map/ppermute | solution.py:263
  72.1 5.2 %collective-permute-start.26 = (f32[128,128]{1,0:T(8,128)S(1)}, f32[128,128]{1,0:T(8,128)S(1)}, u32[]{:S(2)}, u32[]{:S(2)}) collective-permute-start(f32[128,128]{1,0:T(8,128)S(1)} %get-tuple-element.63.order), channel_id=1, source_target_pairs={{0,4},{1,5},{2,3},{3,2},{4,0},{5,1},{6,7},{7,6},{8,12},{9,13},{10,... | collective-permute-start | bytes 196616 | tf_op jit(solution)/shard_map/ppermute | solution.py:283
  75.3 5.5 %collective-permute-start.23 = (f32[128,128]{1,0:T(8,128)S(1)}, f32[128,128]{1,0:T(8,128)S(1)}, u32[]{:S(2)}, u32[]{:S(2)}) collective-permute-start(f32[128,128]{1,0:T(8,128)S(1)} %get-tuple-element.65), channel_id=1, source_target_pairs={{0,4},{1,5},{2,3},{3,2},{4,0},{5,1},{6,7},{7,6},{8,12},{9,13},{10,... | collective-permute-start | bytes 196616 | tf_op jit(solution)/shard_map/ppermute | solution.py:283
  77.4 4.8 %collective-permute-start.27 = (f32[128,128]{1,0:T(8,128)S(1)}, f32[128,128]{1,0:T(8,128)S(1)}, u32[]{:S(2)}, u32[]{:S(2)}) collective-permute-start(f32[128,128]{1,0:T(8,128)S(1)} %add.86), channel_id=1, source_target_pairs={{0,1},{1,0},{2,6},{3,7},{4,5},{5,4},{6,2},{7,3},{8,9},{9,8},{10,14... | collective-permute-start | bytes 196616 | tf_op jit(solution)/shard_map/ppermute | solution.py:283
  80.9 4.3 %collective-permute-start.24 = (f32[128,128]{1,0:T(8,128)S(1)}, f32[128,128]{1,0:T(8,128)S(1)}, u32[]{:S(2)}, u32[]{:S(2)}) collective-permute-start(f32[128,128]{1,0:T(8,128)S(1)} %add.84), channel_id=1, source_target_pairs={{0,1},{1,0},{2,6},{3,7},{4,5},{5,4},{6,2},{7,3},{8,9},{9,8},{10,14... | collective-permute-start | bytes 196616 | tf_op jit(solution)/shard_map/ppermute | solution.py:283
  82.2 4.3 %collective-permute-start.28 = (f32[128,128]{1,0:T(8,128)S(1)}, f32[128,128]{1,0:T(8,128)S(1)}, u32[]{:S(2)}, u32[]{:S(2)}) collective-permute-start(f32[128,128]{1,0:T(8,128)S(1)} %add.87.refs_0_), channel_id=1, source_target_pairs={{0,2},{1,3},{2,0},{3,1},{4,6},{5,7},{6,4},{7,5},{8,10},{9,11},{10,... | collective-permute-start | bytes 196616 | tf_op jit(solution)/shard_map/ppermute | solution.py:283
  85.2 4.3 %collective-permute-start.25 = (f32[128,128]{1,0:T(8,128)S(1)}, f32[128,128]{1,0:T(8,128)S(1)}, u32[]{:S(2)}, u32[]{:S(2)}) collective-permute-start(f32[128,128]{1,0:T(8,128)S(1)} %add.85.refs_0_), channel_id=1, source_target_pairs={{0,2},{1,3},{2,0},{3,1},{4,6},{5,7},{6,4},{7,5},{8,10},{9,11},{10,... | collective-permute-start | bytes 196616 | tf_op jit(solution)/shard_map/ppermute | solution.py:283
  102.4 3.2 %collective-permute-start.31 = (f32[16,128]{1,0:T(8,128)S(1)}, f32[16,128]{1,0:T(8,128)S(1)}, u32[]{:S(2)}, u32[]{:S(2)}) collective-permute-start(f32[16,128]{1,0:T(8,128)S(1)} %fusion.4.order), channel_id=1, source_target_pairs={{0,24},{8,16},{16,8},{24,0},{1,25},{9,17},{17,9},{25,1},{2,26},{10... | collective-permute-start | bytes 24584 | tf_op jit(solution)/shard_map/ppermute | solution.py:263
  102.5 3.7 %collective-permute-start.30 = (f32[16,128]{1,0:T(8,128)S(1)}, f32[16,128]{1,0:T(8,128)S(1)}, u32[]{:S(2)}, u32[]{:S(2)}) collective-permute-start(f32[16,128]{1,0:T(8,128)S(1)} %fusion.4.order), channel_id=1, source_target_pairs={{0,16},{8,24},{16,0},{24,8},{1,17},{9,25},{17,1},{25,9},{2,18},{10... | collective-permute-start | bytes 24584 | tf_op jit(solution)/shard_map/ppermute | solution.py:263
  104.1 2.1 %collective-permute-start.29 = (f32[16,128]{1,0:T(8,128)S(1)}, f32[16,128]{1,0:T(8,128)S(1)}, u32[]{:S(2)}, u32[]{:S(2)}) collective-permute-start(f32[16,128]{1,0:T(8,128)S(1)} %fusion.4.order), channel_id=1, source_target_pairs={{0,8},{8,0},{16,24},{24,16},{1,9},{9,1},{17,25},{25,17},{2,10},{10... | collective-permute-start | bytes 24584 | tf_op jit(solution)/shard_map/ppermute | solution.py:263

commit v12 on v10

--- a/solution.py
+++ b/solution.py
@@ -81,8 +81,8 @@
             for u in range(2):
                 k = kept + 2 * m + u
                 main = jnp.dot(stacks[u], upper[s, 2 * m + u], preferred_element_type=F32)
-                total = main[:8] + rest[8 * u : 8 * u + 8]
-                rows[n, k : k + 1, :] = jnp.sum(total, axis=0, keepdims=True)
+                total = main[0:1] + rest[8 * u : 8 * u + 1]
+                rows[n, k : k + 1, :] = total + main[1:2] + main[2:3]
 
     order = [((k + 0.5) / kept, on_vector_unit, k) for k in range(kept)]
     order += [((m + 0.5) / pairs, on_matrix_unit, m) for m in range(pairs)]

time: 107 us -> 107 us (level)
  no operation moved by 1% of the time
where the time goes in v12:
time: 107 us; the launch traced here: 106 us
  starting transfers between devices  40.3 us (38%)
  waiting for transfers between devices  29.3 us (27%)
  Pallas kernels  24.2 us (23%)
  blocking collectives  10.3 us (10%)
  between operations  1.51 us (1%)
    ppermute x18, starting transfers between devices, reduce_vox(): lax.ppermute(x, 'vox', [(v, v ^ pair[(v & steps[-2]) // steps[-2]]) for v...  26.1 us
    ppermute x18, waiting for transfers between devices, reduce_vox(): lax.ppermute(x, 'vox', [(v, v ^ pair[(v & steps[-2]) // steps[-2]]) for v...  17.5 us
    ppermute x11, waiting for transfers between devices, swap(): lax.ppermute(x, axis, [(i, i ^ bit) for i in range(lax.axis_size(axis))])  11.7 us
    all_to_all x1, blocking collectives, body(): lax.all_to_all(gradient, 'vox', split_axis=0, concat_axis=0, tiled=True)  10.3 us
    pallas_call x4, Pallas kernels, body(): pl.pallas_call(functools.partial(third_kernel, group), name='third', out_...  9.32 us
    ppermute x4, starting transfers between devices, swap_both(): return lax.ppermute(x, ('scen', 'vox'), pairs)  7.1 us
    ppermute x11, starting transfers between devices, swap(): lax.ppermute(x, axis, [(i, i ^ bit) for i in range(lax.axis_size(axis))])  7.08 us
    pallas_call x3, Pallas kernels, body(): pl.pallas_call(functools.partial(second_kernel, group), name='second', ou...  3.96 us
  transfers between devices with their start and end apart: 33, of which 22 were waited for; matrix products, arithmetic and copies ran while one was open for 0% of the time, Pallas kernels for 14%

profile of v12, /device:TPU:0, one launch (start us, length us, event | category | flops | bytes accessed | tf_op | source)
XLA Modules:
  0.0 106.4 jit_solution(10922011007266488637)
XLA Ops:
  0.6 3.5 %collective-permute-start.2 = (f32[16,128]{1,0:T(8,128)}, f32[16,128]{1,0:T(8,128)S(1)}, u32[]{:S(2)}, u32[]{:S(2)}) collective-permute-start(f32[16,128]{1,0:T(8,128)} %bitcast.28), channel_id=1, source_target_pairs={{0,11},{1,10},{2,9},{3,8},{4,15},{5,14},{6,13},{7,12},{8,3},{9,2},... | collective-permute-start | bytes 24584 | tf_op jit(solution)/shard_map/ppermute | solution.py:307
  5.7 2.7 %hot.1 = (bf16[80,128]{1,0:T(8,128)(2,1)S(1)}, bf16[128,80]{1,0:T(8,128)(2,1)S(1)}, bf16[80,80]{1,0:T(8,128)(2,1)S(1)}, bf16[128,80]{1,0:T(8,128)(2,1)S(1)}, f32...) custom-call(s32[2,80]{1,0:T(2,128)} %bitcast.32, ...), custom_call_target="tpu_custom_call" | custom-call | bytes 7864320 | tf_op jit(solution)/shard_map/hot/pallas_call | solution.py:331
  8.4 2.7 %collective-permute-start.3 = (f32[64,128]{1,0:T(8,128)S(1)}, f32[64,128]{1,0:T(8,128)S(1)}, u32[]{:S(2)}, u32[]{:S(2)}) collective-permute-start(f32[64,128]{1,0:T(8,128)S(1)} %collect.1.order.mine), channel_id=1, source_target_pairs={{0,12},{1,13},{2,14},{3,15},{4,8},{5,9},{6,10},{7,11},{8,4},{9,5},... | collective-permute-start | bytes 98312 | tf_op jit(solution)/shard_map/ppermute | solution.py:307
  11.2 3.6 %split.1 = (bf16[2,48,256,128]{3,2,1,0:T(8,128)(2,1)S(1)}, bf16[2,48,256,128]{3,2,1,0:T(8,128)(2,1)S(1)}, bf16[2,24,256,128]{3,2,1,0:T(8,128)(2,1)S(1)}, bf16[2,24,256,128]{3,2,1,0:T(8,128)(2,1)S(1)}) custom-call(f32[2,80,128,128]{3,2,1,0:T(8,128)} %source.3, f32[64,128]{1,0:T(8,128)S(1)} %collect.1.order.mine), custom_call_target="tpu_custom_call" | custom-call | bytes 13107200 | tf_op jit(solution)/shard_map/split/pallas_call | solution.py:386
  14.8 1.9 %first.2 = (f32[80,128]{1,0:T(8,128)S(1)}, f32[80,128]{1,0:T(8,128)S(1)}, f32[80,128]{1,0:T(8,128)S(1)}) custom-call(f32[2,32,128,128]{3,2,1,0:T(8,128)S(1)} %get-tuple-element.43.whole.whole_t, bf16[2,48,256,128]{3,2,1,0:T(8,128)(2,1)S(1)} %get-tuple-element.44.upper.upper_t, bf16[2,24,256,128]{3,2,1,0:T(8,128)(2,1)S(1)} %get-tuple-element.45.lower.lower_t, ...), custom_call_target="tpu_custom_call" | custom-call | tf_op jit(solution)/shard_map/first/pallas_call | solution.py:405
  16.6 1.2 %collective-permute-start.6 = (f32[80,128]{1,0:T(8,128)S(1)}, f32[80,128]{1,0:T(8,128)S(1)}, u32[]{:S(2)}, u32[]{:S(2)}) collective-permute-start(f32[80,128]{1,0:T(8,128)S(1)} %get-tuple-element.50.order.refs_0_), channel_id=1, source_target_pairs={{0,24},{8,16},{16,8},{24,0},{1,25},{9,17},{17,9},{25,1},{2,26},{10... | collective-permute-start | bytes 122888 | tf_op jit(solution)/shard_map/ppermute | solution.py:263
  18.6 1.8 %collective-permute-done.6.refs_3_ = f32[80,128]{1,0:T(8,128)S(1)} collective-permute-done((f32[80,128]{1,0:T(8,128)S(1)}, f32[80,128]{1,0:T(8,128)S(1)}, u32[]{:S(2)}, u32[]{:S(2)}) %collective-permute-start.6) | collective-permute-done | bytes 40992 | tf_op jit(solution)/shard_map/ppermute | solution.py:263
  20.3 1.5 %collective-permute-done.5.refs_2_ = f32[80,128]{1,0:T(8,128)S(1)} collective-permute-done((f32[80,128]{1,0:T(8,128)S(1)}, f32[80,128]{1,0:T(8,128)S(1)}, u32[]{:S(2)}, u32[]{:S(2)}) %collective-permute-start.5) | collective-permute-done | bytes 40992 | tf_op jit(solution)/shard_map/ppermute | solution.py:263
  21.9 1.7 %second.3 = (f32[80,128]{1,0:T(8,128)S(1)}, f32[80,128]{1,0:T(8,128)S(1)}, f32[128,128]{1,0:T(8,128)S(1)}, f32[128,128]{1,0:T(8,128)S(1)}) custom-call(f32[2,32,128,128]{3,2,1,0:T(8,128)S(1)} %get-tuple-element.39.whole, bf16[2,48,256,128]{3,2,1,0:T(8,128)(2,1)S(1)} %get-tuple-element.41.upper, bf16[2,24,256,128]{3,2,1,0:T(8,128)(2,1)S(1)} %get-tuple-element.42.lower, ...), custom_call_target="tpu_custom_call" | custom-call | tf_op jit(solution)/shard_map/second/pallas_call | solution.py:420
  23.6 1.0 collective-permute-start.7
  24.7 1.9 %collective-permute-start.13 = (f32[128,128]{1,0:T(8,128)S(1)}, f32[128,128]{1,0:T(8,128)S(1)}, u32[]{:S(2)}, u32[]{:S(2)}) collective-permute-start(f32[128,128]{1,0:T(8,128)S(1)} %get-tuple-element.57), channel_id=1, source_target_pairs={{0,4},{1,5},{2,3},{3,2},{4,0},{5,1},{6,7},{7,6},{8,12},{9,13},{10,... | collective-permute-start | bytes 196616 | tf_op jit(solution)/shard_map/ppermute | solution.py:283
  26.6 2.2 %collective-permute-done.7 = f32[128,128]{1,0:T(8,128)S(1)} collective-permute-done((f32[128,128]{1,0:T(8,128)S(1)}, f32[128,128]{1,0:T(8,128)S(1)}, u32[]{:S(2)}, u32[]{:S(2)}) %collective-permute-start.7) | collective-permute-done | bytes 65568 | tf_op jit(solution)/shard_map/ppermute | solution.py:283
  28.9 1.7 %collective-permute-start.8 = (f32[128,128]{1,0:T(8,128)S(1)}, f32[128,128]{1,0:T(8,128)S(1)}, u32[]{:S(2)}, u32[]{:S(2)}) collective-permute-start(f32[128,128]{1,0:T(8,128)S(1)} %add.63), channel_id=1, source_target_pairs={{0,1},{1,0},{2,6},{3,7},{4,5},{5,4},{6,2},{7,3},{8,9},{9,8},{10,14... | collective-permute-start | bytes 196616 | tf_op jit(solution)/shard_map/ppermute | solution.py:283
  30.6 0.8 collective-permute-start.14
  31.4 1.8 %collective-permute-done.8 = f32[128,128]{1,0:T(8,128)S(1)} collective-permute-done((f32[128,128]{1,0:T(8,128)S(1)}, f32[128,128]{1,0:T(8,128)S(1)}, u32[]{:S(2)}, u32[]{:S(2)}) %collective-permute-start.8) | collective-permute-done | bytes 65568 | tf_op jit(solution)/shard_map/ppermute | solution.py:283
  33.2 2.8 %collective-permute-start.9 = (f32[128,128]{1,0:T(8,128)S(1)}, f32[128,128]{1,0:T(8,128)S(1)}, u32[]{:S(2)}, u32[]{:S(2)}) collective-permute-start(f32[128,128]{1,0:T(8,128)S(1)} %add.64.refs_0_), channel_id=1, source_target_pairs={{0,2},{1,3},{2,0},{3,1},{4,6},{5,7},{6,4},{7,5},{8,10},{9,11},{10,... | collective-permute-start | bytes 196616 | tf_op jit(solution)/shard_map/ppermute | solution.py:283
  36.7 1.5 %collective-permute-done.9.refs_1_ = f32[128,128]{1,0:T(8,128)S(1)} collective-permute-done((f32[128,128]{1,0:T(8,128)S(1)}, f32[128,128]{1,0:T(8,128)S(1)}, u32[]{:S(2)}, u32[]{:S(2)}) %collective-permute-start.9) | collective-permute-done | bytes 65568 | tf_op jit(solution)/shard_map/ppermute | solution.py:283
  38.2 2.3 %third.4 = (f32[128,128]{1,0:T(8,128)S(1)}, f32[128,128]{1,0:T(8,128)S(1)}) custom-call(f32[2,32,128,128]{3,2,1,0:T(8,128)S(1)} %get-tuple-element.39.whole, bf16[2,48,256,128]{3,2,1,0:T(8,128)(2,1)S(1)} %get-tuple-element.41.upper, bf16[2,24,256,128]{3,2,1,0:T(8,128)(2,1)S(1)} %get-tuple-element.42.lower, ...), custom_call_target="tpu_custom_call" | custom-call | tf_op jit(solution)/shard_map/third/pallas_call | solution.py:440
  40.5 1.1 %collective-permute-start.10 = (f32[128,128]{1,0:T(8,128)S(1)}, f32[128,128]{1,0:T(8,128)S(1)}, u32[]{:S(2)}, u32[]{:S(2)}) collective-permute-start(f32[128,128]{1,0:T(8,128)S(1)} %get-tuple-element.56), channel_id=1, source_target_pairs={{0,4},{1,5},{2,3},{3,2},{4,0},{5,1},{6,7},{7,6},{8,12},{9,13},{10,... | collective-permute-start | bytes 196616 | tf_op jit(solution)/shard_map/ppermute | solution.py:283
  41.6 2.4 %third.5 = (f32[128,128]{1,0:T(8,128)S(1)}, f32[128,128]{1,0:T(8,128)S(1)}) custom-call(f32[2,32,128,128]{3,2,1,0:T(8,128)S(1)} %get-tuple-element.39.whole, bf16[2,48,256,128]{3,2,1,0:T(8,128)(2,1)S(1)} %get-tuple-element.41.upper, bf16[2,24,256,128]{3,2,1,0:T(8,128)(2,1)S(1)} %get-tuple-element.42.lower, ...), custom_call_target="tpu_custom_call" | custom-call | tf_op jit(solution)/shard_map/third/pallas_call | solution.py:440
  44.0 2.0 %collective-permute-start.16 = (f32[128,128]{1,0:T(8,128)S(1)}, f32[128,128]{1,0:T(8,128)S(1)}, u32[]{:S(2)}, u32[]{:S(2)}) collective-permute-start(f32[128,128]{1,0:T(8,128)S(1)} %get-tuple-element.60), channel_id=1, source_target_pairs={{0,4},{1,5},{2,3},{3,2},{4,0},{5,1},{6,7},{7,6},{8,12},{9,13},{10,... | collective-permute-start | bytes 196616 | tf_op jit(solution)/shard_map/ppermute | solution.py:283
  46.4 1.3 %collective-permute-start.11 = (f32[128,128]{1,0:T(8,128)S(1)}, f32[128,128]{1,0:T(8,128)S(1)}, u32[]{:S(2)}, u32[]{:S(2)}) collective-permute-start(f32[128,128]{1,0:T(8,128)S(1)} %add.65), channel_id=1, source_target_pairs={{0,1},{1,0},{2,6},{3,7},{4,5},{5,4},{6,2},{7,3},{8,9},{9,8},{10,14... | collective-permute-start | bytes 196616 | tf_op jit(solution)/shard_map/ppermute | solution.py:283
  47.7 1.7 %collective-permute-done.16 = f32[128,128]{1,0:T(8,128)S(1)} collective-permute-done((f32[128,128]{1,0:T(8,128)S(1)}, f32[128,128]{1,0:T(8,128)S(1)}, u32[]{:S(2)}, u32[]{:S(2)}) %collective-permute-start.16) | collective-permute-done | bytes 65568 | tf_op jit(solution)/shard_map/ppermute | solution.py:283
  49.4 1.1 %collective-permute-start.17 = (f32[128,128]{1,0:T(8,128)S(1)}, f32[128,128]{1,0:T(8,128)S(1)}, u32[]{:S(2)}, u32[]{:S(2)}) collective-permute-start(f32[128,128]{1,0:T(8,128)S(1)} %add.70), channel_id=1, source_target_pairs={{0,1},{1,0},{2,6},{3,7},{4,5},{5,4},{6,2},{7,3},{8,9},{9,8},{10,14... | collective-permute-start | bytes 196616 | tf_op jit(solution)/shard_map/ppermute | solution.py:283
  50.8 2.3 %collective-permute-start.12 = (f32[128,128]{1,0:T(8,128)S(1)}, f32[128,128]{1,0:T(8,128)S(1)}, u32[]{:S(2)}, u32[]{:S(2)}) collective-permute-start(f32[128,128]{1,0:T(8,128)S(1)} %add.66), channel_id=1, source_target_pairs={{0,2},{1,3},{2,0},{3,1},{4,6},{5,7},{6,4},{7,5},{8,10},{9,11},{10,... | collective-permute-start | bytes 196616 | tf_op jit(solution)/shard_map/ppermute | solution.py:283
  53.8 2.1 %collective-permute-start.18 = (f32[128,128]{1,0:T(8,128)S(1)}, f32[128,128]{1,0:T(8,128)S(1)}, u32[]{:S(2)}, u32[]{:S(2)}) collective-permute-start(f32[128,128]{1,0:T(8,128)S(1)} %add.71), channel_id=1, source_target_pairs={{0,2},{1,3},{2,0},{3,1},{4,6},{5,7},{6,4},{7,5},{8,10},{9,11},{10,... | collective-permute-start | bytes 196616 | tf_op jit(solution)/shard_map/ppermute | solution.py:283
  55.8 2.3 %collective-permute-done.18 = f32[128,128]{1,0:T(8,128)S(1)} collective-permute-done((f32[128,128]{1,0:T(8,128)S(1)}, f32[128,128]{1,0:T(8,128)S(1)}, u32[]{:S(2)}, u32[]{:S(2)}) %collective-permute-start.18) | collective-permute-done | bytes 65568 | tf_op jit(solution)/shard_map/ppermute | solution.py:283
  58.2 1.2 %collective-permute-done.19 = f32[128,128]{1,0:T(8,128)S(1)} collective-permute-done((f32[128,128]{1,0:T(8,128)S(1)}, f32[128,128]{1,0:T(8,128)S(1)}, u32[]{:S(2)}, u32[]{:S(2)}) %collective-permute-start.19) | collective-permute-done | bytes 65568 | tf_op jit(solution)/shard_map/ppermute | solution.py:263
  59.5 1.2 %collective-permute-start.20 = (f32[128,128]{1,0:T(8,128)S(1)}, f32[128,128]{1,0:T(8,128)S(1)}, u32[]{:S(2)}, u32[]{:S(2)}) collective-permute-start(f32[128,128]{1,0:T(8,128)S(1)} %add.74), channel_id=1, source_target_pairs={{0,24},{8,16},{16,8},{24,0},{1,25},{9,17},{17,9},{25,1},{2,26},{10... | collective-permute-start | bytes 196616 | tf_op jit(solution)/shard_map/ppermute | solution.py:263
  60.7 2.9 %collective-permute-done.20 = f32[128,128]{1,0:T(8,128)S(1)} collective-permute-done((f32[128,128]{1,0:T(8,128)S(1)}, f32[128,128]{1,0:T(8,128)S(1)}, u32[]{:S(2)}, u32[]{:S(2)}) %collective-permute-start.20) | collective-permute-done | bytes 65568 | tf_op jit(solution)/shard_map/ppermute | solution.py:263
  63.6 1.9 %first.3 = (f32[80,128]{1,0:T(8,128)S(1)}, f32[80,128]{1,0:T(8,128)S(1)}, f32[80,128]{1,0:T(8,128)S(1)}) custom-call(f32[2,32,128,128]{3,2,1,0:T(8,128)S(1)} %get-tuple-element.43.whole.whole_t, bf16[2,48,256,128]{3,2,1,0:T(8,128)(2,1)S(1)} %get-tuple-element.44.upper.upper_t, bf16[2,24,256,128]{3,2,1,0:T(8,128)(2,1)S(1)} %get-tuple-element.45.lower.lower_t, ...), custom_call_target="tpu_custom_call" | custom-call | tf_op jit(solution)/shard_map/first/pallas_call | solution.py:405
  65.5 1.2 %collective-permute-start.23 = (f32[80,128]{1,0:T(8,128)S(1)}, f32[80,128]{1,0:T(8,128)S(1)}, u32[]{:S(2)}, u32[]{:S(2)}) collective-permute-start(f32[80,128]{1,0:T(8,128)S(1)} %get-tuple-element.61.order.refs_0_), channel_id=1, source_target_pairs={{0,24},{8,16},{16,8},{24,0},{1,25},{9,17},{17,9},{25,1},{2,26},{10... | collective-permute-start | bytes 122888 | tf_op jit(solution)/shard_map/ppermute | solution.py:263
  67.4 1.7 %collective-permute-done.23.refs_3_ = f32[80,128]{1,0:T(8,128)S(1)} collective-permute-done((f32[80,128]{1,0:T(8,128)S(1)}, f32[80,128]{1,0:T(8,128)S(1)}, u32[]{:S(2)}, u32[]{:S(2)}) %collective-permute-start.23) | collective-permute-done | bytes 40992 | tf_op jit(solution)/shard_map/ppermute | solution.py:263
  69.1 1.7 %collective-permute-done.22.refs_2_ = f32[80,128]{1,0:T(8,128)S(1)} collective-permute-done((f32[80,128]{1,0:T(8,128)S(1)}, f32[80,128]{1,0:T(8,128)S(1)}, u32[]{:S(2)}, u32[]{:S(2)}) %collective-permute-start.22) | collective-permute-done | bytes 40992 | tf_op jit(solution)/shard_map/ppermute | solution.py:263
  70.7 1.1 %second.4 = (f32[80,128]{1,0:T(8,128)S(1)}, f32[128,128]{1,0:T(8,128)S(1)}) custom-call(f32[2,32,128,128]{3,2,1,0:T(8,128)S(1)} %get-tuple-element.39.whole, bf16[2,48,256,128]{3,2,1,0:T(8,128)(2,1)S(1)} %get-tuple-element.41.upper, bf16[2,24,256,128]{3,2,1,0:T(8,128)(2,1)S(1)} %get-tuple-element.42.lower, bf16[128,80]{1,0:T(8,128)(2,1)S(1)} %get-tuple-element.48.col_hot_t, ...), custom_call_target="tpu_custom_call" | custom-call | tf_op jit(solution)/shard_map/second/pallas_call | solution.py:420
  71.8 2.0 %collective-permute-start.27 = (f32[128,128]{1,0:T(8,128)S(1)}, f32[128,128]{1,0:T(8,128)S(1)}, u32[]{:S(2)}, u32[]{:S(2)}) collective-permute-start(f32[128,128]{1,0:T(8,128)S(1)} %get-tuple-element.63.order), channel_id=1, source_target_pairs={{0,4},{1,5},{2,3},{3,2},{4,0},{5,1},{6,7},{7,6},{8,12},{9,13},{10,... | collective-permute-start | bytes 196616 | tf_op jit(solution)/shard_map/ppermute | solution.py:283
  73.8 1.1 %second.5 = (f32[80,128]{1,0:T(8,128)S(1)}, f32[128,128]{1,0:T(8,128)S(1)}) custom-call(f32[2,32,128,128]{3,2,1,0:T(8,128)S(1)} %get-tuple-element.39.whole, bf16[2,48,256,128]{3,2,1,0:T(8,128)(2,1)S(1)} %get-tuple-element.41.upper, bf16[2,24,256,128]{3,2,1,0:T(8,128)(2,1)S(1)} %get-tuple-element.42.lower, bf16[128,80]{1,0:T(8,128)(2,1)S(1)} %get-tuple-element.48.col_hot_t, ...), custom_call_target="tpu_custom_call" | custom-call | tf_op jit(solution)/shard_map/second/pallas_call | solution.py:420
  74.9 1.1 %collective-permute-start.24 = (f32[128,128]{1,0:T(8,128)S(1)}, f32[128,128]{1,0:T(8,128)S(1)}, u32[]{:S(2)}, u32[]{:S(2)}) collective-permute-start(f32[128,128]{1,0:T(8,128)S(1)} %get-tuple-element.65), channel_id=1, source_target_pairs={{0,4},{1,5},{2,3},{3,2},{4,0},{5,1},{6,7},{7,6},{8,12},{9,13},{10,... | collective-permute-start | bytes 196616 | tf_op jit(solution)/shard_map/ppermute | solution.py:283
  76.0 1.1 collective-permute-done.27
  77.8 2.9 %collective-permute-done.24 = f32[128,128]{1,0:T(8,128)S(1)} collective-permute-done((f32[128,128]{1,0:T(8,128)S(1)}, f32[128,128]{1,0:T(8,128)S(1)}, u32[]{:S(2)}, u32[]{:S(2)}) %collective-permute-start.24) | collective-permute-done | bytes 65568 | tf_op jit(solution)/shard_map/ppermute | solution.py:283
  80.7 1.1 %collective-permute-start.25 = (f32[128,128]{1,0:T(8,128)S(1)}, f32[128,128]{1,0:T(8,128)S(1)}, u32[]{:S(2)}, u32[]{:S(2)}) collective-permute-start(f32[128,128]{1,0:T(8,128)S(1)} %add.76), channel_id=1, source_target_pairs={{0,1},{1,0},{2,6},{3,7},{4,5},{5,4},{6,2},{7,3},{8,9},{9,8},{10,14... | collective-permute-start | bytes 196616 | tf_op jit(solution)/shard_map/ppermute | solution.py:283
  82.0 2.4 %collective-permute-start.29 = (f32[128,128]{1,0:T(8,128)S(1)}, f32[128,128]{1,0:T(8,128)S(1)}, u32[]{:S(2)}, u32[]{:S(2)}) collective-permute-start(f32[128,128]{1,0:T(8,128)S(1)} %add.79.refs_0_), channel_id=1, source_target_pairs={{0,2},{1,3},{2,0},{3,1},{4,6},{5,7},{6,4},{7,5},{8,10},{9,11},{10,... | collective-permute-start | bytes 196616 | tf_op jit(solution)/shard_map/ppermute | solution.py:283
  85.1 1.5 %collective-permute-done.29.refs_1_ = f32[128,128]{1,0:T(8,128)S(1)} collective-permute-done((f32[128,128]{1,0:T(8,128)S(1)}, f32[128,128]{1,0:T(8,128)S(1)}, u32[]{:S(2)}, u32[]{:S(2)}) %collective-permute-start.29) | collective-permute-done | bytes 65568 | tf_op jit(solution)/shard_map/ppermute | solution.py:283
  86.6 2.3 %third.6 = (f32[16,128]{1,0:T(8,128)S(1)}, f32[128,128]{1,0:T(8,128)S(1)}) custom-call(f32[2,32,128,128]{3,2,1,0:T(8,128)S(1)} %get-tuple-element.39.whole, bf16[2,48,256,128]{3,2,1,0:T(8,128)(2,1)S(1)} %get-tuple-element.41.upper, bf16[2,24,256,128]{3,2,1,0:T(8,128)(2,1)S(1)} %get-tuple-element.42.lower, ...), custom_call_target="tpu_custom_call" | custom-call | tf_op jit(solution)/shard_map/third/pallas_call | solution.py:440
  89.3 2.3 %third.7 = (f32[16,128]{1,0:T(8,128)S(1)}, f32[8,2,16,128]{3,2,1,0:T(8,128)S(1)}) custom-call(f32[2,32,128,128]{3,2,1,0:T(8,128)S(1)} %get-tuple-element.39.whole, bf16[2,48,256,128]{3,2,1,0:T(8,128)(2,1)S(1)} %get-tuple-element.41.upper, bf16[2,24,256,128]{3,2,1,0:T(8,128)(2,1)S(1)} %get-tuple-element.42.lower, ...), custom_call_target="tpu_custom_call" | custom-call | tf_op jit(solution)/shard_map/third/pallas_call | solution.py:440
  91.7 10.3 %all_to_all.5 = f32[8,2,16,128]{3,2,1,0:T(8,128)S(1)} all-to-all(f32[8,2,16,128]{3,2,1,0:T(8,128)S(1)} %get-tuple-element.73), channel_id=1, replica_groups=mesh['scen'=4,'vox'=8] {'vox'}, dimensions={0} | all-to-all | bytes 262144 | tf_op jit(solution)/shard_map/all_to_all | solution.py:464
  102.1 1.6 %collective-permute-start.31 = (f32[16,128]{1,0:T(8,128)S(1)}, f32[16,128]{1,0:T(8,128)S(1)}, u32[]{:S(2)}, u32[]{:S(2)}) collective-permute-start(f32[16,128]{1,0:T(8,128)S(1)} %fusion.3.order), channel_id=1, source_target_pairs={{0,16},{8,24},{16,0},{24,8},{1,17},{9,25},{17,1},{25,9},{2,18},{10... | collective-permute-start | bytes 24584 | tf_op jit(solution)/shard_map/ppermute | solution.py:263
  103.9 0.9 place.1
  (51 shorter events, 8.7 us)
Async XLA Ops:
  0.6 7.8 %collective-permute-start.2 = (f32[16,128]{1,0:T(8,128)}, f32[16,128]{1,0:T(8,128)S(1)}, u32[]{:S(2)}, u32[]{:S(2)}) collective-permute-start(f32[16,128]{1,0:T(8,128)} %bitcast.28), channel_id=1, source_target_pairs={{0,11},{1,10},{2,9},{3,8},{4,15},{5,14},{6,13},{7,12},{8,3},{9,2},... | collective-permute-start | bytes 24584 | tf_op jit(solution)/shard_map/ppermute | solution.py:307
  4.1 4.3 %collective-permute-start.1 = (f32[16,128]{1,0:T(8,128)}, f32[16,128]{1,0:T(8,128)S(1)}, u32[]{:S(2)}, u32[]{:S(2)}) collective-permute-start(f32[16,128]{1,0:T(8,128)} %bitcast.29), channel_id=1, source_target_pairs={{0,10},{1,11},{2,8},{3,9},{4,14},{5,15},{6,12},{7,13},{8,2},{9,3},... | collective-permute-start | bytes 24584 | tf_op jit(solution)/shard_map/ppermute | solution.py:307
  4.8 3.6 %collective-permute-start = (f32[16,128]{1,0:T(8,128)}, f32[16,128]{1,0:T(8,128)S(1)}, u32[]{:S(2)}, u32[]{:S(2)}) collective-permute-start(f32[16,128]{1,0:T(8,128)} %bitcast.30), channel_id=1, source_target_pairs={{0,9},{1,8},{2,11},{3,10},{4,13},{5,12},{6,15},{7,14},{8,1},{9,0},... | collective-permute-start | bytes 24584 | tf_op jit(solution)/shard_map/ppermute | solution.py:307
  8.4 6.3 %collective-permute-start.3 = (f32[64,128]{1,0:T(8,128)S(1)}, f32[64,128]{1,0:T(8,128)S(1)}, u32[]{:S(2)}, u32[]{:S(2)}) collective-permute-start(f32[64,128]{1,0:T(8,128)S(1)} %collect.1.order.mine), channel_id=1, source_target_pairs={{0,12},{1,13},{2,14},{3,15},{4,8},{5,9},{6,10},{7,11},{8,4},{9,5},... | collective-permute-start | bytes 98312 | tf_op jit(solution)/shard_map/ppermute | solution.py:307
  16.6 3.7 %collective-permute-start.6 = (f32[80,128]{1,0:T(8,128)S(1)}, f32[80,128]{1,0:T(8,128)S(1)}, u32[]{:S(2)}, u32[]{:S(2)}) collective-permute-start(f32[80,128]{1,0:T(8,128)S(1)} %get-tuple-element.50.order.refs_0_), channel_id=1, source_target_pairs={{0,24},{8,16},{16,8},{24,0},{1,25},{9,17},{17,9},{25,1},{2,26},{10... | collective-permute-start | bytes 122888 | tf_op jit(solution)/shard_map/ppermute | solution.py:263
  17.9 4.0 %collective-permute-start.5 = (f32[80,128]{1,0:T(8,128)S(1)}, f32[80,128]{1,0:T(8,128)S(1)}, u32[]{:S(2)}, u32[]{:S(2)}) collective-permute-start(f32[80,128]{1,0:T(8,128)S(1)} %get-tuple-element.50.order.refs_0_), channel_id=1, source_target_pairs={{0,16},{8,24},{16,0},{24,8},{1,17},{9,25},{17,1},{25,9},{2,18},{10... | collective-permute-start | bytes 122888 | tf_op jit(solution)/shard_map/ppermute | solution.py:263
  18.4 3.5 %collective-permute-start.4 = (f32[80,128]{1,0:T(8,128)S(1)}, f32[80,128]{1,0:T(8,128)S(1)}, u32[]{:S(2)}, u32[]{:S(2)}) collective-permute-start(f32[80,128]{1,0:T(8,128)S(1)} %get-tuple-element.50.order.refs_0_), channel_id=1, source_target_pairs={{0,8},{8,0},{16,24},{24,16},{1,9},{9,1},{17,25},{25,17},{2,10},{10... | collective-permute-start | bytes 122888 | tf_op jit(solution)/shard_map/ppermute | solution.py:263
  23.6 5.2 %collective-permute-start.7 = (f32[128,128]{1,0:T(8,128)S(1)}, f32[128,128]{1,0:T(8,128)S(1)}, u32[]{:S(2)}, u32[]{:S(2)}) collective-permute-start(f32[128,128]{1,0:T(8,128)S(1)} %get-tuple-element.53), channel_id=1, source_target_pairs={{0,4},{1,5},{2,3},{3,2},{4,0},{5,1},{6,7},{7,6},{8,12},{9,13},{10,... | collective-permute-start | bytes 196616 | tf_op jit(solution)/shard_map/ppermute | solution.py:283
  24.7 5.9 %collective-permute-start.13 = (f32[128,128]{1,0:T(8,128)S(1)}, f32[128,128]{1,0:T(8,128)S(1)}, u32[]{:S(2)}, u32[]{:S(2)}) collective-permute-start(f32[128,128]{1,0:T(8,128)S(1)} %get-tuple-element.57), channel_id=1, source_target_pairs={{0,4},{1,5},{2,3},{3,2},{4,0},{5,1},{6,7},{7,6},{8,12},{9,13},{10,... | collective-permute-start | bytes 196616 | tf_op jit(solution)/shard_map/ppermute | solution.py:283
  28.9 4.3 %collective-permute-start.8 = (f32[128,128]{1,0:T(8,128)S(1)}, f32[128,128]{1,0:T(8,128)S(1)}, u32[]{:S(2)}, u32[]{:S(2)}) collective-permute-start(f32[128,128]{1,0:T(8,128)S(1)} %add.63), channel_id=1, source_target_pairs={{0,1},{1,0},{2,6},{3,7},{4,5},{5,4},{6,2},{7,3},{8,9},{9,8},{10,14... | collective-permute-start | bytes 196616 | tf_op jit(solution)/shard_map/ppermute | solution.py:283
  30.6 5.4 %collective-permute-start.14 = (f32[128,128]{1,0:T(8,128)S(1)}, f32[128,128]{1,0:T(8,128)S(1)}, u32[]{:S(2)}, u32[]{:S(2)}) collective-permute-start(f32[128,128]{1,0:T(8,128)S(1)} %add.68), channel_id=1, source_target_pairs={{0,1},{1,0},{2,6},{3,7},{4,5},{5,4},{6,2},{7,3},{8,9},{9,8},{10,14... | collective-permute-start | bytes 196616 | tf_op jit(solution)/shard_map/ppermute | solution.py:283
  33.2 5.0 %collective-permute-start.9 = (f32[128,128]{1,0:T(8,128)S(1)}, f32[128,128]{1,0:T(8,128)S(1)}, u32[]{:S(2)}, u32[]{:S(2)}) collective-permute-start(f32[128,128]{1,0:T(8,128)S(1)} %add.64.refs_0_), channel_id=1, source_target_pairs={{0,2},{1,3},{2,0},{3,1},{4,6},{5,7},{6,4},{7,5},{8,10},{9,11},{10,... | collective-permute-start | bytes 196616 | tf_op jit(solution)/shard_map/ppermute | solution.py:283
  36.0 5.6 %collective-permute-start.15 = (f32[128,128]{1,0:T(8,128)S(1)}, f32[128,128]{1,0:T(8,128)S(1)}, u32[]{:S(2)}, u32[]{:S(2)}) collective-permute-start(f32[128,128]{1,0:T(8,128)S(1)} %add.69.refs_0_), channel_id=1, source_target_pairs={{0,2},{1,3},{2,0},{3,1},{4,6},{5,7},{6,4},{7,5},{8,10},{9,11},{10,... | collective-permute-start | bytes 196616 | tf_op jit(solution)/shard_map/ppermute | solution.py:283
  40.5 5.9 %collective-permute-start.10 = (f32[128,128]{1,0:T(8,128)S(1)}, f32[128,128]{1,0:T(8,128)S(1)}, u32[]{:S(2)}, u32[]{:S(2)}) collective-permute-start(f32[128,128]{1,0:T(8,128)S(1)} %get-tuple-element.56), channel_id=1, source_target_pairs={{0,4},{1,5},{2,3},{3,2},{4,0},{5,1},{6,7},{7,6},{8,12},{9,13},{10,... | collective-permute-start | bytes 196616 | tf_op jit(solution)/shard_map/ppermute | solution.py:283
  44.0 5.4 %collective-permute-start.16 = (f32[128,128]{1,0:T(8,128)S(1)}, f32[128,128]{1,0:T(8,128)S(1)}, u32[]{:S(2)}, u32[]{:S(2)}) collective-permute-start(f32[128,128]{1,0:T(8,128)S(1)} %get-tuple-element.60), channel_id=1, source_target_pairs={{0,4},{1,5},{2,3},{3,2},{4,0},{5,1},{6,7},{7,6},{8,12},{9,13},{10,... | collective-permute-start | bytes 196616 | tf_op jit(solution)/shard_map/ppermute | solution.py:283
  46.4 4.3 %collective-permute-start.11 = (f32[128,128]{1,0:T(8,128)S(1)}, f32[128,128]{1,0:T(8,128)S(1)}, u32[]{:S(2)}, u32[]{:S(2)}) collective-permute-start(f32[128,128]{1,0:T(8,128)S(1)} %add.65), channel_id=1, source_target_pairs={{0,1},{1,0},{2,6},{3,7},{4,5},{5,4},{6,2},{7,3},{8,9},{9,8},{10,14... | collective-permute-start | bytes 196616 | tf_op jit(solution)/shard_map/ppermute | solution.py:283
  49.4 4.3 %collective-permute-start.17 = (f32[128,128]{1,0:T(8,128)S(1)}, f32[128,128]{1,0:T(8,128)S(1)}, u32[]{:S(2)}, u32[]{:S(2)}) collective-permute-start(f32[128,128]{1,0:T(8,128)S(1)} %add.70), channel_id=1, source_target_pairs={{0,1},{1,0},{2,6},{3,7},{4,5},{5,4},{6,2},{7,3},{8,9},{9,8},{10,14... | collective-permute-start | bytes 196616 | tf_op jit(solution)/shard_map/ppermute | solution.py:283
  50.8 5.1 %collective-permute-start.12 = (f32[128,128]{1,0:T(8,128)S(1)}, f32[128,128]{1,0:T(8,128)S(1)}, u32[]{:S(2)}, u32[]{:S(2)}) collective-permute-start(f32[128,128]{1,0:T(8,128)S(1)} %add.66), channel_id=1, source_target_pairs={{0,2},{1,3},{2,0},{3,1},{4,6},{5,7},{6,4},{7,5},{8,10},{9,11},{10,... | collective-permute-start | bytes 196616 | tf_op jit(solution)/shard_map/ppermute | solution.py:283
  53.8 4.3 %collective-permute-start.18 = (f32[128,128]{1,0:T(8,128)S(1)}, f32[128,128]{1,0:T(8,128)S(1)}, u32[]{:S(2)}, u32[]{:S(2)}) collective-permute-start(f32[128,128]{1,0:T(8,128)S(1)} %add.71), channel_id=1, source_target_pairs={{0,2},{1,3},{2,0},{3,1},{4,6},{5,7},{6,4},{7,5},{8,10},{9,11},{10,... | collective-permute-start | bytes 196616 | tf_op jit(solution)/shard_map/ppermute | solution.py:283
  58.1 1.3 %collective-permute-start.19 = (f32[128,128]{1,0:T(8,128)S(1)}, f32[128,128]{1,0:T(8,128)S(1)}, u32[]{:S(2)}, u32[]{:S(2)}) collective-permute-start(f32[128,128]{1,0:T(8,128)S(1)} %maximum_add_fusion), channel_id=1, source_target_pairs={{0,8},{8,0},{16,24},{24,16},{1,9},{9,1},{17,25},{25,17},{2,10},{10... | collective-permute-start | bytes 196616 | tf_op jit(solution)/shard_map/ppermute | solution.py:263
  59.5 4.1 %collective-permute-start.20 = (f32[128,128]{1,0:T(8,128)S(1)}, f32[128,128]{1,0:T(8,128)S(1)}, u32[]{:S(2)}, u32[]{:S(2)}) collective-permute-start(f32[128,128]{1,0:T(8,128)S(1)} %add.74), channel_id=1, source_target_pairs={{0,24},{8,16},{16,8},{24,0},{1,25},{9,17},{17,9},{25,1},{2,26},{10... | collective-permute-start | bytes 196616 | tf_op jit(solution)/shard_map/ppermute | solution.py:263
  65.5 3.6 %collective-permute-start.23 = (f32[80,128]{1,0:T(8,128)S(1)}, f32[80,128]{1,0:T(8,128)S(1)}, u32[]{:S(2)}, u32[]{:S(2)}) collective-permute-start(f32[80,128]{1,0:T(8,128)S(1)} %get-tuple-element.61.order.refs_0_), channel_id=1, source_target_pairs={{0,24},{8,16},{16,8},{24,0},{1,25},{9,17},{17,9},{25,1},{2,26},{10... | collective-permute-start | bytes 122888 | tf_op jit(solution)/shard_map/ppermute | solution.py:263
  66.7 4.0 %collective-permute-start.22 = (f32[80,128]{1,0:T(8,128)S(1)}, f32[80,128]{1,0:T(8,128)S(1)}, u32[]{:S(2)}, u32[]{:S(2)}) collective-permute-start(f32[80,128]{1,0:T(8,128)S(1)} %get-tuple-element.61.order.refs_0_), channel_id=1, source_target_pairs={{0,16},{8,24},{16,0},{24,8},{1,17},{9,25},{17,1},{25,9},{2,18},{10... | collective-permute-start | bytes 122888 | tf_op jit(solution)/shard_map/ppermute | solution.py:263
  67.3 3.4 %collective-permute-start.21 = (f32[80,128]{1,0:T(8,128)S(1)}, f32[80,128]{1,0:T(8,128)S(1)}, u32[]{:S(2)}, u32[]{:S(2)}) collective-permute-start(f32[80,128]{1,0:T(8,128)S(1)} %get-tuple-element.61.order.refs_0_), channel_id=1, source_target_pairs={{0,8},{8,0},{16,24},{24,16},{1,9},{9,1},{17,25},{25,17},{2,10},{10... | collective-permute-start | bytes 122888 | tf_op jit(solution)/shard_map/ppermute | solution.py:263
  71.8 5.2 %collective-permute-start.27 = (f32[128,128]{1,0:T(8,128)S(1)}, f32[128,128]{1,0:T(8,128)S(1)}, u32[]{:S(2)}, u32[]{:S(2)}) collective-permute-start(f32[128,128]{1,0:T(8,128)S(1)} %get-tuple-element.63.order), channel_id=1, source_target_pairs={{0,4},{1,5},{2,3},{3,2},{4,0},{5,1},{6,7},{7,6},{8,12},{9,13},{10,... | collective-permute-start | bytes 196616 | tf_op jit(solution)/shard_map/ppermute | solution.py:283
  74.9 5.7 %collective-permute-start.24 = (f32[128,128]{1,0:T(8,128)S(1)}, f32[128,128]{1,0:T(8,128)S(1)}, u32[]{:S(2)}, u32[]{:S(2)}) collective-permute-start(f32[128,128]{1,0:T(8,128)S(1)} %get-tuple-element.65), channel_id=1, source_target_pairs={{0,4},{1,5},{2,3},{3,2},{4,0},{5,1},{6,7},{7,6},{8,12},{9,13},{10,... | collective-permute-start | bytes 196616 | tf_op jit(solution)/shard_map/ppermute | solution.py:283
  77.1 4.9 %collective-permute-start.28 = (f32[128,128]{1,0:T(8,128)S(1)}, f32[128,128]{1,0:T(8,128)S(1)}, u32[]{:S(2)}, u32[]{:S(2)}) collective-permute-start(f32[128,128]{1,0:T(8,128)S(1)} %add.78), channel_id=1, source_target_pairs={{0,1},{1,0},{2,6},{3,7},{4,5},{5,4},{6,2},{7,3},{8,9},{9,8},{10,14... | collective-permute-start | bytes 196616 | tf_op jit(solution)/shard_map/ppermute | solution.py:283
  80.7 4.3 %collective-permute-start.25 = (f32[128,128]{1,0:T(8,128)S(1)}, f32[128,128]{1,0:T(8,128)S(1)}, u32[]{:S(2)}, u32[]{:S(2)}) collective-permute-start(f32[128,128]{1,0:T(8,128)S(1)} %add.76), channel_id=1, source_target_pairs={{0,1},{1,0},{2,6},{3,7},{4,5},{5,4},{6,2},{7,3},{8,9},{9,8},{10,14... | collective-permute-start | bytes 196616 | tf_op jit(solution)/shard_map/ppermute | solution.py:283
  82.0 4.6 %collective-permute-start.29 = (f32[128,128]{1,0:T(8,128)S(1)}, f32[128,128]{1,0:T(8,128)S(1)}, u32[]{:S(2)}, u32[]{:S(2)}) collective-permute-start(f32[128,128]{1,0:T(8,128)S(1)} %add.79.refs_0_), channel_id=1, source_target_pairs={{0,2},{1,3},{2,0},{3,1},{4,6},{5,7},{6,4},{7,5},{8,10},{9,11},{10,... | collective-permute-start | bytes 196616 | tf_op jit(solution)/shard_map/ppermute | solution.py:283
  85.0 4.3 %collective-permute-start.26 = (f32[128,128]{1,0:T(8,128)S(1)}, f32[128,128]{1,0:T(8,128)S(1)}, u32[]{:S(2)}, u32[]{:S(2)}) collective-permute-start(f32[128,128]{1,0:T(8,128)S(1)} %add.77.refs_0_), channel_id=1, source_target_pairs={{0,2},{1,3},{2,0},{3,1},{4,6},{5,7},{6,4},{7,5},{8,10},{9,11},{10,... | collective-permute-start | bytes 196616 | tf_op jit(solution)/shard_map/ppermute | solution.py:283
  102.0 3.2 %collective-permute-start.32 = (f32[16,128]{1,0:T(8,128)S(1)}, f32[16,128]{1,0:T(8,128)S(1)}, u32[]{:S(2)}, u32[]{:S(2)}) collective-permute-start(f32[16,128]{1,0:T(8,128)S(1)} %fusion.3.order), channel_id=1, source_target_pairs={{0,24},{8,16},{16,8},{24,0},{1,25},{9,17},{17,9},{25,1},{2,26},{10... | collective-permute-start | bytes 24584 | tf_op jit(solution)/shard_map/ppermute | solution.py:263
  102.1 3.7 %collective-permute-start.31 = (f32[16,128]{1,0:T(8,128)S(1)}, f32[16,128]{1,0:T(8,128)S(1)}, u32[]{:S(2)}, u32[]{:S(2)}) collective-permute-start(f32[16,128]{1,0:T(8,128)S(1)} %fusion.3.order), channel_id=1, source_target_pairs={{0,16},{8,24},{16,0},{24,8},{1,17},{9,25},{17,1},{25,9},{2,18},{10... | collective-permute-start | bytes 24584 | tf_op jit(solution)/shard_map/ppermute | solution.py:263
  103.6 2.1 %collective-permute-start.30 = (f32[16,128]{1,0:T(8,128)S(1)}, f32[16,128]{1,0:T(8,128)S(1)}, u32[]{:S(2)}, u32[]{:S(2)}) collective-permute-start(f32[16,128]{1,0:T(8,128)S(1)} %fusion.3.order), channel_id=1, source_target_pairs={{0,8},{8,0},{16,24},{24,16},{1,9},{9,1},{17,25},{25,17},{2,10},{10... | collective-permute-start | bytes 24584 | tf_op jit(solution)/shard_map/ppermute | solution.py:263
